TPU v7x, 128 devices: a whole 4x4x4 slice. The times are simulated.
128 devices in a mesh: dp: 16 (over y_hi, z, core), mp: 8 (over x, y_lo).
Axes of the slice: x: 4, y: 4 (y_hi: 2, y_lo: 2; y = y_hi * 2 + y_lo), z: 4, core: 2. Of those that a mesh axis runs over, the one named last changes fastest.
Arguments:
- tokens: bfloat16 [16384, 2048], P('dp'), may hold values from -6 to 6
- doc_lengths: int32 [16, 4], P('dp'), may hold values from 1 to 512, 1024 in all within a row
- gain_one: float32 [2048], P('dp'), may hold values from 0.5 to 1.5
- bias_one: float32 [2048], P('dp'), may hold values from -3 to 3
- w_qkv: float32 [2048, 3, 2048], P('dp', None, 'mp'), may hold values from -0.125 to 0.125
- w_out: float32 [2048, 2048], P('dp', 'mp'), may hold values from -0.75 to 0.75
- gain_two: float32 [2048], P('dp'), may hold values from 0.5 to 1.5
- bias_two: float32 [2048], P('dp'), may hold values from -3 to 3
- w_up: float32 [2048, 8192], P('dp', 'mp'), may hold values from -0.125 to 0.125
- w_down: float32 [2048, 8192], P('dp', 'mp'), may hold values from -0.1875 to 0.1875
- cotangent: bfloat16 [16384, 2048], P('dp'), may hold values from -6 to 6
Outputs:
- output: bfloat16 [16384, 2048], P('dp')
- input_grad: float32 [16384, 2048], P('dp')
- grad_gain_one: float32 [2048], P('dp')
- grad_bias_one: float32 [2048], P('dp')
- grad_qkv: float32 [2048, 3, 2048], P('dp', None, 'mp')
- grad_out: float32 [2048, 2048], P('dp', 'mp')
- grad_gain_two: float32 [2048], P('dp')
- grad_bias_two: float32 [2048], P('dp')
- grad_up: float32 [2048, 8192], P('dp', 'mp')
- grad_down: float32 [2048, 8192], P('dp', 'mp')
Inputs may be any that keep to these rules, and one draw needn't show every extreme that they name: `doc_lengths`: the lengths of each row sum to 1024, and in each row the longest document has exactly 512 tokens.
All inputs are finite; a program needn't handle non-finite values.
Results may differ from a plain program's by a relative error of at most 0.013.
The roundings to bfloat16 on the way count: a program that leaves them out, or rounds other values in their place, can miss the bound.
Values may be sent and summed in bfloat16 or wider, within the bound.
No kernel may reach another device: no remote copies, remote signals or barrier semaphores. Data moves between devices by JAX's collectives and lax.ppermute only.
A program may use at most 192 MiB of HBM per device.

v0:
```python
import jax
import jax.numpy as jnp
from jax import lax
from jax.sharding import PartitionSpec as P

HEAD_SIZE = 128


eps = 1e-05


def shortened(array):

    def short(part):
        return part.astype(jnp.bfloat16) if part.dtype == jnp.float32 else part

    return jax.tree.map(short, array)


def normalize(values):
    center = values - jnp.mean(values, axis=-1, keepdims=True)
    inverse_std = lax.rsqrt(jnp.mean(center * center, axis=-1, keepdims=True) + eps)
    return (center * inverse_std, inverse_std)


def norm_back(grad_norm, normed, inverse_std, gain):
    scaled = grad_norm * gain
    return inverse_std * (
        scaled
        - jnp.mean(scaled, axis=-1, keepdims=True)
        - normed * jnp.mean(scaled * normed, axis=-1, keepdims=True)
    )


def block_scores(query_block, keys, doc_index, begin, block_rows, scale):
    scores = (
        jnp.einsum("qhe,khe->hqk", query_block, keys, preferred_element_type=jnp.float32) * scale
    )
    seq_len = keys.shape[0]
    places = jnp.arange(seq_len, dtype=jnp.int32)
    query_places = begin + jnp.arange(block_rows, dtype=jnp.int32)
    query_docs = lax.dynamic_slice_in_dim(doc_index, begin, block_rows, 0)
    allowed = (query_docs[:, None] == doc_index[None, :]) & (
        places[None, :] <= query_places[:, None]
    )
    return jnp.where(allowed[None], scores, jnp.float32(-1e30))


def local(
    tokens,
    doc_lengths,
    gain_one,
    bias_one,
    w_qkv,
    w_out,
    gain_two,
    bias_two,
    w_up,
    w_down,
    cotangent,
):
    masters = (gain_one, bias_one, gain_two, bias_two, w_qkv, w_out, w_up, w_down)
    narrow = tuple((piece.astype(jnp.bfloat16) for piece in masters))
    gathered = jax.tree.map(
        lambda part, own: part.astype(own.dtype),
        lax.all_gather(shortened(narrow), "dp", axis=0, tiled=True),
        narrow,
    )
    gain_a, bias_a, gain_b, bias_b, qkv_weight, out_weight, up_weight, down_weight = gathered
    seq_len = tokens.shape[0]
    local_width = qkv_weight.shape[2]
    local_heads = local_width // HEAD_SIZE
    block_rows = min(512, seq_len)
    scale = 1.0 / jnp.sqrt(jnp.float32(HEAD_SIZE))
    ends = jnp.cumsum(doc_lengths[0])
    positions = jnp.arange(seq_len, dtype=jnp.int32)
    doc_index = jnp.sum((positions[:, None] >= ends[None, :]).astype(jnp.int32), axis=1)
    inputs = tokens.astype(jnp.float32)
    normed_one, inverse_one = normalize(inputs)
    first = (normed_one * gain_a.astype(jnp.float32) + bias_a.astype(jnp.float32)).astype(
        jnp.bfloat16
    )
    mixed = jnp.einsum("td,dcf->tcf", first, qkv_weight, preferred_element_type=jnp.float32).astype(
        jnp.bfloat16
    )
    queries = mixed[:, 0].reshape(seq_len, local_heads, HEAD_SIZE)
    keys = mixed[:, 1].reshape(seq_len, local_heads, HEAD_SIZE)
    values = mixed[:, 2].reshape(seq_len, local_heads, HEAD_SIZE)
    attended_blocks = []
    lse_blocks = []
    for begin in range(0, seq_len, block_rows):
        query_block = queries[begin : begin + block_rows]
        scores = block_scores(query_block, keys, doc_index, begin, block_rows, scale)
        largest = jnp.max(scores, axis=-1, keepdims=True)
        expo = jnp.exp(scores - largest)
        totals = jnp.sum(expo, axis=-1, keepdims=True)
        probs = (expo / totals).astype(jnp.bfloat16)
        lse_blocks.append((largest + jnp.log(totals))[..., 0])
        attended_blocks.append(
            jnp.einsum("hqk,khe->qhe", probs, values, preferred_element_type=jnp.float32)
        )
    attended = (
        jnp.concatenate(attended_blocks, axis=0).reshape(seq_len, local_width).astype(jnp.bfloat16)
    )
    log_totals = jnp.concatenate(lse_blocks, axis=1)
    attn_terms = jnp.einsum("tf,df->td", attended, out_weight, preferred_element_type=jnp.float32)
    branch = lax.psum(attn_terms, "mp")
    middle = inputs + branch
    normed_two, inverse_two = normalize(middle)
    second = (normed_two * gain_b.astype(jnp.float32) + bias_b.astype(jnp.float32)).astype(
        jnp.bfloat16
    )
    hidden = jnp.einsum("td,df->tf", second, up_weight, preferred_element_type=jnp.float32)

    def gelu_tanh(values_in):
        return jax.nn.gelu(values_in, approximate=True)

    active_f, gelu_pull = jax.vjp(gelu_tanh, hidden)
    active = active_f.astype(jnp.bfloat16)
    down_terms = jnp.einsum("tf,df->td", active, down_weight, preferred_element_type=jnp.float32)
    branch_two = lax.psum(down_terms, "mp")
    output_full = middle + branch_two
    regathered = jax.tree.map(
        lambda part, own: part.astype(own.dtype),
        lax.all_gather(shortened(narrow), "dp", axis=0, tiled=True),
        narrow,
    )
    gain_a, bias_a, gain_b, bias_b, qkv_weight, out_weight, up_weight, down_weight = regathered
    grad_output = cotangent.astype(jnp.float32)
    grad_active = jnp.einsum(
        "td,df->tf", cotangent, down_weight, preferred_element_type=jnp.float32
    )
    grad_down_local = jnp.einsum("td,tf->df", cotangent, active, preferred_element_type=jnp.float32)
    grad_hidden = gelu_pull(grad_active)[0].astype(jnp.bfloat16)
    grad_up_local = jnp.einsum("td,tf->df", second, grad_hidden, preferred_element_type=jnp.float32)
    second_terms = jnp.einsum(
        "tf,df->td", grad_hidden, up_weight, preferred_element_type=jnp.float32
    )
    grad_second = lax.psum(second_terms, "mp")
    grad_gain_b = jnp.sum(grad_second * normed_two, axis=0)
    grad_bias_b = jnp.sum(grad_second, axis=0)
    grad_middle = grad_output + norm_back(
        grad_second, normed_two, inverse_two, gain_b.astype(jnp.float32)
    )
    grad_branch = grad_middle.astype(jnp.bfloat16)
    grad_out_local = jnp.einsum(
        "td,tf->df", grad_branch, attended, preferred_element_type=jnp.float32
    )
    grad_attended = jnp.einsum(
        "td,df->tf", grad_branch, out_weight, preferred_element_type=jnp.float32
    ).astype(jnp.bfloat16)
    grad_att_heads = grad_attended.reshape(seq_len, local_heads, HEAD_SIZE)
    grad_query_blocks = []
    grad_keys = jnp.zeros((seq_len, local_heads, HEAD_SIZE), jnp.float32)
    grad_values = jnp.zeros((seq_len, local_heads, HEAD_SIZE), jnp.float32)
    for begin in range(0, seq_len, block_rows):
        query_block = queries[begin : begin + block_rows]
        scores = block_scores(query_block, keys, doc_index, begin, block_rows, scale)
        probs = jnp.exp(scores - log_totals[:, begin : begin + block_rows, None])
        grad_block = grad_att_heads[begin : begin + block_rows]
        grad_probs = jnp.einsum(
            "qhe,khe->hqk", grad_block, values, preferred_element_type=jnp.float32
        )
        inner = jnp.sum(probs * grad_probs, axis=-1, keepdims=True)
        grad_scores = (probs * (grad_probs - inner)).astype(jnp.bfloat16)
        grad_query_blocks.append(
            jnp.einsum("hqk,khe->qhe", grad_scores, keys, preferred_element_type=jnp.float32)
            * scale
        )
        grad_keys = (
            grad_keys
            + jnp.einsum(
                "hqk,qhe->khe", grad_scores, query_block, preferred_element_type=jnp.float32
            )
            * scale
        )
        grad_values = grad_values + jnp.einsum(
            "hqk,qhe->khe",
            probs.astype(jnp.bfloat16),
            grad_block,
            preferred_element_type=jnp.float32,
        )
    grad_queries = jnp.concatenate(grad_query_blocks, axis=0)
    grad_mixed = jnp.stack(
        (
            grad_queries.reshape(seq_len, local_width),
            grad_keys.reshape(seq_len, local_width),
            grad_values.reshape(seq_len, local_width),
        ),
        axis=1,
    ).astype(jnp.bfloat16)
    grad_qkv_local = jnp.einsum(
        "td,tcf->dcf", first, grad_mixed, preferred_element_type=jnp.float32
    )
    first_terms = jnp.einsum(
        "tcf,dcf->td", grad_mixed, qkv_weight, preferred_element_type=jnp.float32
    )
    grad_first = lax.psum(first_terms, "mp")
    grad_gain_a = jnp.sum(grad_first * normed_one, axis=0)
    grad_bias_a = jnp.sum(grad_first, axis=0)
    input_grad = grad_middle + norm_back(
        grad_first, normed_one, inverse_one, gain_a.astype(jnp.float32)
    )
    output = output_full.astype(jnp.bfloat16)
    summed = (
        lax.psum_scatter(grad_gain_a, "dp", scatter_dimension=0, tiled=True),
        lax.psum_scatter(grad_bias_a, "dp", scatter_dimension=0, tiled=True),
        lax.psum_scatter(grad_gain_b, "dp", scatter_dimension=0, tiled=True),
        lax.psum_scatter(grad_bias_b, "dp", scatter_dimension=0, tiled=True),
        lax.psum_scatter(grad_qkv_local, "dp", scatter_dimension=0, tiled=True),
        lax.psum_scatter(grad_out_local, "dp", scatter_dimension=0, tiled=True),
        lax.psum_scatter(grad_up_local, "dp", scatter_dimension=0, tiled=True),
        lax.psum_scatter(grad_down_local, "dp", scatter_dimension=0, tiled=True),
    )
    return (
        output,
        input_grad,
        summed[0],
        summed[1],
        summed[4],
        summed[5],
        summed[2],
        summed[3],
        summed[6],
        summed[7],
    )


def solution(mesh):
    return jax.shard_map(
        local,
        mesh=mesh,
        in_specs=(
            P("dp", None),
            P("dp", None),
            P("dp"),
            P("dp"),
            P("dp", None, "mp"),
            P("dp", "mp"),
            P("dp"),
            P("dp"),
            P("dp", "mp"),
            P("dp", "mp"),
            P("dp", None),
        ),
        out_specs=(
            P("dp", None),
            P("dp", None),
            P("dp"),
            P("dp"),
            P("dp", None, "mp"),
            P("dp", "mp"),
            P("dp"),
            P("dp"),
            P("dp", "mp"),
            P("dp", "mp"),
        ),
        check_vma=False,
    )
```

profile of v0, /device:TPU:2, one launch (start us, length us, event | category | flops | bytes accessed | tf_op | source)
XLA Modules:
  0.0 1988.6 jit_solution(6314011263899943825)
XLA Ops:
  7.2 1.8 copy.51
  9.1 1.5 convert_element_type.106
  10.7 1.8 convert_element_type.114
  13.2 25.5 %all-gather.1 = bf16[16,1,128]{2,1,0:T(2,128)(2,1)S(1)} all-gather(bf16[1,1,128]{2,1,0:T(2,128)(2,1)S(1)} %convert_bitcast_fusion.2), channel_id=1, replica_groups=mesh['dp'=16,'mp'=8] {'dp'}, dimensions={0}, use_global_device_ids=true | all-gather | bytes 4352 | tf_op jit(solution)/shard_map/all_gather | solution.py:66
  39.4 19.1 all-gather
  59.4 3.0 convert_reduce_fusion
  62.8 1.2 fusion.13
  64.0 1.4 fusion.36
  65.4 6.8 convolution_convert_fusion
  72.4 1.2 fusion.70
  73.6 1.1 fusion.23
  74.7 1.2 fusion.71
  75.9 1.1 fusion.22
  77.0 1.1 fusion.61
  78.2 1.1 fusion.60
  79.4 31.6 %all-gather.11.cloned.1.call-done = bf16[2048,256]{1,0:T(8,128)(2,1)} async-done(((bf16[128,256]{1,0:T(8,128)(2,1)}), bf16[2048,256]{1,0:T(8,128)(2,1)}) %all-gather.11.cloned.1.call-update) | async-done | bytes 1048592 | tf_op jit(solution)/shard_map/all_gather | solution.py:66
  110.9 5.9 fusion.73
  117.0 1.0 copy-done.21
  118.7 21.2 %all-gather.3 = bf16[16,1,128]{2,1,0:T(2,128)(2,1)S(1)} all-gather(bf16[1,1,128]{2,1,0:T(2,128)(2,1)S(1)} %convert_bitcast_fusion), channel_id=1, replica_groups=mesh['dp'=16,'mp'=8] {'dp'}, dimensions={0}, use_global_device_ids=true | all-gather | bytes 4352 | tf_op jit(solution)/shard_map/all_gather | solution.py:66
  139.9 19.4 all-gather.2
  159.3 8.8 all-gather.15.cloned.1.call-done
  168.1 10.1 fusion.74
  178.2 330.5 %all-reduce.10.cloned.1.call-done = f32[1024,2048]{1,0:T(8,128)} async-done(((f32[1024,2048]{1,0:T(8,128)}), f32[1024,2048]{1,0:T(8,128)}) %all-reduce.10.cloned.1.call-update) | async-done | bytes 8388624 | tf_op jit(solution)/shard_map/psum | solution.py:107
  508.8 5.5 fusion.65
  514.3 1.0 multiply_reduce_fusion.2
  515.2 2.4 copy-done
  517.6 54.3 %all-gather.13.cloned.1.call-done = bf16[2048,1024]{1,0:T(8,128)(2,1)} async-done(((bf16[128,1024]{1,0:T(8,128)(2,1)}), bf16[2048,1024]{1,0:T(8,128)(2,1)}) %all-gather.13.cloned.1.call-update) | async-done | bytes 4194320 | tf_op jit(solution)/shard_map/all_gather | solution.py:66
  571.9 14.1 fusion.20
  586.1 1.3 copy-done.28
  587.4 6.7 fusion.75
  594.6 11.6 convolution_bitcast_fusion
  606.4 11.5 fusion.64
  617.9 314.1 %all-reduce.12.cloned.1.call-done = f32[1024,2048]{1,0:T(8,128)} async-done(((f32[1024,2048]{1,0:T(8,128)}), f32[1024,2048]{1,0:T(8,128)}) %all-reduce.12.cloned.1.call-update) | async-done | bytes 8388624 | tf_op jit(solution)/shard_map/psum | solution.py:139
  931.9 7.9 multiply_reduce_fusion
  940.2 1.2 copy-done.16
  941.4 5.3 multiply_add_fusion
  946.7 1.3 fusion.44
  948.0 3.0 copy-done.1
  951.1 1.0 copy-done.3
  952.1 0.9 fusion.26
  953.1 1.0 copy-done.6
  954.1 1.7 fusion.48
  955.8 2.1 copy.62
  957.9 4.0 multiply_reduce_fusion.6
  963.9 0.9 copy-done.4
  965.0 1.3 multiply_reduce_fusion.5
  966.3 0.9 multiply_convert_fusion
  967.2 1.3 copy-done.11
  969.4 0.9 pad_maximum_fusion.4
  970.2 2.0 copy.60
  972.7 1.1 copy-done.12
  975.1 7.6 convolution_bitcast_fusion.1
  982.8 6.0 fusion.31
  988.9 12.2 fusion.72
  1001.4 9.2 fusion.55
  1012.5 31.0 %reduce-scatter.11.cloned.1.call-done = f32[128,1024]{0,1:T(8,128)} async-done(((f32[2048,1024]{0,1:T(8,128)}), f32[128,1024]{0,1:T(8,128)}) %reduce-scatter.11.cloned.1.call-update) | async-done | bytes 524304 | tf_op jit(solution)/shard_map/reduce_scatter | solution.py:213
  1043.5 2.0 copy.65
  1045.5 659.5 %all-reduce.14.cloned.1.call-done = (f32[1024,2048]{1,0:T(8,128)}, f32[1024,2048]{1,0:T(8,128)}) async-done(((f32[1024,2048]{1,0:T(8,128)}, f32[1024,2048]{1,0:T(8,128)}), (f32[1024,2048]{1,0:T(8,128)}, f32[1024,2048]{1,0:T(8,128)})) %all-reduce.14.cloned.1.call-update) | async-done | bytes 16777232 | tf_op jit(solution)/shard_map/psum | solution.py:121
  1705.1 6.5 fusion.12
  1711.6 68.6 %all-reduce.4 = (f32[2048]{0:T(1024)S(1)}, f32[2048]{0:T(1024)S(1)}, f32[2048]{0:T(1024)S(1)}, f32[2048]{0:T(1024)S(1)}) all-reduce(f32[2048]{0:T(1024)S(1)} %get-tuple-element.42, f32[2048]{0:T(1024)S(1)} %get-tuple-element.47, f32[2048]{0:T(1024)S(1)} %get-tuple-element.40, ...), channel_id=2, replica_groups=mesh['dp'=16,'mp'=8] {'dp'}, use_global_device_ids=true, to_apply=%region_21.22.clone | all-reduce | flops 8192 | bytes 65536
  1782.5 9.4 add_convert_fusion
  1791.9 12.1 fusion.11
  1804.0 84.0 %reduce-scatter.9.cloned.1.call-done = f32[128,1024]{1,0:T(8,128)} async-done(((f32[2048,1024]{1,0:T(8,128)}), f32[128,1024]{1,0:T(8,128)}) %reduce-scatter.9.cloned.1.call-update) | async-done | bytes 524304 | tf_op jit(solution)/shard_map/reduce_scatter | solution.py:212
  1888.0 93.9 %reduce-scatter.5.cloned.1.call-done = f32[128,3,256]{2,0,1:T(8,128)} async-done(((f32[2048,3,256]{2,0,1:T(8,128)}), f32[128,3,256]{2,0,1:T(8,128)}) %reduce-scatter.5.cloned.1.call-update) | async-done | bytes 393232 | tf_op jit(solution)/shard_map/reduce_scatter | solution.py:210
  (109 shorter events, 13.6 us)
Async XLA Ops:
  7.2 58.3 %all-gather.9.cloned.1.call-start = ((), (), s32[]{:S(2)}) async-start(), calls=%async_computation.4 | async-start | bytes 3342336 | tf_op jit(solution)/shard_map/all_gather | solution.py:66
  9.1 101.9 %all-gather.11.cloned.1.call-start = ((), (), s32[]{:S(2)}) async-start(), calls=%async_computation.5 | async-start | bytes 1114112 | tf_op jit(solution)/shard_map/all_gather | solution.py:66
  10.7 157.5 %all-gather.15.cloned.1.call-start = ((), (), s32[]{:S(2)}) async-start(), calls=%async_computation.8 | async-start | bytes 4456448 | tf_op jit(solution)/shard_map/all_gather | solution.py:66
  12.5 496.2 %all-reduce.10.cloned.1.call-start = ((), (), s32[]{:S(2)}) async-start(), calls=%async_computation.6 | async-start | bytes 16777216 | tf_op jit(solution)/shard_map/psum | solution.py:107
  59.3 3.4 copy-start.8
  72.3 2.4 copy-start.17
  72.4 885.5 %copy-start.13 = (bf16[1024,1,256]{0,2,1:T(8,128)(2,1)}, bf16[1024,1,256]{0,2,1:T(8,128)(2,1)S(1)}, u32[]{:S(2)}) copy-start(bf16[1024,1,256]{0,2,1:T(8,128)(2,1)S(1)} %get-tuple-element.59) | copy-start | bytes 1572868
  73.6 3.4 copy-start.2
  75.9 2.3 copy-start.5
  116.9 1.0 copy-start.21
  116.9 1.9 copy-start.25
  116.9 23.0 %copy-start.26 = (f32[128]{0:T(128)S(1)}, f32[128]{0:T(128)}, u32[]{:S(2)}) copy-start(f32[128]{0:T(128)} %param.17) | copy-start | bytes 1540
  116.9 455.0 %all-gather.13.cloned.1.call-start = ((), (), s32[]{:S(2)}) async-start(), calls=%async_computation.7 | async-start | bytes 4456448 | tf_op jit(solution)/shard_map/all_gather | solution.py:66
  118.7 813.3 %all-reduce.12.cloned.1.call-start = ((), (), s32[]{:S(2)}) async-start(), calls=%async_computation.9 | async-start | bytes 16777216 | tf_op jit(solution)/shard_map/psum | solution.py:139
  514.2 3.4 copy-start
  571.9 15.5 copy-start.24
  586.1 1.3 copy-start.28
  594.1 449.3 %reduce-scatter.11.cloned.1.call-start = ((), (), s32[]{:S(2)}) async-start(), calls=%async_computation.13 | async-start | bytes 8912896 | tf_op jit(solution)/shard_map/reduce_scatter | solution.py:213
  606.3 1098.8 %all-reduce.14.cloned.1.call-start = ((), (), s32[]{:S(2)}) async-start(), calls=%async_computation.14 | async-start | bytes 33554432 | tf_op jit(solution)/shard_map/psum | solution.py:121
  931.9 8.2 copy-start.10
  931.9 9.4 copy-start.16
  941.3 5.4 copy-start.15
  946.7 4.4 copy-start.1
  946.7 5.4 copy-start.3
  951.1 3.0 copy-start.6
  951.1 4.7 copy-start.19
  957.9 4.3 copy-start.7
  962.2 2.6 copy-start.4
  962.2 2.8 copy-start.14
  962.2 2.8 copy-start.20
  967.2 1.3 copy-start.11
  969.4 3.4 copy-start.18
  972.3 1.6 copy-start.12
  973.9 1.0 copy-start.22
  973.9 1.2 copy-start.23
  982.7 821.3 %reduce-scatter.7.cloned.1.call-start = ((), (), s32[]{:S(2)}) async-start(), calls=%async_computation.11 | async-start | bytes 2228224 | tf_op jit(solution)/shard_map/reduce_scatter | solution.py:211
  988.8 899.1 %reduce-scatter.9.cloned.1.call-start = ((), (), s32[]{:S(2)}) async-start(), calls=%async_computation.12 | async-start | bytes 8912896 | tf_op jit(solution)/shard_map/reduce_scatter | solution.py:212
  1001.1 980.8 %reduce-scatter.5.cloned.1.call-start = ((), (), s32[]{:S(2)}) async-start(), calls=%async_computation.10 | async-start | bytes 6684672 | tf_op jit(solution)/shard_map/reduce_scatter | solution.py:210
  1010.6 0.7 copy-start.27
  1782.5 9.4 copy-start.9
Sparse Core Ops, SparseCore 0:
  10.9 54.3 all-gather.8
  68.3 42.5 all-gather.10
  114.0 54.1 all-gather.14
  171.1 337.6 all-reduce.9
  511.7 60.2 all-gather.12
  594.3 337.6 all-reduce.11
  936.2 107.2 reduce-scatter.10
  1046.2 658.7 all-reduce.13
  1709.5 71.7 reduce-scatter.6
  1786.6 101.3 reduce-scatter.8
  1893.3 88.4 reduce-scatter.4
where the time goes:
time: 1990 us
  waiting for transfers between devices  1610 us (81%)
  blocking collectives  154 us (8%)
  matrix products  118 us (6%)
  other arithmetic  64.4 us (3%)
  local copies, waits for them, and re-layouts  28.1 us (1%)
    psum x1, waiting for transfers between devices, local(): branch_two = lax.psum(down_terms, 'mp')  660 us
    psum x1, waiting for transfers between devices, local(): branch = lax.psum(attn_terms, 'mp')  331 us
    psum x1, waiting for transfers between devices, local(): grad_second = lax.psum(second_terms, 'mp')  314 us
    all_gather x4, waiting for transfers between devices, local(): lax.all_gather(shortened(narrow), 'dp', axis=0, tiled=True)  94.7 us
    reduce_scatter x1, waiting for transfers between devices, local(): lax.psum_scatter(grad_qkv_local, 'dp', scatter_dimension=0, tiled=True)  93.9 us
    all_gather x4, blocking collectives, local(): lax.all_gather(shortened(narrow), 'dp', axis=0, tiled=True)  85.1 us
    reduce_scatter x1, waiting for transfers between devices, local(): lax.psum_scatter(grad_up_local, 'dp', scatter_dimension=0, tiled=True)  84 us
    unnamed x1, blocking collectives  68.6 us
  transfers between devices with their start and end apart: 11, of which 9 were waited for; matrix products, arithmetic and copies ran while one was open for 9% of the time, Pallas kernels for 0%

commit v1 on v0

v1 whole, which is shorter than its diff:
```python
import jax
import jax.numpy as jnp
from jax import lax
from jax.sharding import Mesh, PartitionSpec as P

HEAD_SIZE = 128
eps = 1e-05
bf16 = jnp.bfloat16
f32 = jnp.float32

NX, NYL, NZ, NYH, NC = 4, 2, 4, 2, 2
MP = ("x", "yl")
DP = ("yh", "z", "c")
CMP = ("c", "x", "yl")


def up(values):
    return values.astype(f32)


def normalize(values):
    center = values - jnp.mean(values, axis=-1, keepdims=True)
    inverse_std = lax.rsqrt(jnp.mean(center * center, axis=-1, keepdims=True) + eps)
    return (center * inverse_std, inverse_std)


def norm_back(grad_norm, normed, inverse_std, gain):
    scaled = grad_norm * gain
    return inverse_std * (
        scaled
        - jnp.mean(scaled, axis=-1, keepdims=True)
        - normed * jnp.mean(scaled * normed, axis=-1, keepdims=True)
    )


def to_xp(x, y):
    return (x + 1, y)


def to_xm(x, y):
    return (x - 1, y)


def to_y(x, y):
    return (x, y + 1)


def send(values, zero, one):
    pairs = []
    for c in range(NC):
        for x in range(NX):
            for y in range(NYL):
                tx, ty = (zero, one)[c](x, y)
                pairs.append(((c * NX + x) * NYL + y, (c * NX + tx % NX) * NYL + ty % NYL))
    return lax.ppermute(values, CMP, pairs)


def halves(values):
    middle = values.shape[0] // 2
    return values[:middle], values[middle:]


def gather_blocks(own):
    core = lax.axis_index("c")

    def pick(zero, one):
        return jnp.where(core == 0, zero, one)

    p1 = send(own, to_xp, to_xp)
    p2 = send(own, to_xm, to_xm)
    q = send(own, to_y, to_y)
    o1 = send(halves(p1)[0], to_xp, to_xp)
    o2 = send(halves(p2)[1], to_xm, to_xm)
    r1 = send(pick(p1, q), to_y, to_xp)
    r2 = send(pick(p2, q), to_y, to_xm)
    s1 = send(pick(o1, halves(r1)[0]), to_y, to_xp)
    s2 = send(pick(o2, halves(r2)[1]), to_y, to_xm)
    return {
        (0, 0): (own,),
        (1, 0): (p2,),
        (2, 0): (o1, o2),
        (3, 0): (p1,),
        (0, 1): (q,),
        (1, 1): (r2,),
        (2, 1): (s1, s2),
        (3, 1): (r1,),
    }


def scatter_sum(blocks):
    core = lax.axis_index("c")
    zero = jnp.where(core == 0, 1.0, 0.0).astype(f32)
    one = 1.0 - zero

    def add_half(block, piece, which, factor):
        first, second = halves(up(block))
        if which == 0:
            first = first + factor * up(piece)
        else:
            second = second + factor * up(piece)
        return jnp.concatenate([first, second], 0)

    h1, h2 = halves(blocks[2, 1])
    s1 = send(h1, to_y, to_xp)
    s2 = send(h2, to_y, to_xm)
    p = send(add_half(blocks[1, 1], s1, 0, one).astype(bf16), to_y, to_xp)
    q = send(add_half(blocks[3, 1], s2, 1, one).astype(bf16), to_y, to_xm)
    g1, g2 = halves(up(blocks[2, 0]))
    r1 = send((g1 + zero * up(s1)).astype(bf16), to_xp, to_xp)
    r2 = send((g2 + zero * up(s2)).astype(bf16), to_xm, to_xm)
    u = send((up(blocks[0, 1]) + one * (up(p) + up(q))).astype(bf16), to_y, to_y)
    t1 = send((add_half(blocks[1, 0], r1, 0, 1.0) + zero * up(p)).astype(bf16), to_xp, to_xp)
    t2 = send((add_half(blocks[3, 0], r2, 1, 1.0) + zero * up(q)).astype(bf16), to_xm, to_xm)
    return up(blocks[0, 0]) + up(t1) + up(t2) + up(u)


REL = [(dx, dy) for dy in range(NYL) for dx in range(NX)]


def to_relative(values):
    x, y = lax.axis_index("x"), lax.axis_index("yl")
    rows = values.shape[0] // (NX * NYL)
    parts = []
    for dx, dy in REL:
        block = ((x + dx) % NX) * NYL + (y + dy) % NYL
        parts.append(lax.dynamic_slice_in_dim(values, block * rows, rows, 0))
    return jnp.concatenate(parts, 0)


def to_row_order(values):
    x, y = lax.axis_index("x"), lax.axis_index("yl")
    rows = values.shape[0] // (NX * NYL)
    parts = []
    for bx in range(NX):
        for by in range(NYL):
            place = ((by - y) % NYL) * NX + (bx - x) % NX
            parts.append(lax.dynamic_slice_in_dim(values, place * rows, rows, 0))
    return jnp.concatenate(parts, 0)


def split_blocks(values):
    rows = values.shape[0] // len(REL)
    return {key: values[i * rows : (i + 1) * rows] for i, key in enumerate(REL)}


def join_blocks(blocks):
    return jnp.concatenate([piece for key in REL for piece in blocks[key]], 0)


def gather_direct(own):
    yh, z, core = lax.axis_index("yh"), lax.axis_index("z"), lax.axis_index("c")
    got = []
    for dy in range(NYH):
        for dz in range(NZ):
            if dy == 0 and dz == 0:
                got.append(own)
                continue
            pairs = [
                (((a + dy) % NYH) * NZ + (b + dz) % NZ, a * NZ + b)
                for a in range(NYH)
                for b in range(NZ)
            ]
            got.append(lax.ppermute(own, ("yh", "z"), pairs))
    mine = jnp.stack(got, 0)
    other = lax.ppermute(mine, "c", [(0, 1), (1, 0)])
    parts = []
    for a in range(NYH):
        for b in range(NZ):
            place = ((a - yh) % NYH) * NZ + (b - z) % NZ
            one = lax.dynamic_index_in_dim(mine, place, 0, keepdims=False)
            two = lax.dynamic_index_in_dim(other, place, 0, keepdims=False)
            parts.append(jnp.where(core == 0, one, two))
            parts.append(jnp.where(core == 0, two, one))
    return jnp.stack(parts, 0)


def scatter_dp(values):
    yh, z, core = lax.axis_index("yh"), lax.axis_index("z"), lax.axis_index("c")
    rows = values.shape[0] // (NYH * NZ * NC)
    parts = values.reshape(NYH, NZ, NC, rows, values.shape[1])

    def of_core(which):
        return lax.dynamic_index_in_dim(parts, which, 2, keepdims=False)

    swapped = lax.ppermute(of_core(1 - core), "c", [(0, 1), (1, 0)])
    both = (up(of_core(core)) + up(swapped)).astype(bf16)

    def of_z(dz):
        return lax.dynamic_index_in_dim(both, (z + dz) % NZ, 1, keepdims=False)

    total = up(of_z(0))
    for dz in (1, 3, 2):
        total = total + up(lax.ppermute(of_z(dz), "z", [(i, (i + dz) % NZ) for i in range(NZ)]))
    total = total.astype(bf16)
    away = lax.dynamic_index_in_dim(total, 1 - yh, 0, keepdims=False)
    home = lax.dynamic_index_in_dim(total, yh, 0, keepdims=False)
    return up(home) + up(lax.ppermute(away, "yh", [(0, 1), (1, 0)]))


def sum_vectors(vectors):
    count, width = vectors.shape
    slices = NYH * NZ * NC
    apart = vectors.reshape(count, slices, width // slices).transpose(1, 0, 2)
    got = lax.all_to_all(apart, DP, split_axis=0, concat_axis=0, tiled=True)
    part = jnp.sum(got, axis=0)
    copies = jnp.broadcast_to(part[None], (NX * NYL,) + part.shape)
    return jnp.sum(lax.all_to_all(copies, MP, split_axis=0, concat_axis=0, tiled=True), axis=0)


def block_scores(query_block, keys, doc_index, begin, block_rows, scale):
    scores = (
        jnp.einsum("qhe,khe->hqk", query_block, keys, preferred_element_type=f32) * scale
    )
    seq_len = keys.shape[0]
    places = jnp.arange(seq_len, dtype=jnp.int32)
    query_places = begin + jnp.arange(block_rows, dtype=jnp.int32)
    query_docs = lax.dynamic_slice_in_dim(doc_index, begin, block_rows, 0)
    allowed = (query_docs[:, None] == doc_index[None, :]) & (
        places[None, :] <= query_places[:, None]
    )
    return jnp.where(allowed[None], scores, f32(-1e30))


def attend(queries, keys, values, doc_index, scale):
    seq_len = queries.shape[0]
    block_rows = min(512, seq_len)
    out, lse = [], []
    for begin in range(0, seq_len, block_rows):
        scores = block_scores(
            queries[begin : begin + block_rows], keys, doc_index, begin, block_rows, scale
        )
        largest = jnp.max(scores, axis=-1, keepdims=True)
        expo = jnp.exp(scores - largest)
        totals = jnp.sum(expo, axis=-1, keepdims=True)
        probs = (expo / totals).astype(bf16)
        lse.append((largest + jnp.log(totals))[..., 0])
        out.append(jnp.einsum("hqk,khe->qhe", probs, values, preferred_element_type=f32))
    return jnp.concatenate(out, axis=0), jnp.concatenate(lse, axis=1)


def attend_back(queries, keys, values, lse, grad_out, doc_index, scale):
    seq_len = queries.shape[0]
    block_rows = min(512, seq_len)
    grad_queries = []
    grad_keys = jnp.zeros(keys.shape, f32)
    grad_values = jnp.zeros(keys.shape, f32)
    for begin in range(0, seq_len, block_rows):
        query_block = queries[begin : begin + block_rows]
        scores = block_scores(query_block, keys, doc_index, begin, block_rows, scale)
        probs = jnp.exp(scores - lse[:, begin : begin + block_rows, None])
        grad_block = grad_out[begin : begin + block_rows]
        grad_probs = jnp.einsum("qhe,khe->hqk", grad_block, values, preferred_element_type=f32)
        inner = jnp.sum(probs * grad_probs, axis=-1, keepdims=True)
        grad_scores = (probs * (grad_probs - inner)).astype(bf16)
        grad_queries.append(
            jnp.einsum("hqk,khe->qhe", grad_scores, keys, preferred_element_type=f32) * scale
        )
        grad_keys = (
            grad_keys
            + jnp.einsum("hqk,qhe->khe", grad_scores, query_block, preferred_element_type=f32)
            * scale
        )
        grad_values = grad_values + jnp.einsum(
            "hqk,qhe->khe", probs.astype(bf16), grad_block, preferred_element_type=f32
        )
    return jnp.concatenate(grad_queries, axis=0), grad_keys, grad_values


def local(
    tokens,
    doc_lengths,
    gain_one,
    bias_one,
    w_qkv,
    w_out,
    gain_two,
    bias_two,
    w_up,
    w_down,
    cotangent,
):
    seq_len, width = tokens.shape
    shard = w_qkv.shape[0]
    local_width = w_qkv.shape[2]
    local_heads = local_width // HEAD_SIZE
    rows = seq_len // (NX * NYL)
    x, y = lax.axis_index("x"), lax.axis_index("yl")
    my_rows = (x * NYL + y) * rows
    scale = 1.0 / jnp.sqrt(f32(HEAD_SIZE))

    small = jnp.stack([gain_one, bias_one, gain_two, bias_two], 0).astype(bf16)
    small = jnp.pad(small.reshape(1, -1), ((0, 15), (0, 0)))
    columns = max(3 * local_width, small.shape[1])
    packed = jnp.concatenate(
        [
            jnp.pad(
                w_qkv.reshape(shard, 3 * local_width).astype(bf16),
                ((0, 0), (0, columns - 3 * local_width)),
            ),
            jnp.pad(small, ((0, 0), (0, columns - small.shape[1]))),
        ],
        0,
    )
    first_full = gather_direct(packed)
    qkv_weight = first_full[:, :shard, : 3 * local_width].reshape(width, 3 * local_width)
    vectors = (
        first_full[:, shard, : 4 * shard].reshape(-1, 4, shard).transpose(1, 0, 2).reshape(4, width)
    )
    gain_a, bias_a, gain_b, bias_b = (up(vectors[i]) for i in range(4))
    up_weight = lax.all_gather(w_up.astype(bf16), DP, axis=0, tiled=True)
    down_weight = lax.all_gather(w_down.astype(bf16), DP, axis=0, tiled=True)
    out_weight = gather_direct(w_out.astype(bf16)).reshape(width, local_width)

    ends = jnp.cumsum(doc_lengths[0])
    positions = jnp.arange(seq_len, dtype=jnp.int32)
    doc_index = jnp.sum((positions[:, None] >= ends[None, :]).astype(jnp.int32), axis=1)

    normed_one, _ = normalize(up(tokens))
    first = (normed_one * gain_a + bias_a).astype(bf16)
    mixed = jnp.dot(first, qkv_weight, preferred_element_type=f32).astype(bf16)
    mixed = mixed.reshape(seq_len, 3, local_heads, HEAD_SIZE)
    queries, keys, values = mixed[:, 0], mixed[:, 1], mixed[:, 2]
    attended, lse = attend(queries, keys, values, doc_index, scale)
    attended = attended.reshape(seq_len, local_width).astype(bf16)
    attended = to_relative(attended)
    terms = jnp.einsum("tf,df->td", attended, out_weight, preferred_element_type=f32).astype(bf16)
    own_tokens = up(lax.dynamic_slice_in_dim(tokens, my_rows, rows, 0))
    own_cot = up(lax.dynamic_slice_in_dim(cotangent, my_rows, rows, 0))
    middle = own_tokens + scatter_sum(split_blocks(terms))

    normed_two, inverse_two = normalize(middle)
    second_own = (normed_two * gain_b + bias_b).astype(bf16)
    second = join_blocks(gather_blocks(second_own))
    cot_rel = to_relative(cotangent)
    grad_active = jnp.dot(cot_rel, down_weight, preferred_element_type=f32)
    hidden = jnp.dot(second, up_weight, preferred_element_type=f32)

    def gelu_tanh(values_in):
        return jax.nn.gelu(values_in, approximate=True)

    active_f, gelu_pull = jax.vjp(gelu_tanh, hidden)
    active = active_f.astype(bf16)
    grad_hidden = gelu_pull(grad_active)[0].astype(bf16)
    second_terms = jnp.einsum(
        "tf,df->td", grad_hidden, up_weight, preferred_element_type=f32
    ).astype(bf16)
    grad_second = scatter_sum(split_blocks(second_terms))
    down_terms = jnp.einsum(
        "tf,df->td", to_row_order(active), down_weight, preferred_element_type=f32
    ).astype(bf16)
    branch_two = lax.psum_scatter(down_terms, MP, scatter_dimension=0, tiled=True)
    output_own = (middle + up(branch_two)).astype(bf16)
    output = lax.all_gather(output_own, MP, axis=0, tiled=True)
    grad_down = scatter_dp(
        jnp.einsum("td,tf->df", cot_rel, active, preferred_element_type=f32).astype(bf16)
    )
    grad_up = scatter_dp(
        jnp.einsum("td,tf->df", second, grad_hidden, preferred_element_type=f32).astype(bf16)
    )

    vec_gain_b = jnp.sum(grad_second * normed_two, axis=0)
    vec_bias_b = jnp.sum(grad_second, axis=0)
    grad_middle = own_cot + norm_back(grad_second, normed_two, inverse_two, gain_b)
    grad_branch = join_blocks(gather_blocks(grad_middle.astype(bf16)))
    grad_out = scatter_dp(
        jnp.einsum("td,tf->df", grad_branch, attended, preferred_element_type=f32).astype(bf16)
    )
    grad_attended = jnp.dot(grad_branch, out_weight, preferred_element_type=f32).astype(bf16)
    grad_attended = to_row_order(grad_attended).reshape(seq_len, local_heads, HEAD_SIZE)
    grad_queries, grad_keys, grad_values = attend_back(
        queries, keys, values, lse, grad_attended, doc_index, scale
    )
    grad_mixed = jnp.concatenate(
        [v.reshape(seq_len, local_width) for v in (grad_queries, grad_keys, grad_values)], axis=1
    ).astype(bf16)
    first_terms = jnp.einsum(
        "tf,df->td", to_relative(grad_mixed), qkv_weight, preferred_element_type=f32
    ).astype(bf16)
    grad_first = scatter_sum(split_blocks(first_terms))
    grad_qkv = scatter_dp(
        jnp.einsum("td,tf->df", first, grad_mixed, preferred_element_type=f32).astype(bf16)
    ).reshape(shard, 3, local_width)

    own_normed, own_inverse = normalize(own_tokens)
    vec_gain_a = jnp.sum(grad_first * own_normed, axis=0)
    vec_bias_a = jnp.sum(grad_first, axis=0)
    grad_tokens = grad_middle + norm_back(grad_first, own_normed, own_inverse, gain_a)
    input_grad = up(to_row_order(join_blocks(gather_blocks(grad_tokens.astype(bf16)))))
    sums = sum_vectors(jnp.stack([vec_gain_a, vec_bias_a, vec_gain_b, vec_bias_b], 0))
    return (
        output,
        input_grad,
        sums[0],
        sums[1],
        grad_qkv,
        grad_out,
        sums[2],
        sums[3],
        grad_up,
        grad_down,
    )


def solution(mesh):
    fine = Mesh(mesh.devices.reshape(NYH, NZ, NC, NX, NYL), ("yh", "z", "c", "x", "yl"))
    return jax.shard_map(
        local,
        mesh=fine,
        in_specs=(
            P(DP, None),
            P(DP, None),
            P(DP),
            P(DP),
            P(DP, None, MP),
            P(DP, MP),
            P(DP),
            P(DP),
            P(DP, MP),
            P(DP, MP),
            P(DP, None),
        ),
        out_specs=(
            P(DP, None),
            P(DP, None),
            P(DP),
            P(DP),
            P(DP, None, MP),
            P(DP, MP),
            P(DP),
            P(DP),
            P(DP, MP),
            P(DP, MP),
        ),
        check_vma=False,
    )
```

time: 1990 us -> 729 us (0.37)
  waiting for transfers between devices: 1610 us -> 282 us
  blocking collectives: 154 us -> 0 us
  starting transfers between devices: 1.11 us -> 150 us
  local copies, waits for them, and re-layouts: 28.1 us -> 82.5 us
  other arithmetic: 64.4 us -> 98.5 us
  matrix products: 118 us -> 89.5 us
    psum x3 -> x0, waiting for transfers between devices: 1300 us -> none  [the longest x1 660 us: local(): branch_two = lax.psum(down_terms, 'mp')]
    ppermute x0 -> x90, waiting for transfers between devices: none -> 280 us  [the longest x54 226 us: send(): return lax.ppermute(values, CMP, pairs)]
    reduce_scatter x4 -> x1, waiting for transfers between devices: 209 us -> 0.01 us  [local(): lax.psum_scatter(down_terms, MP, scatter_dimension=0, tiled=True)]
    ppermute x0 -> x90, starting transfers between devices: none -> 137 us  [the longest x54 75.3 us: send(): return lax.ppermute(values, CMP, pairs)]
    all_gather x4 -> x3, waiting for transfers between devices: 94.7 us -> 0.01 us  [the longest x1 0.01 us: local(): down_weight = lax.all_gather(w_down.astype(bf16), DP, axis=0, tiled=True)]
    all_gather x4 -> x0, blocking collectives: 85.1 us -> none  [local(): lax.all_gather(shortened(narrow), 'dp', axis=0, tiled=True)]
    unnamed x1 -> x0, blocking collectives: 68.6 us -> none
    unnamed x4 -> x36, other arithmetic: 1.33 us -> 42.4 us
  transfers between devices with their start and end apart: 11 -> 96, of which waited for: 9 -> 47; matrix products, arithmetic and copies ran while one was open for 9% -> 33% of each run, Pallas kernels for 0% -> 0%
where the time goes in v1:
time: 729 us; the launch traced here: 718 us
  waiting for transfers between devices  282 us (39%)
  starting transfers between devices  150 us (21%)
  other arithmetic  98.5 us (14%)
  matrix products  89.5 us (12%)
  local copies, waits for them, and re-layouts  82.5 us (11%)
  between operations  16.1 us (2%)
    ppermute x54, waiting for transfers between devices, send(): return lax.ppermute(values, CMP, pairs)  226 us
    ppermute x54, starting transfers between devices, send(): return lax.ppermute(values, CMP, pairs)  75.3 us
    unnamed x161, local copies, waits for them, and re-layouts  55.9 us
    unnamed x36, other arithmetic  42.4 us
    ppermute x14, waiting for transfers between devices, gather_direct(): got.append(lax.ppermute(own, ('yh', 'z'), pairs))  33.4 us
    ppermute x14, starting transfers between devices, gather_direct(): got.append(lax.ppermute(own, ('yh', 'z'), pairs))  32.8 us
    ppermute x12, starting transfers between devices, scatter_dp(): lax.ppermute(of_z(dz), 'z', [(i, (i + dz) % NZ) for i in range(NZ)])  20.3 us
  transfers between devices with their start and end apart: 96, of which 47 were waited for; matrix products, arithmetic and copies ran while one was open for 33% of the time, Pallas kernels for 0%

profile of v1, /device:TPU:2, one launch (start us, length us, event | category | flops | bytes accessed | tf_op | source)
XLA Modules:
  0.0 718.4 jit_solution(7543021237580133295)
XLA Ops:
  8.8 4.0 collective-permute-start.8
  14.1 3.2 collective-permute-start.11
  31.7 5.0 collective-permute-start.13
  39.7 3.0 collective-permute-start
  47.2 3.2 collective-permute-start.3
  53.8 12.3 %collective-permute-done = bf16[144,768]{0,1:T(8,128)(2,1)S(1)} collective-permute-done((bf16[144,768]{0,1:T(8,128)(2,1)}, bf16[144,768]{0,1:T(8,128)(2,1)S(1)}, u32[]{:S(2)}, u32[]{:S(2)}) %collective-permute-start) | collective-permute-done | bytes 221216 | tf_op jit(solution)/shard_map/ppermute | solution.py:163
  66.2 8.3 %collective-permute-start.6 = (bf16[144,768]{0,1:T(8,128)(2,1)}, bf16[144,768]{0,1:T(8,128)(2,1)S(1)}, u32[]{:S(2)}, u32[]{:S(2)}) collective-permute-start(bf16[144,768]{0,1:T(8,128)(2,1)} %fusion.114), channel_id=1, source_target_pairs={{112,0},{64,16},{80,32},{96,48},{48,64},{0,80},{16,96},{32,112},{1... | collective-permute-start | bytes 663560 | tf_op jit(solution)/shard_map/ppermute | solution.py:163
  74.7 4.9 collective-permute-done.4
  79.5 11.8 %collective-permute-done.5 = bf16[144,768]{0,1:T(8,128)(2,1)S(1)} collective-permute-done((bf16[144,768]{0,1:T(8,128)(2,1)}, bf16[144,768]{0,1:T(8,128)(2,1)S(1)}, u32[]{:S(2)}, u32[]{:S(2)}) %collective-permute-start.5) | collective-permute-done | bytes 221216 | tf_op jit(solution)/shard_map/ppermute | solution.py:163
  91.4 4.4 collective-permute-done.6
  153.5 7.1 convolution_convert_fusion.8
  173.8 4.0 collective-permute-done.16
  185.2 5.0 collective-permute-done.21
  190.2 3.0 collective-permute-done.17
  205.6 4.4 collective-permute-done.19
  219.3 6.5 collective-permute-done.26
  233.2 3.5 collective-permute-done.28
  236.8 3.6 collective-permute-done.29
  247.1 7.0 collective-permute-done.31
  255.9 3.8 collective-permute-done.30
  263.3 3.1 collective-permute-done.33
  267.9 10.0 %fusion.134 = f32[1024,1024]{1,0:T(8,128)} fusion(bf16[1024,2048]{1,0:T(8,128)(2,1)} %dynamic-slice_dynamic-update-slice_fusion.8, bf16[2048,1024]{1,0:T(8,128)(2,1)} %all-gather.6.cloned.1.call-done), kind=kOutput, calls=%fused_computation.442 | convolution fusion | flops 4294967296 | bytes 12582912 | tf_op jit(solution)/shard_map/dot_general | solution.py:335
  277.9 12.9 %fusion.12 = (bf16[1024,1024]{1,0:T(8,128)(2,1)}, bf16[1024,1024]{1,0:T(8,128)(2,1)S(1)}) fusion(f32[1024,1024]{1,0:T(8,128)} %fusion.134, bf16[1024,2048]{1,0:T(8,128)(2,1)} %constant_dynamic-update-slice_fusion.32, bf16[2048,1024]{1,0:T(8,128)(2,1)} %all-gather.4.cloned.1.call-done), kind=kOutput, calls=%fused_computation.16 | convolution fusion | flops 4318035968 | bytes 16777216 | tf_op jit(solution)/shard_map/dot_general | solution.py:336
  293.0 6.2 convolution_convert_fusion.5
  299.6 7.4 %convolution_convert_fusion.4 = bf16[1024,2048]{1,0:T(8,128)(2,1)S(1)} fusion(bf16[1024,1024]{1,0:T(8,128)(2,1)} %get-tuple-element.104, bf16[2048,1024]{1,0:T(8,128)(2,1)} %all-gather.4.cloned.1.call-done), kind=kOutput, calls=%fused_computation.38 | convolution fusion | flops 4297064448 | bytes 10485760 | tf_op jit(solution)/shard_map/tf,df->td/dot_general | solution.py:344
  309.5 7.2 %convolution_convert_fusion.2 = bf16[2048,1024]{1,0:T(8,128)(2,1)S(1)} fusion(bf16[1024,2048]{1,0:T(8,128)(2,1)} %dynamic-slice_dynamic-update-slice_fusion.8, bf16[1024,1024]{1,0:T(8,128)(2,1)S(1)} %get-tuple-element.105), kind=kOutput, calls=%fused_computation.36 | convolution fusion | flops 4297064448 | bytes 10485760 | tf_op jit(solution)/shard_map/td,tf->df/dot_general | solution.py:355
  316.8 4.9 convolution_convert_fusion.3
  324.0 4.4 collective-permute-done.34
  328.4 14.0 %collective-permute-done.38 = bf16[64,2048]{1,0:T(8,128)(2,1)S(1)} collective-permute-done((bf16[64,2048]{1,0:T(8,128)(2,1)S(1)}, bf16[64,2048]{1,0:T(8,128)(2,1)S(1)}, u32[]{:S(2)}, u32[]{:S(2)}) %collective-permute-start.38) | collective-permute-done | bytes 262176 | tf_op jit(solution)/shard_map/ppermute | solution.py:55
  346.0 6.3 collective-permute-done.39
  354.9 28.4 %collective-permute-done.40 = bf16[128,2048]{1,0:T(8,128)(2,1)S(1)} collective-permute-done((bf16[128,2048]{1,0:T(8,128)(2,1)S(1)}, bf16[128,2048]{1,0:T(8,128)(2,1)S(1)}, u32[]{:S(2)}, u32[]{:S(2)}) %collective-permute-start.40) | collective-permute-done | bytes 524320 | tf_op jit(solution)/shard_map/ppermute | solution.py:55
  383.2 24.6 %collective-permute-done.36 = bf16[128,2048]{1,0:T(8,128)(2,1)S(1)} collective-permute-done((bf16[128,2048]{1,0:T(8,128)(2,1)S(1)}, bf16[128,2048]{1,0:T(8,128)(2,1)S(1)}, u32[]{:S(2)}, u32[]{:S(2)}) %collective-permute-start.36) | collective-permute-done | bytes 524320 | tf_op jit(solution)/shard_map/ppermute | solution.py:55
  426.7 3.9 multiply_reduce_fusion.2
  432.4 7.6 %collective-permute-start.83 = (bf16[2,128,1024]{2,1,0:T(8,128)(2,1)S(1)}, bf16[2,128,1024]{2,1,0:T(8,128)(2,1)S(1)}, u32[]{:S(2)}, u32[]{:S(2)}) collective-permute-start(bf16[2,128,1024]{2,1,0:T(8,128)(2,1)S(1)} %copy-done.21), channel_id=1, source_target_pairs={{0,32},{16,48},{32,0},{48,16},{1,33},{17,49},{33,1},{49,17},{2,34}... | collective-permute-start | bytes 1572872 | tf_op jit(solution)/shard_map/ppermute | solution.py:193
  450.7 3.6 collective-permute-done.44
  456.2 5.4 collective-permute-start.47
  461.7 3.6 collective-permute-start.46
  465.3 3.8 collective-permute-done.46
  476.5 4.7 collective-permute-done.49
  481.3 5.5 collective-permute-done.48
  487.7 14.6 %collective-permute-done.50 = bf16[64,2048]{1,0:T(8,128)(2,1)S(1)} collective-permute-done((bf16[64,2048]{1,0:T(8,128)(2,1)S(1)}, bf16[64,2048]{1,0:T(8,128)(2,1)S(1)}, u32[]{:S(2)}, u32[]{:S(2)}) %collective-permute-start.50) | collective-permute-done | bytes 262176 | tf_op jit(solution)/shard_map/ppermute | solution.py:55
  503.1 14.7 %collective-permute-done.51 = bf16[64,2048]{1,0:T(8,128)(2,1)S(1)} collective-permute-done((bf16[64,2048]{1,0:T(8,128)(2,1)S(1)}, bf16[64,2048]{1,0:T(8,128)(2,1)S(1)}, u32[]{:S(2)}, u32[]{:S(2)}) %collective-permute-start.51) | collective-permute-done | bytes 262176 | tf_op jit(solution)/shard_map/ppermute | solution.py:55
  519.3 3.9 convolution_convert_fusion.9
  523.5 3.5 multiply_reduce_fusion.1
  530.1 3.6 multiply_reduce_fusion
  539.9 5.1 convolution_convert_fusion.6
  546.9 3.7 convolution_convert_fusion.1
  556.1 16.2 %collective-permute-done.52 = bf16[64,2048]{1,0:T(8,128)(2,1)S(1)} collective-permute-done((bf16[64,2048]{1,0:T(8,128)(2,1)S(1)}, bf16[64,2048]{1,0:T(8,128)(2,1)S(1)}, u32[]{:S(2)}, u32[]{:S(2)}) %collective-permute-start.52) | collective-permute-done | bytes 262176 | tf_op jit(solution)/shard_map/ppermute | solution.py:55
  572.2 4.4 collective-permute-done.56
  576.9 3.6 collective-permute-start.57
  580.6 3.2 collective-permute-start.53
  588.3 4.8 collective-permute-done.53
  598.2 4.0 collective-permute-start.59
  606.4 4.4 collective-permute-start.79
  615.7 6.2 all-to-all-start
  624.7 3.2 collective-permute-start.61
  630.2 6.4 all-to-all-start.1
  650.1 9.9 %collective-permute-done.71 = bf16[2,128,768]{1,2,0:T(8,128)(2,1)} collective-permute-done((bf16[2,128,768]{1,2,0:T(8,128)(2,1)}, bf16[2,128,768]{1,2,0:T(8,128)(2,1)}, u32[]{:S(2)}, u32[]{:S(2)}) %collective-permute-start.71) | collective-permute-done | bytes 393248 | tf_op jit(solution)/shard_map/ppermute | solution.py:193
  662.6 3.8 collective-permute-done.64
  674.1 7.6 %collective-permute-done.74 = bf16[128,768]{0,1:T(8,128)(2,1)S(1)} collective-permute-done((bf16[128,768]{0,1:T(8,128)(2,1)S(1)}, bf16[128,768]{0,1:T(8,128)(2,1)S(1)}, u32[]{:S(2)}, u32[]{:S(2)}) %collective-permute-start.74) | collective-permute-done | bytes 196640 | tf_op jit(solution)/shard_map/ppermute | solution.py:197
  683.3 5.0 collective-permute-done.66
  692.4 3.3 collective-permute-done.69
  702.2 4.4 convert_element_type.609
  706.6 4.8 copy.338
  (486 shorter events, 282.2 us)
Async XLA Ops:
  7.2 260.7 %all-gather.6.cloned.1.call-start = ((), (), s32[]{:S(2)}) async-start(), calls=%async_computation.4 | async-start | bytes 4456448 | tf_op jit(solution)/shard_map/all_gather | solution.py:311
  8.8 22.9 %collective-permute-start.8 = (bf16[128,256]{1,0:T(8,128)(2,1)}, bf16[128,256]{1,0:T(8,128)(2,1)}, u32[]{:S(2)}, u32[]{:S(2)}) collective-permute-start(bf16[128,256]{1,0:T(8,128)(2,1)} %get-tuple-element.80), channel_id=1, source_target_pairs={{16,0},{32,16},{48,32},{0,48},{80,64},{96,80},{112,96},{64,112},{1... | collective-permute-start | bytes 196616 | tf_op jit(solution)/shard_map/ppermute | solution.py:163
  12.8 25.4 %collective-permute-start.9 = (bf16[128,256]{1,0:T(8,128)(2,1)}, bf16[128,256]{1,0:T(8,128)(2,1)}, u32[]{:S(2)}, u32[]{:S(2)}) collective-permute-start(bf16[128,256]{1,0:T(8,128)(2,1)} %get-tuple-element.80), channel_id=1, source_target_pairs={{32,0},{48,16},{0,32},{16,48},{96,64},{112,80},{64,96},{80,112},{3... | collective-permute-start | bytes 196616 | tf_op jit(solution)/shard_map/ppermute | solution.py:163
  12.8 26.9 %collective-permute-start.10 = (bf16[128,256]{1,0:T(8,128)(2,1)}, bf16[128,256]{1,0:T(8,128)(2,1)}, u32[]{:S(2)}, u32[]{:S(2)}) collective-permute-start(bf16[128,256]{1,0:T(8,128)(2,1)} %get-tuple-element.80), channel_id=1, source_target_pairs={{48,0},{0,16},{16,32},{32,48},{112,64},{64,80},{80,96},{96,112},{4... | collective-permute-start | bytes 196616 | tf_op jit(solution)/shard_map/ppermute | solution.py:163
  14.1 30.1 %collective-permute-start.11 = (bf16[128,256]{1,0:T(8,128)(2,1)}, bf16[128,256]{1,0:T(8,128)(2,1)}, u32[]{:S(2)}, u32[]{:S(2)}) collective-permute-start(bf16[128,256]{1,0:T(8,128)(2,1)} %get-tuple-element.80), channel_id=1, source_target_pairs={{64,0},{80,16},{96,32},{112,48},{0,64},{16,80},{32,96},{48,112},{6... | collective-permute-start | bytes 196616 | tf_op jit(solution)/shard_map/ppermute | solution.py:163
  17.3 28.4 %collective-permute-start.12 = (bf16[128,256]{1,0:T(8,128)(2,1)}, bf16[128,256]{1,0:T(8,128)(2,1)S(1)}, u32[]{:S(2)}, u32[]{:S(2)}) collective-permute-start(bf16[128,256]{1,0:T(8,128)(2,1)} %get-tuple-element.80), channel_id=1, source_target_pairs={{80,0},{96,16},{112,32},{64,48},{16,64},{32,80},{48,96},{0,112},{8... | collective-permute-start | bytes 196616 | tf_op jit(solution)/shard_map/ppermute | solution.py:163
  20.9 257.0 %all-gather.4.cloned.1.call-start = ((), (), s32[]{:S(2)}) async-start(), calls=%async_computation.3 | async-start | bytes 4456448 | tf_op jit(solution)/shard_map/all_gather | solution.py:310
  31.7 15.4 %collective-permute-start.13 = (bf16[128,256]{1,0:T(8,128)(2,1)}, bf16[128,256]{1,0:T(8,128)(2,1)S(1)}, u32[]{:S(2)}, u32[]{:S(2)}) collective-permute-start(bf16[128,256]{1,0:T(8,128)(2,1)} %get-tuple-element.80), channel_id=1, source_target_pairs={{96,0},{112,16},{64,32},{80,48},{32,64},{48,80},{0,96},{16,112},{9... | collective-permute-start | bytes 196616 | tf_op jit(solution)/shard_map/ppermute | solution.py:163
  38.2 12.8 %collective-permute-start.14 = (bf16[128,256]{1,0:T(8,128)(2,1)}, bf16[128,256]{1,0:T(8,128)(2,1)S(1)}, u32[]{:S(2)}, u32[]{:S(2)}) collective-permute-start(bf16[128,256]{1,0:T(8,128)(2,1)} %get-tuple-element.80), channel_id=1, source_target_pairs={{112,0},{64,16},{80,32},{96,48},{48,64},{0,80},{16,96},{32,112},{1... | collective-permute-start | bytes 196616 | tf_op jit(solution)/shard_map/ppermute | solution.py:163
  39.7 26.4 %collective-permute-start = (bf16[144,768]{0,1:T(8,128)(2,1)}, bf16[144,768]{0,1:T(8,128)(2,1)S(1)}, u32[]{:S(2)}, u32[]{:S(2)}) collective-permute-start(bf16[144,768]{0,1:T(8,128)(2,1)} %fusion.114), channel_id=1, source_target_pairs={{16,0},{32,16},{48,32},{0,48},{80,64},{96,80},{112,96},{64,112},{1... | collective-permute-start | bytes 663560 | tf_op jit(solution)/shard_map/ppermute | solution.py:163
  44.2 22.0 %collective-permute-start.1 = (bf16[144,768]{0,1:T(8,128)(2,1)}, bf16[144,768]{0,1:T(8,128)(2,1)S(1)}, u32[]{:S(2)}, u32[]{:S(2)}) collective-permute-start(bf16[144,768]{0,1:T(8,128)(2,1)} %fusion.114), channel_id=1, source_target_pairs={{32,0},{48,16},{0,32},{16,48},{96,64},{112,80},{64,96},{80,112},{3... | collective-permute-start | bytes 663560 | tf_op jit(solution)/shard_map/ppermute | solution.py:163
  45.7 28.8 %collective-permute-start.2 = (bf16[144,768]{0,1:T(8,128)(2,1)}, bf16[144,768]{0,1:T(8,128)(2,1)S(1)}, u32[]{:S(2)}, u32[]{:S(2)}) collective-permute-start(bf16[144,768]{0,1:T(8,128)(2,1)} %fusion.114), channel_id=1, source_target_pairs={{48,0},{0,16},{16,32},{32,48},{112,64},{64,80},{80,96},{96,112},{4... | collective-permute-start | bytes 663560 | tf_op jit(solution)/shard_map/ppermute | solution.py:163
  47.2 27.5 %collective-permute-start.3 = (bf16[144,768]{0,1:T(8,128)(2,1)}, bf16[144,768]{0,1:T(8,128)(2,1)S(1)}, u32[]{:S(2)}, u32[]{:S(2)}) collective-permute-start(bf16[144,768]{0,1:T(8,128)(2,1)} %fusion.114), channel_id=1, source_target_pairs={{64,0},{80,16},{96,32},{112,48},{0,64},{16,80},{32,96},{48,112},{6... | collective-permute-start | bytes 663560 | tf_op jit(solution)/shard_map/ppermute | solution.py:163
  51.0 28.5 %collective-permute-start.4 = (bf16[144,768]{0,1:T(8,128)(2,1)}, bf16[144,768]{0,1:T(8,128)(2,1)S(1)}, u32[]{:S(2)}, u32[]{:S(2)}) collective-permute-start(bf16[144,768]{0,1:T(8,128)(2,1)} %fusion.114), channel_id=1, source_target_pairs={{80,0},{96,16},{112,32},{64,48},{16,64},{32,80},{48,96},{0,112},{8... | collective-permute-start | bytes 663560 | tf_op jit(solution)/shard_map/ppermute | solution.py:163
  66.1 25.2 %collective-permute-start.5 = (bf16[144,768]{0,1:T(8,128)(2,1)}, bf16[144,768]{0,1:T(8,128)(2,1)S(1)}, u32[]{:S(2)}, u32[]{:S(2)}) collective-permute-start(bf16[144,768]{0,1:T(8,128)(2,1)} %fusion.114), channel_id=1, source_target_pairs={{96,0},{112,16},{64,32},{80,48},{32,64},{48,80},{0,96},{16,112},{9... | collective-permute-start | bytes 663560 | tf_op jit(solution)/shard_map/ppermute | solution.py:163
  66.2 29.6 %collective-permute-start.6 = (bf16[144,768]{0,1:T(8,128)(2,1)}, bf16[144,768]{0,1:T(8,128)(2,1)S(1)}, u32[]{:S(2)}, u32[]{:S(2)}) collective-permute-start(bf16[144,768]{0,1:T(8,128)(2,1)} %fusion.114), channel_id=1, source_target_pairs={{112,0},{64,16},{80,32},{96,48},{48,64},{0,80},{16,96},{32,112},{1... | collective-permute-start | bytes 663560 | tf_op jit(solution)/shard_map/ppermute | solution.py:163
  74.5 24.0 %collective-permute-start.15 = (bf16[8,128,256]{2,1,0:T(8,128)(2,1)}, bf16[8,128,256]{2,1,0:T(8,128)(2,1)}, u32[]{:S(2)}, u32[]{:S(2)}) collective-permute-start(bf16[8,128,256]{2,1,0:T(8,128)(2,1)} %constant_dynamic-update-slice_fusion.8), channel_id=1, source_target_pairs={{0,8},{8,0},{1,9},{9,1},{2,10},{10,2},{3,11},{11,3},{4,12},{12,4},... | collective-permute-start | bytes 1572872 | tf_op jit(solution)/shard_map/ppermute | solution.py:165
  98.2 24.4 %collective-permute-start.7 = (bf16[8,144,768]{2,1,0:T(8,128)(2,1)}, bf16[8,144,768]{2,1,0:T(8,128)(2,1)S(1)}, u32[]{:S(2)}, u32[]{:S(2)}) collective-permute-start(bf16[8,144,768]{2,1,0:T(8,128)(2,1)} %copy.153), channel_id=1, source_target_pairs={{0,8},{8,0},{1,9},{9,1},{2,10},{10,2},{3,11},{11,3},{4,12},{12,4},... | collective-permute-start | bytes 5308424 | tf_op jit(solution)/shard_map/ppermute | solution.py:165
  196.8 13.2 %collective-permute-start.19 = (bf16[128,2048]{1,0:T(8,128)(2,1)S(1)}, bf16[128,2048]{1,0:T(8,128)(2,1)S(1)}, u32[]{:S(2)}, u32[]{:S(2)}) collective-permute-start(bf16[128,2048]{1,0:T(8,128)(2,1)S(1)} %get-tuple-element.187), channel_id=1, source_target_pairs={{0,2},{1,3},{2,4},{3,5},{4,6},{5,7},{6,0},{7,1},{8,10},{9,11},{10,... | collective-permute-start | bytes 1572872 | tf_op jit(solution)/shard_map/ppermute | solution.py:55
  202.3 224.4 %reduce-scatter.2.cloned.1.call-start = ((), (), s32[]{:S(2)}) async-start(), calls=%async_computation.5 | async-start | bytes 4718592 | tf_op jit(solution)/shard_map/reduce_scatter | solution.py:351
  215.5 14.3 %collective-permute-start.25 = (bf16[128,2048]{1,0:T(8,128)(2,1)S(1)}, bf16[128,2048]{1,0:T(8,128)(2,1)S(1)}, u32[]{:S(2)}, u32[]{:S(2)}) collective-permute-start(bf16[128,2048]{1,0:T(8,128)(2,1)S(1)} %get-tuple-element.76), channel_id=1, source_target_pairs={{0,6},{1,7},{2,0},{3,1},{4,2},{5,3},{6,4},{7,5},{8,14},{9,15},{10,... | collective-permute-start | bytes 1572872 | tf_op jit(solution)/shard_map/ppermute | solution.py:55
  241.5 12.6 %collective-permute-start.31 = (bf16[128,2048]{1,0:T(8,128)(2,1)}, bf16[128,2048]{1,0:T(8,128)(2,1)S(1)}, u32[]{:S(2)}, u32[]{:S(2)}) collective-permute-start(bf16[128,2048]{1,0:T(8,128)(2,1)} %get-tuple-element.184), channel_id=1, source_target_pairs={{0,1},{1,0},{2,3},{3,2},{4,5},{5,4},{6,7},{7,6},{8,10},{9,11},{10,... | collective-permute-start | bytes 1572872 | tf_op jit(solution)/shard_map/ppermute | solution.py:55
  245.7 14.0 %collective-permute-start.30 = (bf16[128,2048]{1,0:T(8,128)(2,1)S(1)}, bf16[128,2048]{1,0:T(8,128)(2,1)S(1)}, u32[]{:S(2)}, u32[]{:S(2)}) collective-permute-start(bf16[128,2048]{1,0:T(8,128)(2,1)S(1)} %get-tuple-element.186), channel_id=1, source_target_pairs={{0,1},{1,0},{2,3},{3,2},{4,5},{5,4},{6,7},{7,6},{8,14},{9,15},{10,... | collective-permute-start | bytes 1572872 | tf_op jit(solution)/shard_map/ppermute | solution.py:55
  299.3 407.4 %all-gather.8.cloned.1.call-start = ((), (), s32[]{:S(2)}) async-start(), calls=%async_computation.6 | async-start | bytes 4718592 | tf_op jit(solution)/shard_map/all_gather | solution.py:353
  307.0 21.3 %collective-permute-start.34 = (bf16[64,2048]{1,0:T(8,128)(2,1)S(1)}, bf16[64,2048]{1,0:T(8,128)(2,1)S(1)}, u32[]{:S(2)}, u32[]{:S(2)}) collective-permute-start(bf16[64,2048]{1,0:T(8,128)(2,1)S(1)} %get-tuple-element.100), channel_id=1, source_target_pairs={{0,1},{1,0},{2,3},{3,2},{4,5},{5,4},{6,7},{7,6},{8,10},{9,11},{10,... | collective-permute-start | bytes 786440 | tf_op jit(solution)/shard_map/ppermute | solution.py:55
  308.8 33.6 %collective-permute-start.38 = (bf16[64,2048]{1,0:T(8,128)(2,1)S(1)}, bf16[64,2048]{1,0:T(8,128)(2,1)S(1)}, u32[]{:S(2)}, u32[]{:S(2)}) collective-permute-start(bf16[64,2048]{1,0:T(8,128)(2,1)S(1)} %get-tuple-element.102), channel_id=1, source_target_pairs={{0,1},{1,0},{2,3},{3,2},{4,5},{5,4},{6,7},{7,6},{8,14},{9,15},{10,... | collective-permute-start | bytes 786440 | tf_op jit(solution)/shard_map/ppermute | solution.py:55
  322.5 91.4 %collective-permute-start.85 = (bf16[2,4,128,1024]{3,2,0,1:T(8,128)(2,1)S(1)}, bf16[2,4,128,1024]{3,2,0,1:T(8,128)(2,1)S(1)}, u32[]{:S(2)}, u32[]{:S(2)}) collective-permute-start(bf16[2,4,128,1024]{3,2,0,1:T(8,128)(2,1)S(1)} %bitcast.275), channel_id=1, source_target_pairs={{0,8},{8,0},{1,9},{9,1},{2,10},{10,2},{3,11},{11,3},{4,12},{12,4},... | collective-permute-start | bytes 6291464 | tf_op jit(solution)/shard_map/ppermute | solution.py:185
  323.4 94.1 %collective-permute-start.80 = (bf16[2,4,128,1024]{3,2,0,1:T(8,128)(2,1)S(1)}, bf16[2,4,128,1024]{3,2,0,1:T(8,128)(2,1)S(1)}, u32[]{:S(2)}, u32[]{:S(2)}) collective-permute-start(bf16[2,4,128,1024]{3,2,0,1:T(8,128)(2,1)S(1)} %bitcast.274), channel_id=1, source_target_pairs={{0,8},{8,0},{1,9},{9,1},{2,10},{10,2},{3,11},{11,3},{4,12},{12,4},... | collective-permute-start | bytes 6291464 | tf_op jit(solution)/shard_map/ppermute | solution.py:185
  343.4 39.8 %collective-permute-start.40 = (bf16[128,2048]{1,0:T(8,128)(2,1)S(1)}, bf16[128,2048]{1,0:T(8,128)(2,1)S(1)}, u32[]{:S(2)}, u32[]{:S(2)}) collective-permute-start(bf16[128,2048]{1,0:T(8,128)(2,1)S(1)} %pad_maximum_fusion.5), channel_id=1, source_target_pairs={{0,1},{1,0},{2,3},{3,2},{4,5},{5,4},{6,7},{7,6},{8,14},{9,15},{10,... | collective-permute-start | bytes 1572872 | tf_op jit(solution)/shard_map/ppermute | solution.py:55
  352.2 55.6 %collective-permute-start.36 = (bf16[128,2048]{1,0:T(8,128)(2,1)S(1)}, bf16[128,2048]{1,0:T(8,128)(2,1)S(1)}, u32[]{:S(2)}, u32[]{:S(2)}) collective-permute-start(bf16[128,2048]{1,0:T(8,128)(2,1)S(1)} %pad_maximum_fusion.4), channel_id=1, source_target_pairs={{0,1},{1,0},{2,3},{3,2},{4,5},{5,4},{6,7},{7,6},{8,10},{9,11},{10,... | collective-permute-start | bytes 1572872 | tf_op jit(solution)/shard_map/ppermute | solution.py:55
  408.4 13.3 %collective-permute-start.37 = (bf16[128,2048]{1,0:T(8,128)(2,1)S(1)}, bf16[128,2048]{1,0:T(8,128)(2,1)}, u32[]{:S(2)}, u32[]{:S(2)}) collective-permute-start(bf16[128,2048]{1,0:T(8,128)(2,1)S(1)} %get-tuple-element.181), channel_id=1, source_target_pairs={{0,2},{1,3},{2,4},{3,5},{4,6},{5,7},{6,0},{7,1},{8,10},{9,11},{10,... | collective-permute-start | bytes 1572872 | tf_op jit(solution)/shard_map/ppermute | solution.py:55
  416.2 16.2 %collective-permute-start.86 = (bf16[2,128,1024]{2,1,0:T(8,128)(2,1)}, bf16[2,128,1024]{2,1,0:T(8,128)(2,1)}, u32[]{:S(2)}, u32[]{:S(2)}) collective-permute-start(bf16[2,128,1024]{2,1,0:T(8,128)(2,1)} %get-tuple-element.117), channel_id=1, source_target_pairs={{0,16},{16,32},{32,48},{48,0},{1,17},{17,33},{33,49},{49,1},{2,18}... | collective-permute-start | bytes 1572872 | tf_op jit(solution)/shard_map/ppermute | solution.py:193
  417.5 24.9 %collective-permute-start.87 = (bf16[2,128,1024]{2,1,0:T(8,128)(2,1)}, bf16[2,128,1024]{2,1,0:T(8,128)(2,1)}, u32[]{:S(2)}, u32[]{:S(2)}) collective-permute-start(bf16[2,128,1024]{2,1,0:T(8,128)(2,1)} %get-tuple-element.119), channel_id=1, source_target_pairs={{0,48},{16,0},{32,16},{48,32},{1,49},{17,1},{33,17},{49,33},{2,50}... | collective-permute-start | bytes 1572872 | tf_op jit(solution)/shard_map/ppermute | solution.py:193
  421.6 20.8 %collective-permute-start.88 = (bf16[2,128,1024]{2,1,0:T(8,128)(2,1)}, bf16[2,128,1024]{2,1,0:T(8,128)(2,1)}, u32[]{:S(2)}, u32[]{:S(2)}) collective-permute-start(bf16[2,128,1024]{2,1,0:T(8,128)(2,1)} %get-tuple-element.118), channel_id=1, source_target_pairs={{0,32},{16,48},{32,0},{48,16},{1,33},{17,49},{33,1},{49,17},{2,34}... | collective-permute-start | bytes 1572872 | tf_op jit(solution)/shard_map/ppermute | solution.py:193
  423.4 22.9 %collective-permute-start.81 = (bf16[2,128,1024]{2,1,0:T(8,128)(2,1)}, bf16[2,128,1024]{2,1,0:T(8,128)(2,1)}, u32[]{:S(2)}, u32[]{:S(2)}) collective-permute-start(bf16[2,128,1024]{2,1,0:T(8,128)(2,1)} %get-tuple-element.120), channel_id=1, source_target_pairs={{0,16},{16,32},{32,48},{48,0},{1,17},{17,33},{33,49},{49,1},{2,18}... | collective-permute-start | bytes 1572872 | tf_op jit(solution)/shard_map/ppermute | solution.py:193
  424.0 23.6 %collective-permute-start.82 = (bf16[2,128,1024]{2,1,0:T(8,128)(2,1)}, bf16[2,128,1024]{2,1,0:T(8,128)(2,1)}, u32[]{:S(2)}, u32[]{:S(2)}) collective-permute-start(bf16[2,128,1024]{2,1,0:T(8,128)(2,1)} %get-tuple-element.122), channel_id=1, source_target_pairs={{0,48},{16,0},{32,16},{48,32},{1,49},{17,1},{33,17},{49,33},{2,50}... | collective-permute-start | bytes 1572872 | tf_op jit(solution)/shard_map/ppermute | solution.py:193
  432.4 16.8 %collective-permute-start.83 = (bf16[2,128,1024]{2,1,0:T(8,128)(2,1)S(1)}, bf16[2,128,1024]{2,1,0:T(8,128)(2,1)S(1)}, u32[]{:S(2)}, u32[]{:S(2)}) collective-permute-start(bf16[2,128,1024]{2,1,0:T(8,128)(2,1)S(1)} %copy-done.21), channel_id=1, source_target_pairs={{0,32},{16,48},{32,0},{48,16},{1,33},{17,49},{33,1},{49,17},{2,34}... | collective-permute-start | bytes 1572872 | tf_op jit(solution)/shard_map/ppermute | solution.py:193
  442.4 19.2 %collective-permute-start.43 = (bf16[128,2048]{1,0:T(8,128)(2,1)S(1)}, bf16[128,2048]{1,0:T(8,128)(2,1)S(1)}, u32[]{:S(2)}, u32[]{:S(2)}) collective-permute-start(bf16[128,2048]{1,0:T(8,128)(2,1)S(1)} %get-tuple-element.72), channel_id=1, source_target_pairs={{0,6},{1,7},{2,0},{3,1},{4,2},{5,3},{6,4},{7,5},{8,14},{9,15},{10,... | collective-permute-start | bytes 1572872 | tf_op jit(solution)/shard_map/ppermute | solution.py:55
  446.4 26.3 %collective-permute-start.89 = (bf16[128,1024]{1,0:T(8,128)(2,1)S(1)}, bf16[128,1024]{1,0:T(8,128)(2,1)S(1)}, u32[]{:S(2)}, u32[]{:S(2)}) collective-permute-start(bf16[128,1024]{1,0:T(8,128)(2,1)S(1)} %dynamic-slice_bitcast_fusion.9), channel_id=1, source_target_pairs={{0,64},{64,0},{1,65},{65,1},{2,66},{66,2},{3,67},{67,3},{4,68},{68... | collective-permute-start | bytes 786440 | tf_op jit(solution)/shard_map/ppermute | solution.py:197
  455.0 20.6 %collective-permute-start.84 = (bf16[128,1024]{1,0:T(8,128)(2,1)S(1)}, bf16[128,1024]{1,0:T(8,128)(2,1)S(1)}, u32[]{:S(2)}, u32[]{:S(2)}) collective-permute-start(bf16[128,1024]{1,0:T(8,128)(2,1)S(1)} %dynamic-slice_bitcast_fusion.10), channel_id=1, source_target_pairs={{0,64},{64,0},{1,65},{65,1},{2,66},{66,2},{3,67},{67,3},{4,68},{68... | collective-permute-start | bytes 786440 | tf_op jit(solution)/shard_map/ppermute | solution.py:197
  456.2 15.4 %collective-permute-start.47 = (bf16[128,2048]{1,0:T(8,128)(2,1)S(1)}, bf16[128,2048]{1,0:T(8,128)(2,1)S(1)}, u32[]{:S(2)}, u32[]{:S(2)}) collective-permute-start(bf16[128,2048]{1,0:T(8,128)(2,1)S(1)} %get-tuple-element.72), channel_id=1, source_target_pairs={{0,1},{1,0},{2,3},{3,2},{4,5},{5,4},{6,7},{7,6},{8,9},{9,8},{10,11... | collective-permute-start | bytes 1572872 | tf_op jit(solution)/shard_map/ppermute | solution.py:55
  474.0 12.8 %collective-permute-start.48 = (bf16[128,2048]{1,0:T(8,128)(2,1)S(1)}, bf16[128,2048]{1,0:T(8,128)(2,1)S(1)}, u32[]{:S(2)}, u32[]{:S(2)}) collective-permute-start(bf16[128,2048]{1,0:T(8,128)(2,1)S(1)} %get-tuple-element.180), channel_id=1, source_target_pairs={{0,1},{1,0},{2,3},{3,2},{4,5},{5,4},{6,7},{7,6},{8,14},{9,15},{10,... | collective-permute-start | bytes 1572872 | tf_op jit(solution)/shard_map/ppermute | solution.py:55
  481.2 21.1 %collective-permute-start.50 = (bf16[64,2048]{1,0:T(8,128)(2,1)S(1)}, bf16[64,2048]{1,0:T(8,128)(2,1)S(1)}, u32[]{:S(2)}, u32[]{:S(2)}) collective-permute-start(bf16[64,2048]{1,0:T(8,128)(2,1)S(1)} %slice_select_fusion.3), channel_id=1, source_target_pairs={{0,1},{1,0},{2,3},{3,2},{4,5},{5,4},{6,7},{7,6},{8,10},{9,11},{10,... | collective-permute-start | bytes 786440 | tf_op jit(solution)/shard_map/ppermute | solution.py:55
  486.8 31.0 %collective-permute-start.51 = (bf16[64,2048]{1,0:T(8,128)(2,1)S(1)}, bf16[64,2048]{1,0:T(8,128)(2,1)S(1)}, u32[]{:S(2)}, u32[]{:S(2)}) collective-permute-start(bf16[64,2048]{1,0:T(8,128)(2,1)S(1)} %slice_select_fusion.2), channel_id=1, source_target_pairs={{0,1},{1,0},{2,3},{3,2},{4,5},{5,4},{6,7},{7,6},{8,14},{9,15},{10,... | collective-permute-start | bytes 786440 | tf_op jit(solution)/shard_map/ppermute | solution.py:55
  551.1 21.1 %collective-permute-start.52 = (bf16[64,2048]{1,0:T(8,128)(2,1)S(1)}, bf16[64,2048]{1,0:T(8,128)(2,1)S(1)}, u32[]{:S(2)}, u32[]{:S(2)}) collective-permute-start(bf16[64,2048]{1,0:T(8,128)(2,1)S(1)} %get-tuple-element.90), channel_id=1, source_target_pairs={{0,1},{1,0},{2,3},{3,2},{4,5},{5,4},{6,7},{7,6},{8,10},{9,11},{10,... | collective-permute-start | bytes 786440 | tf_op jit(solution)/shard_map/ppermute | solution.py:55
  551.2 25.5 %collective-permute-start.56 = (bf16[64,2048]{1,0:T(8,128)(2,1)S(1)}, bf16[64,2048]{1,0:T(8,128)(2,1)S(1)}, u32[]{:S(2)}, u32[]{:S(2)}) collective-permute-start(bf16[64,2048]{1,0:T(8,128)(2,1)S(1)} %get-tuple-element.92), channel_id=1, source_target_pairs={{0,1},{1,0},{2,3},{3,2},{4,5},{5,4},{6,7},{7,6},{8,14},{9,15},{10,... | collective-permute-start | bytes 786440 | tf_op jit(solution)/shard_map/ppermute | solution.py:55
  556.0 28.0 %collective-permute-start.75 = (bf16[2,4,128,256]{3,2,0,1:T(8,128)(2,1)S(1)}, bf16[2,4,128,256]{3,2,0,1:T(8,128)(2,1)S(1)}, u32[]{:S(2)}, u32[]{:S(2)}) collective-permute-start(bf16[2,4,128,256]{3,2,0,1:T(8,128)(2,1)S(1)} %bitcast.287), channel_id=1, source_target_pairs={{0,8},{8,0},{1,9},{9,1},{2,10},{10,2},{3,11},{11,3},{4,12},{12,4},... | collective-permute-start | bytes 1572872 | tf_op jit(solution)/shard_map/ppermute | solution.py:185
  580.6 12.6 %collective-permute-start.58 = (bf16[128,2048]{1,0:T(8,128)(2,1)S(1)}, bf16[128,2048]{1,0:T(8,128)(2,1)S(1)}, u32[]{:S(2)}, u32[]{:S(2)}) collective-permute-start(bf16[128,2048]{1,0:T(8,128)(2,1)S(1)} %pad_maximum_fusion.8), channel_id=1, source_target_pairs={{0,1},{1,0},{2,3},{3,2},{4,5},{5,4},{6,7},{7,6},{8,14},{9,15},{10,... | collective-permute-start | bytes 1572872 | tf_op jit(solution)/shard_map/ppermute | solution.py:55
  584.9 17.3 %collective-permute-start.76 = (bf16[2,128,256]{2,1,0:T(8,128)(2,1)S(1)}, bf16[2,128,256]{2,1,0:T(8,128)(2,1)S(1)}, u32[]{:S(2)}, u32[]{:S(2)}) collective-permute-start(bf16[2,128,256]{2,1,0:T(8,128)(2,1)S(1)} %get-tuple-element.161), channel_id=1, source_target_pairs={{0,16},{16,32},{32,48},{48,0},{1,17},{17,33},{33,49},{49,1},{2,18}... | collective-permute-start | bytes 393224 | tf_op jit(solution)/shard_map/ppermute | solution.py:193
  587.0 18.0 %collective-permute-start.77 = (bf16[2,128,256]{2,1,0:T(8,128)(2,1)}, bf16[2,128,256]{2,1,0:T(8,128)(2,1)S(1)}, u32[]{:S(2)}, u32[]{:S(2)}) collective-permute-start(bf16[2,128,256]{2,1,0:T(8,128)(2,1)} %get-tuple-element.163), channel_id=1, source_target_pairs={{0,48},{16,0},{32,16},{48,32},{1,49},{17,1},{33,17},{49,33},{2,50}... | collective-permute-start | bytes 393224 | tf_op jit(solution)/shard_map/ppermute | solution.py:193
  597.0 14.1 %collective-permute-start.55 = (bf16[128,2048]{1,0:T(8,128)(2,1)}, bf16[128,2048]{1,0:T(8,128)(2,1)}, u32[]{:S(2)}, u32[]{:S(2)}) collective-permute-start(bf16[128,2048]{1,0:T(8,128)(2,1)} %get-tuple-element.167), channel_id=1, source_target_pairs={{0,2},{1,3},{2,4},{3,5},{4,6},{5,7},{6,0},{7,1},{8,10},{9,11},{10,... | collective-permute-start | bytes 1572872 | tf_op jit(solution)/shard_map/ppermute | solution.py:55
  598.2 13.0 %collective-permute-start.59 = (bf16[128,2048]{1,0:T(8,128)(2,1)}, bf16[128,2048]{1,0:T(8,128)(2,1)}, u32[]{:S(2)}, u32[]{:S(2)}) collective-permute-start(bf16[128,2048]{1,0:T(8,128)(2,1)} %get-tuple-element.169), channel_id=1, source_target_pairs={{0,6},{1,7},{2,0},{3,1},{4,2},{5,3},{6,4},{7,5},{8,14},{9,15},{10,... | collective-permute-start | bytes 1572872 | tf_op jit(solution)/shard_map/ppermute | solution.py:55
  605.0 31.6 %collective-permute-start.70 = (bf16[2,4,128,768]{2,3,0,1:T(8,128)(2,1)}, bf16[2,4,128,768]{2,3,0,1:T(8,128)(2,1)}, u32[]{:S(2)}, u32[]{:S(2)}) collective-permute-start(bf16[2,4,128,768]{2,3,0,1:T(8,128)(2,1)} %bitcast.284), channel_id=1, source_target_pairs={{0,8},{8,0},{1,9},{9,1},{2,10},{10,2},{3,11},{11,3},{4,12},{12,4},... | collective-permute-start | bytes 4718600 | tf_op jit(solution)/shard_map/ppermute | solution.py:185
  606.4 36.1 %collective-permute-start.79 = (bf16[128,256]{1,0:T(8,128)(2,1)S(1)}, bf16[128,256]{1,0:T(8,128)(2,1)S(1)}, u32[]{:S(2)}, u32[]{:S(2)}) collective-permute-start(bf16[128,256]{1,0:T(8,128)(2,1)S(1)} %dynamic-slice_bitcast_fusion.15), channel_id=1, source_target_pairs={{0,64},{64,0},{1,65},{65,1},{2,66},{66,2},{3,67},{67,3},{4,68},{68... | collective-permute-start | bytes 196616 | tf_op jit(solution)/shard_map/ppermute | solution.py:197
  615.7 13.8 %all-to-all-start = ((f32[16,4,128]{2,1,0:T(4,128)}), f32[16,4,128]{2,1,0:T(4,128)S(1)}, u32[]{:S(2)}, u32[]{:S(2)}) async-start(f32[16,4,128]{2,1,0:T(4,128)} %maximum_bitcast_fusion), calls=%async_computation.1 | async-start | bytes 65536 | tf_op jit(solution)/shard_map/all_to_all | solution.py:204
  624.7 21.0 %collective-permute-start.61 = (bf16[128,2048]{1,0:T(8,128)(2,1)}, bf16[128,2048]{1,0:T(8,128)(2,1)}, u32[]{:S(2)}, u32[]{:S(2)}) collective-permute-start(bf16[128,2048]{1,0:T(8,128)(2,1)} %get-tuple-element.69), channel_id=1, source_target_pairs={{0,6},{1,7},{2,0},{3,1},{4,2},{5,3},{6,4},{7,5},{8,14},{9,15},{10,... | collective-permute-start | bytes 1572872 | tf_op jit(solution)/shard_map/ppermute | solution.py:55
  627.9 15.3 %collective-permute-start.62 = (bf16[128,2048]{1,0:T(8,128)(2,1)}, bf16[128,2048]{1,0:T(8,128)(2,1)}, u32[]{:S(2)}, u32[]{:S(2)}) collective-permute-start(bf16[128,2048]{1,0:T(8,128)(2,1)} %get-tuple-element.69), channel_id=1, source_target_pairs={{0,2},{1,3},{2,4},{3,5},{4,6},{5,7},{6,0},{7,1},{8,10},{9,11},{10,... | collective-permute-start | bytes 1572872 | tf_op jit(solution)/shard_map/ppermute | solution.py:55
  630.2 13.0 %all-to-all-start.1 = ((f32[8,4,128]{2,1,0:T(4,128)}), f32[8,4,128]{2,1,0:T(4,128)S(1)}, u32[]{:S(2)}, u32[]{:S(2)}) async-start(f32[8,4,128]{2,1,0:T(4,128)} %broadcast_in_dim.31), calls=%async_computation.2 | async-start | bytes 32768 | tf_op jit(solution)/shard_map/all_to_all | solution.py:207
  639.2 20.8 %collective-permute-start.71 = (bf16[2,128,768]{1,2,0:T(8,128)(2,1)}, bf16[2,128,768]{1,2,0:T(8,128)(2,1)}, u32[]{:S(2)}, u32[]{:S(2)}) collective-permute-start(bf16[2,128,768]{1,2,0:T(8,128)(2,1)} %get-tuple-element.131), channel_id=1, source_target_pairs={{0,16},{16,32},{32,48},{48,0},{1,17},{17,33},{33,49},{49,1},{2,18}... | collective-permute-start | bytes 1179656 | tf_op jit(solution)/shard_map/ppermute | solution.py:193
  639.8 20.6 %collective-permute-start.72 = (bf16[2,128,768]{1,2,0:T(8,128)(2,1)S(1)}, bf16[2,128,768]{1,2,0:T(8,128)(2,1)}, u32[]{:S(2)}, u32[]{:S(2)}) collective-permute-start(bf16[2,128,768]{1,2,0:T(8,128)(2,1)S(1)} %get-tuple-element.133), channel_id=1, source_target_pairs={{0,48},{16,0},{32,16},{48,32},{1,49},{17,1},{33,17},{49,33},{2,50}... | collective-permute-start | bytes 1179656 | tf_op jit(solution)/shard_map/ppermute | solution.py:193
  642.5 18.0 %collective-permute-start.73 = (bf16[2,128,768]{1,2,0:T(8,128)(2,1)S(1)}, bf16[2,128,768]{1,2,0:T(8,128)(2,1)}, u32[]{:S(2)}, u32[]{:S(2)}) collective-permute-start(bf16[2,128,768]{1,2,0:T(8,128)(2,1)S(1)} %get-tuple-element.132), channel_id=1, source_target_pairs={{0,32},{16,48},{32,0},{48,16},{1,33},{17,49},{33,1},{49,17},{2,34}... | collective-permute-start | bytes 1179656 | tf_op jit(solution)/shard_map/ppermute | solution.py:193
  643.2 25.9 %collective-permute-start.65 = (bf16[128,2048]{1,0:T(8,128)(2,1)}, bf16[128,2048]{1,0:T(8,128)(2,1)S(1)}, u32[]{:S(2)}, u32[]{:S(2)}) collective-permute-start(bf16[128,2048]{1,0:T(8,128)(2,1)} %get-tuple-element.69), channel_id=1, source_target_pairs={{0,1},{1,0},{2,3},{3,2},{4,5},{5,4},{6,7},{7,6},{8,9},{9,8},{10,11... | collective-permute-start | bytes 1572872 | tf_op jit(solution)/shard_map/ppermute | solution.py:55
  645.7 16.2 %collective-permute-start.63 = (bf16[64,2048]{1,0:T(8,128)(2,1)S(1)}, bf16[64,2048]{1,0:T(8,128)(2,1)S(1)}, u32[]{:S(2)}, u32[]{:S(2)}) collective-permute-start(bf16[64,2048]{1,0:T(8,128)(2,1)S(1)} %slice.463), channel_id=1, source_target_pairs={{0,2},{1,3},{2,4},{3,5},{4,6},{5,7},{6,0},{7,1},{8,10},{9,11},{10,... | collective-permute-start | bytes 786440 | tf_op jit(solution)/shard_map/ppermute | solution.py:55
  673.5 14.8 %collective-permute-start.66 = (bf16[128,2048]{1,0:T(8,128)(2,1)S(1)}, bf16[128,2048]{1,0:T(8,128)(2,1)S(1)}, u32[]{:S(2)}, u32[]{:S(2)}) collective-permute-start(bf16[128,2048]{1,0:T(8,128)(2,1)S(1)} %get-tuple-element.166), channel_id=1, source_target_pairs={{0,1},{1,0},{2,3},{3,2},{4,5},{5,4},{6,7},{7,6},{8,14},{9,15},{10,... | collective-permute-start | bytes 1572872 | tf_op jit(solution)/shard_map/ppermute | solution.py:55
  (72 other events, 938.2 us)
Sparse Core Ops, SparseCore 0:
  21.0 81.3 all-gather.5
  202.4 58.6 all-gather.3
  299.4 113.4 reduce-scatter.1
  476.6 98.8 all-gather.7

commit v2 on v1

v2 whole, which is shorter than its diff:
```python
import jax
import jax.numpy as jnp
from jax import lax
from jax.experimental import pallas as pl
from jax.experimental.pallas import tpu as pltpu
from jax.sharding import Mesh, PartitionSpec as P

HEAD_SIZE = 128
eps = 1e-05
bf16 = jnp.bfloat16
f32 = jnp.float32

SMALL = pl.CostEstimate(flops=1, bytes_accessed=1, transcendentals=0)

NX, NYL, NZ, NYH, NC = 4, 2, 4, 2, 2
MP = ("x", "yl")
DP = ("yh", "z", "c")
CMP = ("c", "x", "yl")


def up(values):
    return values.astype(f32)


def normalize(values):
    center = values - jnp.mean(values, axis=-1, keepdims=True)
    inverse_std = lax.rsqrt(jnp.mean(center * center, axis=-1, keepdims=True) + eps)
    return (center * inverse_std, inverse_std)


def norm_back(grad_norm, normed, inverse_std, gain):
    scaled = grad_norm * gain
    return inverse_std * (
        scaled
        - jnp.mean(scaled, axis=-1, keepdims=True)
        - normed * jnp.mean(scaled * normed, axis=-1, keepdims=True)
    )


def to_xp(x, y):
    return (x + 1, y)


def to_xm(x, y):
    return (x - 1, y)


def to_y(x, y):
    return (x, y + 1)


def send(values, zero, one):
    pairs = []
    for c in range(NC):
        for x in range(NX):
            for y in range(NYL):
                tx, ty = (zero, one)[c](x, y)
                pairs.append(((c * NX + x) * NYL + y, (c * NX + tx % NX) * NYL + ty % NYL))
    return lax.ppermute(values, CMP, pairs)


def halves(values):
    middle = values.shape[0] // 2
    return values[:middle], values[middle:]


def pick(zero, one):
    return jnp.where(lax.axis_index("c") == 0, zero, one)


def gather_one(own):
    return send(own, to_xp, to_xp), send(own, to_xm, to_xm), send(own, to_y, to_y)


def gather_two(one):
    p1, p2, q = one
    return (
        send(halves(p1)[0], to_xp, to_xp),
        send(halves(p2)[1], to_xm, to_xm),
        send(pick(p1, q), to_y, to_xp),
        send(pick(p2, q), to_y, to_xm),
    )


def gather_three(own, one, two):
    (p1, p2, q), (o1, o2, r1, r2) = one, two
    s1 = send(pick(o1, halves(r1)[0]), to_y, to_xp)
    s2 = send(pick(o2, halves(r2)[1]), to_y, to_xm)
    return {
        (0, 0): (own,),
        (1, 0): (p2,),
        (2, 0): (o1, o2),
        (3, 0): (p1,),
        (0, 1): (q,),
        (1, 1): (r2,),
        (2, 1): (s1, s2),
        (3, 1): (r1,),
    }


STEP_ONE = [(2, 1)]
LATER_STEPS = [(1, 1), (3, 1), (2, 0), (1, 0), (3, 0), (0, 1), (0, 0)]


def core_factors():
    zero = jnp.where(lax.axis_index("c") == 0, 1.0, 0.0).astype(f32)
    return zero, 1.0 - zero


def add_half(block, piece, which, factor):
    first, second = halves(up(block))
    if which == 0:
        first = first + factor * up(piece)
    else:
        second = second + factor * up(piece)
    return jnp.concatenate([first, second], 0)


def scatter_one(blocks):
    h1, h2 = blocks[2, 1]
    return send(h1, to_y, to_xp), send(h2, to_y, to_xm)


def scatter_two(blocks, one):
    zero, single = core_factors()
    s1, s2 = one
    g1, g2 = halves(up(blocks[2, 0]))
    sent = (
        add_half(blocks[1, 1], s1, 0, single).astype(bf16),
        add_half(blocks[3, 1], s2, 1, single).astype(bf16),
        (g1 + zero * up(s1)).astype(bf16),
        (g2 + zero * up(s2)).astype(bf16),
    )
    return (
        send(sent[0], to_y, to_xp),
        send(sent[1], to_y, to_xm),
        send(sent[2], to_xp, to_xp),
        send(sent[3], to_xm, to_xm),
    )


def scatter_three(blocks, two):
    zero, single = core_factors()
    p, q, r1, r2 = two
    u = send((up(blocks[0, 1]) + single * (up(p) + up(q))).astype(bf16), to_y, to_y)
    t1 = send((add_half(blocks[1, 0], r1, 0, 1.0) + zero * up(p)).astype(bf16), to_xp, to_xp)
    t2 = send((add_half(blocks[3, 0], r2, 1, 1.0) + zero * up(q)).astype(bf16), to_xm, to_xm)
    return up(blocks[0, 0]) + up(t1) + up(t2) + up(u)


REL = [(dx, dy) for dy in range(NYL) for dx in range(NX)]
ORDER = [(0, 0), (1, 0), (3, 0), (0, 1), (2, 0), (1, 1), (3, 1), (2, 1)]


def block_index(dx, dy):
    x, y = lax.axis_index("x"), lax.axis_index("yl")
    return ((x + dx) % NX) * NYL + (y + dy) % NYL


def bounce(pieces, starts, rows, dtype=bf16, first_column=0):
    width = pieces[0].shape[1] - first_column
    count = len(pieces)

    def kernel(*refs):
        place_ref, in_refs, out_ref = refs[0], refs[1 : count + 1], refs[count + 1]
        got = refs[count + 2 : 2 * count + 2]
        cast = refs[2 * count + 2 : -2]
        in_sem, out_sem = refs[-2:]
        loads = [
            pltpu.make_async_copy(
                in_refs[k].at[:, pl.ds(first_column, width)], got[k], in_sem.at[k]
            )
            for k in range(count)
        ]
        for load in loads:
            load.start()
        stores = []
        for k in range(count):
            loads[k].wait()
            source = got[k]
            if cast:
                cast[k][...] = got[k][...].astype(dtype)
                source = cast[k]
            begin = pl.multiple_of(place_ref[k], min(16, pieces[k].shape[0]))
            store = pltpu.make_async_copy(
                source, out_ref.at[pl.ds(begin, pieces[k].shape[0])], out_sem.at[k]
            )
            store.start()
            stores.append(store)
        for store in stores:
            store.wait()

    scratch = [pltpu.VMEM((piece.shape[0], width), bf16) for piece in pieces]
    if dtype != bf16:
        scratch += [pltpu.VMEM((piece.shape[0], width), dtype) for piece in pieces]
    return pl.pallas_call(
        kernel,
        out_shape=jax.ShapeDtypeStruct((rows, width), dtype),
        in_specs=[pl.BlockSpec(memory_space=pltpu.SMEM)]
        + [pl.BlockSpec(memory_space=pl.ANY)] * count,
        out_specs=pl.BlockSpec(memory_space=pl.ANY),
        scratch_shapes=scratch
        + [pltpu.SemaphoreType.DMA((count,)), pltpu.SemaphoreType.DMA((count,))],
        compiler_params=pltpu.CompilerParams(vmem_limit_bytes=32 * 2**20),
        cost_estimate=SMALL,
    )(jnp.stack([jnp.asarray(start, jnp.int32) for start in starts]), *pieces)


def assemble(blocks, dtype, first_column=0):
    rows = blocks[0, 0][0].shape[0]
    pieces, starts = [], []
    for key in ORDER:
        begin = block_index(*key) * rows
        for piece in blocks[key]:
            pieces.append(piece)
            starts.append(begin)
            begin = begin + piece.shape[0]
    return bounce(pieces, starts, rows * len(REL), dtype, first_column)


def sum_mp(values):
    copies = jnp.broadcast_to(values[None], (NX * NYL,) + values.shape)
    return jnp.sum(lax.all_to_all(copies, MP, split_axis=0, concat_axis=0, tiled=True), axis=0)


def after(values, *done):
    return lax.optimization_barrier((values,) + done)[0]


def gather_yz(own):
    copies = jnp.broadcast_to(own[None], (NYH * NZ,) + own.shape)
    return lax.all_to_all(copies, ("yh", "z"), split_axis=0, concat_axis=0, tiled=True)


def row_pieces(blocks, rows):
    pieces, starts = [], []
    for i, key in enumerate(REL):
        begin = i * rows
        for piece in blocks[key]:
            pieces.append(piece)
            starts.append(begin)
            begin += piece.shape[0]
    return pieces, starts


def block_places():
    return jnp.stack([block_index(*key) for key in REL]).astype(jnp.int32)


def terms_by_block(keys, parts_of, weight, first=0, relative=False, norm=None):
    seq_len, depth = parts_of[0].shape
    parts, blocks = len(parts_of), len(keys)
    scattered = weight.ndim == 3
    width = weight.shape[0] * weight.shape[1] if scattered else weight.shape[0]
    rows = seq_len // len(REL)
    tile = min(512, width // 4)
    steps = width // tile
    outs = []
    for k, key in enumerate(keys):
        if key == (2, 1):
            outs += [(k, 0, rows // 2), (k, rows // 2, rows // 2)]
        else:
            outs.append((k, 0, rows))

    def kernel(place_ref, *refs):
        lhs_refs = [refs[n * blocks : (n + 1) * blocks] for n in range(parts)]
        w_ref, refs = refs[parts * blocks], refs[parts * blocks + 1 :]
        if norm is not None:
            x_refs, mean_refs, inverse_refs = (
                refs[n * blocks : (n + 1) * blocks] for n in range(3)
            )
            refs = refs[3 * blocks :]
        out_refs, refs = refs[: len(outs)], refs[len(outs) :]
        for part in range(parts):

            @pl.when(pl.program_id(0) // steps == part)
            def _():
                lhs = jnp.concatenate([ref[...] for ref in lhs_refs[part]], 0)
                total = lax.dot_general(
                    lhs,
                    w_ref[...].reshape(tile, depth),
                    (((1,), (1,)), ((), ())),
                    preferred_element_type=f32,
                )
                for out_ref, (k, inside, count) in zip(out_refs, outs):
                    begin = k * rows + inside
                    out_ref[...] = total[begin : begin + count, :].astype(bf16)
                if norm is not None:
                    one = jnp.zeros((1, tile), f32)
                    two = jnp.zeros((1, tile), f32)
                    for k in range(blocks):
                        part_of = total[k * rows : (k + 1) * rows, :]
                        normed = (
                            x_refs[k][...].astype(f32) - mean_refs[k][:, 0:1]
                        ) * inverse_refs[k][:, 0:1]
                        one = one + jnp.sum(part_of * normed, axis=0, keepdims=True)
                        two = two + jnp.sum(part_of, axis=0, keepdims=True)
                    refs[0][0:1, :] = one
                    refs[0][1:2, :] = two

    def rows_spec(k, cols):
        return pl.BlockSpec((rows, cols), lambda j, p: (p[k], 0))

    def tile_spec(k):
        return pl.BlockSpec((rows, tile), lambda j, p: (p[k], j))

    in_specs, operands = [], []
    for lhs in parts_of:
        in_specs += [rows_spec(k, depth) for k in range(blocks)]
        operands += [lhs] * blocks
    if scattered:
        slices, lanes, cols = weight.shape
        half = steps // NYH
        in_specs.append(
            pl.BlockSpec(
                (tile // lanes, 1, lanes, depth),
                lambda j, p: (j % steps % half, j % steps // half, 0, first + j // steps),
            )
        )
        weight = weight.reshape(slices // NYH, NYH, lanes, cols)
    else:
        in_specs.append(pl.BlockSpec((tile, depth), lambda j, p: (j % steps, first + j // steps)))
    operands.append(weight)
    out_specs = [pl.BlockSpec((count, tile), lambda j, p: (0, j)) for _, _, count in outs]
    out_shape = [jax.ShapeDtypeStruct((count, parts * width), bf16) for _, _, count in outs]
    if norm is not None:
        in_specs += [tile_spec(k) for k in range(blocks)]
        in_specs += [rows_spec(k, norm[1].shape[1]) for k in range(blocks)] * 2
        operands += [norm[0]] * blocks + [norm[1]] * blocks + [norm[2]] * blocks
        out_specs.append(pl.BlockSpec((8, tile), lambda j, p: (0, j)))
        out_shape.append(jax.ShapeDtypeStruct((8, width), f32))
    place = jnp.stack(
        [jnp.int32(REL.index(key)) if relative else block_index(*key) for key in keys]
    ).astype(jnp.int32)
    got = pl.pallas_call(
        kernel,
        grid_spec=pltpu.PrefetchScalarGridSpec(
            num_scalar_prefetch=1,
            grid=(parts * steps,),
            in_specs=in_specs,
            out_specs=out_specs,
        ),
        out_shape=out_shape,
        compiler_params=pltpu.CompilerParams(vmem_limit_bytes=48 * 2**20),
        cost_estimate=SMALL,
    )(place, *operands)
    found = {}
    for out, (k, inside, count) in zip(got, outs):
        if keys[k] == (2, 1):
            found.setdefault((2, 1), []).append(out)
        else:
            found[keys[k]] = out
    if norm is not None:
        return found, got[-1]
    return found


def mlp(second, cotangent, weight):
    seq_len, width = cotangent.shape
    rows = seq_len // len(REL)
    slices, lanes, units = weight.shape
    units = units // 2
    weight = weight.reshape(width, 2 * units)
    columns = [
        (n * lanes, ((n % (NZ * NC)) * NYH + n // (NZ * NC)) * lanes) for n in range(slices)
    ]
    tile = min(256, units // 2)
    steps = units // tile
    root, cubic = (2.0 / jnp.pi) ** 0.5, 0.044715
    pieces, starts = row_pieces(second, rows)
    count = len(pieces)

    def kernel(place_ref, *refs):
        cot_ref, down_ref, up_ref, du_ref, z_ref, h_ref, order_ref = refs[count:]

        @pl.when(pl.program_id(0) == 0)
        def _():
            for plain, place in columns:
                for k, start in enumerate(starts):
                    h_ref[start : start + pieces[k].shape[0], place : place + lanes] = refs[k][
                        :, plain : plain + lanes
                    ]
                for i in range(len(REL)):
                    begin = pl.multiple_of(place_ref[i] * rows, rows)
                    order_ref[i * rows : (i + 1) * rows, place : place + lanes] = cot_ref[
                        pl.ds(begin, rows), plain : plain + lanes
                    ]

        u = jnp.dot(h_ref[...], up_ref[...], preferred_element_type=f32)
        dz = jnp.dot(order_ref[...], down_ref[...], preferred_element_type=f32)
        square = u * u
        t = jnp.tanh(root * (u + cubic * (square * u)))
        half = 0.5 * (1.0 + t)
        z_ref[...] = (u * half).astype(bf16)
        slope = half + (0.5 * root) * u * (1.0 - t * t) * (1.0 + (3.0 * cubic) * square)
        du_ref[...] = (dz * slope).astype(bf16)

    whole = lambda shape: pl.BlockSpec(shape, lambda j, p: (0,) * len(shape))
    return pl.pallas_call(
        kernel,
        grid_spec=pltpu.PrefetchScalarGridSpec(
            num_scalar_prefetch=1,
            grid=(steps,),
            in_specs=[whole(piece.shape) for piece in pieces]
            + [
                whole(cotangent.shape),
                pl.BlockSpec((width, tile), lambda j, p: (0, j)),
                pl.BlockSpec((width, tile), lambda j, p: (0, steps + j)),
            ],
            out_specs=[
                pl.BlockSpec((seq_len, tile), lambda j, p: (0, j)),
                pl.BlockSpec((seq_len, tile), lambda j, p: (0, j)),
                whole((seq_len, width)),
            ],
            scratch_shapes=[pltpu.VMEM((seq_len, width), bf16)],
        ),
        out_shape=[
            jax.ShapeDtypeStruct((seq_len, units), bf16),
            jax.ShapeDtypeStruct((seq_len, units), bf16),
            jax.ShapeDtypeStruct((seq_len, width), bf16),
        ],
        compiler_params=pltpu.CompilerParams(vmem_limit_bytes=56 * 2**20),
        cost_estimate=SMALL,
    )(block_places(), *pieces, cotangent, weight, weight)


def mlp_gradients(second, grad_hidden, cotangent, active):
    seq_len, width = second.shape
    rows = seq_len // len(REL)
    cols = active.shape[1]
    slices = NZ * NC
    lanes = width // (slices * NYH)
    tile = NYH * lanes

    def kernel(place_ref, h_ref, du_ref, cot0_ref, cot1_ref, z_ref, out_ref, order_ref):
        @pl.when(pl.program_id(0) == 0)
        def _():
            for i in range(len(REL)):
                begin = pl.multiple_of(place_ref[i] * rows, rows)
                order_ref[pl.ds(begin, rows), :] = z_ref[i * rows : (i + 1) * rows, :]

        over = (((0,), (0,)), ((), ()))
        out_ref[:, :cols] = lax.dot_general(
            h_ref[...], du_ref[...], over, preferred_element_type=f32
        ).astype(bf16)
        cot = jnp.concatenate([cot0_ref[...], cot1_ref[...]], 1)
        out_ref[:, cols:] = lax.dot_general(
            cot, order_ref[...], over, preferred_element_type=f32
        ).astype(bf16)

    near = pl.BlockSpec((seq_len, lanes), lambda i, p: (0, i))
    far = pl.BlockSpec((seq_len, lanes), lambda i, p: (0, slices + i))
    whole = pl.BlockSpec((seq_len, cols), lambda i, p: (0, 0))
    return pl.pallas_call(
        kernel,
        grid_spec=pltpu.PrefetchScalarGridSpec(
            num_scalar_prefetch=1,
            grid=(slices,),
            in_specs=[
                pl.BlockSpec((seq_len, tile), lambda i, p: (0, i)),
                whole,
                near,
                far,
                whole,
            ],
            out_specs=pl.BlockSpec((tile, 2 * cols), lambda i, p: (i, 0)),
            scratch_shapes=[pltpu.VMEM((seq_len, cols), bf16)],
        ),
        out_shape=jax.ShapeDtypeStruct((width, 2 * cols), bf16),
        compiler_params=pltpu.CompilerParams(vmem_limit_bytes=48 * 2**20),
        cost_estimate=SMALL,
    )(block_places(), second, grad_hidden, cotangent, cotangent, active)


def late_gradients(first, grad_mixed, branch, attended, vectors):
    seq_len, width = first.shape
    rows = seq_len // len(REL)
    wide, narrow = grad_mixed.shape[1], attended.shape[1]
    slices = NZ * NC
    part = width // (slices * NYH)
    tile = NYH * part
    lanes = 128
    pieces, starts = row_pieces(branch, rows)
    count = len(pieces)

    def kernel(place_ref, *refs):
        h_ref, mixed_ref, o_ref, vec_ref = refs[:4]
        da_refs = refs[4 : 4 + NYH * count]
        out_ref, lhs_ref, rhs_ref = refs[4 + NYH * count :]

        @pl.when(pl.program_id(0) == 0)
        def _():
            for i in range(len(REL)):
                begin = pl.multiple_of(place_ref[i] * rows, rows)
                rhs_ref[i * rows : (i + 1) * rows, :] = o_ref[pl.ds(begin, rows), :]

        for k, start in enumerate(starts):
            for n in range(NYH):
                lhs_ref[start : start + pieces[k].shape[0], n * part : (n + 1) * part] = da_refs[
                    n * count + k
                ][...]
        over = (((0,), (0,)), ((), ()))
        out_ref[:, :wide] = lax.dot_general(
            h_ref[...], mixed_ref[...], over, preferred_element_type=f32
        ).astype(bf16)
        out_ref[:, wide : wide + narrow] = lax.dot_general(
            lhs_ref[...], rhs_ref[...], over, preferred_element_type=f32
        ).astype(bf16)
        padded = jnp.concatenate([vec_ref[...], jnp.zeros((lanes - 8, tile), f32)], 0)
        out_ref[:, wide + narrow :] = padded.T.astype(bf16)

    whole = lambda shape: pl.BlockSpec(shape, lambda i, p: (0,) * len(shape))
    near = [pl.BlockSpec((piece.shape[0], part), lambda i, p: (0, i)) for piece in pieces]
    far = [pl.BlockSpec((piece.shape[0], part), lambda i, p: (0, slices + i)) for piece in pieces]
    return pl.pallas_call(
        kernel,
        grid_spec=pltpu.PrefetchScalarGridSpec(
            num_scalar_prefetch=1,
            grid=(slices,),
            in_specs=[
                pl.BlockSpec((seq_len, tile), lambda i, p: (0, i)),
                whole(grad_mixed.shape),
                whole(attended.shape),
                pl.BlockSpec((8, tile), lambda i, p: (0, i)),
            ]
            + near
            + far,
            out_specs=pl.BlockSpec((tile, wide + narrow + lanes), lambda i, p: (i, 0)),
            scratch_shapes=[
                pltpu.VMEM((seq_len, tile), bf16),
                pltpu.VMEM((seq_len, narrow), bf16),
            ],
        ),
        out_shape=jax.ShapeDtypeStruct((width, wide + narrow + lanes), bf16),
        compiler_params=pltpu.CompilerParams(vmem_limit_bytes=48 * 2**20),
        cost_estimate=SMALL,
    )(block_places(), first, grad_mixed, attended, vectors, *pieces, *pieces)


def scatter_order(values):
    shape = values.shape
    values = values.reshape(shape[:-1] + (NYH, NZ * NC, -1))
    return jnp.swapaxes(values, -3, -2).reshape(shape)


def pair_yh(own):
    other = lax.ppermute(own, "yh", [(0, 1), (1, 0)])
    first = lax.axis_index("yh") == 0
    return jnp.stack([jnp.where(first, own, other), jnp.where(first, other, own)], 0)


def gather_zc(pair):
    return lax.all_gather(pair, ("z", "c"), axis=0, tiled=True)


def scatter_dp(values):
    values = lax.psum_scatter(values, ("z", "c"), scatter_dimension=0, tiled=True)
    yh = lax.axis_index("yh")
    rows = values.shape[0] // NYH
    home = lax.dynamic_slice_in_dim(values, yh * rows, rows, 0)
    away = lax.dynamic_slice_in_dim(values, (1 - yh) * rows, rows, 0)
    return up(home) + up(lax.ppermute(away, "yh", [(0, 1), (1, 0)]))


def exchange_dp(values):
    rows, cols = values.shape
    values = values.reshape(NZ * NC, NYH, rows // (NZ * NC * NYH), cols)
    values = lax.all_to_all(values, ("z", "c"), split_axis=0, concat_axis=0, tiled=True)
    values = jnp.sum(up(values), axis=0)
    yh = lax.axis_index("yh")
    home = lax.dynamic_index_in_dim(values, yh, 0, keepdims=False)
    away = lax.dynamic_index_in_dim(values, 1 - yh, 0, keepdims=False).astype(bf16)
    return home + up(lax.ppermute(away, "yh", [(0, 1), (1, 0)]))


def norm_and_qkv(tokens, mine, other, cols):
    seq_len, width = tokens.shape
    slices, packed_rows, all_cols = mine.shape
    shard = packed_rows - 16
    tile = min(256, seq_len // 4)

    def kernel(
        place_ref, x_ref, mine_ref, other_ref, h_ref, qkv_ref, w_ref, vec_ref, mean_ref, inverse_ref
    ):
        core = place_ref[0]

        @pl.when(pl.program_id(0) == 0)
        def _():
            for ref, parity in ((mine_ref, core), (other_ref, 1 - core)):
                for s in range(slices):
                    begin = pl.multiple_of((NC * s + parity) * shard, shard)
                    w_ref[pl.ds(begin, shard), :] = ref[s, :shard, :]
                    row = ref[s, shard:, :].astype(f32)
                    for k in range(4):
                        vec_ref[k : k + 1, pl.ds(begin, shard)] = row[
                            0:1, k * shard : (k + 1) * shard
                        ]

        x = x_ref[...].astype(f32)
        mean = jnp.mean(x, axis=-1, keepdims=True)
        center = x - mean
        inverse = lax.rsqrt(jnp.mean(center * center, axis=-1, keepdims=True) + eps)
        mean_ref[...] = jnp.broadcast_to(mean, mean_ref.shape)
        inverse_ref[...] = jnp.broadcast_to(inverse, inverse_ref.shape)
        h = (center * inverse * vec_ref[0:1, :] + vec_ref[1:2, :]).astype(bf16)
        for n in range(NYH * NZ * NC):
            place = (n % (NZ * NC)) * NYH + n // (NZ * NC)
            h_ref[:, place * shard : (place + 1) * shard] = h[:, n * shard : (n + 1) * shard]
        qkv_ref[...] = jnp.dot(h, w_ref[:, :cols], preferred_element_type=f32).astype(bf16)

    whole = lambda shape: pl.BlockSpec(shape, lambda i, p: (0,) * len(shape))
    place = lax.axis_index("c").astype(jnp.int32).reshape(1)
    return pl.pallas_call(
        kernel,
        grid_spec=pltpu.PrefetchScalarGridSpec(
            num_scalar_prefetch=1,
            grid=(seq_len // tile,),
            in_specs=[
                pl.BlockSpec((tile, width), lambda i, p: (i, 0)),
                whole(mine.shape),
                whole(other.shape),
            ],
            out_specs=[
                pl.BlockSpec((tile, width), lambda i, p: (i, 0)),
                pl.BlockSpec((tile, cols), lambda i, p: (i, 0)),
                whole((width, all_cols)),
                whole((8, width)),
                pl.BlockSpec((tile, 128), lambda i, p: (i, 0)),
                pl.BlockSpec((tile, 128), lambda i, p: (i, 0)),
            ],
        ),
        out_shape=[
            jax.ShapeDtypeStruct((seq_len, width), bf16),
            jax.ShapeDtypeStruct((seq_len, cols), bf16),
            jax.ShapeDtypeStruct((width, all_cols), bf16),
            jax.ShapeDtypeStruct((8, width), f32),
            jax.ShapeDtypeStruct((seq_len, 128), f32),
            jax.ShapeDtypeStruct((seq_len, 128), f32),
        ],
        compiler_params=pltpu.CompilerParams(vmem_limit_bytes=48 * 2**20),
        cost_estimate=SMALL,
    )(place, tokens, mine, other)


def scores_of(query, keys, begin, ends_ref, scale):
    rows, seen = query.shape[0], keys.shape[0]
    scores = (
        lax.dot_general(query, keys, (((1,), (1,)), ((), ())), preferred_element_type=f32) * scale
    )
    place = begin + lax.broadcasted_iota(jnp.int32, (rows, 1), 0)
    first = jnp.zeros((rows, 1), jnp.int32)
    for k in range(4):
        first = jnp.where(place >= ends_ref[k], ends_ref[k], first)
    column = lax.broadcasted_iota(jnp.int32, (rows, seen), 1)
    return jnp.where((column >= first) & (column <= place), scores, f32(-1e30))


def attend(qkv, ends, scale):
    seq_len, cols = qkv.shape
    heads = cols // (3 * HEAD_SIZE)
    tile = min(256, seq_len // 4)

    def kernel(ends_ref, q_ref, k_ref, v_ref, o_ref, lse_ref):
        for begin in range(0, seq_len, tile):
            seen = begin + tile
            scores = scores_of(q_ref[begin:seen, :], k_ref[:seen, :], begin, ends_ref, scale)
            largest = jnp.max(scores, axis=-1, keepdims=True)
            expo = jnp.exp(scores - largest)
            totals = jnp.sum(expo, axis=-1, keepdims=True)
            probs = (expo / totals).astype(bf16)
            o_ref[begin:seen, :] = jnp.dot(
                probs, v_ref[:seen, :], preferred_element_type=f32
            ).astype(bf16)
            lse_ref[begin:seen, :] = jnp.broadcast_to(
                largest + jnp.log(totals), (tile, HEAD_SIZE)
            )

    def spec(kind):
        return pl.BlockSpec((seq_len, HEAD_SIZE), lambda h, e: (0, kind * heads + h))

    return pl.pallas_call(
        kernel,
        grid_spec=pltpu.PrefetchScalarGridSpec(
            num_scalar_prefetch=1,
            grid=(heads,),
            in_specs=[spec(0), spec(1), spec(2)],
            out_specs=[spec(0), spec(0)],
        ),
        out_shape=[
            jax.ShapeDtypeStruct((seq_len, heads * HEAD_SIZE), bf16),
            jax.ShapeDtypeStruct((seq_len, heads * HEAD_SIZE), f32),
        ],
        compiler_params=pltpu.CompilerParams(vmem_limit_bytes=48 * 2**20),
        cost_estimate=SMALL,
    )(ends, qkv, qkv, qkv)


def attend_back(qkv, lse, branch, weight, ends, scale):
    seq_len, cols = qkv.shape
    heads = cols // (3 * HEAD_SIZE)
    own = heads * HEAD_SIZE
    width = weight.shape[0]
    rows = seq_len // len(REL)
    tile = min(256, seq_len // 4)
    pieces, starts = row_pieces(branch, rows)
    count = len(pieces)

    def kernel(ends_ref, place_ref, *refs):
        q_ref, k_ref, v_ref, lse_ref, w_ref = refs[:5]
        out_ref, dk_ref, dv_ref, da_ref, go_ref = refs[5 + count :]
        h = pl.program_id(0)

        @pl.when(h == 0)
        def _():
            for k, start in enumerate(starts):
                i, inside = start // rows, start % rows
                begin = pl.multiple_of(place_ref[i] * rows + inside, rows // 2)
                da_ref[pl.ds(begin, pieces[k].shape[0]), :] = refs[5 + k][...]
            grad = jnp.dot(da_ref[...], w_ref[...], preferred_element_type=f32).astype(bf16)
            for n in range(heads):
                go_ref[n] = grad[:, n * HEAD_SIZE : (n + 1) * HEAD_SIZE]

        def columns(kind):
            return pl.ds(pl.multiple_of((kind * heads + h) * HEAD_SIZE, HEAD_SIZE), HEAD_SIZE)

        dk_ref[...] = jnp.zeros_like(dk_ref)
        dv_ref[...] = jnp.zeros_like(dv_ref)
        for begin in range(0, seq_len, tile):
            seen = begin + tile
            query = q_ref[begin:seen, :]
            scores = scores_of(query, k_ref[:seen, :], begin, ends_ref, scale)
            probs = jnp.exp(scores - lse_ref[begin:seen, 0:1])
            grad = go_ref[h, begin:seen, :]
            grad_probs = lax.dot_general(
                grad, v_ref[:seen, :], (((1,), (1,)), ((), ())), preferred_element_type=f32
            )
            inner = jnp.sum(probs * grad_probs, axis=-1, keepdims=True)
            grad_scores = (probs * (grad_probs - inner)).astype(bf16)
            out_ref[begin:seen, columns(0)] = (
                jnp.dot(grad_scores, k_ref[:seen, :], preferred_element_type=f32) * scale
            ).astype(bf16)
            over_rows = (((0,), (0,)), ((), ()))
            dk_ref[:seen, :] += lax.dot_general(
                grad_scores, query, over_rows, preferred_element_type=f32
            )
            dv_ref[:seen, :] += lax.dot_general(
                probs.astype(bf16), grad, over_rows, preferred_element_type=f32
            )
        out_ref[:, columns(1)] = (dk_ref[...] * scale).astype(bf16)
        out_ref[:, columns(2)] = dv_ref[...].astype(bf16)

    def spec(kind):
        return pl.BlockSpec((seq_len, HEAD_SIZE), lambda h, e, p: (0, kind * heads + h))

    whole = lambda shape: pl.BlockSpec(shape, lambda h, e, p: (0,) * len(shape))
    return pl.pallas_call(
        kernel,
        grid_spec=pltpu.PrefetchScalarGridSpec(
            num_scalar_prefetch=2,
            grid=(heads,),
            in_specs=[
                spec(0),
                spec(1),
                spec(2),
                spec(0),
                pl.BlockSpec((width, own), lambda h, e, p: (0, cols // own)),
            ]
            + [whole(piece.shape) for piece in pieces],
            out_specs=whole((seq_len, cols)),
            scratch_shapes=[
                pltpu.VMEM((seq_len, HEAD_SIZE), f32),
                pltpu.VMEM((seq_len, HEAD_SIZE), f32),
                pltpu.VMEM((seq_len, width), bf16),
                pltpu.VMEM((heads, seq_len, HEAD_SIZE), bf16),
            ],
        ),
        out_shape=jax.ShapeDtypeStruct((seq_len, cols), bf16),
        compiler_params=pltpu.CompilerParams(vmem_limit_bytes=56 * 2**20),
        cost_estimate=SMALL,
    )(ends, block_places(), qkv, qkv, qkv, lse, weight, *pieces)


def local(
    tokens,
    doc_lengths,
    gain_one,
    bias_one,
    w_qkv,
    w_out,
    gain_two,
    bias_two,
    w_up,
    w_down,
    cotangent,
):
    seq_len, width = tokens.shape
    shard = w_qkv.shape[0]
    local_width = w_qkv.shape[2]
    local_heads = local_width // HEAD_SIZE
    rows = seq_len // (NX * NYL)
    x, y = lax.axis_index("x"), lax.axis_index("yl")
    my_rows = (x * NYL + y) * rows
    scale = HEAD_SIZE**-0.5

    wide = 3 * local_width
    small = jnp.stack([gain_one, bias_one, gain_two, bias_two], 0).astype(bf16)
    small = jnp.pad(small.reshape(1, -1), ((0, 15), (0, wide + local_width - 4 * shard)))
    packed = jnp.concatenate([w_qkv.reshape(shard, wide).astype(bf16), w_out.astype(bf16)], 1)
    first_mine = gather_yz(jnp.concatenate([packed, small], 0))
    first_other = lax.ppermute(first_mine, "c", [(0, 1), (1, 0)])
    mlp_weight = jnp.concatenate([w_down.astype(bf16), w_up.astype(bf16)], 1)
    mlp_weight = gather_zc(pair_yh(after(mlp_weight, first_mine)))
    ends = jnp.cumsum(doc_lengths[0])

    first, mixed, weight, vectors, mean_one, inverse_one = norm_and_qkv(
        tokens, first_mine, first_other, wide
    )
    gain_a, gain_b, bias_b = vectors[0], vectors[2], vectors[3]
    attended, lse = attend(mixed, ends, scale)
    terms = terms_by_block(STEP_ONE, [attended], weight, first=3)
    sum_one = scatter_one(terms)
    later = terms_by_block(LATER_STEPS, [after(attended, *terms[2, 1])], weight, first=3)
    own_tokens = up(lax.dynamic_slice_in_dim(tokens, my_rows, rows, 0))
    own_cot = up(lax.dynamic_slice_in_dim(cotangent, my_rows, rows, 0))
    own_middle = own_tokens + scatter_three(later, scatter_two(later, sum_one))

    own_two, inverse_two = normalize(own_middle)
    second = (own_two * gain_b + bias_b).astype(bf16)
    second_one = gather_one(second)
    second_two = gather_two(second_one)
    grad_hidden, active, second = mlp(
        gather_three(second, second_one, second_two), cotangent, mlp_weight
    )
    hidden = [active, grad_hidden]
    terms = terms_by_block(STEP_ONE, hidden, mlp_weight, relative=True)
    sum_one = scatter_one(terms)
    later = terms_by_block(
        LATER_STEPS, after(hidden, *terms[2, 1]), mlp_weight, relative=True
    )
    sum_two = scatter_two(later, sum_one)
    both = scatter_three(later, sum_two)
    mlp_terms = mlp_gradients(after(second, sum_two[2]), grad_hidden, cotangent, active)
    both = after(both, mlp_terms)
    mlp_grads = scatter_dp(mlp_terms)
    branch_two, grad_second = both[:, :width], both[:, width:]
    output_own = (own_middle + branch_two).astype(bf16)

    grad_middle = own_cot + norm_back(grad_second, own_two, inverse_two, gain_b)
    own_branch = grad_middle.astype(bf16)
    branch_one = gather_one(own_branch)
    branch_two = gather_two(branch_one)
    branch = gather_three(own_branch, branch_one, branch_two)
    output_one = gather_one(after(output_own, branch_two[0]))
    grad_mixed = attend_back(mixed, lse, branch, weight, ends, scale)
    norm = (tokens, mean_one, inverse_one)
    terms, vec_a = terms_by_block(STEP_ONE, [grad_mixed], weight, norm=norm)
    sum_one = scatter_one(terms)
    output_two = gather_two(output_one)
    later, vec_b = terms_by_block(
        LATER_STEPS, [after(grad_mixed, *terms[2, 1])], weight, norm=norm
    )
    sum_two = scatter_two(later, sum_one)
    vec_one = vec_a + vec_b
    vec_two = jnp.stack([jnp.sum(grad_second * own_two, 0), jnp.sum(grad_second, 0)], 0)
    late_vectors = scatter_order(
        jnp.concatenate([vec_one[:2], vec_two, jnp.zeros((4, width), f32)], 0)
    )
    output_two = after(output_two, *sum_two)
    grad_first = scatter_three(later, sum_two)
    late = exchange_dp(
        late_gradients(after(first, sum_two[2]), grad_mixed, branch, attended, late_vectors)
    )

    own_one, own_inverse = normalize(own_tokens)
    grad_tokens = (grad_middle + norm_back(grad_first, own_one, own_inverse, gain_a)).astype(bf16)
    grad_one = gather_one(grad_tokens)
    grad_two = after(gather_two(grad_one), late)
    output = gather_three(output_own, output_one, output_two)
    output = assemble(after(output, *grad_two), bf16)
    input_grad = assemble(gather_three(grad_tokens, grad_one, grad_two), f32)
    sums = sum_mp(late[:, wide + local_width : wide + local_width + 4].T)
    return (
        output,
        input_grad,
        sums[0],
        sums[1],
        late[:, :wide].reshape(shard, 3, local_width),
        late[:, wide : wide + local_width],
        sums[2],
        sums[3],
        mlp_grads[:, : w_up.shape[1]],
        mlp_grads[:, w_up.shape[1] :],
    )


def solution(mesh):
    fine = Mesh(mesh.devices.reshape(NYH, NZ, NC, NX, NYL), ("yh", "z", "c", "x", "yl"))
    return jax.shard_map(
        local,
        mesh=fine,
        in_specs=(
            P(DP, None),
            P(DP, None),
            P(DP),
            P(DP),
            P(DP, None, MP),
            P(DP, MP),
            P(DP),
            P(DP),
            P(DP, MP),
            P(DP, MP),
            P(DP, None),
        ),
        out_specs=(
            P(DP, None),
            P(DP, None),
            P(DP),
            P(DP),
            P(DP, None, MP),
            P(DP, MP),
            P(DP),
            P(DP),
            P(DP, MP),
            P(DP, MP),
        ),
        check_vma=False,
    )
```

time: 729 us -> 517 us (0.71)
  Pallas kernels: 0 us -> 121 us
  waiting for transfers between devices: 282 us -> 191 us
  matrix products: 89.5 us -> 0 us
  local copies, waits for them, and re-layouts: 82.5 us -> 28.6 us
  other arithmetic: 98.5 us -> 49.1 us
  starting transfers between devices: 150 us -> 101 us
    pallas_call x0 -> x14, Pallas kernels: none -> 121 us  [the longest x6 39.7 us: terms_by_block(): pl.pallas_call(kernel, grid_spec=pltpu.PrefetchScalarGridSpec(num_scalar_...]
    ppermute x54 -> x63, waiting for transfers between devices: 226 us -> 133 us  [send(): return lax.ppermute(values, CMP, pairs)]
    dot_general x24 -> x0, matrix products: 89.5 us -> none  [the longest x1 12.9 us: local(): hidden = jnp.dot(second, up_weight, preferred_element_type=f32)]
    ppermute x32 -> x3, starting transfers between devices: 54.4 us -> 5.78 us  [the longest x1 3.1 us: exchange_dp(): return home + up(lax.ppermute(away, 'yh', [(0, 1), (1, 0)]))]
    unnamed x36 -> x2, other arithmetic: 42.4 us -> 0.03 us
    unnamed x161 -> x141, local copies, waits for them, and re-layouts: 55.9 us -> 14.6 us
    all_to_all x2 -> x3, waiting for transfers between devices: 1.6 us -> 31.2 us  [the longest x1 29 us: gather_yz(): lax.all_to_all(copies, ('yh', 'z'), split_axis=0, concat_axis=0, tiled=True)]
    ppermute x32 -> x3, waiting for transfers between devices: 46.8 us -> 27.6 us  [the longest x1 12 us: pair_yh(): other = lax.ppermute(own, 'yh', [(0, 1), (1, 0)])]
  transfers between devices with their start and end apart: 96 -> 72, of which waited for: 47 -> 35; matrix products, arithmetic and copies ran while one was open for 33% -> 11% of each run, Pallas kernels for 0% -> 19%
where the time goes in v2:
time: 517 us; the launch traced here: 507 us
  waiting for transfers between devices  191 us (37%)
  Pallas kernels  121 us (23%)
  starting transfers between devices  101 us (20%)
  other arithmetic  49.1 us (9%)
  local copies, waits for them, and re-layouts  28.6 us (6%)
  between operations  15.6 us (3%)
    ppermute x63, waiting for transfers between devices, send(): return lax.ppermute(values, CMP, pairs)  133 us
    ppermute x63, starting transfers between devices, send(): return lax.ppermute(values, CMP, pairs)  72.8 us
    pallas_call x6, Pallas kernels, terms_by_block(): pl.pallas_call(kernel, grid_spec=pltpu.PrefetchScalarGridSpec(num_scalar_...  39.7 us
    all_to_all x1, waiting for transfers between devices, gather_yz(): lax.all_to_all(copies, ('yh', 'z'), split_axis=0, concat_axis=0, tiled=True)  29 us
    pallas_call x1, Pallas kernels, mlp(): pl.pallas_call(kernel, grid_spec=pltpu.PrefetchScalarGridSpec(num_scalar_...  19.2 us
    unnamed x141, local copies, waits for them, and re-layouts  14.6 us
    pallas_call x1, Pallas kernels, mlp_gradients(): pl.pallas_call(kernel, grid_spec=pltpu.PrefetchScalarGridSpec(num_scalar_...  14.3 us
    pallas_call x1, Pallas kernels, attend_back(): pl.pallas_call(kernel, grid_spec=pltpu.PrefetchScalarGridSpec(num_scalar_...  12.6 us
  transfers between devices with their start and end apart: 72, of which 35 were waited for; matrix products, arithmetic and copies ran while one was open for 11% of the time, Pallas kernels for 19%

profile of v2, /device:TPU:2, one launch (start us, length us, event | category | flops | bytes accessed | tf_op | source)
XLA Modules:
  0.0 507.3 jit_solution(10983750119351125297)
XLA Ops:
  12.9 8.1 %all-to-all-start = ((bf16[8,144,1024]{2,1,0:T(8,128)(2,1)}), bf16[8,144,1024]{2,1,0:T(8,128)(2,1)S(1)}, u32[]{:S(2)}, u32[]{:S(2)}) async-start(bf16[8,144,1024]{2,1,0:T(8,128)(2,1)} %broadcast_in_dim.6), calls=%async_computation | async-start | bytes 4718592 | tf_op jit(solution)/shard_map/all_to_all | solution.py:232
  21.2 29.0 %all-to-all-done.mine_ref = bf16[8,144,1024]{2,1,0:T(8,128)(2,1)S(1)} async-done(((bf16[8,144,1024]{2,1,0:T(8,128)(2,1)}), bf16[8,144,1024]{2,1,0:T(8,128)(2,1)S(1)}, u32[]{:S(2)}, u32[]{:S(2)}) %all-to-all-start) | async-done | bytes 2359328 | tf_op jit(solution)/shard_map/all_to_all | solution.py:232
  50.2 2.6 collective-permute-start.19
  52.8 12.0 %collective-permute-done.19 = bf16[128,2048]{1,0:T(8,128)(2,1)S(1)} collective-permute-done((bf16[128,2048]{1,0:T(8,128)(2,1)S(1)}, bf16[128,2048]{1,0:T(8,128)(2,1)S(1)}, u32[]{:S(2)}, u32[]{:S(2)}) %collective-permute-start.19) | collective-permute-done | bytes 524320 | tf_op jit(solution)/shard_map/ppermute | solution.py:547
  66.4 4.4 collective-permute-done.other_ref
  72.5 10.6 %shard_map.186 = (bf16[1024,2048]{1,0:T(8,128)(2,1)}, bf16[1024,768]{1,0:T(8,128)(2,1)S(1)}, bf16[2048,1024]{1,0:T(8,128)(2,1)}, f32[8,2048]{1,0:T(8,128)S(1)}, ...) custom-call(s32[1]{0:T(128)} %bitcast.19.place_ref, bf16[1024,2048]{1,0:T(8,128)(2,1)} %refs_14_.1, ...), custom_call_target="tpu_custom_call" | custom-call | flops 1 | bytes 1 | tf_op jit(solution)/shard_map/pallas_call | solution.py:613
  83.0 5.7 %shard_map.187 = (bf16[1024,256]{1,0:T(8,128)(2,1)S(1)}, f32[1024,256]{1,0:T(8,128)S(1)}) custom-call(s32[4]{0:T(128)S(1)} %bitcast.75, bf16[1024,768]{1,0:T(8,128)(2,1)S(1)} %get-tuple-element.77.q_ref.k_ref.v_ref.refs_0_.refs_1_.refs_2_, bf16[1024,768]{1,0:T(8,128)(2,1)S(1)} %get-tuple-element.77.q_ref.k_ref.v_ref.refs_0_.refs_1_.refs_2_, ...), custom_call_target="tpu_custom_call" | custom-call | flops 1 | bytes 1 | tf_op jit(solution)/shard_map/pallas_call | solution.py:681
  93.5 4.2 shard_map.189
  105.0 5.0 collective-permute-done.2
  110.0 3.7 collective-permute-done.6
  113.8 3.4 collective-permute-done.7
  118.9 1.9 collective-permute-start.4
  120.9 8.9 %collective-permute-done.9 = bf16[128,2048]{1,0:T(8,128)(2,1)S(1)} collective-permute-done((bf16[128,2048]{1,0:T(8,128)(2,1)S(1)}, bf16[128,2048]{1,0:T(8,128)(2,1)S(1)}, u32[]{:S(2)}, u32[]{:S(2)}) %collective-permute-start.9) | collective-permute-done | bytes 524320 | tf_op jit(solution)/shard_map/ppermute | solution.py:59
  134.3 3.0 collective-permute-start.10
  138.7 7.9 %collective-permute-done.10.refs_1_ = bf16[128,2048]{1,0:T(8,128)(2,1)S(1)} collective-permute-done((bf16[128,2048]{1,0:T(8,128)(2,1)S(1)}, bf16[128,2048]{1,0:T(8,128)(2,1)S(1)}, u32[]{:S(2)}, u32[]{:S(2)}) %collective-permute-start.10) | collective-permute-done | bytes 524320 | tf_op jit(solution)/shard_map/ppermute | solution.py:59
  146.7 2.4 collective-permute-done.11.refs_4_
  151.6 2.0 collective-permute-start.13
  153.5 6.5 %collective-permute-done.12.refs_2_ = bf16[64,2048]{1,0:T(8,128)(2,1)S(1)} collective-permute-done((bf16[64,2048]{1,0:T(8,128)(2,1)S(1)}, bf16[64,2048]{1,0:T(8,128)(2,1)S(1)}, u32[]{:S(2)}, u32[]{:S(2)}) %collective-permute-start.12) | collective-permute-done | bytes 262176 | tf_op jit(solution)/shard_map/ppermute | solution.py:59
  161.6 2.5 collective-permute-done.15.refs_6_
  167.6 3.8 collective-permute-done.18.refs_8_
  172.1 19.2 %shard_map.190 = (bf16[1024,1024]{1,0:T(8,128)(2,1)}, bf16[1024,1024]{1,0:T(8,128)(2,1)}, bf16[1024,2048]{1,0:T(8,128)(2,1)}) custom-call(s32[8]{0:T(128)} %stack.174.place_ref, bf16[128,2048]{1,0:T(8,128)(2,1)} %copy-done.53, bf16[128,2048]{1,0:T(8,128)(2,1)} %copy-done.50, bf16[64,2048]{1,0:T(8,128)(2,1)} %copy-done.59, bf16[64,2048]{1,0:T(8,128)(2,1)} %copy-done.60, ...), custom_call_target="tpu_custom_call" | custom-call | flops 1 | bytes 1 | tf_op jit(solution)/shard_map/pallas_call | solution.py:399
  194.5 7.9 %shard_map.191 = (bf16[64,4096]{1,0:T(8,128)(2,1)S(1)}, bf16[64,4096]{1,0:T(8,128)(2,1)S(1)}) custom-call(s32[1]{0:T(128)} %constant.340.clone.1.place_ref, bf16[1024,1024]{1,0:T(8,128)(2,1)S(1)} %copy-done.2, bf16[1024,1024]{1,0:T(8,128)(2,1)S(1)} %copy-done, bf16[8,2,128,2048]{3,2,1,0:T(8,128)(2,1)} %bitcast.79), custom_call_target="tpu_custom_call" | custom-call | flops 1 | bytes 1 | tf_op jit(solution)/shard_map/pallas_call | solution.py:335
  204.7 14.7 %shard_map.192 = (bf16[128,4096]{1,0:T(8,128)(2,1)S(1)}, bf16[128,4096]{1,0:T(8,128)(2,1)S(1)}, bf16[128,4096]{1,0:T(8,128)(2,1)S(1)}, bf16[128,4096]{1,0:T(8,12...) custom-call(s32[7]{0:T(128)S(1)} %copy-done.45, ...), custom_call_target="tpu_custom_call" | custom-call | flops 1 | bytes 1 | tf_op jit(solution)/shard_map/pallas_call | solution.py:335
  230.6 1.9 collective-permute-start.25
  232.5 8.7 %collective-permute-done.21 = bf16[64,4096]{1,0:T(8,128)(2,1)} collective-permute-done((bf16[64,4096]{1,0:T(8,128)(2,1)S(1)}, bf16[64,4096]{1,0:T(8,128)(2,1)}, u32[]{:S(2)}, u32[]{:S(2)}) %collective-permute-start.21) | collective-permute-done | bytes 524320 | tf_op jit(solution)/shard_map/ppermute | solution.py:59
  241.2 14.3 %shard_map.193 = bf16[2048,2048]{1,0:T(8,128)(2,1)} custom-call(s32[8]{0:T(128)S(1)} %copy-done.42, bf16[1024,2048]{1,0:T(8,128)(2,1)} %get-tuple-element.106.h_ref, bf16[1024,1024]{1,0:T(8,128)(2,1)S(1)} %copy-done.1, bf16[1024,2048]{1,0:T(8,128)(2,1)} %cot1_ref.1, bf16[1024,2048]{1,0:T(8,128)(2,1)} %cot1_ref.1, bf16[1024,1024]{1,0:T(8,128)(2,1)S(1)} %copy-done.3), custom_call_target="tpu_custom_call" | custom-call | flops 1 | bytes 1 | tf_op jit(solution)/shard_map/pallas_call | solution.py:454
  258.5 2.6 fusion.1
  262.6 2.8 collective-permute-start.27
  265.4 17.0 %collective-permute-done.28 = bf16[128,4096]{1,0:T(8,128)(2,1)S(1)} collective-permute-done((bf16[128,4096]{1,0:T(8,128)(2,1)S(1)}, bf16[128,4096]{1,0:T(8,128)(2,1)S(1)}, u32[]{:S(2)}, u32[]{:S(2)}) %collective-permute-start.28) | collective-permute-done | bytes 1048608 | tf_op jit(solution)/shard_map/ppermute | solution.py:59
  283.6 1.9 collective-permute-done.23
  286.6 2.8 fusion.60
  289.7 2.2 collective-permute-start.38
  292.6 6.6 %collective-permute-done.29.refs_9_.refs_8_.refs_18_ = bf16[128,2048]{1,0:T(8,128)(2,1)S(1)} collective-permute-done((bf16[128,2048]{1,0:T(8,128)(2,1)S(1)}, bf16[128,2048]{1,0:T(8,128)(2,1)S(1)}, u32[]{:S(2)}, u32[]{:S(2)}) %collective-permute-start.29) | collective-permute-done | bytes 524320 | tf_op jit(solution)/shard_map/ppermute | solution.py:59
  299.2 1.9 collective-permute-done.40.refs_10_.refs_9_.refs_19_
  304.0 3.2 collective-permute-start.39
  307.2 3.3 collective-permute-done.30.refs_7_.refs_6_.refs_16_
  312.6 4.9 collective-permute-done.41.refs_11_.refs_10_.refs_20_
  319.9 3.5 collective-permute-start.32
  323.4 3.9 collective-permute-done.44.refs_13_.refs_12_.refs_22_
  328.0 12.6 %shard_map.194.refs_0_.refs_1_.refs_2_.refs_3_.refs_4_.refs_5_.refs_6_ = bf16[1024,768]{1,0:T(8,128)(2,1)} custom-call(s32[4]{0:T(128)} %bitcast.76, s32[8]{0:T(128)} %stack.174.place_ref, bf16[1024,768]{1,0:T(8,128)(2,1)} %copy-done.6, bf16[1024,768]{1,0:T(8,128)(2,1)} %copy-done.6, bf16[1024,768]{1,0:T(8,128)(2,1)} %copy-done.6, f32[1024,256]{1,0:T(8,128)} %copy-done.33, ...), custom_call_target="tpu_custom_call" | custom-call | flops 1 | bytes 1 | tf_op jit(solution)/shard_map/pallas_call | solution.py:756
  342.0 3.8 shard_map.195
  347.8 7.9 %shard_map.196 = (bf16[128,2048]{1,0:T(8,128)(2,1)S(1)}, bf16[128,2048]{1,0:T(8,128)(2,1)S(1)}, bf16[128,2048]{1,0:T(8,128)(2,1)S(1)}, bf16[128,2048]{1,0:T(8,12...) custom-call(s32[7]{0:T(128)S(1)} %stack.81.place_ref, ...), custom_call_target="tpu_custom_call" | custom-call | flops 1 | bytes 1 | tf_op jit(solution)/shard_map/pallas_call | solution.py:335
  363.8 3.3 collective-permute-done.49
  367.1 3.2 collective-permute-start.50
  370.4 11.2 %shard_map.197 = bf16[2048,1152]{1,0:T(8,128)(2,1)} custom-call(s32[8]{0:T(128)S(1)} %copy-done.43, bf16[1024,2048]{1,0:T(8,128)(2,1)} %get-tuple-element.127.refs_0_, bf16[1024,768]{1,0:T(8,128)(2,1)} %shard_map.194.refs_0_.refs_1_.refs_2_.refs_3_.refs_4_.refs_5_.refs_6_, ...), custom_call_target="tpu_custom_call" | custom-call | flops 1 | bytes 1 | tf_op jit(solution)/shard_map/pallas_call | solution.py:515
  381.6 4.6 all-to-all-start.1
  391.2 2.0 collective-permute-start.54
  393.2 8.9 %collective-permute-done.33.refs_3_ = bf16[128,2048]{1,0:T(8,128)(2,1)S(1)} collective-permute-done((bf16[128,2048]{1,0:T(8,128)(2,1)}, bf16[128,2048]{1,0:T(8,128)(2,1)S(1)}, u32[]{:S(2)}, u32[]{:S(2)}) %collective-permute-start.33) | collective-permute-done | bytes 524320 | tf_op jit(solution)/shard_map/ppermute | solution.py:59
  402.7 2.0 collective-permute-start.35
  407.7 9.2 %collective-permute-done.53 = bf16[128,2048]{1,0:T(8,128)(2,1)S(1)} collective-permute-done((bf16[128,2048]{1,0:T(8,128)(2,1)S(1)}, bf16[128,2048]{1,0:T(8,128)(2,1)S(1)}, u32[]{:S(2)}, u32[]{:S(2)}) %collective-permute-start.53) | collective-permute-done | bytes 524320 | tf_op jit(solution)/shard_map/ppermute | solution.py:59
  420.4 2.1 collective-permute-done.34.refs_5_
  422.6 2.6 collective-permute-start.58
  428.9 6.7 %collective-permute-done.56.refs_3_ = bf16[128,2048]{1,0:T(8,128)(2,1)S(1)} collective-permute-done((bf16[128,2048]{1,0:T(8,128)(2,1)S(1)}, bf16[128,2048]{1,0:T(8,128)(2,1)S(1)}, u32[]{:S(2)}, u32[]{:S(2)}) %collective-permute-start.56) | collective-permute-done | bytes 524320 | tf_op jit(solution)/shard_map/ppermute | solution.py:59
  439.3 2.1 all-to-all-done.1
  441.5 3.1 convert_reduce_fusion
  444.7 3.1 collective-permute-start.63
  449.7 11.2 %collective-permute-done.63 = bf16[128,1152]{1,0:T(8,128)(2,1)S(1)} collective-permute-done((bf16[128,1152]{1,0:T(8,128)(2,1)S(1)}, bf16[128,1152]{1,0:T(8,128)(2,1)S(1)}, u32[]{:S(2)}, u32[]{:S(2)}) %collective-permute-start.63) | collective-permute-done | bytes 294944 | tf_op jit(solution)/shard_map/ppermute | solution.py:573
  460.8 2.6 collective-permute-start.59
  464.6 2.8 collective-permute-done.59.refs_6_
  472.5 3.7 collective-permute-start.66
  479.5 6.2 %all-to-all-start.2 = ((f32[8,4,128]{2,1,0:T(4,128)}), f32[8,4,128]{2,1,0:T(4,128)S(1)}, u32[]{:S(2)}, u32[]{:S(2)}) async-start(f32[8,4,128]{2,1,0:T(4,128)} %broadcast_in_dim.8), calls=%async_computation.2 | async-start | bytes 32768 | tf_op jit(solution)/shard_map/all_to_all | solution.py:223
  485.8 3.8 shard_map.198
  491.2 1.9 copy.70
  493.7 4.2 shard_map.199
  (351 shorter events, 115.9 us)
Async XLA Ops:
  12.9 37.3 %all-to-all-start = ((bf16[8,144,1024]{2,1,0:T(8,128)(2,1)}), bf16[8,144,1024]{2,1,0:T(8,128)(2,1)S(1)}, u32[]{:S(2)}, u32[]{:S(2)}) async-start(bf16[8,144,1024]{2,1,0:T(8,128)(2,1)} %broadcast_in_dim.6), calls=%async_computation | async-start | bytes 4718592 | tf_op jit(solution)/shard_map/all_to_all | solution.py:232
  21.0 150.4 %all-gather.2.cloned.1.call-start = ((), (), s32[]{:S(2)}) async-start(), calls=%async_computation.4 | async-start | bytes 9437184 | tf_op jit(solution)/shard_map/all_gather | solution.py:553
  50.2 14.6 %collective-permute-start.19 = (bf16[128,2048]{1,0:T(8,128)(2,1)S(1)}, bf16[128,2048]{1,0:T(8,128)(2,1)S(1)}, u32[]{:S(2)}, u32[]{:S(2)}) collective-permute-start(bf16[128,2048]{1,0:T(8,128)(2,1)S(1)} %pad_maximum_fusion.5), channel_id=1, source_target_pairs={{0,64},{64,0},{1,65},{65,1},{2,66},{66,2},{3,67},{67,3},{4,68},{68... | collective-permute-start | bytes 1572872 | tf_op jit(solution)/shard_map/ppermute | solution.py:547
  66.0 404.6 %reduce-scatter.2.cloned.1.call-start = ((), (), s32[]{:S(2)}) async-start(), calls=%async_computation.5 | async-start | bytes 9437184 | tf_op jit(solution)/shard_map/reduce_scatter | solution.py:557
  90.8 8.6 %collective-permute-start.5 = (bf16[64,2048]{1,0:T(8,128)(2,1)S(1)}, bf16[64,2048]{1,0:T(8,128)(2,1)}, u32[]{:S(2)}, u32[]{:S(2)}) collective-permute-start(bf16[64,2048]{1,0:T(8,128)(2,1)S(1)} %get-tuple-element.81), channel_id=1, source_target_pairs={{0,1},{1,0},{2,3},{3,2},{4,5},{5,4},{6,7},{7,6},{8,14},{9,15},{10,... | collective-permute-start | bytes 786440 | tf_op jit(solution)/shard_map/ppermute | solution.py:59
  100.7 9.3 %collective-permute-start.2 = (bf16[64,2048]{1,0:T(8,128)(2,1)S(1)}, bf16[64,2048]{1,0:T(8,128)(2,1)S(1)}, u32[]{:S(2)}, u32[]{:S(2)}) collective-permute-start(bf16[64,2048]{1,0:T(8,128)(2,1)S(1)} %get-tuple-element.218), channel_id=1, source_target_pairs={{0,2},{1,3},{2,4},{3,5},{4,6},{5,7},{6,0},{7,1},{8,10},{9,11},{10,... | collective-permute-start | bytes 786440 | tf_op jit(solution)/shard_map/ppermute | solution.py:59
  102.3 11.5 %collective-permute-start.3 = (bf16[128,2048]{1,0:T(8,128)(2,1)S(1)}, bf16[128,2048]{1,0:T(8,128)(2,1)S(1)}, u32[]{:S(2)}, u32[]{:S(2)}) collective-permute-start(bf16[128,2048]{1,0:T(8,128)(2,1)S(1)} %pad_maximum_fusion.3), channel_id=1, source_target_pairs={{0,1},{1,0},{2,3},{3,2},{4,5},{5,4},{6,7},{7,6},{8,10},{9,11},{10,... | collective-permute-start | bytes 1572872 | tf_op jit(solution)/shard_map/ppermute | solution.py:59
  103.1 14.1 %collective-permute-start.7 = (bf16[128,2048]{1,0:T(8,128)(2,1)S(1)}, bf16[128,2048]{1,0:T(8,128)(2,1)S(1)}, u32[]{:S(2)}, u32[]{:S(2)}) collective-permute-start(bf16[128,2048]{1,0:T(8,128)(2,1)S(1)} %pad_maximum_fusion.4), channel_id=1, source_target_pairs={{0,1},{1,0},{2,3},{3,2},{4,5},{5,4},{6,7},{7,6},{8,14},{9,15},{10,... | collective-permute-start | bytes 1572872 | tf_op jit(solution)/shard_map/ppermute | solution.py:59
  104.5 9.2 %collective-permute-start.6 = (bf16[64,2048]{1,0:T(8,128)(2,1)S(1)}, bf16[64,2048]{1,0:T(8,128)(2,1)S(1)}, u32[]{:S(2)}, u32[]{:S(2)}) collective-permute-start(bf16[64,2048]{1,0:T(8,128)(2,1)S(1)} %get-tuple-element.219), channel_id=1, source_target_pairs={{0,6},{1,7},{2,0},{3,1},{4,2},{5,3},{6,4},{7,5},{8,14},{9,15},{10,... | collective-permute-start | bytes 786440 | tf_op jit(solution)/shard_map/ppermute | solution.py:59
  117.6 12.2 %collective-permute-start.9 = (bf16[128,2048]{1,0:T(8,128)(2,1)S(1)}, bf16[128,2048]{1,0:T(8,128)(2,1)S(1)}, u32[]{:S(2)}, u32[]{:S(2)}) collective-permute-start(bf16[128,2048]{1,0:T(8,128)(2,1)S(1)} %get-tuple-element.234), channel_id=1, source_target_pairs={{0,1},{1,0},{2,3},{3,2},{4,5},{5,4},{6,7},{7,6},{8,9},{9,8},{10,11... | collective-permute-start | bytes 1572872 | tf_op jit(solution)/shard_map/ppermute | solution.py:59
  118.4 11.8 %collective-permute-start.8 = (bf16[128,2048]{1,0:T(8,128)(2,1)S(1)}, bf16[128,2048]{1,0:T(8,128)(2,1)S(1)}, u32[]{:S(2)}, u32[]{:S(2)}) collective-permute-start(bf16[128,2048]{1,0:T(8,128)(2,1)S(1)} %get-tuple-element.235), channel_id=1, source_target_pairs={{0,6},{1,7},{2,0},{3,1},{4,2},{5,3},{6,4},{7,5},{8,14},{9,15},{10,... | collective-permute-start | bytes 1572872 | tf_op jit(solution)/shard_map/ppermute | solution.py:59
  118.9 13.2 %collective-permute-start.4 = (bf16[128,2048]{1,0:T(8,128)(2,1)S(1)}, bf16[128,2048]{1,0:T(8,128)(2,1)S(1)}, u32[]{:S(2)}, u32[]{:S(2)}) collective-permute-start(bf16[128,2048]{1,0:T(8,128)(2,1)S(1)} %get-tuple-element.233), channel_id=1, source_target_pairs={{0,2},{1,3},{2,4},{3,5},{4,6},{5,7},{6,0},{7,1},{8,10},{9,11},{10,... | collective-permute-start | bytes 1572872 | tf_op jit(solution)/shard_map/ppermute | solution.py:59
  134.3 12.4 %collective-permute-start.10 = (bf16[128,2048]{1,0:T(8,128)(2,1)S(1)}, bf16[128,2048]{1,0:T(8,128)(2,1)S(1)}, u32[]{:S(2)}, u32[]{:S(2)}) collective-permute-start(bf16[128,2048]{1,0:T(8,128)(2,1)S(1)} %add_convert_fusion.1.refs_0_), channel_id=1, source_target_pairs={{0,6},{1,7},{2,0},{3,1},{4,2},{5,3},{6,4},{7,5},{8,14},{9,15},{10,... | collective-permute-start | bytes 1572872 | tf_op jit(solution)/shard_map/ppermute | solution.py:59
  137.3 11.8 %collective-permute-start.11 = (bf16[128,2048]{1,0:T(8,128)(2,1)S(1)}, bf16[128,2048]{1,0:T(8,128)(2,1)S(1)}, u32[]{:S(2)}, u32[]{:S(2)}) collective-permute-start(bf16[128,2048]{1,0:T(8,128)(2,1)S(1)} %add_convert_fusion.1.refs_0_), channel_id=1, source_target_pairs={{0,2},{1,3},{2,4},{3,5},{4,6},{5,7},{6,0},{7,1},{8,10},{9,11},{10,... | collective-permute-start | bytes 1572872 | tf_op jit(solution)/shard_map/ppermute | solution.py:59
  137.3 11.8 %collective-permute-start.14 = (bf16[128,2048]{1,0:T(8,128)(2,1)S(1)}, bf16[128,2048]{1,0:T(8,128)(2,1)S(1)}, u32[]{:S(2)}, u32[]{:S(2)}) collective-permute-start(bf16[128,2048]{1,0:T(8,128)(2,1)S(1)} %add_convert_fusion.1.refs_0_), channel_id=1, source_target_pairs={{0,1},{1,0},{2,3},{3,2},{4,5},{5,4},{6,7},{7,6},{8,9},{9,8},{10,11... | collective-permute-start | bytes 1572872 | tf_op jit(solution)/shard_map/ppermute | solution.py:59
  149.2 10.8 %collective-permute-start.16 = (bf16[128,2048]{1,0:T(8,128)(2,1)S(1)}, bf16[128,2048]{1,0:T(8,128)(2,1)S(1)}, u32[]{:S(2)}, u32[]{:S(2)}) collective-permute-start(bf16[128,2048]{1,0:T(8,128)(2,1)S(1)} %get-tuple-element.231), channel_id=1, source_target_pairs={{0,1},{1,0},{2,3},{3,2},{4,5},{5,4},{6,7},{7,6},{8,10},{9,11},{10,... | collective-permute-start | bytes 1572872 | tf_op jit(solution)/shard_map/ppermute | solution.py:59
  150.7 9.3 %collective-permute-start.12 = (bf16[64,2048]{1,0:T(8,128)(2,1)S(1)}, bf16[64,2048]{1,0:T(8,128)(2,1)S(1)}, u32[]{:S(2)}, u32[]{:S(2)}) collective-permute-start(bf16[64,2048]{1,0:T(8,128)(2,1)S(1)} %slice.280), channel_id=1, source_target_pairs={{0,2},{1,3},{2,4},{3,5},{4,6},{5,7},{6,0},{7,1},{8,10},{9,11},{10,... | collective-permute-start | bytes 786440 | tf_op jit(solution)/shard_map/ppermute | solution.py:59
  150.9 13.2 %collective-permute-start.15 = (bf16[128,2048]{1,0:T(8,128)(2,1)S(1)}, bf16[128,2048]{1,0:T(8,128)(2,1)S(1)}, u32[]{:S(2)}, u32[]{:S(2)}) collective-permute-start(bf16[128,2048]{1,0:T(8,128)(2,1)S(1)} %get-tuple-element.232), channel_id=1, source_target_pairs={{0,1},{1,0},{2,3},{3,2},{4,5},{5,4},{6,7},{7,6},{8,14},{9,15},{10,... | collective-permute-start | bytes 1572872 | tf_op jit(solution)/shard_map/ppermute | solution.py:59
  151.6 10.0 %collective-permute-start.13 = (bf16[64,2048]{1,0:T(8,128)(2,1)S(1)}, bf16[64,2048]{1,0:T(8,128)(2,1)S(1)}, u32[]{:S(2)}, u32[]{:S(2)}) collective-permute-start(bf16[64,2048]{1,0:T(8,128)(2,1)S(1)} %slice.281), channel_id=1, source_target_pairs={{0,6},{1,7},{2,0},{3,1},{4,2},{5,3},{6,4},{7,5},{8,14},{9,15},{10,... | collective-permute-start | bytes 786440 | tf_op jit(solution)/shard_map/ppermute | solution.py:59
  202.4 22.5 %collective-permute-start.20 = (bf16[64,4096]{1,0:T(8,128)(2,1)S(1)}, bf16[64,4096]{1,0:T(8,128)(2,1)S(1)}, u32[]{:S(2)}, u32[]{:S(2)}) collective-permute-start(bf16[64,4096]{1,0:T(8,128)(2,1)S(1)} %get-tuple-element.94), channel_id=1, source_target_pairs={{0,1},{1,0},{2,3},{3,2},{4,5},{5,4},{6,7},{7,6},{8,10},{9,11},{10,... | collective-permute-start | bytes 1572872 | tf_op jit(solution)/shard_map/ppermute | solution.py:59
  203.9 21.0 %collective-permute-start.24 = (bf16[64,4096]{1,0:T(8,128)(2,1)S(1)}, bf16[64,4096]{1,0:T(8,128)(2,1)S(1)}, u32[]{:S(2)}, u32[]{:S(2)}) collective-permute-start(bf16[64,4096]{1,0:T(8,128)(2,1)S(1)} %get-tuple-element.95), channel_id=1, source_target_pairs={{0,1},{1,0},{2,3},{3,2},{4,5},{5,4},{6,7},{7,6},{8,14},{9,15},{10,... | collective-permute-start | bytes 1572872 | tf_op jit(solution)/shard_map/ppermute | solution.py:59
  226.2 15.0 %collective-permute-start.21 = (bf16[64,4096]{1,0:T(8,128)(2,1)S(1)}, bf16[64,4096]{1,0:T(8,128)(2,1)}, u32[]{:S(2)}, u32[]{:S(2)}) collective-permute-start(bf16[64,4096]{1,0:T(8,128)(2,1)S(1)} %get-tuple-element.207), channel_id=1, source_target_pairs={{0,2},{1,3},{2,4},{3,5},{4,6},{5,7},{6,0},{7,1},{8,10},{9,11},{10,... | collective-permute-start | bytes 1572872 | tf_op jit(solution)/shard_map/ppermute | solution.py:59
  227.4 30.3 %collective-permute-start.22 = (bf16[128,4096]{1,0:T(8,128)(2,1)}, bf16[128,4096]{1,0:T(8,128)(2,1)}, u32[]{:S(2)}, u32[]{:S(2)}) collective-permute-start(bf16[128,4096]{1,0:T(8,128)(2,1)} %pad_maximum_fusion.1), channel_id=1, source_target_pairs={{0,1},{1,0},{2,3},{3,2},{4,5},{5,4},{6,7},{7,6},{8,10},{9,11},{10,... | collective-permute-start | bytes 3145736 | tf_op jit(solution)/shard_map/ppermute | solution.py:59
  229.9 27.8 %collective-permute-start.26 = (bf16[128,4096]{1,0:T(8,128)(2,1)}, bf16[128,4096]{1,0:T(8,128)(2,1)}, u32[]{:S(2)}, u32[]{:S(2)}) collective-permute-start(bf16[128,4096]{1,0:T(8,128)(2,1)} %pad_maximum_fusion.2), channel_id=1, source_target_pairs={{0,1},{1,0},{2,3},{3,2},{4,5},{5,4},{6,7},{7,6},{8,14},{9,15},{10,... | collective-permute-start | bytes 3145736 | tf_op jit(solution)/shard_map/ppermute | solution.py:59
  230.6 26.7 %collective-permute-start.25 = (bf16[64,4096]{1,0:T(8,128)(2,1)}, bf16[64,4096]{1,0:T(8,128)(2,1)S(1)}, u32[]{:S(2)}, u32[]{:S(2)}) collective-permute-start(bf16[64,4096]{1,0:T(8,128)(2,1)} %get-tuple-element.208), channel_id=1, source_target_pairs={{0,6},{1,7},{2,0},{3,1},{4,2},{5,3},{6,4},{7,5},{8,14},{9,15},{10,... | collective-permute-start | bytes 1572872 | tf_op jit(solution)/shard_map/ppermute | solution.py:59
  261.1 21.2 %collective-permute-start.28 = (bf16[128,4096]{1,0:T(8,128)(2,1)S(1)}, bf16[128,4096]{1,0:T(8,128)(2,1)S(1)}, u32[]{:S(2)}, u32[]{:S(2)}) collective-permute-start(bf16[128,4096]{1,0:T(8,128)(2,1)S(1)} %get-tuple-element.214), channel_id=1, source_target_pairs={{0,1},{1,0},{2,3},{3,2},{4,5},{5,4},{6,7},{7,6},{8,9},{9,8},{10,11... | collective-permute-start | bytes 3145736 | tf_op jit(solution)/shard_map/ppermute | solution.py:59
  262.6 21.0 %collective-permute-start.27 = (bf16[128,4096]{1,0:T(8,128)(2,1)S(1)}, bf16[128,4096]{1,0:T(8,128)(2,1)S(1)}, u32[]{:S(2)}, u32[]{:S(2)}) collective-permute-start(bf16[128,4096]{1,0:T(8,128)(2,1)S(1)} %get-tuple-element.215), channel_id=1, source_target_pairs={{0,6},{1,7},{2,0},{3,1},{4,2},{5,3},{6,4},{7,5},{8,14},{9,15},{10,... | collective-permute-start | bytes 3145736 | tf_op jit(solution)/shard_map/ppermute | solution.py:59
  265.4 20.2 %collective-permute-start.23 = (bf16[128,4096]{1,0:T(8,128)(2,1)S(1)}, bf16[128,4096]{1,0:T(8,128)(2,1)S(1)}, u32[]{:S(2)}, u32[]{:S(2)}) collective-permute-start(bf16[128,4096]{1,0:T(8,128)(2,1)S(1)} %get-tuple-element.213), channel_id=1, source_target_pairs={{0,2},{1,3},{2,4},{3,5},{4,6},{5,7},{6,0},{7,1},{8,10},{9,11},{10,... | collective-permute-start | bytes 3145736 | tf_op jit(solution)/shard_map/ppermute | solution.py:59
  289.4 9.7 %collective-permute-start.29 = (bf16[128,2048]{1,0:T(8,128)(2,1)S(1)}, bf16[128,2048]{1,0:T(8,128)(2,1)S(1)}, u32[]{:S(2)}, u32[]{:S(2)}) collective-permute-start(bf16[128,2048]{1,0:T(8,128)(2,1)S(1)} %get-tuple-element.201.refs_5_.refs_4_.refs_14_), channel_id=1, source_target_pairs={{0,2},{1,3},{2,4},{3,5},{4,6},{5,7},{6,0},{7,1},{8,10},{9,11},{10,... | collective-permute-start | bytes 1572872 | tf_op jit(solution)/shard_map/ppermute | solution.py:59
  289.7 9.5 %collective-permute-start.38 = (bf16[128,2048]{1,0:T(8,128)(2,1)S(1)}, bf16[128,2048]{1,0:T(8,128)(2,1)S(1)}, u32[]{:S(2)}, u32[]{:S(2)}) collective-permute-start(bf16[128,2048]{1,0:T(8,128)(2,1)S(1)} %get-tuple-element.201.refs_5_.refs_4_.refs_14_), channel_id=1, source_target_pairs={{0,6},{1,7},{2,0},{3,1},{4,2},{5,3},{6,4},{7,5},{8,14},{9,15},{10,... | collective-permute-start | bytes 1572872 | tf_op jit(solution)/shard_map/ppermute | solution.py:59
  291.9 9.2 %collective-permute-start.40 = (bf16[128,2048]{1,0:T(8,128)(2,1)S(1)}, bf16[128,2048]{1,0:T(8,128)(2,1)S(1)}, u32[]{:S(2)}, u32[]{:S(2)}) collective-permute-start(bf16[128,2048]{1,0:T(8,128)(2,1)S(1)} %get-tuple-element.201.refs_5_.refs_4_.refs_14_), channel_id=1, source_target_pairs={{0,1},{1,0},{2,3},{3,2},{4,5},{5,4},{6,7},{7,6},{8,9},{9,8},{10,11... | collective-permute-start | bytes 1572872 | tf_op jit(solution)/shard_map/ppermute | solution.py:59
  301.2 9.3 %collective-permute-start.42 = (bf16[128,2048]{1,0:T(8,128)(2,1)S(1)}, bf16[128,2048]{1,0:T(8,128)(2,1)S(1)}, u32[]{:S(2)}, u32[]{:S(2)}) collective-permute-start(bf16[128,2048]{1,0:T(8,128)(2,1)S(1)} %get-tuple-element.226), channel_id=1, source_target_pairs={{0,1},{1,0},{2,3},{3,2},{4,5},{5,4},{6,7},{7,6},{8,10},{9,11},{10,... | collective-permute-start | bytes 1572872 | tf_op jit(solution)/shard_map/ppermute | solution.py:59
  302.6 14.9 %collective-permute-start.41 = (bf16[128,2048]{1,0:T(8,128)(2,1)S(1)}, bf16[128,2048]{1,0:T(8,128)(2,1)S(1)}, u32[]{:S(2)}, u32[]{:S(2)}) collective-permute-start(bf16[128,2048]{1,0:T(8,128)(2,1)S(1)} %get-tuple-element.227), channel_id=1, source_target_pairs={{0,1},{1,0},{2,3},{3,2},{4,5},{5,4},{6,7},{7,6},{8,14},{9,15},{10,... | collective-permute-start | bytes 1572872 | tf_op jit(solution)/shard_map/ppermute | solution.py:59
  310.5 12.9 %collective-permute-start.43 = (bf16[64,2048]{1,0:T(8,128)(2,1)S(1)}, bf16[64,2048]{1,0:T(8,128)(2,1)S(1)}, u32[]{:S(2)}, u32[]{:S(2)}) collective-permute-start(bf16[64,2048]{1,0:T(8,128)(2,1)S(1)} %slice_select_fusion.1), channel_id=1, source_target_pairs={{0,1},{1,0},{2,3},{3,2},{4,5},{5,4},{6,7},{7,6},{8,10},{9,11},{10,... | collective-permute-start | bytes 786440 | tf_op jit(solution)/shard_map/ppermute | solution.py:59
  317.6 9.7 %collective-permute-start.44 = (bf16[64,2048]{1,0:T(8,128)(2,1)S(1)}, bf16[64,2048]{1,0:T(8,128)(2,1)S(1)}, u32[]{:S(2)}, u32[]{:S(2)}) collective-permute-start(bf16[64,2048]{1,0:T(8,128)(2,1)S(1)} %slice_select_fusion), channel_id=1, source_target_pairs={{0,1},{1,0},{2,3},{3,2},{4,5},{5,4},{6,7},{7,6},{8,14},{9,15},{10,... | collective-permute-start | bytes 786440 | tf_op jit(solution)/shard_map/ppermute | solution.py:59
  318.8 83.8 %collective-permute-start.31 = (bf16[128,2048]{1,0:T(8,128)(2,1)}, bf16[128,2048]{1,0:T(8,128)(2,1)S(1)}, u32[]{:S(2)}, u32[]{:S(2)}) collective-permute-start(bf16[128,2048]{1,0:T(8,128)(2,1)} %get-tuple-element.134.refs_1_), channel_id=1, source_target_pairs={{0,1},{1,0},{2,3},{3,2},{4,5},{5,4},{6,7},{7,6},{8,9},{9,8},{10,11... | collective-permute-start | bytes 1572872 | tf_op jit(solution)/shard_map/ppermute | solution.py:59
  319.9 82.6 %collective-permute-start.32 = (bf16[128,2048]{1,0:T(8,128)(2,1)}, bf16[128,2048]{1,0:T(8,128)(2,1)S(1)}, u32[]{:S(2)}, u32[]{:S(2)}) collective-permute-start(bf16[128,2048]{1,0:T(8,128)(2,1)} %get-tuple-element.134.refs_1_), channel_id=1, source_target_pairs={{0,6},{1,7},{2,0},{3,1},{4,2},{5,3},{6,4},{7,5},{8,14},{9,15},{10,... | collective-permute-start | bytes 1572872 | tf_op jit(solution)/shard_map/ppermute | solution.py:59
  345.7 13.4 %collective-permute-start.47 = (bf16[64,2048]{1,0:T(8,128)(2,1)S(1)}, bf16[64,2048]{1,0:T(8,128)(2,1)S(1)}, u32[]{:S(2)}, u32[]{:S(2)}) collective-permute-start(bf16[64,2048]{1,0:T(8,128)(2,1)S(1)} %get-tuple-element.113), channel_id=1, source_target_pairs={{0,1},{1,0},{2,3},{3,2},{4,5},{5,4},{6,7},{7,6},{8,14},{9,15},{10,... | collective-permute-start | bytes 786440 | tf_op jit(solution)/shard_map/ppermute | solution.py:59
  346.5 12.6 %collective-permute-start.45 = (bf16[64,2048]{1,0:T(8,128)(2,1)S(1)}, bf16[64,2048]{1,0:T(8,128)(2,1)S(1)}, u32[]{:S(2)}, u32[]{:S(2)}) collective-permute-start(bf16[64,2048]{1,0:T(8,128)(2,1)S(1)} %get-tuple-element.112), channel_id=1, source_target_pairs={{0,1},{1,0},{2,3},{3,2},{4,5},{5,4},{6,7},{7,6},{8,10},{9,11},{10,... | collective-permute-start | bytes 786440 | tf_op jit(solution)/shard_map/ppermute | solution.py:59
  360.9 27.8 %collective-permute-start.46 = (bf16[128,2048]{1,0:T(8,128)(2,1)}, bf16[128,2048]{1,0:T(8,128)(2,1)}, u32[]{:S(2)}, u32[]{:S(2)}) collective-permute-start(bf16[128,2048]{1,0:T(8,128)(2,1)} %pad_maximum_fusion.6), channel_id=1, source_target_pairs={{0,1},{1,0},{2,3},{3,2},{4,5},{5,4},{6,7},{7,6},{8,10},{9,11},{10,... | collective-permute-start | bytes 1572872 | tf_op jit(solution)/shard_map/ppermute | solution.py:59
  362.5 26.3 %collective-permute-start.48 = (bf16[128,2048]{1,0:T(8,128)(2,1)}, bf16[128,2048]{1,0:T(8,128)(2,1)}, u32[]{:S(2)}, u32[]{:S(2)}) collective-permute-start(bf16[128,2048]{1,0:T(8,128)(2,1)} %pad_maximum_fusion.7), channel_id=1, source_target_pairs={{0,1},{1,0},{2,3},{3,2},{4,5},{5,4},{6,7},{7,6},{8,14},{9,15},{10,... | collective-permute-start | bytes 1572872 | tf_op jit(solution)/shard_map/ppermute | solution.py:59
  367.1 20.4 %collective-permute-start.50 = (bf16[64,2048]{1,0:T(8,128)(2,1)S(1)}, bf16[64,2048]{1,0:T(8,128)(2,1)}, u32[]{:S(2)}, u32[]{:S(2)}) collective-permute-start(bf16[64,2048]{1,0:T(8,128)(2,1)S(1)} %get-tuple-element.211), channel_id=1, source_target_pairs={{0,6},{1,7},{2,0},{3,1},{4,2},{5,3},{6,4},{7,5},{8,14},{9,15},{10,... | collective-permute-start | bytes 786440 | tf_op jit(solution)/shard_map/ppermute | solution.py:59
  381.6 59.9 %all-to-all-start.1 = ((bf16[8,2,128,1152]{3,2,1,0:T(8,128)(2,1)}), bf16[8,2,128,1152]{3,2,1,0:T(8,128)(2,1)}, u32[]{:S(2)}, u32[]{:S(2)}) async-start(bf16[8,2,128,1152]{3,2,1,0:T(8,128)(2,1)} %bitcast.81), calls=%async_computation.1 | async-start | bytes 9437184 | tf_op jit(solution)/shard_map/all_to_all | solution.py:568
  387.5 14.6 %collective-permute-start.33 = (bf16[128,2048]{1,0:T(8,128)(2,1)}, bf16[128,2048]{1,0:T(8,128)(2,1)S(1)}, u32[]{:S(2)}, u32[]{:S(2)}) collective-permute-start(bf16[128,2048]{1,0:T(8,128)(2,1)} %get-tuple-element.134.refs_1_), channel_id=1, source_target_pairs={{0,2},{1,3},{2,4},{3,5},{4,6},{5,7},{6,0},{7,1},{8,10},{9,11},{10,... | collective-permute-start | bytes 1572872 | tf_op jit(solution)/shard_map/ppermute | solution.py:59
  390.5 15.2 %collective-permute-start.55 = (bf16[128,2048]{1,0:T(8,128)(2,1)S(1)}, bf16[128,2048]{1,0:T(8,128)(2,1)S(1)}, u32[]{:S(2)}, u32[]{:S(2)}) collective-permute-start(bf16[128,2048]{1,0:T(8,128)(2,1)S(1)} %get-tuple-element.224), channel_id=1, source_target_pairs={{0,1},{1,0},{2,3},{3,2},{4,5},{5,4},{6,7},{7,6},{8,9},{9,8},{10,11... | collective-permute-start | bytes 1572872 | tf_op jit(solution)/shard_map/ppermute | solution.py:59
  391.2 15.1 %collective-permute-start.54 = (bf16[128,2048]{1,0:T(8,128)(2,1)S(1)}, bf16[128,2048]{1,0:T(8,128)(2,1)S(1)}, u32[]{:S(2)}, u32[]{:S(2)}) collective-permute-start(bf16[128,2048]{1,0:T(8,128)(2,1)S(1)} %get-tuple-element.225), channel_id=1, source_target_pairs={{0,6},{1,7},{2,0},{3,1},{4,2},{5,3},{6,4},{7,5},{8,14},{9,15},{10,... | collective-permute-start | bytes 1572872 | tf_op jit(solution)/shard_map/ppermute | solution.py:59
  402.1 14.8 %collective-permute-start.53 = (bf16[128,2048]{1,0:T(8,128)(2,1)S(1)}, bf16[128,2048]{1,0:T(8,128)(2,1)S(1)}, u32[]{:S(2)}, u32[]{:S(2)}) collective-permute-start(bf16[128,2048]{1,0:T(8,128)(2,1)S(1)} %get-tuple-element.223), channel_id=1, source_target_pairs={{0,2},{1,3},{2,4},{3,5},{4,6},{5,7},{6,0},{7,1},{8,10},{9,11},{10,... | collective-permute-start | bytes 1572872 | tf_op jit(solution)/shard_map/ppermute | solution.py:59
  402.4 20.1 %collective-permute-start.34 = (bf16[64,2048]{1,0:T(8,128)(2,1)S(1)}, bf16[64,2048]{1,0:T(8,128)(2,1)S(1)}, u32[]{:S(2)}, u32[]{:S(2)}) collective-permute-start(bf16[64,2048]{1,0:T(8,128)(2,1)S(1)} %slice.291), channel_id=1, source_target_pairs={{0,2},{1,3},{2,4},{3,5},{4,6},{5,7},{6,0},{7,1},{8,10},{9,11},{10,... | collective-permute-start | bytes 786440 | tf_op jit(solution)/shard_map/ppermute | solution.py:59
  402.7 22.5 %collective-permute-start.35 = (bf16[64,2048]{1,0:T(8,128)(2,1)S(1)}, bf16[64,2048]{1,0:T(8,128)(2,1)}, u32[]{:S(2)}, u32[]{:S(2)}) collective-permute-start(bf16[64,2048]{1,0:T(8,128)(2,1)S(1)} %slice.292), channel_id=1, source_target_pairs={{0,6},{1,7},{2,0},{3,1},{4,2},{5,3},{6,4},{7,5},{8,14},{9,15},{10,... | collective-permute-start | bytes 786440 | tf_op jit(solution)/shard_map/ppermute | solution.py:59
  405.7 20.0 %collective-permute-start.36 = (bf16[128,2048]{1,0:T(8,128)(2,1)}, bf16[128,2048]{1,0:T(8,128)(2,1)}, u32[]{:S(2)}, u32[]{:S(2)}) collective-permute-start(bf16[128,2048]{1,0:T(8,128)(2,1)} %get-tuple-element.229), channel_id=1, source_target_pairs={{0,1},{1,0},{2,3},{3,2},{4,5},{5,4},{6,7},{7,6},{8,10},{9,11},{10,... | collective-permute-start | bytes 1572872 | tf_op jit(solution)/shard_map/ppermute | solution.py:59
  406.4 19.3 %collective-permute-start.37 = (bf16[128,2048]{1,0:T(8,128)(2,1)}, bf16[128,2048]{1,0:T(8,128)(2,1)}, u32[]{:S(2)}, u32[]{:S(2)}) collective-permute-start(bf16[128,2048]{1,0:T(8,128)(2,1)} %get-tuple-element.228), channel_id=1, source_target_pairs={{0,1},{1,0},{2,3},{3,2},{4,5},{5,4},{6,7},{7,6},{8,14},{9,15},{10,... | collective-permute-start | bytes 1572872 | tf_op jit(solution)/shard_map/ppermute | solution.py:59
  420.1 15.5 %collective-permute-start.56 = (bf16[128,2048]{1,0:T(8,128)(2,1)S(1)}, bf16[128,2048]{1,0:T(8,128)(2,1)S(1)}, u32[]{:S(2)}, u32[]{:S(2)}) collective-permute-start(bf16[128,2048]{1,0:T(8,128)(2,1)S(1)} %fusion.15.refs_1_), channel_id=1, source_target_pairs={{0,2},{1,3},{2,4},{3,5},{4,6},{5,7},{6,0},{7,1},{8,10},{9,11},{10,... | collective-permute-start | bytes 1572872 | tf_op jit(solution)/shard_map/ppermute | solution.py:59
  422.6 13.1 %collective-permute-start.58 = (bf16[128,2048]{1,0:T(8,128)(2,1)S(1)}, bf16[128,2048]{1,0:T(8,128)(2,1)S(1)}, u32[]{:S(2)}, u32[]{:S(2)}) collective-permute-start(bf16[128,2048]{1,0:T(8,128)(2,1)S(1)} %fusion.15.refs_1_), channel_id=1, source_target_pairs={{0,6},{1,7},{2,0},{3,1},{4,2},{5,3},{6,4},{7,5},{8,14},{9,15},{10,... | collective-permute-start | bytes 1572872 | tf_op jit(solution)/shard_map/ppermute | solution.py:59
  425.1 11.0 %collective-permute-start.60 = (bf16[128,2048]{1,0:T(8,128)(2,1)S(1)}, bf16[128,2048]{1,0:T(8,128)(2,1)S(1)}, u32[]{:S(2)}, u32[]{:S(2)}) collective-permute-start(bf16[128,2048]{1,0:T(8,128)(2,1)S(1)} %fusion.15.refs_1_), channel_id=1, source_target_pairs={{0,1},{1,0},{2,3},{3,2},{4,5},{5,4},{6,7},{7,6},{8,9},{9,8},{10,11... | collective-permute-start | bytes 1572872 | tf_op jit(solution)/shard_map/ppermute | solution.py:59
  427.4 58.4 %collective-permute-start.51 = (bf16[64,2048]{1,0:T(8,128)(2,1)}, bf16[64,2048]{1,0:T(8,128)(2,1)}, u32[]{:S(2)}, u32[]{:S(2)}) collective-permute-start(bf16[64,2048]{1,0:T(8,128)(2,1)} %slice_select_fusion.7), channel_id=1, source_target_pairs={{0,1},{1,0},{2,3},{3,2},{4,5},{5,4},{6,7},{7,6},{8,10},{9,11},{10,... | collective-permute-start | bytes 786440 | tf_op jit(solution)/shard_map/ppermute | solution.py:59
  437.3 30.1 %collective-permute-start.61 = (bf16[128,2048]{1,0:T(8,128)(2,1)}, bf16[128,2048]{1,0:T(8,128)(2,1)}, u32[]{:S(2)}, u32[]{:S(2)}) collective-permute-start(bf16[128,2048]{1,0:T(8,128)(2,1)} %get-tuple-element.222), channel_id=1, source_target_pairs={{0,1},{1,0},{2,3},{3,2},{4,5},{5,4},{6,7},{7,6},{8,10},{9,11},{10,... | collective-permute-start | bytes 1572872 | tf_op jit(solution)/shard_map/ppermute | solution.py:59
  437.8 29.5 %collective-permute-start.62 = (bf16[128,2048]{1,0:T(8,128)(2,1)}, bf16[128,2048]{1,0:T(8,128)(2,1)}, u32[]{:S(2)}, u32[]{:S(2)}) collective-permute-start(bf16[128,2048]{1,0:T(8,128)(2,1)} %get-tuple-element.221), channel_id=1, source_target_pairs={{0,1},{1,0},{2,3},{3,2},{4,5},{5,4},{6,7},{7,6},{8,14},{9,15},{10,... | collective-permute-start | bytes 1572872 | tf_op jit(solution)/shard_map/ppermute | solution.py:59
  444.7 16.1 %collective-permute-start.63 = (bf16[128,1152]{1,0:T(8,128)(2,1)S(1)}, bf16[128,1152]{1,0:T(8,128)(2,1)S(1)}, u32[]{:S(2)}, u32[]{:S(2)}) collective-permute-start(bf16[128,1152]{1,0:T(8,128)(2,1)S(1)} %fusion.57), channel_id=1, source_target_pairs={{0,64},{64,0},{1,65},{65,1},{2,66},{66,2},{3,67},{67,3},{4,68},{68... | collective-permute-start | bytes 884744 | tf_op jit(solution)/shard_map/ppermute | solution.py:573
  449.6 14.8 %collective-permute-start.57 = (bf16[64,2048]{1,0:T(8,128)(2,1)S(1)}, bf16[64,2048]{1,0:T(8,128)(2,1)S(1)}, u32[]{:S(2)}, u32[]{:S(2)}) collective-permute-start(bf16[64,2048]{1,0:T(8,128)(2,1)S(1)} %slice.302), channel_id=1, source_target_pairs={{0,2},{1,3},{2,4},{3,5},{4,6},{5,7},{6,0},{7,1},{8,10},{9,11},{10,... | collective-permute-start | bytes 786440 | tf_op jit(solution)/shard_map/ppermute | solution.py:59
  464.4 21.4 %collective-permute-start.52 = (bf16[64,2048]{1,0:T(8,128)(2,1)}, bf16[64,2048]{1,0:T(8,128)(2,1)}, u32[]{:S(2)}, u32[]{:S(2)}) collective-permute-start(bf16[64,2048]{1,0:T(8,128)(2,1)} %slice_select_fusion.6), channel_id=1, source_target_pairs={{0,1},{1,0},{2,3},{3,2},{4,5},{5,4},{6,7},{7,6},{8,14},{9,15},{10,... | collective-permute-start | bytes 786440 | tf_op jit(solution)/shard_map/ppermute | solution.py:59
  469.9 23.8 %collective-permute-start.64 = (bf16[64,2048]{1,0:T(8,128)(2,1)}, bf16[64,2048]{1,0:T(8,128)(2,1)}, u32[]{:S(2)}, u32[]{:S(2)}) collective-permute-start(bf16[64,2048]{1,0:T(8,128)(2,1)} %slice_select_fusion.5), channel_id=1, source_target_pairs={{0,1},{1,0},{2,3},{3,2},{4,5},{5,4},{6,7},{7,6},{8,10},{9,11},{10,... | collective-permute-start | bytes 786440 | tf_op jit(solution)/shard_map/ppermute | solution.py:59
  472.5 25.5 %collective-permute-start.66 = (bf16[128,2048]{1,0:T(8,128)(2,1)}, bf16[128,2048]{1,0:T(8,128)(2,1)}, u32[]{:S(2)}, u32[]{:S(2)}) collective-permute-start(bf16[128,2048]{1,0:T(8,128)(2,1)} %constant_dynamic-slice_fusion), channel_id=1, source_target_pairs={{0,64},{64,0},{1,65},{65,1},{2,66},{66,2},{3,67},{67,3},{4,68},{68... | collective-permute-start | bytes 1572872 | tf_op jit(solution)/shard_map/ppermute | solution.py:562
  477.9 15.7 %collective-permute-start.65 = (bf16[64,2048]{1,0:T(8,128)(2,1)}, bf16[64,2048]{1,0:T(8,128)(2,1)}, u32[]{:S(2)}, u32[]{:S(2)}) collective-permute-start(bf16[64,2048]{1,0:T(8,128)(2,1)} %slice_select_fusion.4), channel_id=1, source_target_pairs={{0,1},{1,0},{2,3},{3,2},{4,5},{5,4},{6,7},{7,6},{8,14},{9,15},{10,... | collective-permute-start | bytes 786440 | tf_op jit(solution)/shard_map/ppermute | solution.py:59
  479.5 13.7 %all-to-all-start.2 = ((f32[8,4,128]{2,1,0:T(4,128)}), f32[8,4,128]{2,1,0:T(4,128)S(1)}, u32[]{:S(2)}, u32[]{:S(2)}) async-start(f32[8,4,128]{2,1,0:T(4,128)} %broadcast_in_dim.8), calls=%async_computation.2 | async-start | bytes 32768 | tf_op jit(solution)/shard_map/all_to_all | solution.py:223
  (76 other events, 663.2 us)
Sparse Core Ops, SparseCore 0:
  66.1 49.8 all-gather.1
  255.7 52.8 reduce-scatter.1

commit v3 on v2

--- a/solution.py
+++ b/solution.py
@@ -11,6 +11,13 @@
 f32 = jnp.float32
 
 SMALL = pl.CostEstimate(flops=1, bytes_accessed=1, transcendentals=0)
+
+
+def cost(micros):
+    return pl.CostEstimate(
+        flops=int(micros * 1.1e9), bytes_accessed=int(micros * 3.0e6), transcendentals=0
+    )
+
 
 NX, NYL, NZ, NYH, NC = 4, 2, 4, 2, 2
 MP = ("x", "yl")
@@ -64,28 +71,69 @@
     return values[:middle], values[middle:]
 
 
-def pick(zero, one):
-    return jnp.where(lax.axis_index("c") == 0, zero, one)
-
-
 def gather_one(own):
     return send(own, to_xp, to_xp), send(own, to_xm, to_xm), send(own, to_y, to_y)
 
 
+def columnwise(body, ins, out_rows):
+    width = ins[0].shape[1]
+    tile = min(1024, width)
+
+    def kernel(core_ref, *refs):
+        outs = body(core_ref[0], [ref[...] for ref in refs[: len(ins)]])
+        for ref, out in zip(refs[len(ins) :], outs):
+            ref[...] = out.astype(bf16)
+
+    return pl.pallas_call(
+        kernel,
+        grid_spec=pltpu.PrefetchScalarGridSpec(
+            num_scalar_prefetch=1,
+            grid=(width // tile,),
+            in_specs=[pl.BlockSpec((v.shape[0], tile), lambda j, c: (0, j)) for v in ins],
+            out_specs=[pl.BlockSpec((rows, tile), lambda j, c: (0, j)) for rows in out_rows],
+        ),
+        out_shape=[jax.ShapeDtypeStruct((rows, width), bf16) for rows in out_rows],
+        compiler_params=pltpu.CompilerParams(vmem_limit_bytes=16 * 2**20),
+        cost_estimate=SMALL,
+    )(lax.axis_index("c").astype(jnp.int32).reshape(1), *ins)
+
+
 def gather_two(one):
     p1, p2, q = one
+    rows = q.shape[0]
+
+    def body(core, values):
+        p1, p2, q = values
+        return (
+            halves(p1)[0],
+            halves(p2)[1],
+            jnp.where(core == 0, p1, q),
+            jnp.where(core == 0, p2, q),
+        )
+
+    o1, o2, r1, r2 = columnwise(body, one, [rows // 2, rows // 2, rows, rows])
     return (
-        send(halves(p1)[0], to_xp, to_xp),
-        send(halves(p2)[1], to_xm, to_xm),
-        send(pick(p1, q), to_y, to_xp),
-        send(pick(p2, q), to_y, to_xm),
+        send(o1, to_xp, to_xp),
+        send(o2, to_xm, to_xm),
+        send(r1, to_y, to_xp),
+        send(r2, to_y, to_xm),
     )
 
 
 def gather_three(own, one, two):
     (p1, p2, q), (o1, o2, r1, r2) = one, two
-    s1 = send(pick(o1, halves(r1)[0]), to_y, to_xp)
-    s2 = send(pick(o2, halves(r2)[1]), to_y, to_xm)
+    half = o1.shape[0]
+
+    def body(core, values):
+        o1, o2, r1, r2 = values
+        return (
+            jnp.where(core == 0, o1, halves(r1)[0]),
+            jnp.where(core == 0, o2, halves(r2)[1]),
+        )
+
+    s1, s2 = columnwise(body, two, [half, half])
+    s1 = send(s1, to_y, to_xp)
+    s2 = send(s2, to_y, to_xm)
     return {
         (0, 0): (own,),
         (1, 0): (p2,),
@@ -102,18 +150,9 @@
 LATER_STEPS = [(1, 1), (3, 1), (2, 0), (1, 0), (3, 0), (0, 1), (0, 0)]
 
 
-def core_factors():
-    zero = jnp.where(lax.axis_index("c") == 0, 1.0, 0.0).astype(f32)
+def core_factors(core):
+    zero = jnp.where(core == 0, 1.0, 0.0).astype(f32)
     return zero, 1.0 - zero
-
-
-def add_half(block, piece, which, factor):
-    first, second = halves(up(block))
-    if which == 0:
-        first = first + factor * up(piece)
-    else:
-        second = second + factor * up(piece)
-    return jnp.concatenate([first, second], 0)
 
 
 def scatter_one(blocks):
@@ -122,29 +161,54 @@
 
 
 def scatter_two(blocks, one):
-    zero, single = core_factors()
-    s1, s2 = one
-    g1, g2 = halves(up(blocks[2, 0]))
-    sent = (
-        add_half(blocks[1, 1], s1, 0, single).astype(bf16),
-        add_half(blocks[3, 1], s2, 1, single).astype(bf16),
-        (g1 + zero * up(s1)).astype(bf16),
-        (g2 + zero * up(s2)).astype(bf16),
+    rows = blocks[2, 0].shape[0]
+
+    def body(core, values):
+        zero, single = core_factors(core)
+        b1, b3, b2, s1, s2 = (up(v) for v in values)
+        first, second = halves(b1)
+        third, fourth = halves(b3)
+        g1, g2 = halves(b2)
+        return (
+            jnp.concatenate([first + single * s1, second], 0),
+            jnp.concatenate([third, fourth + single * s2], 0),
+            g1 + zero * s1,
+            g2 + zero * s2,
+        )
+
+    p, q, r1, r2 = columnwise(
+        body,
+        [blocks[1, 1], blocks[3, 1], blocks[2, 0], *one],
+        [rows, rows, rows // 2, rows // 2],
     )
     return (
-        send(sent[0], to_y, to_xp),
-        send(sent[1], to_y, to_xm),
-        send(sent[2], to_xp, to_xp),
-        send(sent[3], to_xm, to_xm),
+        send(p, to_y, to_xp),
+        send(q, to_y, to_xm),
+        send(r1, to_xp, to_xp),
+        send(r2, to_xm, to_xm),
     )
 
 
 def scatter_three(blocks, two):
-    zero, single = core_factors()
-    p, q, r1, r2 = two
-    u = send((up(blocks[0, 1]) + single * (up(p) + up(q))).astype(bf16), to_y, to_y)
-    t1 = send((add_half(blocks[1, 0], r1, 0, 1.0) + zero * up(p)).astype(bf16), to_xp, to_xp)
-    t2 = send((add_half(blocks[3, 0], r2, 1, 1.0) + zero * up(q)).astype(bf16), to_xm, to_xm)
+    rows = blocks[0, 0].shape[0]
+
+    def body(core, values):
+        zero, single = core_factors(core)
+        b1, b3, b0, p, q, r1, r2 = (up(v) for v in values)
+        first, second = halves(b1 + zero * p)
+        third, fourth = halves(b3 + zero * q)
+        return (
+            jnp.concatenate([first + r1, second], 0),
+            jnp.concatenate([third, fourth + r2], 0),
+            b0 + single * (p + q),
+        )
+
+    t1, t2, u = columnwise(
+        body, [blocks[1, 0], blocks[3, 0], blocks[0, 1], *two], [rows, rows, rows]
+    )
+    t1 = send(t1, to_xp, to_xp)
+    t2 = send(t2, to_xm, to_xm)
+    u = send(u, to_y, to_y)
     return up(blocks[0, 0]) + up(t1) + up(t2) + up(u)
 
 
@@ -157,8 +221,7 @@
     return ((x + dx) % NX) * NYL + (y + dy) % NYL
 
 
-def bounce(pieces, starts, rows, dtype=bf16, first_column=0):
-    width = pieces[0].shape[1] - first_column
+def bounce(pieces, starts, rows, width, dtype, first_column):
     count = len(pieces)
 
     def kernel(*refs):
@@ -201,12 +264,12 @@
         out_specs=pl.BlockSpec(memory_space=pl.ANY),
         scratch_shapes=scratch
         + [pltpu.SemaphoreType.DMA((count,)), pltpu.SemaphoreType.DMA((count,))],
-        compiler_params=pltpu.CompilerParams(vmem_limit_bytes=32 * 2**20),
+        compiler_params=pltpu.CompilerParams(vmem_limit_bytes=20 * 2**20),
         cost_estimate=SMALL,
     )(jnp.stack([jnp.asarray(start, jnp.int32) for start in starts]), *pieces)
 
 
-def assemble(blocks, dtype, first_column=0):
+def assemble(blocks, width, dtype, first_column):
     rows = blocks[0, 0][0].shape[0]
     pieces, starts = [], []
     for key in ORDER:
@@ -215,7 +278,7 @@
             pieces.append(piece)
             starts.append(begin)
             begin = begin + piece.shape[0]
-    return bounce(pieces, starts, rows * len(REL), dtype, first_column)
+    return bounce(pieces, starts, rows * len(REL), width, dtype, first_column)
 
 
 def sum_mp(values):
@@ -341,8 +404,8 @@
             out_specs=out_specs,
         ),
         out_shape=out_shape,
-        compiler_params=pltpu.CompilerParams(vmem_limit_bytes=48 * 2**20),
-        cost_estimate=SMALL,
+        compiler_params=pltpu.CompilerParams(vmem_limit_bytes=28 * 2**20),
+        cost_estimate=cost(1 + blocks),
     )(place, *operands)
     found = {}
     for out, (k, inside, count) in zip(got, outs):
@@ -419,8 +482,8 @@
             jax.ShapeDtypeStruct((seq_len, units), bf16),
             jax.ShapeDtypeStruct((seq_len, width), bf16),
         ],
-        compiler_params=pltpu.CompilerParams(vmem_limit_bytes=56 * 2**20),
-        cost_estimate=SMALL,
+        compiler_params=pltpu.CompilerParams(vmem_limit_bytes=48 * 2**20),
+        cost_estimate=cost(18),
     )(block_places(), *pieces, cotangent, weight, weight)
 
 
@@ -467,8 +530,8 @@
             scratch_shapes=[pltpu.VMEM((seq_len, cols), bf16)],
         ),
         out_shape=jax.ShapeDtypeStruct((width, 2 * cols), bf16),
-        compiler_params=pltpu.CompilerParams(vmem_limit_bytes=48 * 2**20),
-        cost_estimate=SMALL,
+        compiler_params=pltpu.CompilerParams(vmem_limit_bytes=24 * 2**20),
+        cost_estimate=cost(14),
     )(block_places(), second, grad_hidden, cotangent, cotangent, active)
 
 
@@ -532,8 +595,8 @@
             ],
         ),
         out_shape=jax.ShapeDtypeStruct((width, wide + narrow + lanes), bf16),
-        compiler_params=pltpu.CompilerParams(vmem_limit_bytes=48 * 2**20),
-        cost_estimate=SMALL,
+        compiler_params=pltpu.CompilerParams(vmem_limit_bytes=24 * 2**20),
+        cost_estimate=cost(11),
     )(block_places(), first, grad_mixed, attended, vectors, *pieces, *pieces)
 
 
@@ -560,17 +623,6 @@
     home = lax.dynamic_slice_in_dim(values, yh * rows, rows, 0)
     away = lax.dynamic_slice_in_dim(values, (1 - yh) * rows, rows, 0)
     return up(home) + up(lax.ppermute(away, "yh", [(0, 1), (1, 0)]))
-
-
-def exchange_dp(values):
-    rows, cols = values.shape
-    values = values.reshape(NZ * NC, NYH, rows // (NZ * NC * NYH), cols)
-    values = lax.all_to_all(values, ("z", "c"), split_axis=0, concat_axis=0, tiled=True)
-    values = jnp.sum(up(values), axis=0)
-    yh = lax.axis_index("yh")
-    home = lax.dynamic_index_in_dim(values, yh, 0, keepdims=False)
-    away = lax.dynamic_index_in_dim(values, 1 - yh, 0, keepdims=False).astype(bf16)
-    return home + up(lax.ppermute(away, "yh", [(0, 1), (1, 0)]))
 
 
 def norm_and_qkv(tokens, mine, other, cols):
@@ -637,8 +689,8 @@
             jax.ShapeDtypeStruct((seq_len, 128), f32),
             jax.ShapeDtypeStruct((seq_len, 128), f32),
         ],
-        compiler_params=pltpu.CompilerParams(vmem_limit_bytes=48 * 2**20),
-        cost_estimate=SMALL,
+        compiler_params=pltpu.CompilerParams(vmem_limit_bytes=36 * 2**20),
+        cost_estimate=cost(9),
     )(place, tokens, mine, other)
 
 
@@ -690,8 +742,8 @@
             jax.ShapeDtypeStruct((seq_len, heads * HEAD_SIZE), bf16),
             jax.ShapeDtypeStruct((seq_len, heads * HEAD_SIZE), f32),
         ],
-        compiler_params=pltpu.CompilerParams(vmem_limit_bytes=48 * 2**20),
-        cost_estimate=SMALL,
+        compiler_params=pltpu.CompilerParams(vmem_limit_bytes=24 * 2**20),
+        cost_estimate=cost(6),
     )(ends, qkv, qkv, qkv)
 
 
@@ -775,8 +827,8 @@
             ],
         ),
         out_shape=jax.ShapeDtypeStruct((seq_len, cols), bf16),
-        compiler_params=pltpu.CompilerParams(vmem_limit_bytes=56 * 2**20),
-        cost_estimate=SMALL,
+        compiler_params=pltpu.CompilerParams(vmem_limit_bytes=36 * 2**20),
+        cost_estimate=cost(12),
     )(ends, block_places(), qkv, qkv, qkv, lse, weight, *pieces)
 
 
@@ -808,18 +860,19 @@
     packed = jnp.concatenate([w_qkv.reshape(shard, wide).astype(bf16), w_out.astype(bf16)], 1)
     first_mine = gather_yz(jnp.concatenate([packed, small], 0))
     first_other = lax.ppermute(first_mine, "c", [(0, 1), (1, 0)])
-    mlp_weight = jnp.concatenate([w_down.astype(bf16), w_up.astype(bf16)], 1)
-    mlp_weight = gather_zc(pair_yh(after(mlp_weight, first_mine)))
     ends = jnp.cumsum(doc_lengths[0])
 
     first, mixed, weight, vectors, mean_one, inverse_one = norm_and_qkv(
         tokens, first_mine, first_other, wide
     )
+    mlp_weight = jnp.concatenate([w_down.astype(bf16), w_up.astype(bf16)], 1)
+    mlp_weight = pair_yh(after(mlp_weight, first_other))
     gain_a, gain_b, bias_b = vectors[0], vectors[2], vectors[3]
     attended, lse = attend(mixed, ends, scale)
     terms = terms_by_block(STEP_ONE, [attended], weight, first=3)
     sum_one = scatter_one(terms)
     later = terms_by_block(LATER_STEPS, [after(attended, *terms[2, 1])], weight, first=3)
+    mlp_weight = gather_zc(after(mlp_weight, attended))
     own_tokens = up(lax.dynamic_slice_in_dim(tokens, my_rows, rows, 0))
     own_cot = up(lax.dynamic_slice_in_dim(cotangent, my_rows, rows, 0))
     own_middle = own_tokens + scatter_three(later, scatter_two(later, sum_one))
@@ -855,7 +908,6 @@
     norm = (tokens, mean_one, inverse_one)
     terms, vec_a = terms_by_block(STEP_ONE, [grad_mixed], weight, norm=norm)
     sum_one = scatter_one(terms)
-    output_two = gather_two(output_one)
     later, vec_b = terms_by_block(
         LATER_STEPS, [after(grad_mixed, *terms[2, 1])], weight, norm=norm
     )
@@ -865,19 +917,17 @@
     late_vectors = scatter_order(
         jnp.concatenate([vec_one[:2], vec_two, jnp.zeros((4, width), f32)], 0)
     )
-    output_two = after(output_two, *sum_two)
     grad_first = scatter_three(later, sum_two)
-    late = exchange_dp(
-        late_gradients(after(first, sum_two[2]), grad_mixed, branch, attended, late_vectors)
-    )
+    late = late_gradients(after(first, *sum_one), grad_mixed, branch, attended, late_vectors)
+    late = scatter_dp(late)
 
     own_one, own_inverse = normalize(own_tokens)
     grad_tokens = (grad_middle + norm_back(grad_first, own_one, own_inverse, gain_a)).astype(bf16)
+    output = gather_three(output_own, output_one, gather_two(output_one))
+    output = assemble(output, width, bf16, 0)
     grad_one = gather_one(grad_tokens)
-    grad_two = after(gather_two(grad_one), late)
-    output = gather_three(output_own, output_one, output_two)
-    output = assemble(after(output, *grad_two), bf16)
-    input_grad = assemble(gather_three(grad_tokens, grad_one, grad_two), f32)
+    input_grad = gather_three(grad_tokens, grad_one, gather_two(grad_one))
+    input_grad = assemble(input_grad, width, f32, 0)
     sums = sum_mp(late[:, wide + local_width : wide + local_width + 4].T)
     return (
         output,

time: 517 us -> 478 us (0.925)
  waiting for transfers between devices: 191 us -> 140 us
  blocking collectives: 0 us -> 39.1 us
  other arithmetic: 49.1 us -> 19.9 us
  local copies, waits for them, and re-layouts: 28.6 us -> 39.4 us
    all_to_all x0 -> x1, blocking collectives: none -> 39.1 us  [gather_yz(): lax.all_to_all(copies, ('yh', 'z'), split_axis=0, concat_axis=0, tiled=True)]
    all_to_all x2 -> x0, waiting for transfers between devices: 31.2 us -> none  [the longest x1 29 us: gather_yz(): lax.all_to_all(copies, ('yh', 'z'), split_axis=0, concat_axis=0, tiled=True)]
    pallas_call x0 -> x14, Pallas kernels: none -> 18 us  [columnwise(): pl.pallas_call(kernel, grid_spec=pltpu.PrefetchScalarGridSpec(num_scalar_...]
    all_to_all x2 -> x0, starting transfers between devices: 12.7 us -> none  [the longest x1 8.08 us: gather_yz(): lax.all_to_all(copies, ('yh', 'z'), split_axis=0, concat_axis=0, tiled=True)]
    convert_element_type x15 -> x0, other arithmetic: 12.4 us -> none  [the longest x9 4.84 us: up(): return values.astype(f32)]
    unnamed x141 -> x109, local copies, waits for them, and re-layouts: 14.6 us -> 27 us
    ppermute x1, waiting for transfers between devices: 12 us -> 0.01 us  [pair_yh(): other = lax.ppermute(own, 'yh', [(0, 1), (1, 0)])]
    ppermute x1 -> x0, waiting for transfers between devices: 11.2 us -> none  [exchange_dp(): return home + up(lax.ppermute(away, 'yh', [(0, 1), (1, 0)]))]
  transfers between devices with their start and end apart: 72 -> 71, of which waited for: 35 -> 39; matrix products, arithmetic and copies ran while one was open for 11% -> 5% of each run, Pallas kernels for 19% -> 15%
where the time goes in v3:
time: 478 us; the launch traced here: 469 us
  waiting for transfers between devices  140 us (29%)
  Pallas kernels  120 us (25%)
  starting transfers between devices  95.9 us (20%)
  local copies, waits for them, and re-layouts  39.4 us (8%)
  blocking collectives  39.1 us (8%)
  other arithmetic  19.9 us (4%)
  between operations  15 us (3%)
    ppermute x63, waiting for transfers between devices, send(): return lax.ppermute(values, CMP, pairs)  133 us
    ppermute x63, starting transfers between devices, send(): return lax.ppermute(values, CMP, pairs)  83.1 us
    all_to_all x1, blocking collectives, gather_yz(): lax.all_to_all(copies, ('yh', 'z'), split_axis=0, concat_axis=0, tiled=True)  39.1 us
    pallas_call x6, Pallas kernels, terms_by_block(): pl.pallas_call(kernel, grid_spec=pltpu.PrefetchScalarGridSpec(num_scalar_...  29.6 us
    unnamed x109, local copies, waits for them, and re-layouts  27 us
    pallas_call x1, Pallas kernels, mlp(): pl.pallas_call(kernel, grid_spec=pltpu.PrefetchScalarGridSpec(num_scalar_...  18.2 us
    pallas_call x14, Pallas kernels, columnwise(): pl.pallas_call(kernel, grid_spec=pltpu.PrefetchScalarGridSpec(num_scalar_...  18 us
    pallas_call x1, Pallas kernels, mlp_gradients(): pl.pallas_call(kernel, grid_spec=pltpu.PrefetchScalarGridSpec(num_scalar_...  12.8 us
  transfers between devices with their start and end apart: 71, of which 39 were waited for; matrix products, arithmetic and copies ran while one was open for 5% of the time, Pallas kernels for 15%

profile of v3, /device:TPU:2, one launch (start us, length us, event | category | flops | bytes accessed | tf_op | source)
XLA Modules:
  0.0 469.1 jit_solution(12904884122177302280)
XLA Ops:
  11.6 39.1 %all_to_all.10.mine_ref = bf16[8,144,1024]{2,1,0:T(8,128)(2,1)S(1)} all-to-all(bf16[8,144,1024]{2,1,0:T(8,128)(2,1)S(1)} %broadcast_in_dim.6), channel_id=1, replica_groups=mesh['yh'=2,'z'=4,'c'=2,'x'=4,'yl'=2] {'yh','z'}, dimensions={0} | all-to-all | bytes 4718592 | tf_op jit(solution)/shard_map/all_to_all | solution.py:295
  52.0 3.3 collective-permute-done.other_ref
  56.2 8.8 %shard_map.186 = (bf16[1024,2048]{1,0:T(8,128)(2,1)S(1)}, bf16[1024,768]{1,0:T(8,128)(2,1)S(1)}, bf16[2048,1024]{1,0:T(8,128)(2,1)S(1)}, f32[8,2048]{1,0:T(8,128...) custom-call(s32[1]{0:T(128)} %bitcast.19.place_ref.core_ref, bf16[1024,2048]{1,0:T(8,128)(2,1)} %refs_14_.1, ...), custom_call_target="tpu_custom_call" | custom-call | flops 9900000256 | bytes 27000000 | tf_op jit(solution)/shard_map/pallas_call | solution.py:665
  65.0 5.7 %shard_map.187 = (bf16[1024,256]{1,0:T(8,128)(2,1)S(1)}, f32[1024,256]{1,0:T(8,128)S(1)}) custom-call(s32[4]{0:T(128)S(1)} %bitcast.76, bf16[1024,768]{1,0:T(8,128)(2,1)S(1)} %get-tuple-element.105.q_ref.k_ref.v_ref.refs_0_.refs_1_.refs_2_, bf16[1024,768]{1,0:T(8,128)(2,1)S(1)} %get-tuple-element.105.q_ref.k_ref.v_ref.refs_0_.refs_1_.refs_2_, ...), custom_call_target="tpu_custom_call" | custom-call | flops 6600000000 | bytes 18000000 | tf_op jit(solution)/shard_map/pallas_call | solution.py:733
  72.3 2.2 copy-done.6
  78.9 3.0 shard_map.189
  82.2 2.8 collective-permute-done.2.refs_4_
  91.6 6.2 %collective-permute-done.5.refs_5_ = bf16[64,2048]{1,0:T(8,128)(2,1)S(1)} collective-permute-done((bf16[64,2048]{1,0:T(8,128)(2,1)}, bf16[64,2048]{1,0:T(8,128)(2,1)S(1)}, u32[]{:S(2)}, u32[]{:S(2)}) %collective-permute-start.5) | collective-permute-done | bytes 262176 | tf_op jit(solution)/shard_map/ppermute | solution.py:66
  98.8 2.6 collective-permute-done.4.refs_4_
  106.3 7.8 %collective-permute-done.9 = bf16[128,2048]{1,0:T(8,128)(2,1)S(1)} collective-permute-done((bf16[128,2048]{1,0:T(8,128)(2,1)S(1)}, bf16[128,2048]{1,0:T(8,128)(2,1)S(1)}, u32[]{:S(2)}, u32[]{:S(2)}) %collective-permute-start.9) | collective-permute-done | bytes 524320 | tf_op jit(solution)/shard_map/ppermute | solution.py:66
  114.2 2.2 collective-permute-done.7
  119.0 3.4 collective-permute-start.10
  124.9 5.0 %collective-permute-done.10.refs_1_ = bf16[128,2048]{1,0:T(8,128)(2,1)S(1)} collective-permute-done((bf16[128,2048]{1,0:T(8,128)(2,1)S(1)}, bf16[128,2048]{1,0:T(8,128)(2,1)S(1)}, u32[]{:S(2)}, u32[]{:S(2)}) %collective-permute-start.10) | collective-permute-done | bytes 524320 | tf_op jit(solution)/shard_map/ppermute | solution.py:66
  136.8 6.4 %collective-permute-done.13.refs_0_.refs_2_ = bf16[64,2048]{1,0:T(8,128)(2,1)S(1)} collective-permute-done((bf16[64,2048]{1,0:T(8,128)(2,1)S(1)}, bf16[64,2048]{1,0:T(8,128)(2,1)S(1)}, u32[]{:S(2)}, u32[]{:S(2)}) %collective-permute-start.13) | collective-permute-done | bytes 262176 | tf_op jit(solution)/shard_map/ppermute | solution.py:66
  143.2 4.4 collective-permute-done.16.refs_2_.refs_9_
  151.5 4.6 collective-permute-done.17.refs_7_
  156.0 2.8 collective-permute-done.18.refs_8_
  162.3 18.2 %shard_map.194 = (bf16[1024,1024]{1,0:T(8,128)(2,1)}, bf16[1024,1024]{1,0:T(8,128)(2,1)}, bf16[1024,2048]{1,0:T(8,128)(2,1)}) custom-call(s32[8]{0:T(128)S(1)} %stack.174.place_ref, bf16[128,2048]{1,0:T(8,128)(2,1)S(1)} %copy-done.25, bf16[128,2048]{1,0:T(8,128)(2,1)S(1)} %collective-permute-done.10.refs_1_, ...), custom_call_target="tpu_custom_call" | custom-call | flops 19800000512 | bytes 54000000 | tf_op jit(solution)/shard_map/pallas_call | solution.py:462
  183.6 4.9 %shard_map.195 = (bf16[64,4096]{1,0:T(8,128)(2,1)S(1)}, bf16[64,4096]{1,0:T(8,128)(2,1)S(1)}) custom-call(s32[1]{0:T(128)} %constant.331.clone.1.place_ref, bf16[1024,1024]{1,0:T(8,128)(2,1)S(1)} %copy-done.3, bf16[1024,1024]{1,0:T(8,128)(2,1)S(1)} %copy-done.1, bf16[8,2,128,2048]{3,2,1,0:T(8,128)(2,1)S(1)} %bitcast.73), custom_call_target="tpu_custom_call" | custom-call | flops 2200000000 | bytes 6000000 | tf_op jit(solution)/shard_map/pallas_call | solution.py:398
  190.7 11.6 %shard_map.196 = (bf16[128,4096]{1,0:T(8,128)(2,1)S(1)}, bf16[128,4096]{1,0:T(8,128)(2,1)S(1)}, bf16[128,4096]{1,0:T(8,128)(2,1)S(1)}, bf16[128,4096]{1,0:T(8,12...) custom-call(s32[7]{0:T(128)S(1)} %copy-done.31, ...), custom_call_target="tpu_custom_call" | custom-call | flops 8800000000 | bytes 24000000 | tf_op jit(solution)/shard_map/pallas_call | solution.py:398
  208.9 12.8 %collective-permute-done.24.refs_5_ = bf16[64,4096]{1,0:T(8,128)(2,1)S(1)} collective-permute-done((bf16[64,4096]{1,0:T(8,128)(2,1)S(1)}, bf16[64,4096]{1,0:T(8,128)(2,1)S(1)}, u32[]{:S(2)}, u32[]{:S(2)}) %collective-permute-start.24) | collective-permute-done | bytes 524320 | tf_op jit(solution)/shard_map/ppermute | solution.py:66
  222.7 9.0 %collective-permute-done.23.refs_4_ = bf16[128,4096]{1,0:T(8,128)(2,1)S(1)} collective-permute-done((bf16[128,4096]{1,0:T(8,128)(2,1)S(1)}, bf16[128,4096]{1,0:T(8,128)(2,1)S(1)}, u32[]{:S(2)}, u32[]{:S(2)}) %collective-permute-start.23) | collective-permute-done | bytes 1048608 | tf_op jit(solution)/shard_map/ppermute | solution.py:66
  231.7 3.1 shard_map.198
  238.5 12.8 %shard_map.199 = bf16[2048,2048]{1,0:T(8,128)(2,1)S(1)} custom-call(s32[8]{0:T(128)S(1)} %stack.174.place_ref, bf16[1024,2048]{1,0:T(8,128)(2,1)S(1)} %copy-done.39, bf16[1024,1024]{1,0:T(8,128)(2,1)S(1)} %copy-done.2, bf16[1024,2048]{1,0:T(8,128)(2,1)S(1)} %copy-done.30, bf16[1024,2048]{1,0:T(8,128)(2,1)S(1)} %copy-done.30, bf16[1024,1024]{1,0:T(8,128)(2,1)S(1)} %copy-done.4), custom_call_target="tpu_custom_call" | custom-call | flops 15399999488 | bytes 42000000 | tf_op jit(solution)/shard_map/pallas_call | solution.py:517
  251.3 3.4 copy-done.8
  256.5 2.6 convert_add_fusion
  259.5 3.1 fusion.14
  262.6 3.0 collective-permute-start.30
  265.9 7.1 %collective-permute-done.29.refs_0_.refs_9_.refs_8_.refs_18_ = bf16[128,2048]{1,0:T(8,128)(2,1)S(1)} collective-permute-done((bf16[128,2048]{1,0:T(8,128)(2,1)S(1)}, bf16[128,2048]{1,0:T(8,128)(2,1)S(1)}, u32[]{:S(2)}, u32[]{:S(2)}) %collective-permute-start.29) | collective-permute-done | bytes 524320 | tf_op jit(solution)/shard_map/ppermute | solution.py:66
  273.1 2.7 collective-permute-done.30.refs_1_.refs_6_.refs_5_.refs_15_
  278.2 3.5 collective-permute-start.32
  282.1 5.3 %collective-permute-done.32.refs_0_.refs_7_.refs_6_.refs_16_ = bf16[64,2048]{1,0:T(8,128)(2,1)S(1)} collective-permute-done((bf16[64,2048]{1,0:T(8,128)(2,1)S(1)}, bf16[64,2048]{1,0:T(8,128)(2,1)S(1)}, u32[]{:S(2)}, u32[]{:S(2)}) %collective-permute-start.32) | collective-permute-done | bytes 262176 | tf_op jit(solution)/shard_map/ppermute | solution.py:66
  287.4 3.7 collective-permute-done.42.refs_1_.refs_8_.refs_7_.refs_17_
  293.8 4.0 collective-permute-done.45.refs_12_.refs_11_.refs_21_
  297.8 2.8 collective-permute-done.46.refs_13_.refs_12_.refs_22_
  300.7 8.8 %shard_map.205.refs_0_.refs_1_.refs_2_.refs_3_.refs_4_.refs_5_.refs_6_ = bf16[1024,768]{1,0:T(8,128)(2,1)S(1)} custom-call(s32[4]{0:T(128)S(1)} %bitcast.77, s32[8]{0:T(128)S(1)} %stack.174.place_ref, bf16[1024,768]{1,0:T(8,128)(2,1)S(1)} %copy-done.41, bf16[1024,768]{1,0:T(8,128)(2,1)S(1)} %copy-done.41, bf16[1024,768]{1,0:T(8,128)(2,1)S(1)} %copy-done.41, ...), custom_call_target="tpu_custom_call" | custom-call | flops 13200000000 | bytes 36000000 | tf_op jit(solution)/shard_map/pallas_call | solution.py:808
  309.5 2.5 shard_map.206
  314.1 6.3 %shard_map.207 = (bf16[128,2048]{1,0:T(8,128)(2,1)S(1)}, bf16[128,2048]{1,0:T(8,128)(2,1)S(1)}, bf16[128,2048]{1,0:T(8,128)(2,1)S(1)}, bf16[128,2048]{1,0:T(8,12...) custom-call(s32[7]{0:T(128)S(1)} %stack.81.place_ref, ...), custom_call_target="tpu_custom_call" | custom-call | flops 8800000000 | bytes 24000000 | tf_op jit(solution)/shard_map/pallas_call | solution.py:398
  323.7 9.5 %shard_map.213 = bf16[2048,1152]{1,0:T(8,128)(2,1)S(1)} custom-call(s32[8]{0:T(128)S(1)} %stack.174.place_ref, bf16[1024,2048]{1,0:T(8,128)(2,1)S(1)} %copy-done.38, bf16[1024,768]{1,0:T(8,128)(2,1)S(1)} %shard_map.205.refs_0_.refs_1_.refs_2_.refs_3_.refs_4_.refs_5_.refs_6_, bf16[1024,256]{1,0:T(8,128)(2,1)S(1)} %copy-done.36, f32[8,2048]{1,0:T(8,128)S(1)} %bitcast.75, ...), custom_call_target="tpu_custom_call" | custom-call | flops 12099999744 | bytes 33000000 | tf_op jit(solution)/shard_map/pallas_call | solution.py:578
  333.2 2.2 copy-done.9
  339.9 3.3 collective-permute-start.51
  343.7 5.5 %collective-permute-done.51.refs_5_ = bf16[64,2048]{1,0:T(8,128)(2,1)S(1)} collective-permute-done((bf16[64,2048]{1,0:T(8,128)(2,1)S(1)}, bf16[64,2048]{1,0:T(8,128)(2,1)S(1)}, u32[]{:S(2)}, u32[]{:S(2)}) %collective-permute-start.51) | collective-permute-done | bytes 262176 | tf_op jit(solution)/shard_map/ppermute | solution.py:66
  349.2 4.8 %collective-permute-done.52.refs_6_ = bf16[64,2048]{1,0:T(8,128)(2,1)S(1)} collective-permute-done((bf16[64,2048]{1,0:T(8,128)(2,1)S(1)}, bf16[64,2048]{1,0:T(8,128)(2,1)S(1)}, u32[]{:S(2)}, u32[]{:S(2)}) %collective-permute-start.52) | collective-permute-done | bytes 262176 | tf_op jit(solution)/shard_map/ppermute | solution.py:66
  354.0 4.3 collective-permute-done.50.refs_4_
  359.7 4.6 collective-permute-start.54
  364.3 4.5 collective-permute-start.33
  369.1 5.2 %collective-permute-done.55 = bf16[128,2048]{1,0:T(8,128)(2,1)S(1)} collective-permute-done((bf16[128,2048]{1,0:T(8,128)(2,1)S(1)}, bf16[128,2048]{1,0:T(8,128)(2,1)S(1)}, u32[]{:S(2)}, u32[]{:S(2)}) %collective-permute-start.55) | collective-permute-done | bytes 524320 | tf_op jit(solution)/shard_map/ppermute | solution.py:66
  376.2 2.8 collective-permute-done.53
  382.2 3.0 collective-permute-start.56
  385.2 2.2 collective-permute-done.33.refs_1_.refs_2_
  387.4 2.3 collective-permute-start.58
  391.5 3.2 collective-permute-start.38
  394.7 4.0 collective-permute-done.56.refs_1_.refs_2_
  398.7 2.2 collective-permute-start.39
  401.5 3.0 collective-permute-start.37
  408.0 3.2 collective-permute-start.61
  415.0 4.0 collective-permute-start.65
  419.0 2.1 shard_map.202
  424.3 2.2 shard_map.211
  428.5 3.6 reduce-scatter.5.cloned.1.call-done
  434.0 3.0 collective-permute-start.66
  440.5 4.8 %all-to-all-start.1 = ((f32[8,4,128]{2,1,0:T(4,128)}), f32[8,4,128]{2,1,0:T(4,128)S(1)}, u32[]{:S(2)}, u32[]{:S(2)}) async-start(f32[8,4,128]{2,1,0:T(4,128)} %broadcast_in_dim.8), calls=%async_computation.2 | async-start | bytes 32768 | tf_op jit(solution)/shard_map/all_to_all | solution.py:286
  445.4 3.8 shard_map.203
  449.3 4.5 shard_map.212
  (274 shorter events, 115.0 us)
Async XLA Ops:
  7.2 151.7 %all-gather.2.cloned.1.call-start = ((), (), s32[]{:S(2)}) async-start(), calls=%async_computation.4 | async-start | bytes 9437184 | tf_op jit(solution)/shard_map/all_gather | solution.py:616
  55.3 15.5 %collective-permute-start.19 = (bf16[128,2048]{1,0:T(8,128)(2,1)S(1)}, bf16[128,2048]{1,0:T(8,128)(2,1)S(1)}, u32[]{:S(2)}, u32[]{:S(2)}) collective-permute-start(bf16[128,2048]{1,0:T(8,128)(2,1)S(1)} %pad_maximum_fusion.1), channel_id=1, source_target_pairs={{0,64},{64,0},{1,65},{65,1},{2,66},{66,2},{3,67},{67,3},{4,68},{68... | collective-permute-start | bytes 1572872 | tf_op jit(solution)/shard_map/ppermute | solution.py:610
  72.1 341.2 %reduce-scatter.3.cloned.1.call-start = ((), (), s32[]{:S(2)}) async-start(), calls=%async_computation.5 | async-start | bytes 5308416 | tf_op jit(solution)/shard_map/reduce_scatter | solution.py:620
  86.4 12.5 %collective-permute-start.3 = (bf16[128,2048]{1,0:T(8,128)(2,1)}, bf16[128,2048]{1,0:T(8,128)(2,1)}, u32[]{:S(2)}, u32[]{:S(2)}) collective-permute-start(bf16[128,2048]{1,0:T(8,128)(2,1)} %get-tuple-element.118), channel_id=1, source_target_pairs={{0,1},{1,0},{2,3},{3,2},{4,5},{5,4},{6,7},{7,6},{8,10},{9,11},{10,... | collective-permute-start | bytes 1572872 | tf_op jit(solution)/shard_map/ppermute | solution.py:66
  87.2 14.3 %collective-permute-start.4 = (bf16[128,2048]{1,0:T(8,128)(2,1)}, bf16[128,2048]{1,0:T(8,128)(2,1)}, u32[]{:S(2)}, u32[]{:S(2)}) collective-permute-start(bf16[128,2048]{1,0:T(8,128)(2,1)} %get-tuple-element.119), channel_id=1, source_target_pairs={{0,1},{1,0},{2,3},{3,2},{4,5},{5,4},{6,7},{7,6},{8,14},{9,15},{10,... | collective-permute-start | bytes 1572872 | tf_op jit(solution)/shard_map/ppermute | solution.py:66
  88.4 9.4 %collective-permute-start.5 = (bf16[64,2048]{1,0:T(8,128)(2,1)}, bf16[64,2048]{1,0:T(8,128)(2,1)S(1)}, u32[]{:S(2)}, u32[]{:S(2)}) collective-permute-start(bf16[64,2048]{1,0:T(8,128)(2,1)} %get-tuple-element.120), channel_id=1, source_target_pairs={{0,2},{1,3},{2,4},{3,5},{4,6},{5,7},{6,0},{7,1},{8,10},{9,11},{10,... | collective-permute-start | bytes 786440 | tf_op jit(solution)/shard_map/ppermute | solution.py:66
  89.9 8.9 %collective-permute-start.6 = (bf16[64,2048]{1,0:T(8,128)(2,1)}, bf16[64,2048]{1,0:T(8,128)(2,1)}, u32[]{:S(2)}, u32[]{:S(2)}) collective-permute-start(bf16[64,2048]{1,0:T(8,128)(2,1)} %get-tuple-element.121), channel_id=1, source_target_pairs={{0,6},{1,7},{2,0},{3,1},{4,2},{5,3},{6,4},{7,5},{8,14},{9,15},{10,... | collective-permute-start | bytes 786440 | tf_op jit(solution)/shard_map/ppermute | solution.py:66
  103.3 10.8 %collective-permute-start.9 = (bf16[128,2048]{1,0:T(8,128)(2,1)S(1)}, bf16[128,2048]{1,0:T(8,128)(2,1)S(1)}, u32[]{:S(2)}, u32[]{:S(2)}) collective-permute-start(bf16[128,2048]{1,0:T(8,128)(2,1)S(1)} %get-tuple-element.124), channel_id=1, source_target_pairs={{0,1},{1,0},{2,3},{3,2},{4,5},{5,4},{6,7},{7,6},{8,9},{9,8},{10,11... | collective-permute-start | bytes 1572872 | tf_op jit(solution)/shard_map/ppermute | solution.py:66
  104.2 9.9 %collective-permute-start.8 = (bf16[128,2048]{1,0:T(8,128)(2,1)S(1)}, bf16[128,2048]{1,0:T(8,128)(2,1)S(1)}, u32[]{:S(2)}, u32[]{:S(2)}) collective-permute-start(bf16[128,2048]{1,0:T(8,128)(2,1)S(1)} %get-tuple-element.123), channel_id=1, source_target_pairs={{0,6},{1,7},{2,0},{3,1},{4,2},{5,3},{6,4},{7,5},{8,14},{9,15},{10,... | collective-permute-start | bytes 1572872 | tf_op jit(solution)/shard_map/ppermute | solution.py:66
  104.8 11.6 %collective-permute-start.7 = (bf16[128,2048]{1,0:T(8,128)(2,1)S(1)}, bf16[128,2048]{1,0:T(8,128)(2,1)S(1)}, u32[]{:S(2)}, u32[]{:S(2)}) collective-permute-start(bf16[128,2048]{1,0:T(8,128)(2,1)S(1)} %get-tuple-element.122), channel_id=1, source_target_pairs={{0,2},{1,3},{2,4},{3,5},{4,6},{5,7},{6,0},{7,1},{8,10},{9,11},{10,... | collective-permute-start | bytes 1572872 | tf_op jit(solution)/shard_map/ppermute | solution.py:66
  119.0 10.9 %collective-permute-start.10 = (bf16[128,2048]{1,0:T(8,128)(2,1)S(1)}, bf16[128,2048]{1,0:T(8,128)(2,1)S(1)}, u32[]{:S(2)}, u32[]{:S(2)}) collective-permute-start(bf16[128,2048]{1,0:T(8,128)(2,1)S(1)} %add_convert_fusion.1.refs_0_), channel_id=1, source_target_pairs={{0,6},{1,7},{2,0},{3,1},{4,2},{5,3},{6,4},{7,5},{8,14},{9,15},{10,... | collective-permute-start | bytes 1572872 | tf_op jit(solution)/shard_map/ppermute | solution.py:66
  122.4 9.5 %collective-permute-start.11 = (bf16[128,2048]{1,0:T(8,128)(2,1)S(1)}, bf16[128,2048]{1,0:T(8,128)(2,1)S(1)}, u32[]{:S(2)}, u32[]{:S(2)}) collective-permute-start(bf16[128,2048]{1,0:T(8,128)(2,1)S(1)} %add_convert_fusion.1.refs_0_), channel_id=1, source_target_pairs={{0,2},{1,3},{2,4},{3,5},{4,6},{5,7},{6,0},{7,1},{8,10},{9,11},{10,... | collective-permute-start | bytes 1572872 | tf_op jit(solution)/shard_map/ppermute | solution.py:66
  122.4 9.9 %collective-permute-start.12 = (bf16[128,2048]{1,0:T(8,128)(2,1)S(1)}, bf16[128,2048]{1,0:T(8,128)(2,1)S(1)}, u32[]{:S(2)}, u32[]{:S(2)}) collective-permute-start(bf16[128,2048]{1,0:T(8,128)(2,1)S(1)} %add_convert_fusion.1.refs_0_), channel_id=1, source_target_pairs={{0,1},{1,0},{2,3},{3,2},{4,5},{5,4},{6,7},{7,6},{8,9},{9,8},{10,11... | collective-permute-start | bytes 1572872 | tf_op jit(solution)/shard_map/ppermute | solution.py:66
  132.7 10.5 %collective-permute-start.15 = (bf16[128,2048]{1,0:T(8,128)(2,1)S(1)}, bf16[128,2048]{1,0:T(8,128)(2,1)S(1)}, u32[]{:S(2)}, u32[]{:S(2)}) collective-permute-start(bf16[128,2048]{1,0:T(8,128)(2,1)S(1)} %get-tuple-element.128), channel_id=1, source_target_pairs={{0,1},{1,0},{2,3},{3,2},{4,5},{5,4},{6,7},{7,6},{8,14},{9,15},{10,... | collective-permute-start | bytes 1572872 | tf_op jit(solution)/shard_map/ppermute | solution.py:66
  134.5 13.1 %collective-permute-start.16 = (bf16[128,2048]{1,0:T(8,128)(2,1)S(1)}, bf16[128,2048]{1,0:T(8,128)(2,1)S(1)}, u32[]{:S(2)}, u32[]{:S(2)}) collective-permute-start(bf16[128,2048]{1,0:T(8,128)(2,1)S(1)} %get-tuple-element.129), channel_id=1, source_target_pairs={{0,1},{1,0},{2,3},{3,2},{4,5},{5,4},{6,7},{7,6},{8,10},{9,11},{10,... | collective-permute-start | bytes 1572872 | tf_op jit(solution)/shard_map/ppermute | solution.py:66
  134.8 8.4 %collective-permute-start.13 = (bf16[64,2048]{1,0:T(8,128)(2,1)S(1)}, bf16[64,2048]{1,0:T(8,128)(2,1)S(1)}, u32[]{:S(2)}, u32[]{:S(2)}) collective-permute-start(bf16[64,2048]{1,0:T(8,128)(2,1)S(1)} %get-tuple-element.126), channel_id=1, source_target_pairs={{0,2},{1,3},{2,4},{3,5},{4,6},{5,7},{6,0},{7,1},{8,10},{9,11},{10,... | collective-permute-start | bytes 786440 | tf_op jit(solution)/shard_map/ppermute | solution.py:66
  188.6 13.7 %collective-permute-start.20 = (bf16[64,4096]{1,0:T(8,128)(2,1)S(1)}, bf16[64,4096]{1,0:T(8,128)(2,1)S(1)}, u32[]{:S(2)}, u32[]{:S(2)}) collective-permute-start(bf16[64,4096]{1,0:T(8,128)(2,1)S(1)} %get-tuple-element.136), channel_id=1, source_target_pairs={{0,1},{1,0},{2,3},{3,2},{4,5},{5,4},{6,7},{7,6},{8,10},{9,11},{10,... | collective-permute-start | bytes 1572872 | tf_op jit(solution)/shard_map/ppermute | solution.py:66
  190.4 13.0 %collective-permute-start.21 = (bf16[64,4096]{1,0:T(8,128)(2,1)S(1)}, bf16[64,4096]{1,0:T(8,128)(2,1)S(1)}, u32[]{:S(2)}, u32[]{:S(2)}) collective-permute-start(bf16[64,4096]{1,0:T(8,128)(2,1)S(1)} %get-tuple-element.137), channel_id=1, source_target_pairs={{0,1},{1,0},{2,3},{3,2},{4,5},{5,4},{6,7},{7,6},{8,14},{9,15},{10,... | collective-permute-start | bytes 1572872 | tf_op jit(solution)/shard_map/ppermute | solution.py:66
  204.7 18.0 %collective-permute-start.22 = (bf16[128,4096]{1,0:T(8,128)(2,1)S(1)}, bf16[128,4096]{1,0:T(8,128)(2,1)S(1)}, u32[]{:S(2)}, u32[]{:S(2)}) collective-permute-start(bf16[128,4096]{1,0:T(8,128)(2,1)S(1)} %get-tuple-element.147), channel_id=1, source_target_pairs={{0,1},{1,0},{2,3},{3,2},{4,5},{5,4},{6,7},{7,6},{8,10},{9,11},{10,... | collective-permute-start | bytes 3145736 | tf_op jit(solution)/shard_map/ppermute | solution.py:66
  206.5 25.2 %collective-permute-start.23 = (bf16[128,4096]{1,0:T(8,128)(2,1)S(1)}, bf16[128,4096]{1,0:T(8,128)(2,1)S(1)}, u32[]{:S(2)}, u32[]{:S(2)}) collective-permute-start(bf16[128,4096]{1,0:T(8,128)(2,1)S(1)} %get-tuple-element.148), channel_id=1, source_target_pairs={{0,1},{1,0},{2,3},{3,2},{4,5},{5,4},{6,7},{7,6},{8,14},{9,15},{10,... | collective-permute-start | bytes 3145736 | tf_op jit(solution)/shard_map/ppermute | solution.py:66
  206.8 15.0 %collective-permute-start.24 = (bf16[64,4096]{1,0:T(8,128)(2,1)S(1)}, bf16[64,4096]{1,0:T(8,128)(2,1)S(1)}, u32[]{:S(2)}, u32[]{:S(2)}) collective-permute-start(bf16[64,4096]{1,0:T(8,128)(2,1)S(1)} %get-tuple-element.149), channel_id=1, source_target_pairs={{0,2},{1,3},{2,4},{3,5},{4,6},{5,7},{6,0},{7,1},{8,10},{9,11},{10,... | collective-permute-start | bytes 1572872 | tf_op jit(solution)/shard_map/ppermute | solution.py:66
  207.0 15.7 %collective-permute-start.25 = (bf16[64,4096]{1,0:T(8,128)(2,1)S(1)}, bf16[64,4096]{1,0:T(8,128)(2,1)S(1)}, u32[]{:S(2)}, u32[]{:S(2)}) collective-permute-start(bf16[64,4096]{1,0:T(8,128)(2,1)S(1)} %get-tuple-element.150), channel_id=1, source_target_pairs={{0,6},{1,7},{2,0},{3,1},{4,2},{5,3},{6,4},{7,5},{8,14},{9,15},{10,... | collective-permute-start | bytes 1572872 | tf_op jit(solution)/shard_map/ppermute | solution.py:66
  234.7 20.0 %collective-permute-start.28 = (bf16[128,4096]{1,0:T(8,128)(2,1)}, bf16[128,4096]{1,0:T(8,128)(2,1)}, u32[]{:S(2)}, u32[]{:S(2)}) collective-permute-start(bf16[128,4096]{1,0:T(8,128)(2,1)} %get-tuple-element.153), channel_id=1, source_target_pairs={{0,1},{1,0},{2,3},{3,2},{4,5},{5,4},{6,7},{7,6},{8,9},{9,8},{10,11... | collective-permute-start | bytes 3145736 | tf_op jit(solution)/shard_map/ppermute | solution.py:66
  236.5 18.2 %collective-permute-start.27 = (bf16[128,4096]{1,0:T(8,128)(2,1)}, bf16[128,4096]{1,0:T(8,128)(2,1)}, u32[]{:S(2)}, u32[]{:S(2)}) collective-permute-start(bf16[128,4096]{1,0:T(8,128)(2,1)} %get-tuple-element.152), channel_id=1, source_target_pairs={{0,6},{1,7},{2,0},{3,1},{4,2},{5,3},{6,4},{7,5},{8,14},{9,15},{10,... | collective-permute-start | bytes 3145736 | tf_op jit(solution)/shard_map/ppermute | solution.py:66
  238.2 18.3 %collective-permute-start.26 = (bf16[128,4096]{1,0:T(8,128)(2,1)S(1)}, bf16[128,4096]{1,0:T(8,128)(2,1)}, u32[]{:S(2)}, u32[]{:S(2)}) collective-permute-start(bf16[128,4096]{1,0:T(8,128)(2,1)S(1)} %get-tuple-element.151), channel_id=1, source_target_pairs={{0,2},{1,3},{2,4},{3,5},{4,6},{5,7},{6,0},{7,1},{8,10},{9,11},{10,... | collective-permute-start | bytes 3145736 | tf_op jit(solution)/shard_map/ppermute | solution.py:66
  262.6 10.4 %collective-permute-start.29 = (bf16[128,2048]{1,0:T(8,128)(2,1)S(1)}, bf16[128,2048]{1,0:T(8,128)(2,1)S(1)}, u32[]{:S(2)}, u32[]{:S(2)}) collective-permute-start(bf16[128,2048]{1,0:T(8,128)(2,1)S(1)} %get-tuple-element.267.refs_5_.refs_4_.refs_14_), channel_id=1, source_target_pairs={{0,2},{1,3},{2,4},{3,5},{4,6},{5,7},{6,0},{7,1},{8,10},{9,11},{10,... | collective-permute-start | bytes 1572872 | tf_op jit(solution)/shard_map/ppermute | solution.py:66
  262.6 13.1 %collective-permute-start.30 = (bf16[128,2048]{1,0:T(8,128)(2,1)S(1)}, bf16[128,2048]{1,0:T(8,128)(2,1)S(1)}, u32[]{:S(2)}, u32[]{:S(2)}) collective-permute-start(bf16[128,2048]{1,0:T(8,128)(2,1)S(1)} %get-tuple-element.267.refs_5_.refs_4_.refs_14_), channel_id=1, source_target_pairs={{0,6},{1,7},{2,0},{3,1},{4,2},{5,3},{6,4},{7,5},{8,14},{9,15},{10,... | collective-permute-start | bytes 1572872 | tf_op jit(solution)/shard_map/ppermute | solution.py:66
  265.6 10.1 %collective-permute-start.31 = (bf16[128,2048]{1,0:T(8,128)(2,1)S(1)}, bf16[128,2048]{1,0:T(8,128)(2,1)S(1)}, u32[]{:S(2)}, u32[]{:S(2)}) collective-permute-start(bf16[128,2048]{1,0:T(8,128)(2,1)S(1)} %get-tuple-element.267.refs_5_.refs_4_.refs_14_), channel_id=1, source_target_pairs={{0,1},{1,0},{2,3},{3,2},{4,5},{5,4},{6,7},{7,6},{8,9},{9,8},{10,11... | collective-permute-start | bytes 1572872 | tf_op jit(solution)/shard_map/ppermute | solution.py:66
  276.1 15.0 %collective-permute-start.43 = (bf16[128,2048]{1,0:T(8,128)(2,1)S(1)}, bf16[128,2048]{1,0:T(8,128)(2,1)S(1)}, u32[]{:S(2)}, u32[]{:S(2)}) collective-permute-start(bf16[128,2048]{1,0:T(8,128)(2,1)S(1)} %get-tuple-element.167), channel_id=1, source_target_pairs={{0,1},{1,0},{2,3},{3,2},{4,5},{5,4},{6,7},{7,6},{8,14},{9,15},{10,... | collective-permute-start | bytes 1572872 | tf_op jit(solution)/shard_map/ppermute | solution.py:66
  276.5 14.7 %collective-permute-start.44 = (bf16[128,2048]{1,0:T(8,128)(2,1)S(1)}, bf16[128,2048]{1,0:T(8,128)(2,1)S(1)}, u32[]{:S(2)}, u32[]{:S(2)}) collective-permute-start(bf16[128,2048]{1,0:T(8,128)(2,1)S(1)} %get-tuple-element.168), channel_id=1, source_target_pairs={{0,1},{1,0},{2,3},{3,2},{4,5},{5,4},{6,7},{7,6},{8,10},{9,11},{10,... | collective-permute-start | bytes 1572872 | tf_op jit(solution)/shard_map/ppermute | solution.py:66
  278.2 9.2 %collective-permute-start.32 = (bf16[64,2048]{1,0:T(8,128)(2,1)S(1)}, bf16[64,2048]{1,0:T(8,128)(2,1)S(1)}, u32[]{:S(2)}, u32[]{:S(2)}) collective-permute-start(bf16[64,2048]{1,0:T(8,128)(2,1)S(1)} %get-tuple-element.157), channel_id=1, source_target_pairs={{0,2},{1,3},{2,4},{3,5},{4,6},{5,7},{6,0},{7,1},{8,10},{9,11},{10,... | collective-permute-start | bytes 786440 | tf_op jit(solution)/shard_map/ppermute | solution.py:66
  281.7 9.4 %collective-permute-start.42 = (bf16[64,2048]{1,0:T(8,128)(2,1)S(1)}, bf16[64,2048]{1,0:T(8,128)(2,1)S(1)}, u32[]{:S(2)}, u32[]{:S(2)}) collective-permute-start(bf16[64,2048]{1,0:T(8,128)(2,1)S(1)} %get-tuple-element.166), channel_id=1, source_target_pairs={{0,6},{1,7},{2,0},{3,1},{4,2},{5,3},{6,4},{7,5},{8,14},{9,15},{10,... | collective-permute-start | bytes 786440 | tf_op jit(solution)/shard_map/ppermute | solution.py:66
  291.8 8.9 %collective-permute-start.46 = (bf16[64,2048]{1,0:T(8,128)(2,1)S(1)}, bf16[64,2048]{1,0:T(8,128)(2,1)S(1)}, u32[]{:S(2)}, u32[]{:S(2)}) collective-permute-start(bf16[64,2048]{1,0:T(8,128)(2,1)S(1)} %get-tuple-element.170), channel_id=1, source_target_pairs={{0,1},{1,0},{2,3},{3,2},{4,5},{5,4},{6,7},{7,6},{8,14},{9,15},{10,... | collective-permute-start | bytes 786440 | tf_op jit(solution)/shard_map/ppermute | solution.py:66
  312.0 11.0 %collective-permute-start.47 = (bf16[64,2048]{1,0:T(8,128)(2,1)S(1)}, bf16[64,2048]{1,0:T(8,128)(2,1)S(1)}, u32[]{:S(2)}, u32[]{:S(2)}) collective-permute-start(bf16[64,2048]{1,0:T(8,128)(2,1)S(1)} %get-tuple-element.173), channel_id=1, source_target_pairs={{0,1},{1,0},{2,3},{3,2},{4,5},{5,4},{6,7},{7,6},{8,10},{9,11},{10,... | collective-permute-start | bytes 786440 | tf_op jit(solution)/shard_map/ppermute | solution.py:66
  312.4 10.6 %collective-permute-start.48 = (bf16[64,2048]{1,0:T(8,128)(2,1)S(1)}, bf16[64,2048]{1,0:T(8,128)(2,1)S(1)}, u32[]{:S(2)}, u32[]{:S(2)}) collective-permute-start(bf16[64,2048]{1,0:T(8,128)(2,1)S(1)} %get-tuple-element.174), channel_id=1, source_target_pairs={{0,1},{1,0},{2,3},{3,2},{4,5},{5,4},{6,7},{7,6},{8,14},{9,15},{10,... | collective-permute-start | bytes 786440 | tf_op jit(solution)/shard_map/ppermute | solution.py:66
  335.4 96.8 %reduce-scatter.5.cloned.1.call-start = ((), (), s32[]{:S(2)}) async-start(), calls=%async_computation.6 | async-start | bytes 9437184 | tf_op jit(solution)/shard_map/reduce_scatter | solution.py:620
  337.8 16.2 %collective-permute-start.49 = (bf16[128,2048]{1,0:T(8,128)(2,1)S(1)}, bf16[128,2048]{1,0:T(8,128)(2,1)S(1)}, u32[]{:S(2)}, u32[]{:S(2)}) collective-permute-start(bf16[128,2048]{1,0:T(8,128)(2,1)S(1)} %get-tuple-element.183), channel_id=1, source_target_pairs={{0,1},{1,0},{2,3},{3,2},{4,5},{5,4},{6,7},{7,6},{8,10},{9,11},{10,... | collective-permute-start | bytes 1572872 | tf_op jit(solution)/shard_map/ppermute | solution.py:66
  338.2 20.1 %collective-permute-start.50 = (bf16[128,2048]{1,0:T(8,128)(2,1)S(1)}, bf16[128,2048]{1,0:T(8,128)(2,1)S(1)}, u32[]{:S(2)}, u32[]{:S(2)}) collective-permute-start(bf16[128,2048]{1,0:T(8,128)(2,1)S(1)} %get-tuple-element.184), channel_id=1, source_target_pairs={{0,1},{1,0},{2,3},{3,2},{4,5},{5,4},{6,7},{7,6},{8,14},{9,15},{10,... | collective-permute-start | bytes 1572872 | tf_op jit(solution)/shard_map/ppermute | solution.py:66
  339.9 9.3 %collective-permute-start.51 = (bf16[64,2048]{1,0:T(8,128)(2,1)S(1)}, bf16[64,2048]{1,0:T(8,128)(2,1)S(1)}, u32[]{:S(2)}, u32[]{:S(2)}) collective-permute-start(bf16[64,2048]{1,0:T(8,128)(2,1)S(1)} %get-tuple-element.185), channel_id=1, source_target_pairs={{0,2},{1,3},{2,4},{3,5},{4,6},{5,7},{6,0},{7,1},{8,10},{9,11},{10,... | collective-permute-start | bytes 786440 | tf_op jit(solution)/shard_map/ppermute | solution.py:66
  343.2 10.7 %collective-permute-start.52 = (bf16[64,2048]{1,0:T(8,128)(2,1)S(1)}, bf16[64,2048]{1,0:T(8,128)(2,1)S(1)}, u32[]{:S(2)}, u32[]{:S(2)}) collective-permute-start(bf16[64,2048]{1,0:T(8,128)(2,1)S(1)} %get-tuple-element.186), channel_id=1, source_target_pairs={{0,6},{1,7},{2,0},{3,1},{4,2},{5,3},{6,4},{7,5},{8,14},{9,15},{10,... | collective-permute-start | bytes 786440 | tf_op jit(solution)/shard_map/ppermute | solution.py:66
  359.3 14.9 %collective-permute-start.55 = (bf16[128,2048]{1,0:T(8,128)(2,1)S(1)}, bf16[128,2048]{1,0:T(8,128)(2,1)S(1)}, u32[]{:S(2)}, u32[]{:S(2)}) collective-permute-start(bf16[128,2048]{1,0:T(8,128)(2,1)S(1)} %get-tuple-element.189), channel_id=1, source_target_pairs={{0,1},{1,0},{2,3},{3,2},{4,5},{5,4},{6,7},{7,6},{8,9},{9,8},{10,11... | collective-permute-start | bytes 1572872 | tf_op jit(solution)/shard_map/ppermute | solution.py:66
  359.7 16.5 %collective-permute-start.54 = (bf16[128,2048]{1,0:T(8,128)(2,1)S(1)}, bf16[128,2048]{1,0:T(8,128)(2,1)S(1)}, u32[]{:S(2)}, u32[]{:S(2)}) collective-permute-start(bf16[128,2048]{1,0:T(8,128)(2,1)S(1)} %get-tuple-element.188), channel_id=1, source_target_pairs={{0,6},{1,7},{2,0},{3,1},{4,2},{5,3},{6,4},{7,5},{8,14},{9,15},{10,... | collective-permute-start | bytes 1572872 | tf_op jit(solution)/shard_map/ppermute | solution.py:66
  364.3 14.8 %collective-permute-start.53 = (bf16[128,2048]{1,0:T(8,128)(2,1)S(1)}, bf16[128,2048]{1,0:T(8,128)(2,1)S(1)}, u32[]{:S(2)}, u32[]{:S(2)}) collective-permute-start(bf16[128,2048]{1,0:T(8,128)(2,1)S(1)} %get-tuple-element.187), channel_id=1, source_target_pairs={{0,2},{1,3},{2,4},{3,5},{4,6},{5,7},{6,0},{7,1},{8,10},{9,11},{10,... | collective-permute-start | bytes 1572872 | tf_op jit(solution)/shard_map/ppermute | solution.py:66
  364.3 23.2 %collective-permute-start.33 = (bf16[128,2048]{1,0:T(8,128)(2,1)}, bf16[128,2048]{1,0:T(8,128)(2,1)S(1)}, u32[]{:S(2)}, u32[]{:S(2)}) collective-permute-start(bf16[128,2048]{1,0:T(8,128)(2,1)} %get-tuple-element.158.refs_1_), channel_id=1, source_target_pairs={{0,6},{1,7},{2,0},{3,1},{4,2},{5,3},{6,4},{7,5},{8,14},{9,15},{10,... | collective-permute-start | bytes 1572872 | tf_op jit(solution)/shard_map/ppermute | solution.py:66
  368.8 21.5 %collective-permute-start.34 = (bf16[128,2048]{1,0:T(8,128)(2,1)}, bf16[128,2048]{1,0:T(8,128)(2,1)S(1)}, u32[]{:S(2)}, u32[]{:S(2)}) collective-permute-start(bf16[128,2048]{1,0:T(8,128)(2,1)} %get-tuple-element.158.refs_1_), channel_id=1, source_target_pairs={{0,2},{1,3},{2,4},{3,5},{4,6},{5,7},{6,0},{7,1},{8,10},{9,11},{10,... | collective-permute-start | bytes 1572872 | tf_op jit(solution)/shard_map/ppermute | solution.py:66
  374.3 16.0 %collective-permute-start.35 = (bf16[128,2048]{1,0:T(8,128)(2,1)}, bf16[128,2048]{1,0:T(8,128)(2,1)S(1)}, u32[]{:S(2)}, u32[]{:S(2)}) collective-permute-start(bf16[128,2048]{1,0:T(8,128)(2,1)} %get-tuple-element.158.refs_1_), channel_id=1, source_target_pairs={{0,1},{1,0},{2,3},{3,2},{4,5},{5,4},{6,7},{7,6},{8,9},{9,8},{10,11... | collective-permute-start | bytes 1572872 | tf_op jit(solution)/shard_map/ppermute | solution.py:66
  382.2 16.5 %collective-permute-start.56 = (bf16[128,2048]{1,0:T(8,128)(2,1)S(1)}, bf16[128,2048]{1,0:T(8,128)(2,1)S(1)}, u32[]{:S(2)}, u32[]{:S(2)}) collective-permute-start(bf16[128,2048]{1,0:T(8,128)(2,1)S(1)} %fusion.8.refs_1_), channel_id=1, source_target_pairs={{0,6},{1,7},{2,0},{3,1},{4,2},{5,3},{6,4},{7,5},{8,14},{9,15},{10,... | collective-permute-start | bytes 1572872 | tf_op jit(solution)/shard_map/ppermute | solution.py:66
  385.2 16.3 %collective-permute-start.57 = (bf16[128,2048]{1,0:T(8,128)(2,1)S(1)}, bf16[128,2048]{1,0:T(8,128)(2,1)S(1)}, u32[]{:S(2)}, u32[]{:S(2)}) collective-permute-start(bf16[128,2048]{1,0:T(8,128)(2,1)S(1)} %fusion.8.refs_1_), channel_id=1, source_target_pairs={{0,2},{1,3},{2,4},{3,5},{4,6},{5,7},{6,0},{7,1},{8,10},{9,11},{10,... | collective-permute-start | bytes 1572872 | tf_op jit(solution)/shard_map/ppermute | solution.py:66
  387.4 17.0 %collective-permute-start.58 = (bf16[128,2048]{1,0:T(8,128)(2,1)S(1)}, bf16[128,2048]{1,0:T(8,128)(2,1)S(1)}, u32[]{:S(2)}, u32[]{:S(2)}) collective-permute-start(bf16[128,2048]{1,0:T(8,128)(2,1)S(1)} %fusion.8.refs_1_), channel_id=1, source_target_pairs={{0,1},{1,0},{2,3},{3,2},{4,5},{5,4},{6,7},{7,6},{8,9},{9,8},{10,11... | collective-permute-start | bytes 1572872 | tf_op jit(solution)/shard_map/ppermute | solution.py:66
  391.5 20.2 %collective-permute-start.38 = (bf16[128,2048]{1,0:T(8,128)(2,1)}, bf16[128,2048]{1,0:T(8,128)(2,1)}, u32[]{:S(2)}, u32[]{:S(2)}) collective-permute-start(bf16[128,2048]{1,0:T(8,128)(2,1)} %get-tuple-element.161), channel_id=1, source_target_pairs={{0,1},{1,0},{2,3},{3,2},{4,5},{5,4},{6,7},{7,6},{8,14},{9,15},{10,... | collective-permute-start | bytes 1572872 | tf_op jit(solution)/shard_map/ppermute | solution.py:66
  394.7 16.4 %collective-permute-start.36 = (bf16[64,2048]{1,0:T(8,128)(2,1)S(1)}, bf16[64,2048]{1,0:T(8,128)(2,1)S(1)}, u32[]{:S(2)}, u32[]{:S(2)}) collective-permute-start(bf16[64,2048]{1,0:T(8,128)(2,1)S(1)} %get-tuple-element.159), channel_id=1, source_target_pairs={{0,2},{1,3},{2,4},{3,5},{4,6},{5,7},{6,0},{7,1},{8,10},{9,11},{10,... | collective-permute-start | bytes 786440 | tf_op jit(solution)/shard_map/ppermute | solution.py:66
  398.7 16.4 %collective-permute-start.39 = (bf16[128,2048]{1,0:T(8,128)(2,1)}, bf16[128,2048]{1,0:T(8,128)(2,1)}, u32[]{:S(2)}, u32[]{:S(2)}) collective-permute-start(bf16[128,2048]{1,0:T(8,128)(2,1)} %get-tuple-element.162), channel_id=1, source_target_pairs={{0,1},{1,0},{2,3},{3,2},{4,5},{5,4},{6,7},{7,6},{8,10},{9,11},{10,... | collective-permute-start | bytes 1572872 | tf_op jit(solution)/shard_map/ppermute | solution.py:66
  401.5 9.7 %collective-permute-start.37 = (bf16[64,2048]{1,0:T(8,128)(2,1)}, bf16[64,2048]{1,0:T(8,128)(2,1)}, u32[]{:S(2)}, u32[]{:S(2)}) collective-permute-start(bf16[64,2048]{1,0:T(8,128)(2,1)} %get-tuple-element.160), channel_id=1, source_target_pairs={{0,6},{1,7},{2,0},{3,1},{4,2},{5,3},{6,4},{7,5},{8,14},{9,15},{10,... | collective-permute-start | bytes 786440 | tf_op jit(solution)/shard_map/ppermute | solution.py:66
  408.0 15.2 %collective-permute-start.61 = (bf16[128,2048]{1,0:T(8,128)(2,1)}, bf16[128,2048]{1,0:T(8,128)(2,1)}, u32[]{:S(2)}, u32[]{:S(2)}) collective-permute-start(bf16[128,2048]{1,0:T(8,128)(2,1)} %get-tuple-element.192), channel_id=1, source_target_pairs={{0,1},{1,0},{2,3},{3,2},{4,5},{5,4},{6,7},{7,6},{8,14},{9,15},{10,... | collective-permute-start | bytes 1572872 | tf_op jit(solution)/shard_map/ppermute | solution.py:66
  411.2 13.1 %collective-permute-start.62 = (bf16[128,2048]{1,0:T(8,128)(2,1)}, bf16[128,2048]{1,0:T(8,128)(2,1)}, u32[]{:S(2)}, u32[]{:S(2)}) collective-permute-start(bf16[128,2048]{1,0:T(8,128)(2,1)} %get-tuple-element.193), channel_id=1, source_target_pairs={{0,1},{1,0},{2,3},{3,2},{4,5},{5,4},{6,7},{7,6},{8,10},{9,11},{10,... | collective-permute-start | bytes 1572872 | tf_op jit(solution)/shard_map/ppermute | solution.py:66
  411.2 9.8 %collective-permute-start.59 = (bf16[64,2048]{1,0:T(8,128)(2,1)}, bf16[64,2048]{1,0:T(8,128)(2,1)}, u32[]{:S(2)}, u32[]{:S(2)}) collective-permute-start(bf16[64,2048]{1,0:T(8,128)(2,1)} %copy-done.33), channel_id=1, source_target_pairs={{0,2},{1,3},{2,4},{3,5},{4,6},{5,7},{6,0},{7,1},{8,10},{9,11},{10,... | collective-permute-start | bytes 786440 | tf_op jit(solution)/shard_map/ppermute | solution.py:66
  411.8 10.5 %collective-permute-start.60 = (bf16[64,2048]{1,0:T(8,128)(2,1)}, bf16[64,2048]{1,0:T(8,128)(2,1)}, u32[]{:S(2)}, u32[]{:S(2)}) collective-permute-start(bf16[64,2048]{1,0:T(8,128)(2,1)} %copy-done.32), channel_id=1, source_target_pairs={{0,6},{1,7},{2,0},{3,1},{4,2},{5,3},{6,4},{7,5},{8,14},{9,15},{10,... | collective-permute-start | bytes 786440 | tf_op jit(solution)/shard_map/ppermute | solution.py:66
  415.0 19.0 %collective-permute-start.65 = (bf16[128,1152]{1,0:T(8,128)(2,1)}, bf16[128,1152]{1,0:T(8,128)(2,1)}, u32[]{:S(2)}, u32[]{:S(2)}) collective-permute-start(bf16[128,1152]{1,0:T(8,128)(2,1)} %constant_dynamic-slice_fusion.1), channel_id=1, source_target_pairs={{0,64},{64,0},{1,65},{65,1},{2,66},{66,2},{3,67},{67,3},{4,68},{68... | collective-permute-start | bytes 884744 | tf_op jit(solution)/shard_map/ppermute | solution.py:625
  421.1 24.3 %collective-permute-start.40 = (bf16[64,2048]{1,0:T(8,128)(2,1)}, bf16[64,2048]{1,0:T(8,128)(2,1)}, u32[]{:S(2)}, u32[]{:S(2)}) collective-permute-start(bf16[64,2048]{1,0:T(8,128)(2,1)} %get-tuple-element.163), channel_id=1, source_target_pairs={{0,1},{1,0},{2,3},{3,2},{4,5},{5,4},{6,7},{7,6},{8,10},{9,11},{10,... | collective-permute-start | bytes 786440 | tf_op jit(solution)/shard_map/ppermute | solution.py:66
  422.3 23.1 %collective-permute-start.41 = (bf16[64,2048]{1,0:T(8,128)(2,1)}, bf16[64,2048]{1,0:T(8,128)(2,1)}, u32[]{:S(2)}, u32[]{:S(2)}) collective-permute-start(bf16[64,2048]{1,0:T(8,128)(2,1)} %get-tuple-element.164), channel_id=1, source_target_pairs={{0,1},{1,0},{2,3},{3,2},{4,5},{5,4},{6,7},{7,6},{8,14},{9,15},{10,... | collective-permute-start | bytes 786440 | tf_op jit(solution)/shard_map/ppermute | solution.py:66
  426.4 22.8 %collective-permute-start.63 = (bf16[64,2048]{1,0:T(8,128)(2,1)}, bf16[64,2048]{1,0:T(8,128)(2,1)}, u32[]{:S(2)}, u32[]{:S(2)}) collective-permute-start(bf16[64,2048]{1,0:T(8,128)(2,1)} %get-tuple-element.194), channel_id=1, source_target_pairs={{0,1},{1,0},{2,3},{3,2},{4,5},{5,4},{6,7},{7,6},{8,10},{9,11},{10,... | collective-permute-start | bytes 786440 | tf_op jit(solution)/shard_map/ppermute | solution.py:66
  428.5 20.8 %collective-permute-start.64 = (bf16[64,2048]{1,0:T(8,128)(2,1)}, bf16[64,2048]{1,0:T(8,128)(2,1)}, u32[]{:S(2)}, u32[]{:S(2)}) collective-permute-start(bf16[64,2048]{1,0:T(8,128)(2,1)} %get-tuple-element.195), channel_id=1, source_target_pairs={{0,1},{1,0},{2,3},{3,2},{4,5},{5,4},{6,7},{7,6},{8,14},{9,15},{10,... | collective-permute-start | bytes 786440 | tf_op jit(solution)/shard_map/ppermute | solution.py:66
  434.0 25.8 %collective-permute-start.66 = (bf16[128,2048]{1,0:T(8,128)(2,1)}, bf16[128,2048]{1,0:T(8,128)(2,1)}, u32[]{:S(2)}, u32[]{:S(2)}) collective-permute-start(bf16[128,2048]{1,0:T(8,128)(2,1)} %constant_dynamic-slice_fusion), channel_id=1, source_target_pairs={{0,64},{64,0},{1,65},{65,1},{2,66},{66,2},{3,67},{67,3},{4,68},{68... | collective-permute-start | bytes 1572872 | tf_op jit(solution)/shard_map/ppermute | solution.py:625
  440.5 18.8 %all-to-all-start.1 = ((f32[8,4,128]{2,1,0:T(4,128)}), f32[8,4,128]{2,1,0:T(4,128)S(1)}, u32[]{:S(2)}, u32[]{:S(2)}) async-start(f32[8,4,128]{2,1,0:T(4,128)} %broadcast_in_dim.8), calls=%async_computation.2 | async-start | bytes 32768 | tf_op jit(solution)/shard_map/all_to_all | solution.py:286
  (59 other events, 605.2 us)
Sparse Core Ops, SparseCore 0:
  72.2 48.7 all-gather.1
  335.5 41.9 reduce-scatter.2
  380.5 51.6 reduce-scatter.4

commit v4 on v3

--- a/solution.py
+++ b/solution.py
@@ -10,6 +10,7 @@
 bf16 = jnp.bfloat16
 f32 = jnp.float32
 
+MLP_TILE, MLP_VMEM = 256, 44
 SMALL = pl.CostEstimate(flops=1, bytes_accessed=1, transcendentals=0)
 
 
@@ -209,7 +210,7 @@
     t1 = send(t1, to_xp, to_xp)
     t2 = send(t2, to_xm, to_xm)
     u = send(u, to_y, to_y)
-    return up(blocks[0, 0]) + up(t1) + up(t2) + up(u)
+    return [blocks[0, 0], t1, t2, u]
 
 
 REL = [(dx, dy) for dy in range(NYL) for dx in range(NX)]
@@ -418,39 +419,59 @@
     return found
 
 
+SCATTER = [
+    (n, (n % (NZ * NC)) * NYH + n // (NZ * NC)) for n in range(NYH * NZ * NC)
+]
+
+
+def permuted(values):
+    part = values.shape[1] // len(SCATTER)
+    order = sorted(SCATTER, key=lambda pair: pair[1])
+    return jnp.concatenate([values[:, n * part : (n + 1) * part] for n, _ in order], 1)
+
+
+def relative_rows(values):
+    seq_len, width = values.shape
+    rows = seq_len // len(REL)
+
+    def kernel(place_ref, in_ref, out_ref):
+        out_ref[...] = permuted(in_ref[...])
+
+    return pl.pallas_call(
+        kernel,
+        grid_spec=pltpu.PrefetchScalarGridSpec(
+            num_scalar_prefetch=1,
+            grid=(len(REL),),
+            in_specs=[pl.BlockSpec((rows, width), lambda i, p: (p[i], 0))],
+            out_specs=pl.BlockSpec((rows, width), lambda i, p: (i, 0)),
+        ),
+        out_shape=jax.ShapeDtypeStruct((seq_len, width), values.dtype),
+        compiler_params=pltpu.CompilerParams(vmem_limit_bytes=16 * 2**20),
+        cost_estimate=cost(4),
+    )(block_places(), values)
+
+
 def mlp(second, cotangent, weight):
     seq_len, width = cotangent.shape
     rows = seq_len // len(REL)
-    slices, lanes, units = weight.shape
-    units = units // 2
+    units = weight.shape[2] // 2
     weight = weight.reshape(width, 2 * units)
-    columns = [
-        (n * lanes, ((n % (NZ * NC)) * NYH + n // (NZ * NC)) * lanes) for n in range(slices)
-    ]
-    tile = min(256, units // 2)
+    tile = min(MLP_TILE, units // 2)
     steps = units // tile
     root, cubic = (2.0 / jnp.pi) ** 0.5, 0.044715
     pieces, starts = row_pieces(second, rows)
     count = len(pieces)
 
-    def kernel(place_ref, *refs):
-        cot_ref, down_ref, up_ref, du_ref, z_ref, h_ref, order_ref = refs[count:]
+    def kernel(*refs):
+        cot_ref, down_ref, up_ref, du_ref, z_ref, h_ref = refs[count:]
 
         @pl.when(pl.program_id(0) == 0)
         def _():
-            for plain, place in columns:
-                for k, start in enumerate(starts):
-                    h_ref[start : start + pieces[k].shape[0], place : place + lanes] = refs[k][
-                        :, plain : plain + lanes
-                    ]
-                for i in range(len(REL)):
-                    begin = pl.multiple_of(place_ref[i] * rows, rows)
-                    order_ref[i * rows : (i + 1) * rows, place : place + lanes] = cot_ref[
-                        pl.ds(begin, rows), plain : plain + lanes
-                    ]
+            for k, start in enumerate(starts):
+                h_ref[start : start + pieces[k].shape[0], :] = refs[k][...]
 
         u = jnp.dot(h_ref[...], up_ref[...], preferred_element_type=f32)
-        dz = jnp.dot(order_ref[...], down_ref[...], preferred_element_type=f32)
+        dz = jnp.dot(cot_ref[...], down_ref[...], preferred_element_type=f32)
         square = u * u
         t = jnp.tanh(root * (u + cubic * (square * u)))
         half = 0.5 * (1.0 + t)
@@ -458,81 +479,56 @@
         slope = half + (0.5 * root) * u * (1.0 - t * t) * (1.0 + (3.0 * cubic) * square)
         du_ref[...] = (dz * slope).astype(bf16)
 
-    whole = lambda shape: pl.BlockSpec(shape, lambda j, p: (0,) * len(shape))
+    whole = lambda shape: pl.BlockSpec(shape, lambda j: (0,) * len(shape))
     return pl.pallas_call(
         kernel,
-        grid_spec=pltpu.PrefetchScalarGridSpec(
-            num_scalar_prefetch=1,
-            grid=(steps,),
-            in_specs=[whole(piece.shape) for piece in pieces]
-            + [
-                whole(cotangent.shape),
-                pl.BlockSpec((width, tile), lambda j, p: (0, j)),
-                pl.BlockSpec((width, tile), lambda j, p: (0, steps + j)),
-            ],
-            out_specs=[
-                pl.BlockSpec((seq_len, tile), lambda j, p: (0, j)),
-                pl.BlockSpec((seq_len, tile), lambda j, p: (0, j)),
-                whole((seq_len, width)),
-            ],
-            scratch_shapes=[pltpu.VMEM((seq_len, width), bf16)],
-        ),
+        grid=(steps,),
+        in_specs=[whole(piece.shape) for piece in pieces]
+        + [
+            whole(cotangent.shape),
+            pl.BlockSpec((width, tile), lambda j: (0, j)),
+            pl.BlockSpec((width, tile), lambda j: (0, steps + j)),
+        ],
+        out_specs=[
+            pl.BlockSpec((seq_len, tile), lambda j: (0, j)),
+            pl.BlockSpec((seq_len, tile), lambda j: (0, j)),
+            whole((seq_len, width)),
+        ],
         out_shape=[
             jax.ShapeDtypeStruct((seq_len, units), bf16),
             jax.ShapeDtypeStruct((seq_len, units), bf16),
             jax.ShapeDtypeStruct((seq_len, width), bf16),
         ],
-        compiler_params=pltpu.CompilerParams(vmem_limit_bytes=48 * 2**20),
-        cost_estimate=cost(18),
-    )(block_places(), *pieces, cotangent, weight, weight)
+        compiler_params=pltpu.CompilerParams(vmem_limit_bytes=MLP_VMEM * 2**20),
+        cost_estimate=cost(16),
+    )(*pieces, cotangent, weight, weight)
 
 
 def mlp_gradients(second, grad_hidden, cotangent, active):
     seq_len, width = second.shape
-    rows = seq_len // len(REL)
     cols = active.shape[1]
-    slices = NZ * NC
-    lanes = width // (slices * NYH)
-    tile = NYH * lanes
-
-    def kernel(place_ref, h_ref, du_ref, cot0_ref, cot1_ref, z_ref, out_ref, order_ref):
-        @pl.when(pl.program_id(0) == 0)
-        def _():
-            for i in range(len(REL)):
-                begin = pl.multiple_of(place_ref[i] * rows, rows)
-                order_ref[pl.ds(begin, rows), :] = z_ref[i * rows : (i + 1) * rows, :]
-
+    tile = min(512, width // 2)
+
+    def kernel(h_ref, du_ref, cot_ref, z_ref, out_ref):
         over = (((0,), (0,)), ((), ()))
         out_ref[:, :cols] = lax.dot_general(
             h_ref[...], du_ref[...], over, preferred_element_type=f32
         ).astype(bf16)
-        cot = jnp.concatenate([cot0_ref[...], cot1_ref[...]], 1)
         out_ref[:, cols:] = lax.dot_general(
-            cot, order_ref[...], over, preferred_element_type=f32
+            cot_ref[...], z_ref[...], over, preferred_element_type=f32
         ).astype(bf16)
 
-    near = pl.BlockSpec((seq_len, lanes), lambda i, p: (0, i))
-    far = pl.BlockSpec((seq_len, lanes), lambda i, p: (0, slices + i))
-    whole = pl.BlockSpec((seq_len, cols), lambda i, p: (0, 0))
+    lhs = pl.BlockSpec((seq_len, tile), lambda i: (0, i))
+    whole = pl.BlockSpec((seq_len, cols), lambda i: (0, 0))
     return pl.pallas_call(
         kernel,
-        grid_spec=pltpu.PrefetchScalarGridSpec(
-            num_scalar_prefetch=1,
-            grid=(slices,),
-            in_specs=[
-                pl.BlockSpec((seq_len, tile), lambda i, p: (0, i)),
-                whole,
-                near,
-                far,
-                whole,
-            ],
-            out_specs=pl.BlockSpec((tile, 2 * cols), lambda i, p: (i, 0)),
-            scratch_shapes=[pltpu.VMEM((seq_len, cols), bf16)],
-        ),
+        grid=(width // tile,),
+        in_specs=[lhs, whole, lhs, whole],
+        out_specs=pl.BlockSpec((tile, 2 * cols), lambda i: (i, 0)),
         out_shape=jax.ShapeDtypeStruct((width, 2 * cols), bf16),
-        compiler_params=pltpu.CompilerParams(vmem_limit_bytes=24 * 2**20),
-        cost_estimate=cost(14),
-    )(block_places(), second, grad_hidden, cotangent, cotangent, active)
+        compiler_params=pltpu.CompilerParams(vmem_limit_bytes=28 * 2**20),
+        cost_estimate=cost(11),
+    )(second, grad_hidden, cotangent, active)
 
 
 def late_gradients(first, grad_mixed, branch, attended, vectors):
@@ -541,7 +537,8 @@
     wide, narrow = grad_mixed.shape[1], attended.shape[1]
     slices = NZ * NC
     part = width // (slices * NYH)
-    tile = NYH * part
+    group = 2
+    tile = group * NYH * part
     lanes = 128
     pieces, starts = row_pieces(branch, rows)
     count = len(pieces)
@@ -558,10 +555,13 @@
                 rhs_ref[i * rows : (i + 1) * rows, :] = o_ref[pl.ds(begin, rows), :]
 
         for k, start in enumerate(starts):
+            stop = start + pieces[k].shape[0]
             for n in range(NYH):
-                lhs_ref[start : start + pieces[k].shape[0], n * part : (n + 1) * part] = da_refs[
-                    n * count + k
-                ][...]
+                for g in range(group):
+                    place = (g * NYH + n) * part
+                    lhs_ref[start:stop, place : place + part] = da_refs[n * count + k][
+                        :, g * part : (g + 1) * part
+                    ]
         over = (((0,), (0,)), ((), ()))
         out_ref[:, :wide] = lax.dot_general(
             h_ref[...], mixed_ref[...], over, preferred_element_type=f32
@@ -573,13 +573,14 @@
         out_ref[:, wide + narrow :] = padded.T.astype(bf16)
 
     whole = lambda shape: pl.BlockSpec(shape, lambda i, p: (0,) * len(shape))
-    near = [pl.BlockSpec((piece.shape[0], part), lambda i, p: (0, i)) for piece in pieces]
-    far = [pl.BlockSpec((piece.shape[0], part), lambda i, p: (0, slices + i)) for piece in pieces]
+    steps = slices // group
+    near = [pl.BlockSpec((v.shape[0], group * part), lambda i, p: (0, i)) for v in pieces]
+    far = [pl.BlockSpec((v.shape[0], group * part), lambda i, p: (0, steps + i)) for v in pieces]
     return pl.pallas_call(
         kernel,
         grid_spec=pltpu.PrefetchScalarGridSpec(
             num_scalar_prefetch=1,
-            grid=(slices,),
+            grid=(steps,),
             in_specs=[
                 pl.BlockSpec((seq_len, tile), lambda i, p: (0, i)),
                 whole(grad_mixed.shape),
@@ -623,6 +624,36 @@
     home = lax.dynamic_slice_in_dim(values, yh * rows, rows, 0)
     away = lax.dynamic_slice_in_dim(values, (1 - yh) * rows, rows, 0)
     return up(home) + up(lax.ppermute(away, "yh", [(0, 1), (1, 0)]))
+
+
+def on_own_rows(body, terms, row_arrays, own_arrays, gains, outs):
+    rows = terms[0].shape[0]
+    ins = terms + row_arrays + own_arrays + gains
+
+    def kernel(place_ref, *refs):
+        values = [ref[...] for ref in refs[: len(ins)]]
+        total = up(values[0])
+        for value in values[1 : len(terms)]:
+            total = total + up(value)
+        results = body(total, *values[len(terms) :])
+        for ref, result in zip(refs[len(ins) :], results):
+            ref[...] = result.astype(ref.dtype)
+
+    whole = lambda shape: pl.BlockSpec(shape, lambda i, p: (0, 0))
+    return pl.pallas_call(
+        kernel,
+        grid_spec=pltpu.PrefetchScalarGridSpec(
+            num_scalar_prefetch=1,
+            grid=(1,),
+            in_specs=[whole(v.shape) for v in terms]
+            + [pl.BlockSpec((rows, v.shape[1]), lambda i, p: (p[0], 0)) for v in row_arrays]
+            + [whole(v.shape) for v in own_arrays + gains],
+            out_specs=[whole(shape) for shape, _ in outs],
+        ),
+        out_shape=[jax.ShapeDtypeStruct(shape, dtype) for shape, dtype in outs],
+        compiler_params=pltpu.CompilerParams(vmem_limit_bytes=32 * 2**20),
+        cost_estimate=SMALL,
+    )(block_index(0, 0).astype(jnp.int32).reshape(1), *ins)
 
 
 def norm_and_qkv(tokens, mine, other, cols):
@@ -851,7 +882,6 @@
     local_heads = local_width // HEAD_SIZE
     rows = seq_len // (NX * NYL)
     x, y = lax.axis_index("x"), lax.axis_index("yl")
-    my_rows = (x * NYL + y) * rows
     scale = HEAD_SIZE**-0.5
 
     wide = 3 * local_width
@@ -860,6 +890,7 @@
     packed = jnp.concatenate([w_qkv.reshape(shard, wide).astype(bf16), w_out.astype(bf16)], 1)
     first_mine = gather_yz(jnp.concatenate([packed, small], 0))
     first_other = lax.ppermute(first_mine, "c", [(0, 1), (1, 0)])
+    cot_order = relative_rows(cotangent)
     ends = jnp.cumsum(doc_lengths[0])
 
     first, mixed, weight, vectors, mean_one, inverse_one = norm_and_qkv(
@@ -873,16 +904,27 @@
     sum_one = scatter_one(terms)
     later = terms_by_block(LATER_STEPS, [after(attended, *terms[2, 1])], weight, first=3)
     mlp_weight = gather_zc(after(mlp_weight, attended))
-    own_tokens = up(lax.dynamic_slice_in_dim(tokens, my_rows, rows, 0))
-    own_cot = up(lax.dynamic_slice_in_dim(cotangent, my_rows, rows, 0))
-    own_middle = own_tokens + scatter_three(later, scatter_two(later, sum_one))
-
-    own_two, inverse_two = normalize(own_middle)
-    second = (own_two * gain_b + bias_b).astype(bf16)
+    own_f32, own_bf16 = ((rows, width), f32), ((rows, width), bf16)
+    gain_a, gain_b, bias_b = (v.reshape(1, width) for v in (gain_a, gain_b, bias_b))
+
+    def second_norm(branch, x, gain, bias):
+        middle = up(x) + branch
+        normed, _ = normalize(middle)
+        return middle, permuted((normed * gain + bias).astype(bf16))
+
+    own_middle, second = on_own_rows(
+        second_norm,
+        scatter_three(later, scatter_two(later, sum_one)),
+        [tokens],
+        [],
+        [gain_b, bias_b],
+        [own_f32, own_bf16],
+    )
+
     second_one = gather_one(second)
     second_two = gather_two(second_one)
     grad_hidden, active, second = mlp(
-        gather_three(second, second_one, second_two), cotangent, mlp_weight
+        gather_three(second, second_one, second_two), cot_order, mlp_weight
     )
     hidden = [active, grad_hidden]
     terms = terms_by_block(STEP_ONE, hidden, mlp_weight, relative=True)
@@ -892,14 +934,33 @@
     )
     sum_two = scatter_two(later, sum_one)
     both = scatter_three(later, sum_two)
-    mlp_terms = mlp_gradients(after(second, sum_two[2]), grad_hidden, cotangent, active)
+    mlp_terms = mlp_gradients(after(second, sum_two[2]), grad_hidden, cot_order, active)
     both = after(both, mlp_terms)
     mlp_grads = scatter_dp(mlp_terms)
-    branch_two, grad_second = both[:, :width], both[:, width:]
-    output_own = (own_middle + branch_two).astype(bf16)
-
-    grad_middle = own_cot + norm_back(grad_second, own_two, inverse_two, gain_b)
-    own_branch = grad_middle.astype(bf16)
+    grad_up, grad_down = mlp_grads[:, : w_up.shape[1]], mlp_grads[:, w_up.shape[1] :]
+
+    def second_norm_back(both, cot, middle, gain):
+        grad = both[:, width:]
+        normed, inverse = normalize(middle)
+        vector = jnp.concatenate(
+            [
+                jnp.sum(grad * normed, axis=0, keepdims=True),
+                jnp.sum(grad, axis=0, keepdims=True),
+                jnp.zeros((6, width), f32),
+            ],
+            0,
+        )
+        back = up(cot) + norm_back(grad, normed, inverse, gain)
+        return middle + both[:, :width], back, back, vector
+
+    output_own, grad_middle, own_branch, vec_two = on_own_rows(
+        second_norm_back,
+        both,
+        [cotangent],
+        [own_middle],
+        [gain_b],
+        [own_bf16, own_f32, own_bf16, ((8, width), f32)],
+    )
     branch_one = gather_one(own_branch)
     branch_two = gather_two(branch_one)
     branch = gather_three(own_branch, branch_one, branch_two)
@@ -913,22 +974,27 @@
     )
     sum_two = scatter_two(later, sum_one)
     vec_one = vec_a + vec_b
-    vec_two = jnp.stack([jnp.sum(grad_second * own_two, 0), jnp.sum(grad_second, 0)], 0)
     late_vectors = scatter_order(
-        jnp.concatenate([vec_one[:2], vec_two, jnp.zeros((4, width), f32)], 0)
+        jnp.concatenate([vec_one[:2], vec_two[:2], jnp.zeros((4, width), f32)], 0)
     )
     grad_first = scatter_three(later, sum_two)
     late = late_gradients(after(first, *sum_one), grad_mixed, branch, attended, late_vectors)
     late = scatter_dp(late)
 
-    own_one, own_inverse = normalize(own_tokens)
-    grad_tokens = (grad_middle + norm_back(grad_first, own_one, own_inverse, gain_a)).astype(bf16)
+    def first_norm_back(grad, x, middle, gain):
+        normed, inverse = normalize(up(x))
+        return [middle + norm_back(grad, normed, inverse, gain)]
+
+    (grad_tokens,) = on_own_rows(
+        first_norm_back, grad_first, [tokens], [grad_middle], [gain_a], [own_bf16]
+    )
     output = gather_three(output_own, output_one, gather_two(output_one))
     output = assemble(output, width, bf16, 0)
     grad_one = gather_one(grad_tokens)
     input_grad = gather_three(grad_tokens, grad_one, gather_two(grad_one))
+    sums = sum_mp(late[:, wide + local_width : wide + local_width + 4].T)
+    input_grad, sums = lax.optimization_barrier((input_grad, sums))
     input_grad = assemble(input_grad, width, f32, 0)
-    sums = sum_mp(late[:, wide + local_width : wide + local_width + 4].T)
     return (
         output,
         input_grad,
@@ -938,8 +1004,8 @@
         late[:, wide : wide + local_width],
         sums[2],
         sums[3],
-        mlp_grads[:, : w_up.shape[1]],
-        mlp_grads[:, w_up.shape[1] :],
+        grad_up,
+        grad_down,
     )
 
 

time: 478 us -> 468 us (0.979)
  starting transfers between devices: 95.9 us -> 78.3 us
  waiting for transfers between devices: 140 us -> 157 us
  other arithmetic: 19.9 us -> 6.47 us
    ppermute x63, waiting for transfers between devices: 133 us -> 151 us  [send(): return lax.ppermute(values, CMP, pairs)]
    ppermute x63, starting transfers between devices: 83.1 us -> 66.9 us  [send(): return lax.ppermute(values, CMP, pairs)]
    unnamed x109 -> x121, local copies, waits for them, and re-layouts: 27 us -> 35.1 us
    reduce_sum x5 -> x0, other arithmetic: 5.19 us -> none  [the longest x2 2.84 us: normalize(): center = values - jnp.mean(values, axis=-1, keepdims=True)]
    convert_element_type x3 -> x0, other arithmetic: 4.81 us -> none  [the longest x1 3.07 us: local(): own_branch = grad_middle.astype(bf16)]
    pallas_call x2 -> x6, Pallas kernels: 30.9 us -> 34.6 us  [the longest x1 17.2 us: mlp(): pl.pallas_call(kernel, grid=(steps,), in_specs=[whole(piece.shape) for pi...]
  transfers between devices with their start and end apart: 71 -> 71, of which waited for: 39 -> 37; matrix products, arithmetic and copies ran while one was open for 5% -> 2% of each run, Pallas kernels for 15% -> 15%
where the time goes in v4:
time: 468 us; the launch traced here: 459 us
  waiting for transfers between devices  157 us (34%)
  Pallas kernels  121 us (26%)
  starting transfers between devices  78.3 us (17%)
  local copies, waits for them, and re-layouts  42.9 us (9%)
  blocking collectives  39.1 us (8%)
  between operations  15 us (3%)
  other arithmetic  6.47 us (1%)
    ppermute x63, waiting for transfers between devices, send(): return lax.ppermute(values, CMP, pairs)  151 us
    ppermute x63, starting transfers between devices, send(): return lax.ppermute(values, CMP, pairs)  66.9 us
    all_to_all x1, blocking collectives, gather_yz(): lax.all_to_all(copies, ('yh', 'z'), split_axis=0, concat_axis=0, tiled=True)  39.1 us
    unnamed x121, local copies, waits for them, and re-layouts  35.1 us
    pallas_call x6, Pallas kernels, terms_by_block(): pl.pallas_call(kernel, grid_spec=pltpu.PrefetchScalarGridSpec(num_scalar_...  29.6 us
    pallas_call x14, Pallas kernels, columnwise(): pl.pallas_call(kernel, grid_spec=pltpu.PrefetchScalarGridSpec(num_scalar_...  17.4 us
    pallas_call x1, Pallas kernels, mlp(): pl.pallas_call(kernel, grid=(steps,), in_specs=[whole(piece.shape) for pi...  17.2 us
    pallas_call x1, Pallas kernels, mlp_gradients(): pl.pallas_call(kernel, grid=(width // tile,), in_specs=[lhs, whole, lhs,...  10.2 us
  transfers between devices with their start and end apart: 71, of which 37 were waited for; matrix products, arithmetic and copies ran while one was open for 2% of the time, Pallas kernels for 15%

profile of v4, /device:TPU:2, one launch (start us, length us, event | category | flops | bytes accessed | tf_op | source)
XLA Modules:
  0.0 459.4 jit_solution(6579147834242236504)
XLA Ops:
  11.5 39.1 %all_to_all.10.mine_ref = bf16[8,144,1024]{2,1,0:T(8,128)(2,1)S(1)} all-to-all(bf16[8,144,1024]{2,1,0:T(8,128)(2,1)S(1)} %broadcast_in_dim.6), channel_id=1, replica_groups=mesh['yh'=2,'z'=4,'c'=2,'x'=4,'yl'=2] {'yh','z'}, dimensions={0} | all-to-all | bytes 4718592 | tf_op jit(solution)/shard_map/all_to_all | solution.py:296
  52.0 3.3 collective-permute-done.other_ref
  56.2 8.8 %shard_map.186 = (bf16[1024,2048]{1,0:T(8,128)(2,1)S(1)}, bf16[1024,768]{1,0:T(8,128)(2,1)S(1)}, bf16[2048,1024]{1,0:T(8,128)(2,1)S(1)}, f32[8,2048]{1,0:T(8,128...) custom-call(s32[1]{0:T(128)} %bitcast.19.place_ref.core_ref, bf16[1024,2048]{1,0:T(8,128)(2,1)} %refs_4_.5, ...), custom_call_target="tpu_custom_call" | custom-call | flops 9900000256 | bytes 27000000 | tf_op jit(solution)/shard_map/pallas_call | solution.py:696
  65.0 5.7 %shard_map.187 = (bf16[1024,256]{1,0:T(8,128)(2,1)S(1)}, f32[1024,256]{1,0:T(8,128)S(1)}) custom-call(s32[4]{0:T(128)S(1)} %bitcast.72, bf16[1024,768]{1,0:T(8,128)(2,1)S(1)} %get-tuple-element.125.q_ref.k_ref.v_ref.refs_0_.refs_1_.refs_2_, bf16[1024,768]{1,0:T(8,128)(2,1)S(1)} %get-tuple-element.125.q_ref.k_ref.v_ref.refs_0_.refs_1_.refs_2_, ...), custom_call_target="tpu_custom_call" | custom-call | flops 6600000000 | bytes 18000000 | tf_op jit(solution)/shard_map/pallas_call | solution.py:764
  72.3 2.2 copy-done.4
  77.9 3.0 shard_map.189
  82.2 2.8 collective-permute-done.2.refs_4_
  89.8 7.2 %collective-permute-done.5.refs_5_ = bf16[64,2048]{1,0:T(8,128)(2,1)S(1)} collective-permute-done((bf16[64,2048]{1,0:T(8,128)(2,1)S(1)}, bf16[64,2048]{1,0:T(8,128)(2,1)S(1)}, u32[]{:S(2)}, u32[]{:S(2)}) %collective-permute-start.5) | collective-permute-done | bytes 262176 | tf_op jit(solution)/shard_map/ppermute | solution.py:67
  97.9 2.6 collective-permute-done.4.refs_4_
  104.4 7.9 %collective-permute-done.7.refs_1_ = bf16[128,2048]{1,0:T(8,128)(2,1)S(1)} collective-permute-done((bf16[128,2048]{1,0:T(8,128)(2,1)S(1)}, bf16[128,2048]{1,0:T(8,128)(2,1)S(1)}, u32[]{:S(2)}, u32[]{:S(2)}) %collective-permute-start.7) | collective-permute-done | bytes 524320 | tf_op jit(solution)/shard_map/ppermute | solution.py:67
  114.6 3.2 collective-permute-start.10
  118.0 7.6 %collective-permute-done.10.refs_1_ = bf16[128,2048]{1,0:T(8,128)(2,1)S(1)} collective-permute-done((bf16[128,2048]{1,0:T(8,128)(2,1)S(1)}, bf16[128,2048]{1,0:T(8,128)(2,1)S(1)}, u32[]{:S(2)}, u32[]{:S(2)}) %collective-permute-start.10) | collective-permute-done | bytes 524320 | tf_op jit(solution)/shard_map/ppermute | solution.py:67
  125.6 2.2 collective-permute-done.11.refs_0_.refs_4_
  135.0 7.2 %collective-permute-done.13.refs_0_.refs_2_ = bf16[64,2048]{1,0:T(8,128)(2,1)S(1)} collective-permute-done((bf16[64,2048]{1,0:T(8,128)(2,1)}, bf16[64,2048]{1,0:T(8,128)(2,1)S(1)}, u32[]{:S(2)}, u32[]{:S(2)}) %collective-permute-start.13) | collective-permute-done | bytes 262176 | tf_op jit(solution)/shard_map/ppermute | solution.py:67
  142.2 2.8 collective-permute-done.16.refs_2_.refs_9_
  148.5 2.2 copy-done.8
  151.7 2.0 copy-done.40
  160.8 17.2 %shard_map.196 = (bf16[1024,1024]{1,0:T(8,128)(2,1)S(1)}, bf16[1024,1024]{1,0:T(8,128)(2,1)S(1)}, bf16[1024,2048]{1,0:T(8,128)(2,1)}) custom-call(bf16[128,2048]{1,0:T(8,128)(2,1)S(1)} %copy-done.33, bf16[128,2048]{1,0:T(8,128)(2,1)S(1)} %collective-permute-done.10.refs_1_, bf16[64,2048]{1,0:T(8,128)(2,1)S(1)} %collective-permute-done.13.refs_0_.refs_2_, ...), custom_call_target="tpu_custom_call" | custom-call | flops 17600000000 | bytes 48000000 | tf_op jit(solution)/shard_map/pallas_call | solution.py:483
  178.0 5.0 %shard_map.197 = (bf16[64,4096]{1,0:T(8,128)(2,1)S(1)}, bf16[64,4096]{1,0:T(8,128)(2,1)S(1)}) custom-call(s32[1]{0:T(128)} %constant.296.clone.1.place_ref, bf16[1024,1024]{1,0:T(8,128)(2,1)S(1)} %get-tuple-element.159.refs_0_.refs_1_.refs_2_.refs_3_.refs_4_.refs_5_.refs_6_.z_ref, ...), custom_call_target="tpu_custom_call" | custom-call | flops 2200000000 | bytes 6000000 | tf_op jit(solution)/shard_map/pallas_call | solution.py:399
  185.1 11.6 %shard_map.198 = (bf16[128,4096]{1,0:T(8,128)(2,1)S(1)}, bf16[128,4096]{1,0:T(8,128)(2,1)S(1)}, bf16[128,4096]{1,0:T(8,128)(2,1)S(1)}, bf16[128,4096]{1,0:T(8,12...) custom-call(s32[7]{0:T(128)S(1)} %copy-done.31, ...), custom_call_target="tpu_custom_call" | custom-call | flops 8800000000 | bytes 24000000 | tf_op jit(solution)/shard_map/pallas_call | solution.py:399
  204.1 12.8 %collective-permute-done.24.refs_5_ = bf16[64,4096]{1,0:T(8,128)(2,1)S(1)} collective-permute-done((bf16[64,4096]{1,0:T(8,128)(2,1)S(1)}, bf16[64,4096]{1,0:T(8,128)(2,1)S(1)}, u32[]{:S(2)}, u32[]{:S(2)}) %collective-permute-start.24) | collective-permute-done | bytes 524320 | tf_op jit(solution)/shard_map/ppermute | solution.py:67
  218.1 7.1 %collective-permute-done.23.refs_4_ = bf16[128,4096]{1,0:T(8,128)(2,1)S(1)} collective-permute-done((bf16[128,4096]{1,0:T(8,128)(2,1)S(1)}, bf16[128,4096]{1,0:T(8,128)(2,1)S(1)}, u32[]{:S(2)}, u32[]{:S(2)}) %collective-permute-start.23) | collective-permute-done | bytes 1048608 | tf_op jit(solution)/shard_map/ppermute | solution.py:67
  225.2 3.0 shard_map.200
  229.4 1.9 collective-permute-start.27
  231.3 10.2 %shard_map.201 = bf16[2048,2048]{1,0:T(8,128)(2,1)S(1)} custom-call(bf16[1024,2048]{1,0:T(8,128)(2,1)S(1)} %copy-done.44, bf16[1024,1024]{1,0:T(8,128)(2,1)S(1)} %get-tuple-element.160.refs_1_.refs_7_.refs_8_.refs_9_.refs_10_.refs_11_.refs_12_.refs_13_.du_ref, bf16[1024,2048]{1,0:T(8,128)(2,1)S(1)} %copy-done.41, ...), custom_call_target="tpu_custom_call" | custom-call | flops 12099999744 | bytes 33000000 | tf_op jit(solution)/shard_map/pallas_call | solution.py:523
  241.4 3.4 copy-done.6
  244.8 5.3 %collective-permute-done.26.refs_1_ = bf16[128,4096]{1,0:T(8,128)(2,1)} collective-permute-done((bf16[128,4096]{1,0:T(8,128)(2,1)}, bf16[128,4096]{1,0:T(8,128)(2,1)}, u32[]{:S(2)}, u32[]{:S(2)}) %collective-permute-start.26) | collective-permute-done | bytes 1048608 | tf_op jit(solution)/shard_map/ppermute | solution.py:67
  250.1 2.2 collective-permute-done.27.refs_2_
  252.3 2.2 copy-done.9
  254.5 4.6 %shard_map.202 = (bf16[128,2048]{1,0:T(8,128)(2,1)}, f32[128,2048]{1,0:T(8,128)S(1)}, bf16[128,2048]{1,0:T(8,128)(2,1)S(1)}, f32[8,2048]{1,0:T(8,128)S(1)}) custom-call(s32[1]{0:T(128)} %bitcast.10.place_ref, bf16[128,4096]{1,0:T(8,128)(2,1)S(1)} %get-tuple-element.177.refs_0_, bf16[128,4096]{1,0:T(8,128)(2,1)} %collective-permute-done.26.refs_1_, ...), custom_call_target="tpu_custom_call" | custom-call | flops 1 | bytes 1 | tf_op jit(solution)/shard_map/pallas_call | solution.py:643
  259.1 1.8 collective-permute-start.29
  262.1 6.5 %collective-permute-done.29.refs_0_.refs_9_.refs_8_.refs_18_ = bf16[128,2048]{1,0:T(8,128)(2,1)S(1)} collective-permute-done((bf16[128,2048]{1,0:T(8,128)(2,1)S(1)}, bf16[128,2048]{1,0:T(8,128)(2,1)S(1)}, u32[]{:S(2)}, u32[]{:S(2)}) %collective-permute-start.29) | collective-permute-done | bytes 524320 | tf_op jit(solution)/shard_map/ppermute | solution.py:67
  268.6 4.0 collective-permute-done.30.refs_1_.refs_6_.refs_5_.refs_15_
  277.1 4.3 collective-permute-done.32.refs_0_.refs_7_.refs_6_.refs_16_
  281.5 2.7 collective-permute-done.42.refs_1_.refs_8_.refs_7_.refs_17_
  284.2 3.7 collective-permute-done.44.refs_2_.refs_14_.refs_13_.refs_23_
  288.6 1.8 collective-permute-start.46
  290.5 4.1 collective-permute-done.45.refs_12_.refs_11_.refs_21_
  294.6 2.8 collective-permute-done.46.refs_13_.refs_12_.refs_22_
  297.4 8.8 %shard_map.208.refs_0_.refs_1_.refs_2_.refs_3_.refs_4_.refs_5_.refs_6_ = bf16[1024,768]{1,0:T(8,128)(2,1)S(1)} custom-call(s32[4]{0:T(128)S(1)} %bitcast.73, s32[8]{0:T(128)S(1)} %stack.160.place_ref, bf16[1024,768]{1,0:T(8,128)(2,1)S(1)} %copy-done.48, bf16[1024,768]{1,0:T(8,128)(2,1)S(1)} %copy-done.48, bf16[1024,768]{1,0:T(8,128)(2,1)S(1)} %copy-done.48, ...), custom_call_target="tpu_custom_call" | custom-call | flops 13200000000 | bytes 36000000 | tf_op jit(solution)/shard_map/pallas_call | solution.py:839
  306.3 2.5 shard_map.209
  310.9 6.3 %shard_map.210 = (bf16[128,2048]{1,0:T(8,128)(2,1)S(1)}, bf16[128,2048]{1,0:T(8,128)(2,1)S(1)}, bf16[128,2048]{1,0:T(8,128)(2,1)S(1)}, bf16[128,2048]{1,0:T(8,12...) custom-call(s32[7]{0:T(128)S(1)} %stack.153.place_ref, ...), custom_call_target="tpu_custom_call" | custom-call | flops 8800000000 | bytes 24000000 | tf_op jit(solution)/shard_map/pallas_call | solution.py:399
  320.4 7.4 %shard_map.216 = bf16[2048,1152]{1,0:T(8,128)(2,1)S(1)} custom-call(s32[8]{0:T(128)S(1)} %stack.160.place_ref, bf16[1024,2048]{1,0:T(8,128)(2,1)S(1)} %copy-done.46, bf16[1024,768]{1,0:T(8,128)(2,1)S(1)} %shard_map.208.refs_0_.refs_1_.refs_2_.refs_3_.refs_4_.refs_5_.refs_6_, bf16[1024,256]{1,0:T(8,128)(2,1)S(1)} %copy-done.43, f32[8,2048]{1,0:T(8,128)S(1)} %bitcast.71, ...), custom_call_target="tpu_custom_call" | custom-call | flops 12099999744 | bytes 33000000 | tf_op jit(solution)/shard_map/pallas_call | solution.py:579
  327.8 2.2 copy-done.7
  336.7 6.5 %collective-permute-done.51.refs_5_ = bf16[64,2048]{1,0:T(8,128)(2,1)S(1)} collective-permute-done((bf16[64,2048]{1,0:T(8,128)(2,1)S(1)}, bf16[64,2048]{1,0:T(8,128)(2,1)S(1)}, u32[]{:S(2)}, u32[]{:S(2)}) %collective-permute-start.51) | collective-permute-done | bytes 262176 | tf_op jit(solution)/shard_map/ppermute | solution.py:67
  343.1 3.3 collective-permute-done.52.refs_6_
  346.5 7.7 %collective-permute-done.50.refs_4_ = bf16[128,2048]{1,0:T(8,128)(2,1)S(1)} collective-permute-done((bf16[128,2048]{1,0:T(8,128)(2,1)S(1)}, bf16[128,2048]{1,0:T(8,128)(2,1)S(1)}, u32[]{:S(2)}, u32[]{:S(2)}) %collective-permute-start.50) | collective-permute-done | bytes 524320 | tf_op jit(solution)/shard_map/ppermute | solution.py:67
  358.9 3.9 collective-permute-start.33
  362.8 8.3 %collective-permute-done.53.refs_1_ = bf16[128,2048]{1,0:T(8,128)(2,1)S(1)} collective-permute-done((bf16[128,2048]{1,0:T(8,128)(2,1)S(1)}, bf16[128,2048]{1,0:T(8,128)(2,1)S(1)}, u32[]{:S(2)}, u32[]{:S(2)}) %collective-permute-start.53) | collective-permute-done | bytes 524320 | tf_op jit(solution)/shard_map/ppermute | solution.py:67
  371.5 3.1 collective-permute-done.54.refs_2_
  375.6 2.7 collective-permute-start.57
  378.3 7.5 %collective-permute-done.33.refs_1_.refs_2_ = bf16[128,2048]{1,0:T(8,128)(2,1)S(1)} collective-permute-done((bf16[128,2048]{1,0:T(8,128)(2,1)}, bf16[128,2048]{1,0:T(8,128)(2,1)S(1)}, u32[]{:S(2)}, u32[]{:S(2)}) %collective-permute-start.33) | collective-permute-done | bytes 524320 | tf_op jit(solution)/shard_map/ppermute | solution.py:67
  390.7 6.0 %collective-permute-done.57.refs_1_.refs_2_ = bf16[128,2048]{1,0:T(8,128)(2,1)S(1)} collective-permute-done((bf16[128,2048]{1,0:T(8,128)(2,1)S(1)}, bf16[128,2048]{1,0:T(8,128)(2,1)S(1)}, u32[]{:S(2)}, u32[]{:S(2)}) %collective-permute-start.57) | collective-permute-done | bytes 524320 | tf_op jit(solution)/shard_map/ppermute | solution.py:67
  402.1 3.7 collective-permute-done.37.refs_1_.refs_6_
  406.6 2.0 collective-permute-start.61
  410.3 2.6 collective-permute-start.65
  413.9 1.9 shard_map.205
  418.0 2.2 shard_map.215
  422.2 2.3 reduce-scatter.5.cloned.1.call-done
  424.5 1.9 constant_dynamic-slice_fusion
  426.4 3.0 collective-permute-start.66
  431.3 4.8 %all-to-all-start.1 = ((f32[8,4,128]{2,1,0:T(4,128)}), f32[8,4,128]{2,1,0:T(4,128)S(1)}, u32[]{:S(2)}, u32[]{:S(2)}) async-start(f32[8,4,128]{2,1,0:T(4,128)} %broadcast_in_dim.8), calls=%async_computation.2 | async-start | bytes 32768 | tf_op jit(solution)/shard_map/all_to_all | solution.py:287
  438.4 3.8 shard_map.206
  445.1 4.5 shard_map.217
  (272 shorter events, 107.6 us)
Async XLA Ops:
  7.2 149.2 %all-gather.2.cloned.1.call-start = ((), (), s32[]{:S(2)}) async-start(), calls=%async_computation.4 | async-start | bytes 9437184 | tf_op jit(solution)/shard_map/all_gather | solution.py:617
  55.3 15.5 %collective-permute-start.19 = (bf16[128,2048]{1,0:T(8,128)(2,1)S(1)}, bf16[128,2048]{1,0:T(8,128)(2,1)S(1)}, u32[]{:S(2)}, u32[]{:S(2)}) collective-permute-start(bf16[128,2048]{1,0:T(8,128)(2,1)S(1)} %pad_maximum_fusion.1), channel_id=1, source_target_pairs={{0,64},{64,0},{1,65},{65,1},{2,66},{66,2},{3,67},{67,3},{4,68},{68... | collective-permute-start | bytes 1572872 | tf_op jit(solution)/shard_map/ppermute | solution.py:611
  72.1 336.5 %reduce-scatter.3.cloned.1.call-start = ((), (), s32[]{:S(2)}) async-start(), calls=%async_computation.5 | async-start | bytes 5308416 | tf_op jit(solution)/shard_map/reduce_scatter | solution.py:621
  85.6 12.2 %collective-permute-start.3 = (bf16[128,2048]{1,0:T(8,128)(2,1)S(1)}, bf16[128,2048]{1,0:T(8,128)(2,1)S(1)}, u32[]{:S(2)}, u32[]{:S(2)}) collective-permute-start(bf16[128,2048]{1,0:T(8,128)(2,1)S(1)} %get-tuple-element.138), channel_id=1, source_target_pairs={{0,1},{1,0},{2,3},{3,2},{4,5},{5,4},{6,7},{7,6},{8,10},{9,11},{10,... | collective-permute-start | bytes 1572872 | tf_op jit(solution)/shard_map/ppermute | solution.py:67
  86.5 14.0 %collective-permute-start.4 = (bf16[128,2048]{1,0:T(8,128)(2,1)S(1)}, bf16[128,2048]{1,0:T(8,128)(2,1)S(1)}, u32[]{:S(2)}, u32[]{:S(2)}) collective-permute-start(bf16[128,2048]{1,0:T(8,128)(2,1)S(1)} %get-tuple-element.139), channel_id=1, source_target_pairs={{0,1},{1,0},{2,3},{3,2},{4,5},{5,4},{6,7},{7,6},{8,14},{9,15},{10,... | collective-permute-start | bytes 1572872 | tf_op jit(solution)/shard_map/ppermute | solution.py:67
  87.7 9.2 %collective-permute-start.5 = (bf16[64,2048]{1,0:T(8,128)(2,1)S(1)}, bf16[64,2048]{1,0:T(8,128)(2,1)S(1)}, u32[]{:S(2)}, u32[]{:S(2)}) collective-permute-start(bf16[64,2048]{1,0:T(8,128)(2,1)S(1)} %get-tuple-element.140), channel_id=1, source_target_pairs={{0,2},{1,3},{2,4},{3,5},{4,6},{5,7},{6,0},{7,1},{8,10},{9,11},{10,... | collective-permute-start | bytes 786440 | tf_op jit(solution)/shard_map/ppermute | solution.py:67
  89.2 8.6 %collective-permute-start.6 = (bf16[64,2048]{1,0:T(8,128)(2,1)S(1)}, bf16[64,2048]{1,0:T(8,128)(2,1)S(1)}, u32[]{:S(2)}, u32[]{:S(2)}) collective-permute-start(bf16[64,2048]{1,0:T(8,128)(2,1)S(1)} %get-tuple-element.141), channel_id=1, source_target_pairs={{0,6},{1,7},{2,0},{3,1},{4,2},{5,3},{6,4},{7,5},{8,14},{9,15},{10,... | collective-permute-start | bytes 786440 | tf_op jit(solution)/shard_map/ppermute | solution.py:67
  101.5 10.9 %collective-permute-start.7 = (bf16[128,2048]{1,0:T(8,128)(2,1)S(1)}, bf16[128,2048]{1,0:T(8,128)(2,1)S(1)}, u32[]{:S(2)}, u32[]{:S(2)}) collective-permute-start(bf16[128,2048]{1,0:T(8,128)(2,1)S(1)} %get-tuple-element.142), channel_id=1, source_target_pairs={{0,2},{1,3},{2,4},{3,5},{4,6},{5,7},{6,0},{7,1},{8,10},{9,11},{10,... | collective-permute-start | bytes 1572872 | tf_op jit(solution)/shard_map/ppermute | solution.py:67
  103.0 10.8 %collective-permute-start.8 = (bf16[128,2048]{1,0:T(8,128)(2,1)S(1)}, bf16[128,2048]{1,0:T(8,128)(2,1)S(1)}, u32[]{:S(2)}, u32[]{:S(2)}) collective-permute-start(bf16[128,2048]{1,0:T(8,128)(2,1)S(1)} %get-tuple-element.143), channel_id=1, source_target_pairs={{0,6},{1,7},{2,0},{3,1},{4,2},{5,3},{6,4},{7,5},{8,14},{9,15},{10,... | collective-permute-start | bytes 1572872 | tf_op jit(solution)/shard_map/ppermute | solution.py:67
  103.6 10.2 %collective-permute-start.9 = (bf16[128,2048]{1,0:T(8,128)(2,1)S(1)}, bf16[128,2048]{1,0:T(8,128)(2,1)S(1)}, u32[]{:S(2)}, u32[]{:S(2)}) collective-permute-start(bf16[128,2048]{1,0:T(8,128)(2,1)S(1)} %get-tuple-element.144), channel_id=1, source_target_pairs={{0,1},{1,0},{2,3},{3,2},{4,5},{5,4},{6,7},{7,6},{8,9},{9,8},{10,11... | collective-permute-start | bytes 1572872 | tf_op jit(solution)/shard_map/ppermute | solution.py:67
  114.6 11.0 %collective-permute-start.10 = (bf16[128,2048]{1,0:T(8,128)(2,1)S(1)}, bf16[128,2048]{1,0:T(8,128)(2,1)S(1)}, u32[]{:S(2)}, u32[]{:S(2)}) collective-permute-start(bf16[128,2048]{1,0:T(8,128)(2,1)S(1)} %get-tuple-element.146.refs_0_), channel_id=1, source_target_pairs={{0,6},{1,7},{2,0},{3,1},{4,2},{5,3},{6,4},{7,5},{8,14},{9,15},{10,... | collective-permute-start | bytes 1572872 | tf_op jit(solution)/shard_map/ppermute | solution.py:67
  117.7 10.1 %collective-permute-start.11 = (bf16[128,2048]{1,0:T(8,128)(2,1)S(1)}, bf16[128,2048]{1,0:T(8,128)(2,1)S(1)}, u32[]{:S(2)}, u32[]{:S(2)}) collective-permute-start(bf16[128,2048]{1,0:T(8,128)(2,1)S(1)} %get-tuple-element.146.refs_0_), channel_id=1, source_target_pairs={{0,2},{1,3},{2,4},{3,5},{4,6},{5,7},{6,0},{7,1},{8,10},{9,11},{10,... | collective-permute-start | bytes 1572872 | tf_op jit(solution)/shard_map/ppermute | solution.py:67
  117.7 10.1 %collective-permute-start.12 = (bf16[128,2048]{1,0:T(8,128)(2,1)S(1)}, bf16[128,2048]{1,0:T(8,128)(2,1)S(1)}, u32[]{:S(2)}, u32[]{:S(2)}) collective-permute-start(bf16[128,2048]{1,0:T(8,128)(2,1)S(1)} %get-tuple-element.146.refs_0_), channel_id=1, source_target_pairs={{0,1},{1,0},{2,3},{3,2},{4,5},{5,4},{6,7},{7,6},{8,9},{9,8},{10,11... | collective-permute-start | bytes 1572872 | tf_op jit(solution)/shard_map/ppermute | solution.py:67
  130.0 12.3 %collective-permute-start.15 = (bf16[128,2048]{1,0:T(8,128)(2,1)}, bf16[128,2048]{1,0:T(8,128)(2,1)}, u32[]{:S(2)}, u32[]{:S(2)}) collective-permute-start(bf16[128,2048]{1,0:T(8,128)(2,1)} %get-tuple-element.149), channel_id=1, source_target_pairs={{0,1},{1,0},{2,3},{3,2},{4,5},{5,4},{6,7},{7,6},{8,14},{9,15},{10,... | collective-permute-start | bytes 1572872 | tf_op jit(solution)/shard_map/ppermute | solution.py:67
  130.2 14.9 %collective-permute-start.16 = (bf16[128,2048]{1,0:T(8,128)(2,1)}, bf16[128,2048]{1,0:T(8,128)(2,1)}, u32[]{:S(2)}, u32[]{:S(2)}) collective-permute-start(bf16[128,2048]{1,0:T(8,128)(2,1)} %get-tuple-element.150), channel_id=1, source_target_pairs={{0,1},{1,0},{2,3},{3,2},{4,5},{5,4},{6,7},{7,6},{8,10},{9,11},{10,... | collective-permute-start | bytes 1572872 | tf_op jit(solution)/shard_map/ppermute | solution.py:67
  132.0 10.2 %collective-permute-start.13 = (bf16[64,2048]{1,0:T(8,128)(2,1)}, bf16[64,2048]{1,0:T(8,128)(2,1)S(1)}, u32[]{:S(2)}, u32[]{:S(2)}) collective-permute-start(bf16[64,2048]{1,0:T(8,128)(2,1)} %get-tuple-element.147), channel_id=1, source_target_pairs={{0,2},{1,3},{2,4},{3,5},{4,6},{5,7},{6,0},{7,1},{8,10},{9,11},{10,... | collective-permute-start | bytes 786440 | tf_op jit(solution)/shard_map/ppermute | solution.py:67
  133.2 9.0 %collective-permute-start.14 = (bf16[64,2048]{1,0:T(8,128)(2,1)}, bf16[64,2048]{1,0:T(8,128)(2,1)}, u32[]{:S(2)}, u32[]{:S(2)}) collective-permute-start(bf16[64,2048]{1,0:T(8,128)(2,1)} %get-tuple-element.148), channel_id=1, source_target_pairs={{0,6},{1,7},{2,0},{3,1},{4,2},{5,3},{6,4},{7,5},{8,14},{9,15},{10,... | collective-permute-start | bytes 786440 | tf_op jit(solution)/shard_map/ppermute | solution.py:67
  146.8 8.9 %collective-permute-start.18 = (bf16[64,2048]{1,0:T(8,128)(2,1)S(1)}, bf16[64,2048]{1,0:T(8,128)(2,1)S(1)}, u32[]{:S(2)}, u32[]{:S(2)}) collective-permute-start(bf16[64,2048]{1,0:T(8,128)(2,1)S(1)} %get-tuple-element.152), channel_id=1, source_target_pairs={{0,1},{1,0},{2,3},{3,2},{4,5},{5,4},{6,7},{7,6},{8,14},{9,15},{10,... | collective-permute-start | bytes 786440 | tf_op jit(solution)/shard_map/ppermute | solution.py:67
  183.0 13.7 %collective-permute-start.20 = (bf16[64,4096]{1,0:T(8,128)(2,1)S(1)}, bf16[64,4096]{1,0:T(8,128)(2,1)S(1)}, u32[]{:S(2)}, u32[]{:S(2)}) collective-permute-start(bf16[64,4096]{1,0:T(8,128)(2,1)S(1)} %get-tuple-element.157), channel_id=1, source_target_pairs={{0,1},{1,0},{2,3},{3,2},{4,5},{5,4},{6,7},{7,6},{8,10},{9,11},{10,... | collective-permute-start | bytes 1572872 | tf_op jit(solution)/shard_map/ppermute | solution.py:67
  183.3 14.6 %collective-permute-start.21 = (bf16[64,4096]{1,0:T(8,128)(2,1)S(1)}, bf16[64,4096]{1,0:T(8,128)(2,1)S(1)}, u32[]{:S(2)}, u32[]{:S(2)}) collective-permute-start(bf16[64,4096]{1,0:T(8,128)(2,1)S(1)} %get-tuple-element.158), channel_id=1, source_target_pairs={{0,1},{1,0},{2,3},{3,2},{4,5},{5,4},{6,7},{7,6},{8,14},{9,15},{10,... | collective-permute-start | bytes 1572872 | tf_op jit(solution)/shard_map/ppermute | solution.py:67
  199.1 19.0 %collective-permute-start.22 = (bf16[128,4096]{1,0:T(8,128)(2,1)S(1)}, bf16[128,4096]{1,0:T(8,128)(2,1)S(1)}, u32[]{:S(2)}, u32[]{:S(2)}) collective-permute-start(bf16[128,4096]{1,0:T(8,128)(2,1)S(1)} %get-tuple-element.168), channel_id=1, source_target_pairs={{0,1},{1,0},{2,3},{3,2},{4,5},{5,4},{6,7},{7,6},{8,10},{9,11},{10,... | collective-permute-start | bytes 3145736 | tf_op jit(solution)/shard_map/ppermute | solution.py:67
  199.4 25.8 %collective-permute-start.23 = (bf16[128,4096]{1,0:T(8,128)(2,1)S(1)}, bf16[128,4096]{1,0:T(8,128)(2,1)S(1)}, u32[]{:S(2)}, u32[]{:S(2)}) collective-permute-start(bf16[128,4096]{1,0:T(8,128)(2,1)S(1)} %get-tuple-element.169), channel_id=1, source_target_pairs={{0,1},{1,0},{2,3},{3,2},{4,5},{5,4},{6,7},{7,6},{8,14},{9,15},{10,... | collective-permute-start | bytes 3145736 | tf_op jit(solution)/shard_map/ppermute | solution.py:67
  201.2 15.8 %collective-permute-start.24 = (bf16[64,4096]{1,0:T(8,128)(2,1)S(1)}, bf16[64,4096]{1,0:T(8,128)(2,1)S(1)}, u32[]{:S(2)}, u32[]{:S(2)}) collective-permute-start(bf16[64,4096]{1,0:T(8,128)(2,1)S(1)} %get-tuple-element.170), channel_id=1, source_target_pairs={{0,2},{1,3},{2,4},{3,5},{4,6},{5,7},{6,0},{7,1},{8,10},{9,11},{10,... | collective-permute-start | bytes 1572872 | tf_op jit(solution)/shard_map/ppermute | solution.py:67
  202.4 15.7 %collective-permute-start.25 = (bf16[64,4096]{1,0:T(8,128)(2,1)S(1)}, bf16[64,4096]{1,0:T(8,128)(2,1)S(1)}, u32[]{:S(2)}, u32[]{:S(2)}) collective-permute-start(bf16[64,4096]{1,0:T(8,128)(2,1)S(1)} %get-tuple-element.171), channel_id=1, source_target_pairs={{0,6},{1,7},{2,0},{3,1},{4,2},{5,3},{6,4},{7,5},{8,14},{9,15},{10,... | collective-permute-start | bytes 1572872 | tf_op jit(solution)/shard_map/ppermute | solution.py:67
  228.1 22.0 %collective-permute-start.26 = (bf16[128,4096]{1,0:T(8,128)(2,1)}, bf16[128,4096]{1,0:T(8,128)(2,1)}, u32[]{:S(2)}, u32[]{:S(2)}) collective-permute-start(bf16[128,4096]{1,0:T(8,128)(2,1)} %get-tuple-element.172), channel_id=1, source_target_pairs={{0,2},{1,3},{2,4},{3,5},{4,6},{5,7},{6,0},{7,1},{8,10},{9,11},{10,... | collective-permute-start | bytes 3145736 | tf_op jit(solution)/shard_map/ppermute | solution.py:67
  229.4 22.9 %collective-permute-start.27 = (bf16[128,4096]{1,0:T(8,128)(2,1)}, bf16[128,4096]{1,0:T(8,128)(2,1)}, u32[]{:S(2)}, u32[]{:S(2)}) collective-permute-start(bf16[128,4096]{1,0:T(8,128)(2,1)} %get-tuple-element.173), channel_id=1, source_target_pairs={{0,6},{1,7},{2,0},{3,1},{4,2},{5,3},{6,4},{7,5},{8,14},{9,15},{10,... | collective-permute-start | bytes 3145736 | tf_op jit(solution)/shard_map/ppermute | solution.py:67
  231.2 21.1 %collective-permute-start.28 = (bf16[128,4096]{1,0:T(8,128)(2,1)}, bf16[128,4096]{1,0:T(8,128)(2,1)}, u32[]{:S(2)}, u32[]{:S(2)}) collective-permute-start(bf16[128,4096]{1,0:T(8,128)(2,1)} %get-tuple-element.174), channel_id=1, source_target_pairs={{0,1},{1,0},{2,3},{3,2},{4,5},{5,4},{6,7},{7,6},{8,9},{9,8},{10,11... | collective-permute-start | bytes 3145736 | tf_op jit(solution)/shard_map/ppermute | solution.py:67
  259.1 9.5 %collective-permute-start.29 = (bf16[128,2048]{1,0:T(8,128)(2,1)S(1)}, bf16[128,2048]{1,0:T(8,128)(2,1)S(1)}, u32[]{:S(2)}, u32[]{:S(2)}) collective-permute-start(bf16[128,2048]{1,0:T(8,128)(2,1)S(1)} %get-tuple-element.183.refs_5_.refs_4_.refs_14_), channel_id=1, source_target_pairs={{0,2},{1,3},{2,4},{3,5},{4,6},{5,7},{6,0},{7,1},{8,10},{9,11},{10,... | collective-permute-start | bytes 1572872 | tf_op jit(solution)/shard_map/ppermute | solution.py:67
  261.0 11.6 %collective-permute-start.30 = (bf16[128,2048]{1,0:T(8,128)(2,1)S(1)}, bf16[128,2048]{1,0:T(8,128)(2,1)S(1)}, u32[]{:S(2)}, u32[]{:S(2)}) collective-permute-start(bf16[128,2048]{1,0:T(8,128)(2,1)S(1)} %get-tuple-element.183.refs_5_.refs_4_.refs_14_), channel_id=1, source_target_pairs={{0,6},{1,7},{2,0},{3,1},{4,2},{5,3},{6,4},{7,5},{8,14},{9,15},{10,... | collective-permute-start | bytes 1572872 | tf_op jit(solution)/shard_map/ppermute | solution.py:67
  261.5 11.1 %collective-permute-start.31 = (bf16[128,2048]{1,0:T(8,128)(2,1)S(1)}, bf16[128,2048]{1,0:T(8,128)(2,1)S(1)}, u32[]{:S(2)}, u32[]{:S(2)}) collective-permute-start(bf16[128,2048]{1,0:T(8,128)(2,1)S(1)} %get-tuple-element.183.refs_5_.refs_4_.refs_14_), channel_id=1, source_target_pairs={{0,1},{1,0},{2,3},{3,2},{4,5},{5,4},{6,7},{7,6},{8,9},{9,8},{10,11... | collective-permute-start | bytes 1572872 | tf_op jit(solution)/shard_map/ppermute | solution.py:67
  273.0 11.2 %collective-permute-start.43 = (bf16[128,2048]{1,0:T(8,128)(2,1)S(1)}, bf16[128,2048]{1,0:T(8,128)(2,1)S(1)}, u32[]{:S(2)}, u32[]{:S(2)}) collective-permute-start(bf16[128,2048]{1,0:T(8,128)(2,1)S(1)} %get-tuple-element.194), channel_id=1, source_target_pairs={{0,1},{1,0},{2,3},{3,2},{4,5},{5,4},{6,7},{7,6},{8,14},{9,15},{10,... | collective-permute-start | bytes 1572872 | tf_op jit(solution)/shard_map/ppermute | solution.py:67
  273.5 14.4 %collective-permute-start.44 = (bf16[128,2048]{1,0:T(8,128)(2,1)S(1)}, bf16[128,2048]{1,0:T(8,128)(2,1)S(1)}, u32[]{:S(2)}, u32[]{:S(2)}) collective-permute-start(bf16[128,2048]{1,0:T(8,128)(2,1)S(1)} %get-tuple-element.195), channel_id=1, source_target_pairs={{0,1},{1,0},{2,3},{3,2},{4,5},{5,4},{6,7},{7,6},{8,10},{9,11},{10,... | collective-permute-start | bytes 1572872 | tf_op jit(solution)/shard_map/ppermute | solution.py:67
  288.6 8.8 %collective-permute-start.46 = (bf16[64,2048]{1,0:T(8,128)(2,1)S(1)}, bf16[64,2048]{1,0:T(8,128)(2,1)S(1)}, u32[]{:S(2)}, u32[]{:S(2)}) collective-permute-start(bf16[64,2048]{1,0:T(8,128)(2,1)S(1)} %get-tuple-element.197), channel_id=1, source_target_pairs={{0,1},{1,0},{2,3},{3,2},{4,5},{5,4},{6,7},{7,6},{8,14},{9,15},{10,... | collective-permute-start | bytes 786440 | tf_op jit(solution)/shard_map/ppermute | solution.py:67
  308.8 10.9 %collective-permute-start.47 = (bf16[64,2048]{1,0:T(8,128)(2,1)S(1)}, bf16[64,2048]{1,0:T(8,128)(2,1)S(1)}, u32[]{:S(2)}, u32[]{:S(2)}) collective-permute-start(bf16[64,2048]{1,0:T(8,128)(2,1)S(1)} %get-tuple-element.200), channel_id=1, source_target_pairs={{0,1},{1,0},{2,3},{3,2},{4,5},{5,4},{6,7},{7,6},{8,10},{9,11},{10,... | collective-permute-start | bytes 786440 | tf_op jit(solution)/shard_map/ppermute | solution.py:67
  309.2 10.5 %collective-permute-start.48 = (bf16[64,2048]{1,0:T(8,128)(2,1)S(1)}, bf16[64,2048]{1,0:T(8,128)(2,1)S(1)}, u32[]{:S(2)}, u32[]{:S(2)}) collective-permute-start(bf16[64,2048]{1,0:T(8,128)(2,1)S(1)} %get-tuple-element.201), channel_id=1, source_target_pairs={{0,1},{1,0},{2,3},{3,2},{4,5},{5,4},{6,7},{7,6},{8,14},{9,15},{10,... | collective-permute-start | bytes 786440 | tf_op jit(solution)/shard_map/ppermute | solution.py:67
  330.1 94.4 %reduce-scatter.5.cloned.1.call-start = ((), (), s32[]{:S(2)}) async-start(), calls=%async_computation.6 | async-start | bytes 9437184 | tf_op jit(solution)/shard_map/reduce_scatter | solution.py:621
  332.6 13.9 %collective-permute-start.49 = (bf16[128,2048]{1,0:T(8,128)(2,1)S(1)}, bf16[128,2048]{1,0:T(8,128)(2,1)S(1)}, u32[]{:S(2)}, u32[]{:S(2)}) collective-permute-start(bf16[128,2048]{1,0:T(8,128)(2,1)S(1)} %get-tuple-element.210), channel_id=1, source_target_pairs={{0,1},{1,0},{2,3},{3,2},{4,5},{5,4},{6,7},{7,6},{8,10},{9,11},{10,... | collective-permute-start | bytes 1572872 | tf_op jit(solution)/shard_map/ppermute | solution.py:67
  333.1 21.1 %collective-permute-start.50 = (bf16[128,2048]{1,0:T(8,128)(2,1)S(1)}, bf16[128,2048]{1,0:T(8,128)(2,1)S(1)}, u32[]{:S(2)}, u32[]{:S(2)}) collective-permute-start(bf16[128,2048]{1,0:T(8,128)(2,1)S(1)} %get-tuple-element.211), channel_id=1, source_target_pairs={{0,1},{1,0},{2,3},{3,2},{4,5},{5,4},{6,7},{7,6},{8,14},{9,15},{10,... | collective-permute-start | bytes 1572872 | tf_op jit(solution)/shard_map/ppermute | solution.py:67
  334.7 8.5 %collective-permute-start.51 = (bf16[64,2048]{1,0:T(8,128)(2,1)S(1)}, bf16[64,2048]{1,0:T(8,128)(2,1)S(1)}, u32[]{:S(2)}, u32[]{:S(2)}) collective-permute-start(bf16[64,2048]{1,0:T(8,128)(2,1)S(1)} %get-tuple-element.212), channel_id=1, source_target_pairs={{0,2},{1,3},{2,4},{3,5},{4,6},{5,7},{6,0},{7,1},{8,10},{9,11},{10,... | collective-permute-start | bytes 786440 | tf_op jit(solution)/shard_map/ppermute | solution.py:67
  336.4 10.0 %collective-permute-start.52 = (bf16[64,2048]{1,0:T(8,128)(2,1)S(1)}, bf16[64,2048]{1,0:T(8,128)(2,1)S(1)}, u32[]{:S(2)}, u32[]{:S(2)}) collective-permute-start(bf16[64,2048]{1,0:T(8,128)(2,1)S(1)} %get-tuple-element.213), channel_id=1, source_target_pairs={{0,6},{1,7},{2,0},{3,1},{4,2},{5,3},{6,4},{7,5},{8,14},{9,15},{10,... | collective-permute-start | bytes 786440 | tf_op jit(solution)/shard_map/ppermute | solution.py:67
  356.2 14.9 %collective-permute-start.53 = (bf16[128,2048]{1,0:T(8,128)(2,1)S(1)}, bf16[128,2048]{1,0:T(8,128)(2,1)S(1)}, u32[]{:S(2)}, u32[]{:S(2)}) collective-permute-start(bf16[128,2048]{1,0:T(8,128)(2,1)S(1)} %get-tuple-element.214), channel_id=1, source_target_pairs={{0,2},{1,3},{2,4},{3,5},{4,6},{5,7},{6,0},{7,1},{8,10},{9,11},{10,... | collective-permute-start | bytes 1572872 | tf_op jit(solution)/shard_map/ppermute | solution.py:67
  357.8 16.8 %collective-permute-start.54 = (bf16[128,2048]{1,0:T(8,128)(2,1)S(1)}, bf16[128,2048]{1,0:T(8,128)(2,1)S(1)}, u32[]{:S(2)}, u32[]{:S(2)}) collective-permute-start(bf16[128,2048]{1,0:T(8,128)(2,1)S(1)} %get-tuple-element.215), channel_id=1, source_target_pairs={{0,6},{1,7},{2,0},{3,1},{4,2},{5,3},{6,4},{7,5},{8,14},{9,15},{10,... | collective-permute-start | bytes 1572872 | tf_op jit(solution)/shard_map/ppermute | solution.py:67
  358.3 16.3 %collective-permute-start.55 = (bf16[128,2048]{1,0:T(8,128)(2,1)S(1)}, bf16[128,2048]{1,0:T(8,128)(2,1)S(1)}, u32[]{:S(2)}, u32[]{:S(2)}) collective-permute-start(bf16[128,2048]{1,0:T(8,128)(2,1)S(1)} %get-tuple-element.216), channel_id=1, source_target_pairs={{0,1},{1,0},{2,3},{3,2},{4,5},{5,4},{6,7},{7,6},{8,9},{9,8},{10,11... | collective-permute-start | bytes 1572872 | tf_op jit(solution)/shard_map/ppermute | solution.py:67
  358.9 26.9 %collective-permute-start.33 = (bf16[128,2048]{1,0:T(8,128)(2,1)}, bf16[128,2048]{1,0:T(8,128)(2,1)S(1)}, u32[]{:S(2)}, u32[]{:S(2)}) collective-permute-start(bf16[128,2048]{1,0:T(8,128)(2,1)} %get-tuple-element.185.refs_1_), channel_id=1, source_target_pairs={{0,6},{1,7},{2,0},{3,1},{4,2},{5,3},{6,4},{7,5},{8,14},{9,15},{10,... | collective-permute-start | bytes 1572872 | tf_op jit(solution)/shard_map/ppermute | solution.py:67
  362.8 24.6 %collective-permute-start.34 = (bf16[128,2048]{1,0:T(8,128)(2,1)}, bf16[128,2048]{1,0:T(8,128)(2,1)S(1)}, u32[]{:S(2)}, u32[]{:S(2)}) collective-permute-start(bf16[128,2048]{1,0:T(8,128)(2,1)} %get-tuple-element.185.refs_1_), channel_id=1, source_target_pairs={{0,2},{1,3},{2,4},{3,5},{4,6},{5,7},{6,0},{7,1},{8,10},{9,11},{10,... | collective-permute-start | bytes 1572872 | tf_op jit(solution)/shard_map/ppermute | solution.py:67
  371.1 16.3 %collective-permute-start.35 = (bf16[128,2048]{1,0:T(8,128)(2,1)}, bf16[128,2048]{1,0:T(8,128)(2,1)S(1)}, u32[]{:S(2)}, u32[]{:S(2)}) collective-permute-start(bf16[128,2048]{1,0:T(8,128)(2,1)} %get-tuple-element.185.refs_1_), channel_id=1, source_target_pairs={{0,1},{1,0},{2,3},{3,2},{4,5},{5,4},{6,7},{7,6},{8,9},{9,8},{10,11... | collective-permute-start | bytes 1572872 | tf_op jit(solution)/shard_map/ppermute | solution.py:67
  375.5 14.8 %collective-permute-start.56 = (bf16[128,2048]{1,0:T(8,128)(2,1)S(1)}, bf16[128,2048]{1,0:T(8,128)(2,1)S(1)}, u32[]{:S(2)}, u32[]{:S(2)}) collective-permute-start(bf16[128,2048]{1,0:T(8,128)(2,1)S(1)} %shard_map.213.refs_1_), channel_id=1, source_target_pairs={{0,1},{1,0},{2,3},{3,2},{4,5},{5,4},{6,7},{7,6},{8,9},{9,8},{10,11... | collective-permute-start | bytes 1572872 | tf_op jit(solution)/shard_map/ppermute | solution.py:67
  375.6 21.1 %collective-permute-start.57 = (bf16[128,2048]{1,0:T(8,128)(2,1)S(1)}, bf16[128,2048]{1,0:T(8,128)(2,1)S(1)}, u32[]{:S(2)}, u32[]{:S(2)}) collective-permute-start(bf16[128,2048]{1,0:T(8,128)(2,1)S(1)} %shard_map.213.refs_1_), channel_id=1, source_target_pairs={{0,6},{1,7},{2,0},{3,1},{4,2},{5,3},{6,4},{7,5},{8,14},{9,15},{10,... | collective-permute-start | bytes 1572872 | tf_op jit(solution)/shard_map/ppermute | solution.py:67
  385.8 12.1 %collective-permute-start.58 = (bf16[128,2048]{1,0:T(8,128)(2,1)S(1)}, bf16[128,2048]{1,0:T(8,128)(2,1)S(1)}, u32[]{:S(2)}, u32[]{:S(2)}) collective-permute-start(bf16[128,2048]{1,0:T(8,128)(2,1)S(1)} %shard_map.213.refs_1_), channel_id=1, source_target_pairs={{0,2},{1,3},{2,4},{3,5},{4,6},{5,7},{6,0},{7,1},{8,10},{9,11},{10,... | collective-permute-start | bytes 1572872 | tf_op jit(solution)/shard_map/ppermute | solution.py:67
  388.7 17.1 %collective-permute-start.38 = (bf16[128,2048]{1,0:T(8,128)(2,1)}, bf16[128,2048]{1,0:T(8,128)(2,1)S(1)}, u32[]{:S(2)}, u32[]{:S(2)}) collective-permute-start(bf16[128,2048]{1,0:T(8,128)(2,1)} %get-tuple-element.188), channel_id=1, source_target_pairs={{0,1},{1,0},{2,3},{3,2},{4,5},{5,4},{6,7},{7,6},{8,14},{9,15},{10,... | collective-permute-start | bytes 1572872 | tf_op jit(solution)/shard_map/ppermute | solution.py:67
  388.7 12.9 %collective-permute-start.36 = (bf16[64,2048]{1,0:T(8,128)(2,1)S(1)}, bf16[64,2048]{1,0:T(8,128)(2,1)S(1)}, u32[]{:S(2)}, u32[]{:S(2)}) collective-permute-start(bf16[64,2048]{1,0:T(8,128)(2,1)S(1)} %get-tuple-element.186), channel_id=1, source_target_pairs={{0,2},{1,3},{2,4},{3,5},{4,6},{5,7},{6,0},{7,1},{8,10},{9,11},{10,... | collective-permute-start | bytes 786440 | tf_op jit(solution)/shard_map/ppermute | solution.py:67
  390.3 20.0 %collective-permute-start.39 = (bf16[128,2048]{1,0:T(8,128)(2,1)}, bf16[128,2048]{1,0:T(8,128)(2,1)}, u32[]{:S(2)}, u32[]{:S(2)}) collective-permute-start(bf16[128,2048]{1,0:T(8,128)(2,1)} %get-tuple-element.189), channel_id=1, source_target_pairs={{0,1},{1,0},{2,3},{3,2},{4,5},{5,4},{6,7},{7,6},{8,10},{9,11},{10,... | collective-permute-start | bytes 1572872 | tf_op jit(solution)/shard_map/ppermute | solution.py:67
  396.7 9.1 %collective-permute-start.37 = (bf16[64,2048]{1,0:T(8,128)(2,1)}, bf16[64,2048]{1,0:T(8,128)(2,1)}, u32[]{:S(2)}, u32[]{:S(2)}) collective-permute-start(bf16[64,2048]{1,0:T(8,128)(2,1)} %get-tuple-element.187), channel_id=1, source_target_pairs={{0,6},{1,7},{2,0},{3,1},{4,2},{5,3},{6,4},{7,5},{8,14},{9,15},{10,... | collective-permute-start | bytes 786440 | tf_op jit(solution)/shard_map/ppermute | solution.py:67
  399.9 18.0 %collective-permute-start.59 = (bf16[128,2048]{1,0:T(8,128)(2,1)}, bf16[128,2048]{1,0:T(8,128)(2,1)}, u32[]{:S(2)}, u32[]{:S(2)}) collective-permute-start(bf16[128,2048]{1,0:T(8,128)(2,1)} %get-tuple-element.218), channel_id=1, source_target_pairs={{0,1},{1,0},{2,3},{3,2},{4,5},{5,4},{6,7},{7,6},{8,14},{9,15},{10,... | collective-permute-start | bytes 1572872 | tf_op jit(solution)/shard_map/ppermute | solution.py:67
  401.6 16.4 %collective-permute-start.62 = (bf16[128,2048]{1,0:T(8,128)(2,1)}, bf16[128,2048]{1,0:T(8,128)(2,1)}, u32[]{:S(2)}, u32[]{:S(2)}) collective-permute-start(bf16[128,2048]{1,0:T(8,128)(2,1)} %get-tuple-element.221), channel_id=1, source_target_pairs={{0,1},{1,0},{2,3},{3,2},{4,5},{5,4},{6,7},{7,6},{8,10},{9,11},{10,... | collective-permute-start | bytes 1572872 | tf_op jit(solution)/shard_map/ppermute | solution.py:67
  405.8 10.1 %collective-permute-start.60 = (bf16[64,2048]{1,0:T(8,128)(2,1)}, bf16[64,2048]{1,0:T(8,128)(2,1)}, u32[]{:S(2)}, u32[]{:S(2)}) collective-permute-start(bf16[64,2048]{1,0:T(8,128)(2,1)} %copy-done.35), channel_id=1, source_target_pairs={{0,2},{1,3},{2,4},{3,5},{4,6},{5,7},{6,0},{7,1},{8,10},{9,11},{10,... | collective-permute-start | bytes 786440 | tf_op jit(solution)/shard_map/ppermute | solution.py:67
  406.6 10.5 %collective-permute-start.61 = (bf16[64,2048]{1,0:T(8,128)(2,1)}, bf16[64,2048]{1,0:T(8,128)(2,1)}, u32[]{:S(2)}, u32[]{:S(2)}) collective-permute-start(bf16[64,2048]{1,0:T(8,128)(2,1)} %copy-done.34), channel_id=1, source_target_pairs={{0,6},{1,7},{2,0},{3,1},{4,2},{5,3},{6,4},{7,5},{8,14},{9,15},{10,... | collective-permute-start | bytes 786440 | tf_op jit(solution)/shard_map/ppermute | solution.py:67
  410.3 16.1 %collective-permute-start.65 = (bf16[128,1152]{1,0:T(8,128)(2,1)}, bf16[128,1152]{1,0:T(8,128)(2,1)}, u32[]{:S(2)}, u32[]{:S(2)}) collective-permute-start(bf16[128,1152]{1,0:T(8,128)(2,1)} %constant_dynamic-slice_fusion.1), channel_id=1, source_target_pairs={{0,64},{64,0},{1,65},{65,1},{2,66},{66,2},{3,67},{67,3},{4,68},{68... | collective-permute-start | bytes 884744 | tf_op jit(solution)/shard_map/ppermute | solution.py:626
  415.9 20.4 %collective-permute-start.40 = (bf16[64,2048]{1,0:T(8,128)(2,1)}, bf16[64,2048]{1,0:T(8,128)(2,1)}, u32[]{:S(2)}, u32[]{:S(2)}) collective-permute-start(bf16[64,2048]{1,0:T(8,128)(2,1)} %get-tuple-element.190), channel_id=1, source_target_pairs={{0,1},{1,0},{2,3},{3,2},{4,5},{5,4},{6,7},{7,6},{8,10},{9,11},{10,... | collective-permute-start | bytes 786440 | tf_op jit(solution)/shard_map/ppermute | solution.py:67
  417.1 19.2 %collective-permute-start.41 = (bf16[64,2048]{1,0:T(8,128)(2,1)}, bf16[64,2048]{1,0:T(8,128)(2,1)}, u32[]{:S(2)}, u32[]{:S(2)}) collective-permute-start(bf16[64,2048]{1,0:T(8,128)(2,1)} %get-tuple-element.191), channel_id=1, source_target_pairs={{0,1},{1,0},{2,3},{3,2},{4,5},{5,4},{6,7},{7,6},{8,14},{9,15},{10,... | collective-permute-start | bytes 786440 | tf_op jit(solution)/shard_map/ppermute | solution.py:67
  420.2 23.8 %collective-permute-start.63 = (bf16[64,2048]{1,0:T(8,128)(2,1)}, bf16[64,2048]{1,0:T(8,128)(2,1)}, u32[]{:S(2)}, u32[]{:S(2)}) collective-permute-start(bf16[64,2048]{1,0:T(8,128)(2,1)} %get-tuple-element.222), channel_id=1, source_target_pairs={{0,1},{1,0},{2,3},{3,2},{4,5},{5,4},{6,7},{7,6},{8,10},{9,11},{10,... | collective-permute-start | bytes 786440 | tf_op jit(solution)/shard_map/ppermute | solution.py:67
  421.3 22.7 %collective-permute-start.64 = (bf16[64,2048]{1,0:T(8,128)(2,1)}, bf16[64,2048]{1,0:T(8,128)(2,1)}, u32[]{:S(2)}, u32[]{:S(2)}) collective-permute-start(bf16[64,2048]{1,0:T(8,128)(2,1)} %get-tuple-element.223), channel_id=1, source_target_pairs={{0,1},{1,0},{2,3},{3,2},{4,5},{5,4},{6,7},{7,6},{8,14},{9,15},{10,... | collective-permute-start | bytes 786440 | tf_op jit(solution)/shard_map/ppermute | solution.py:67
  426.4 23.7 %collective-permute-start.66 = (bf16[128,2048]{1,0:T(8,128)(2,1)}, bf16[128,2048]{1,0:T(8,128)(2,1)}, u32[]{:S(2)}, u32[]{:S(2)}) collective-permute-start(bf16[128,2048]{1,0:T(8,128)(2,1)} %constant_dynamic-slice_fusion), channel_id=1, source_target_pairs={{0,64},{64,0},{1,65},{65,1},{2,66},{66,2},{3,67},{67,3},{4,68},{68... | collective-permute-start | bytes 1572872 | tf_op jit(solution)/shard_map/ppermute | solution.py:626
  431.3 12.7 %all-to-all-start.1 = ((f32[8,4,128]{2,1,0:T(4,128)}), f32[8,4,128]{2,1,0:T(4,128)S(1)}, u32[]{:S(2)}, u32[]{:S(2)}) async-start(f32[8,4,128]{2,1,0:T(4,128)} %broadcast_in_dim.8), calls=%async_computation.2 | async-start | bytes 32768 | tf_op jit(solution)/shard_map/all_to_all | solution.py:287
  (65 other events, 725.0 us)
Sparse Core Ops, SparseCore 0:
  72.2 48.7 all-gather.1
  330.2 39.4 reduce-scatter.2
  372.7 51.7 reduce-scatter.4

commit v5 on v4

--- a/solution.py
+++ b/solution.py
@@ -10,7 +10,7 @@
 bf16 = jnp.bfloat16
 f32 = jnp.float32
 
-MLP_TILE, MLP_VMEM = 256, 44
+MLP_TILE, MLP_VMEM = 512, 40
 SMALL = pl.CostEstimate(flops=1, bytes_accessed=1, transcendentals=0)
 
 
@@ -479,7 +479,8 @@
         slope = half + (0.5 * root) * u * (1.0 - t * t) * (1.0 + (3.0 * cubic) * square)
         du_ref[...] = (dz * slope).astype(bf16)
 
-    whole = lambda shape: pl.BlockSpec(shape, lambda j: (0,) * len(shape))
+    once = pl.Buffered(1)
+    whole = lambda shape: pl.BlockSpec(shape, lambda j: (0,) * len(shape), pipeline_mode=once)
     return pl.pallas_call(
         kernel,
         grid=(steps,),

time: 468 us -> 468 us (level)
    unnamed x121 -> x119, local copies, waits for them, and re-layouts: 35.1 us -> 38.1 us
where the time goes in v5:
time: 468 us; the launch traced here: 458 us
  waiting for transfers between devices  156 us (33%)
  Pallas kernels  117 us (25%)
  starting transfers between devices  78.6 us (17%)
  local copies, waits for them, and re-layouts  46 us (10%)
  blocking collectives  39.1 us (8%)
  between operations  15 us (3%)
  other arithmetic  6.47 us (1%)
    ppermute x63, waiting for transfers between devices, send(): return lax.ppermute(values, CMP, pairs)  150 us
    ppermute x63, starting transfers between devices, send(): return lax.ppermute(values, CMP, pairs)  67.1 us
    all_to_all x1, blocking collectives, gather_yz(): lax.all_to_all(copies, ('yh', 'z'), split_axis=0, concat_axis=0, tiled=True)  39.1 us
    unnamed x119, local copies, waits for them, and re-layouts  38.1 us
    pallas_call x6, Pallas kernels, terms_by_block(): pl.pallas_call(kernel, grid_spec=pltpu.PrefetchScalarGridSpec(num_scalar_...  29.6 us
    pallas_call x14, Pallas kernels, columnwise(): pl.pallas_call(kernel, grid_spec=pltpu.PrefetchScalarGridSpec(num_scalar_...  17.4 us
    pallas_call x1, Pallas kernels, mlp(): pl.pallas_call(kernel, grid=(steps,), in_specs=[whole(piece.shape) for pi...  13.5 us
    pallas_call x1, Pallas kernels, mlp_gradients(): pl.pallas_call(kernel, grid=(width // tile,), in_specs=[lhs, whole, lhs,...  10.2 us
  transfers between devices with their start and end apart: 71, of which 37 were waited for; matrix products, arithmetic and copies ran while one was open for 2% of the time, Pallas kernels for 15%

profile of v5, /device:TPU:2, one launch (start us, length us, event | category | flops | bytes accessed | tf_op | source)
XLA Modules:
  0.0 458.4 jit_solution(11025579976963713773)
XLA Ops:
  11.5 39.1 %all_to_all.10.mine_ref = bf16[8,144,1024]{2,1,0:T(8,128)(2,1)S(1)} all-to-all(bf16[8,144,1024]{2,1,0:T(8,128)(2,1)S(1)} %broadcast_in_dim.6), channel_id=1, replica_groups=mesh['yh'=2,'z'=4,'c'=2,'x'=4,'yl'=2] {'yh','z'}, dimensions={0} | all-to-all | bytes 4718592 | tf_op jit(solution)/shard_map/all_to_all | solution.py:296
  52.0 3.3 collective-permute-done.other_ref
  56.2 8.8 %shard_map.186 = (bf16[1024,2048]{1,0:T(8,128)(2,1)S(1)}, bf16[1024,768]{1,0:T(8,128)(2,1)S(1)}, bf16[2048,1024]{1,0:T(8,128)(2,1)S(1)}, f32[8,2048]{1,0:T(8,128...) custom-call(s32[1]{0:T(128)} %bitcast.19.place_ref.core_ref, bf16[1024,2048]{1,0:T(8,128)(2,1)} %refs_4_.5, ...), custom_call_target="tpu_custom_call" | custom-call | flops 9900000256 | bytes 27000000 | tf_op jit(solution)/shard_map/pallas_call | solution.py:697
  65.0 5.7 %shard_map.187 = (bf16[1024,256]{1,0:T(8,128)(2,1)S(1)}, f32[1024,256]{1,0:T(8,128)S(1)}) custom-call(s32[4]{0:T(128)S(1)} %bitcast.70, bf16[1024,768]{1,0:T(8,128)(2,1)S(1)} %get-tuple-element.125.q_ref.k_ref.v_ref.refs_0_.refs_1_.refs_2_, bf16[1024,768]{1,0:T(8,128)(2,1)S(1)} %get-tuple-element.125.q_ref.k_ref.v_ref.refs_0_.refs_1_.refs_2_, ...), custom_call_target="tpu_custom_call" | custom-call | flops 6600000000 | bytes 18000000 | tf_op jit(solution)/shard_map/pallas_call | solution.py:765
  72.3 2.2 copy-done.6
  77.8 3.0 shard_map.189
  82.2 2.8 collective-permute-done.2.refs_4_
  89.8 7.2 %collective-permute-done.5.refs_5_ = bf16[64,2048]{1,0:T(8,128)(2,1)S(1)} collective-permute-done((bf16[64,2048]{1,0:T(8,128)(2,1)S(1)}, bf16[64,2048]{1,0:T(8,128)(2,1)S(1)}, u32[]{:S(2)}, u32[]{:S(2)}) %collective-permute-start.5) | collective-permute-done | bytes 262176 | tf_op jit(solution)/shard_map/ppermute | solution.py:67
  97.9 2.6 collective-permute-done.4.refs_4_
  104.4 7.9 %collective-permute-done.7.refs_1_ = bf16[128,2048]{1,0:T(8,128)(2,1)S(1)} collective-permute-done((bf16[128,2048]{1,0:T(8,128)(2,1)S(1)}, bf16[128,2048]{1,0:T(8,128)(2,1)S(1)}, u32[]{:S(2)}, u32[]{:S(2)}) %collective-permute-start.7) | collective-permute-done | bytes 524320 | tf_op jit(solution)/shard_map/ppermute | solution.py:67
  114.6 3.2 collective-permute-start.10
  118.0 7.6 %collective-permute-done.10.refs_1_ = bf16[128,2048]{1,0:T(8,128)(2,1)S(1)} collective-permute-done((bf16[128,2048]{1,0:T(8,128)(2,1)S(1)}, bf16[128,2048]{1,0:T(8,128)(2,1)S(1)}, u32[]{:S(2)}, u32[]{:S(2)}) %collective-permute-start.10) | collective-permute-done | bytes 524320 | tf_op jit(solution)/shard_map/ppermute | solution.py:67
  125.6 2.2 collective-permute-done.11.refs_0_.refs_4_
  135.0 7.2 %collective-permute-done.13.refs_0_.refs_2_ = bf16[64,2048]{1,0:T(8,128)(2,1)S(1)} collective-permute-done((bf16[64,2048]{1,0:T(8,128)(2,1)}, bf16[64,2048]{1,0:T(8,128)(2,1)S(1)}, u32[]{:S(2)}, u32[]{:S(2)}) %collective-permute-start.13) | collective-permute-done | bytes 262176 | tf_op jit(solution)/shard_map/ppermute | solution.py:67
  142.2 2.8 collective-permute-done.16.refs_2_.refs_9_
  148.5 2.2 copy-done.10
  151.7 2.0 copy-done.42
  160.4 13.5 %shard_map.196 = (bf16[1024,1024]{1,0:T(8,128)(2,1)S(1)}, bf16[1024,1024]{1,0:T(8,128)(2,1)S(1)}, bf16[1024,2048]{1,0:T(8,128)(2,1)S(1)}) custom-call(bf16[128,2048]{1,0:T(8,128)(2,1)S(1)} %copy-done.35, bf16[128,2048]{1,0:T(8,128)(2,1)S(1)} %collective-permute-done.10.refs_1_, bf16[64,2048]{1,0:T(8,128)(2,1)S(1)} %collective-permute-done.13.refs_0_.refs_2_, ...), custom_call_target="tpu_custom_call" | custom-call | flops 17600000000 | bytes 48000000 | tf_op jit(solution)/shard_map/pallas_call | solution.py:484
  173.9 3.4 copy-done.3
  177.3 4.9 %shard_map.197 = (bf16[64,4096]{1,0:T(8,128)(2,1)S(1)}, bf16[64,4096]{1,0:T(8,128)(2,1)S(1)}) custom-call(s32[1]{0:T(128)} %constant.296.clone.1.place_ref, bf16[1024,1024]{1,0:T(8,128)(2,1)S(1)} %get-tuple-element.159.refs_0_.refs_1_.refs_2_.refs_3_.refs_4_.refs_5_.refs_6_.z_ref, ...), custom_call_target="tpu_custom_call" | custom-call | flops 2200000000 | bytes 6000000 | tf_op jit(solution)/shard_map/pallas_call | solution.py:399
  184.4 11.6 %shard_map.198 = (bf16[128,4096]{1,0:T(8,128)(2,1)S(1)}, bf16[128,4096]{1,0:T(8,128)(2,1)S(1)}, bf16[128,4096]{1,0:T(8,128)(2,1)S(1)}, bf16[128,4096]{1,0:T(8,12...) custom-call(s32[7]{0:T(128)S(1)} %copy-done.33, ...), custom_call_target="tpu_custom_call" | custom-call | flops 8800000000 | bytes 24000000 | tf_op jit(solution)/shard_map/pallas_call | solution.py:399
  203.6 12.7 %collective-permute-done.24.refs_5_ = bf16[64,4096]{1,0:T(8,128)(2,1)S(1)} collective-permute-done((bf16[64,4096]{1,0:T(8,128)(2,1)S(1)}, bf16[64,4096]{1,0:T(8,128)(2,1)S(1)}, u32[]{:S(2)}, u32[]{:S(2)}) %collective-permute-start.24) | collective-permute-done | bytes 524320 | tf_op jit(solution)/shard_map/ppermute | solution.py:67
  217.5 6.9 %collective-permute-done.23.refs_4_ = bf16[128,4096]{1,0:T(8,128)(2,1)S(1)} collective-permute-done((bf16[128,4096]{1,0:T(8,128)(2,1)S(1)}, bf16[128,4096]{1,0:T(8,128)(2,1)S(1)}, u32[]{:S(2)}, u32[]{:S(2)}) %collective-permute-start.23) | collective-permute-done | bytes 1048608 | tf_op jit(solution)/shard_map/ppermute | solution.py:67
  224.5 2.9 shard_map.200
  230.3 10.2 %shard_map.201 = bf16[2048,2048]{1,0:T(8,128)(2,1)S(1)} custom-call(bf16[1024,2048]{1,0:T(8,128)(2,1)S(1)} %get-tuple-element.176.h_ref, bf16[1024,1024]{1,0:T(8,128)(2,1)S(1)} %get-tuple-element.160.refs_1_.refs_7_.refs_8_.refs_9_.refs_10_.refs_11_.refs_12_.refs_13_.du_ref, bf16[1024,2048]{1,0:T(8,128)(2,1)S(1)} %copy-done.43, ...), custom_call_target="tpu_custom_call" | custom-call | flops 12099999744 | bytes 33000000 | tf_op jit(solution)/shard_map/pallas_call | solution.py:524
  240.5 3.4 copy-done.8
  243.9 5.4 %collective-permute-done.26.refs_1_ = bf16[128,4096]{1,0:T(8,128)(2,1)} collective-permute-done((bf16[128,4096]{1,0:T(8,128)(2,1)}, bf16[128,4096]{1,0:T(8,128)(2,1)}, u32[]{:S(2)}, u32[]{:S(2)}) %collective-permute-start.26) | collective-permute-done | bytes 1048608 | tf_op jit(solution)/shard_map/ppermute | solution.py:67
  249.3 2.1 collective-permute-done.27.refs_2_
  251.4 2.2 copy-done.11
  253.6 4.6 %shard_map.202 = (bf16[128,2048]{1,0:T(8,128)(2,1)}, f32[128,2048]{1,0:T(8,128)S(1)}, bf16[128,2048]{1,0:T(8,128)(2,1)S(1)}, f32[8,2048]{1,0:T(8,128)S(1)}) custom-call(s32[1]{0:T(128)} %bitcast.10.place_ref, bf16[128,4096]{1,0:T(8,128)(2,1)S(1)} %get-tuple-element.177.refs_0_, bf16[128,4096]{1,0:T(8,128)(2,1)} %collective-permute-done.26.refs_1_, ...), custom_call_target="tpu_custom_call" | custom-call | flops 1 | bytes 1 | tf_op jit(solution)/shard_map/pallas_call | solution.py:644
  261.2 6.5 %collective-permute-done.29.refs_0_.refs_9_.refs_8_.refs_18_ = bf16[128,2048]{1,0:T(8,128)(2,1)S(1)} collective-permute-done((bf16[128,2048]{1,0:T(8,128)(2,1)S(1)}, bf16[128,2048]{1,0:T(8,128)(2,1)S(1)}, u32[]{:S(2)}, u32[]{:S(2)}) %collective-permute-start.29) | collective-permute-done | bytes 524320 | tf_op jit(solution)/shard_map/ppermute | solution.py:67
  267.7 3.8 collective-permute-done.30.refs_1_.refs_6_.refs_5_.refs_15_
  274.0 2.0 collective-permute-start.32
  276.0 4.3 collective-permute-done.32.refs_0_.refs_7_.refs_6_.refs_16_
  280.4 2.9 collective-permute-done.42.refs_1_.refs_8_.refs_7_.refs_17_
  283.2 3.5 collective-permute-done.44.refs_2_.refs_14_.refs_13_.refs_23_
  289.4 4.1 collective-permute-done.45.refs_12_.refs_11_.refs_21_
  293.5 2.8 collective-permute-done.46.refs_13_.refs_12_.refs_22_
  296.3 8.8 %shard_map.208.refs_0_.refs_1_.refs_2_.refs_3_.refs_4_.refs_5_.refs_6_ = bf16[1024,768]{1,0:T(8,128)(2,1)S(1)} custom-call(s32[4]{0:T(128)S(1)} %bitcast.71, s32[8]{0:T(128)S(1)} %stack.160.place_ref, bf16[1024,768]{1,0:T(8,128)(2,1)S(1)} %copy-done.49, bf16[1024,768]{1,0:T(8,128)(2,1)S(1)} %copy-done.49, bf16[1024,768]{1,0:T(8,128)(2,1)S(1)} %copy-done.49, ...), custom_call_target="tpu_custom_call" | custom-call | flops 13200000000 | bytes 36000000 | tf_op jit(solution)/shard_map/pallas_call | solution.py:840
  305.2 2.5 shard_map.209
  309.7 6.3 %shard_map.210 = (bf16[128,2048]{1,0:T(8,128)(2,1)S(1)}, bf16[128,2048]{1,0:T(8,128)(2,1)S(1)}, bf16[128,2048]{1,0:T(8,128)(2,1)S(1)}, bf16[128,2048]{1,0:T(8,12...) custom-call(s32[7]{0:T(128)S(1)} %stack.153.place_ref, ...), custom_call_target="tpu_custom_call" | custom-call | flops 8800000000 | bytes 24000000 | tf_op jit(solution)/shard_map/pallas_call | solution.py:399
  319.3 7.4 %shard_map.216 = bf16[2048,1152]{1,0:T(8,128)(2,1)S(1)} custom-call(s32[8]{0:T(128)S(1)} %stack.160.place_ref, bf16[1024,2048]{1,0:T(8,128)(2,1)S(1)} %copy-done.47, bf16[1024,768]{1,0:T(8,128)(2,1)S(1)} %shard_map.208.refs_0_.refs_1_.refs_2_.refs_3_.refs_4_.refs_5_.refs_6_, bf16[1024,256]{1,0:T(8,128)(2,1)S(1)} %copy-done.45, f32[8,2048]{1,0:T(8,128)S(1)} %bitcast.69, ...), custom_call_target="tpu_custom_call" | custom-call | flops 12099999744 | bytes 33000000 | tf_op jit(solution)/shard_map/pallas_call | solution.py:580
  326.7 2.2 copy-done.9
  333.6 2.0 collective-permute-start.51
  335.6 6.7 %collective-permute-done.51.refs_5_ = bf16[64,2048]{1,0:T(8,128)(2,1)S(1)} collective-permute-done((bf16[64,2048]{1,0:T(8,128)(2,1)S(1)}, bf16[64,2048]{1,0:T(8,128)(2,1)S(1)}, u32[]{:S(2)}, u32[]{:S(2)}) %collective-permute-start.51) | collective-permute-done | bytes 262176 | tf_op jit(solution)/shard_map/ppermute | solution.py:67
  342.3 3.2 collective-permute-done.52.refs_6_
  345.5 7.4 %collective-permute-done.50.refs_4_ = bf16[128,2048]{1,0:T(8,128)(2,1)S(1)} collective-permute-done((bf16[128,2048]{1,0:T(8,128)(2,1)S(1)}, bf16[128,2048]{1,0:T(8,128)(2,1)S(1)}, u32[]{:S(2)}, u32[]{:S(2)}) %collective-permute-start.50) | collective-permute-done | bytes 524320 | tf_op jit(solution)/shard_map/ppermute | solution.py:67
  354.9 2.2 collective-permute-start.53
  357.6 4.2 collective-permute-start.33
  361.9 7.9 %collective-permute-done.53.refs_1_ = bf16[128,2048]{1,0:T(8,128)(2,1)S(1)} collective-permute-done((bf16[128,2048]{1,0:T(8,128)(2,1)S(1)}, bf16[128,2048]{1,0:T(8,128)(2,1)S(1)}, u32[]{:S(2)}, u32[]{:S(2)}) %collective-permute-start.53) | collective-permute-done | bytes 524320 | tf_op jit(solution)/shard_map/ppermute | solution.py:67
  370.1 3.5 collective-permute-done.54.refs_2_
  374.7 2.7 collective-permute-start.57
  377.4 7.5 %collective-permute-done.33.refs_1_.refs_2_ = bf16[128,2048]{1,0:T(8,128)(2,1)S(1)} collective-permute-done((bf16[128,2048]{1,0:T(8,128)(2,1)}, bf16[128,2048]{1,0:T(8,128)(2,1)S(1)}, u32[]{:S(2)}, u32[]{:S(2)}) %collective-permute-start.33) | collective-permute-done | bytes 524320 | tf_op jit(solution)/shard_map/ppermute | solution.py:67
  389.8 6.1 %collective-permute-done.57.refs_1_.refs_2_ = bf16[128,2048]{1,0:T(8,128)(2,1)S(1)} collective-permute-done((bf16[128,2048]{1,0:T(8,128)(2,1)S(1)}, bf16[128,2048]{1,0:T(8,128)(2,1)S(1)}, u32[]{:S(2)}, u32[]{:S(2)}) %collective-permute-start.57) | collective-permute-done | bytes 524320 | tf_op jit(solution)/shard_map/ppermute | solution.py:67
  401.2 3.9 collective-permute-done.37.refs_1_.refs_6_
  405.9 2.0 collective-permute-start.61
  409.6 2.6 collective-permute-start.65
  413.3 1.9 shard_map.205
  417.3 2.2 shard_map.215
  421.5 2.1 reduce-scatter.5.cloned.1.call-done
  425.5 3.0 collective-permute-start.66
  430.4 4.8 %all-to-all-start.1 = ((f32[8,4,128]{2,1,0:T(4,128)}), f32[8,4,128]{2,1,0:T(4,128)S(1)}, u32[]{:S(2)}, u32[]{:S(2)}) async-start(f32[8,4,128]{2,1,0:T(4,128)} %broadcast_in_dim.8), calls=%async_computation.2 | async-start | bytes 32768 | tf_op jit(solution)/shard_map/all_to_all | solution.py:287
  437.5 3.8 shard_map.206
  444.1 4.5 shard_map.217
  (269 shorter events, 108.4 us)
Async XLA Ops:
  7.2 149.2 %all-gather.2.cloned.1.call-start = ((), (), s32[]{:S(2)}) async-start(), calls=%async_computation.4 | async-start | bytes 9437184 | tf_op jit(solution)/shard_map/all_gather | solution.py:618
  55.3 15.5 %collective-permute-start.19 = (bf16[128,2048]{1,0:T(8,128)(2,1)S(1)}, bf16[128,2048]{1,0:T(8,128)(2,1)S(1)}, u32[]{:S(2)}, u32[]{:S(2)}) collective-permute-start(bf16[128,2048]{1,0:T(8,128)(2,1)S(1)} %pad_maximum_fusion.1), channel_id=1, source_target_pairs={{0,64},{64,0},{1,65},{65,1},{2,66},{66,2},{3,67},{67,3},{4,68},{68... | collective-permute-start | bytes 1572872 | tf_op jit(solution)/shard_map/ppermute | solution.py:612
  72.1 335.8 %reduce-scatter.3.cloned.1.call-start = ((), (), s32[]{:S(2)}) async-start(), calls=%async_computation.5 | async-start | bytes 5308416 | tf_op jit(solution)/shard_map/reduce_scatter | solution.py:622
  85.6 12.2 %collective-permute-start.3 = (bf16[128,2048]{1,0:T(8,128)(2,1)S(1)}, bf16[128,2048]{1,0:T(8,128)(2,1)S(1)}, u32[]{:S(2)}, u32[]{:S(2)}) collective-permute-start(bf16[128,2048]{1,0:T(8,128)(2,1)S(1)} %get-tuple-element.138), channel_id=1, source_target_pairs={{0,1},{1,0},{2,3},{3,2},{4,5},{5,4},{6,7},{7,6},{8,10},{9,11},{10,... | collective-permute-start | bytes 1572872 | tf_op jit(solution)/shard_map/ppermute | solution.py:67
  86.5 14.0 %collective-permute-start.4 = (bf16[128,2048]{1,0:T(8,128)(2,1)S(1)}, bf16[128,2048]{1,0:T(8,128)(2,1)S(1)}, u32[]{:S(2)}, u32[]{:S(2)}) collective-permute-start(bf16[128,2048]{1,0:T(8,128)(2,1)S(1)} %get-tuple-element.139), channel_id=1, source_target_pairs={{0,1},{1,0},{2,3},{3,2},{4,5},{5,4},{6,7},{7,6},{8,14},{9,15},{10,... | collective-permute-start | bytes 1572872 | tf_op jit(solution)/shard_map/ppermute | solution.py:67
  87.7 9.2 %collective-permute-start.5 = (bf16[64,2048]{1,0:T(8,128)(2,1)S(1)}, bf16[64,2048]{1,0:T(8,128)(2,1)S(1)}, u32[]{:S(2)}, u32[]{:S(2)}) collective-permute-start(bf16[64,2048]{1,0:T(8,128)(2,1)S(1)} %get-tuple-element.140), channel_id=1, source_target_pairs={{0,2},{1,3},{2,4},{3,5},{4,6},{5,7},{6,0},{7,1},{8,10},{9,11},{10,... | collective-permute-start | bytes 786440 | tf_op jit(solution)/shard_map/ppermute | solution.py:67
  89.2 8.6 %collective-permute-start.6 = (bf16[64,2048]{1,0:T(8,128)(2,1)S(1)}, bf16[64,2048]{1,0:T(8,128)(2,1)S(1)}, u32[]{:S(2)}, u32[]{:S(2)}) collective-permute-start(bf16[64,2048]{1,0:T(8,128)(2,1)S(1)} %get-tuple-element.141), channel_id=1, source_target_pairs={{0,6},{1,7},{2,0},{3,1},{4,2},{5,3},{6,4},{7,5},{8,14},{9,15},{10,... | collective-permute-start | bytes 786440 | tf_op jit(solution)/shard_map/ppermute | solution.py:67
  101.5 10.9 %collective-permute-start.7 = (bf16[128,2048]{1,0:T(8,128)(2,1)S(1)}, bf16[128,2048]{1,0:T(8,128)(2,1)S(1)}, u32[]{:S(2)}, u32[]{:S(2)}) collective-permute-start(bf16[128,2048]{1,0:T(8,128)(2,1)S(1)} %get-tuple-element.142), channel_id=1, source_target_pairs={{0,2},{1,3},{2,4},{3,5},{4,6},{5,7},{6,0},{7,1},{8,10},{9,11},{10,... | collective-permute-start | bytes 1572872 | tf_op jit(solution)/shard_map/ppermute | solution.py:67
  103.0 10.8 %collective-permute-start.8 = (bf16[128,2048]{1,0:T(8,128)(2,1)S(1)}, bf16[128,2048]{1,0:T(8,128)(2,1)S(1)}, u32[]{:S(2)}, u32[]{:S(2)}) collective-permute-start(bf16[128,2048]{1,0:T(8,128)(2,1)S(1)} %get-tuple-element.143), channel_id=1, source_target_pairs={{0,6},{1,7},{2,0},{3,1},{4,2},{5,3},{6,4},{7,5},{8,14},{9,15},{10,... | collective-permute-start | bytes 1572872 | tf_op jit(solution)/shard_map/ppermute | solution.py:67
  103.6 10.2 %collective-permute-start.9 = (bf16[128,2048]{1,0:T(8,128)(2,1)S(1)}, bf16[128,2048]{1,0:T(8,128)(2,1)S(1)}, u32[]{:S(2)}, u32[]{:S(2)}) collective-permute-start(bf16[128,2048]{1,0:T(8,128)(2,1)S(1)} %get-tuple-element.144), channel_id=1, source_target_pairs={{0,1},{1,0},{2,3},{3,2},{4,5},{5,4},{6,7},{7,6},{8,9},{9,8},{10,11... | collective-permute-start | bytes 1572872 | tf_op jit(solution)/shard_map/ppermute | solution.py:67
  114.6 11.0 %collective-permute-start.10 = (bf16[128,2048]{1,0:T(8,128)(2,1)S(1)}, bf16[128,2048]{1,0:T(8,128)(2,1)S(1)}, u32[]{:S(2)}, u32[]{:S(2)}) collective-permute-start(bf16[128,2048]{1,0:T(8,128)(2,1)S(1)} %get-tuple-element.146.refs_0_), channel_id=1, source_target_pairs={{0,6},{1,7},{2,0},{3,1},{4,2},{5,3},{6,4},{7,5},{8,14},{9,15},{10,... | collective-permute-start | bytes 1572872 | tf_op jit(solution)/shard_map/ppermute | solution.py:67
  117.7 10.1 %collective-permute-start.11 = (bf16[128,2048]{1,0:T(8,128)(2,1)S(1)}, bf16[128,2048]{1,0:T(8,128)(2,1)S(1)}, u32[]{:S(2)}, u32[]{:S(2)}) collective-permute-start(bf16[128,2048]{1,0:T(8,128)(2,1)S(1)} %get-tuple-element.146.refs_0_), channel_id=1, source_target_pairs={{0,2},{1,3},{2,4},{3,5},{4,6},{5,7},{6,0},{7,1},{8,10},{9,11},{10,... | collective-permute-start | bytes 1572872 | tf_op jit(solution)/shard_map/ppermute | solution.py:67
  117.7 10.1 %collective-permute-start.12 = (bf16[128,2048]{1,0:T(8,128)(2,1)S(1)}, bf16[128,2048]{1,0:T(8,128)(2,1)S(1)}, u32[]{:S(2)}, u32[]{:S(2)}) collective-permute-start(bf16[128,2048]{1,0:T(8,128)(2,1)S(1)} %get-tuple-element.146.refs_0_), channel_id=1, source_target_pairs={{0,1},{1,0},{2,3},{3,2},{4,5},{5,4},{6,7},{7,6},{8,9},{9,8},{10,11... | collective-permute-start | bytes 1572872 | tf_op jit(solution)/shard_map/ppermute | solution.py:67
  129.9 12.3 %collective-permute-start.15 = (bf16[128,2048]{1,0:T(8,128)(2,1)}, bf16[128,2048]{1,0:T(8,128)(2,1)}, u32[]{:S(2)}, u32[]{:S(2)}) collective-permute-start(bf16[128,2048]{1,0:T(8,128)(2,1)} %get-tuple-element.149), channel_id=1, source_target_pairs={{0,1},{1,0},{2,3},{3,2},{4,5},{5,4},{6,7},{7,6},{8,14},{9,15},{10,... | collective-permute-start | bytes 1572872 | tf_op jit(solution)/shard_map/ppermute | solution.py:67
  130.2 14.9 %collective-permute-start.16 = (bf16[128,2048]{1,0:T(8,128)(2,1)}, bf16[128,2048]{1,0:T(8,128)(2,1)}, u32[]{:S(2)}, u32[]{:S(2)}) collective-permute-start(bf16[128,2048]{1,0:T(8,128)(2,1)} %get-tuple-element.150), channel_id=1, source_target_pairs={{0,1},{1,0},{2,3},{3,2},{4,5},{5,4},{6,7},{7,6},{8,10},{9,11},{10,... | collective-permute-start | bytes 1572872 | tf_op jit(solution)/shard_map/ppermute | solution.py:67
  132.0 10.2 %collective-permute-start.13 = (bf16[64,2048]{1,0:T(8,128)(2,1)}, bf16[64,2048]{1,0:T(8,128)(2,1)S(1)}, u32[]{:S(2)}, u32[]{:S(2)}) collective-permute-start(bf16[64,2048]{1,0:T(8,128)(2,1)} %get-tuple-element.147), channel_id=1, source_target_pairs={{0,2},{1,3},{2,4},{3,5},{4,6},{5,7},{6,0},{7,1},{8,10},{9,11},{10,... | collective-permute-start | bytes 786440 | tf_op jit(solution)/shard_map/ppermute | solution.py:67
  133.2 9.0 %collective-permute-start.14 = (bf16[64,2048]{1,0:T(8,128)(2,1)}, bf16[64,2048]{1,0:T(8,128)(2,1)}, u32[]{:S(2)}, u32[]{:S(2)}) collective-permute-start(bf16[64,2048]{1,0:T(8,128)(2,1)} %get-tuple-element.148), channel_id=1, source_target_pairs={{0,6},{1,7},{2,0},{3,1},{4,2},{5,3},{6,4},{7,5},{8,14},{9,15},{10,... | collective-permute-start | bytes 786440 | tf_op jit(solution)/shard_map/ppermute | solution.py:67
  146.8 8.9 %collective-permute-start.18 = (bf16[64,2048]{1,0:T(8,128)(2,1)S(1)}, bf16[64,2048]{1,0:T(8,128)(2,1)S(1)}, u32[]{:S(2)}, u32[]{:S(2)}) collective-permute-start(bf16[64,2048]{1,0:T(8,128)(2,1)S(1)} %get-tuple-element.152), channel_id=1, source_target_pairs={{0,1},{1,0},{2,3},{3,2},{4,5},{5,4},{6,7},{7,6},{8,14},{9,15},{10,... | collective-permute-start | bytes 786440 | tf_op jit(solution)/shard_map/ppermute | solution.py:67
  182.3 13.7 %collective-permute-start.20 = (bf16[64,4096]{1,0:T(8,128)(2,1)S(1)}, bf16[64,4096]{1,0:T(8,128)(2,1)S(1)}, u32[]{:S(2)}, u32[]{:S(2)}) collective-permute-start(bf16[64,4096]{1,0:T(8,128)(2,1)S(1)} %get-tuple-element.157), channel_id=1, source_target_pairs={{0,1},{1,0},{2,3},{3,2},{4,5},{5,4},{6,7},{7,6},{8,10},{9,11},{10,... | collective-permute-start | bytes 1572872 | tf_op jit(solution)/shard_map/ppermute | solution.py:67
  182.6 14.5 %collective-permute-start.21 = (bf16[64,4096]{1,0:T(8,128)(2,1)S(1)}, bf16[64,4096]{1,0:T(8,128)(2,1)S(1)}, u32[]{:S(2)}, u32[]{:S(2)}) collective-permute-start(bf16[64,4096]{1,0:T(8,128)(2,1)S(1)} %get-tuple-element.158), channel_id=1, source_target_pairs={{0,1},{1,0},{2,3},{3,2},{4,5},{5,4},{6,7},{7,6},{8,14},{9,15},{10,... | collective-permute-start | bytes 1572872 | tf_op jit(solution)/shard_map/ppermute | solution.py:67
  198.4 19.2 %collective-permute-start.22 = (bf16[128,4096]{1,0:T(8,128)(2,1)S(1)}, bf16[128,4096]{1,0:T(8,128)(2,1)S(1)}, u32[]{:S(2)}, u32[]{:S(2)}) collective-permute-start(bf16[128,4096]{1,0:T(8,128)(2,1)S(1)} %get-tuple-element.168), channel_id=1, source_target_pairs={{0,1},{1,0},{2,3},{3,2},{4,5},{5,4},{6,7},{7,6},{8,10},{9,11},{10,... | collective-permute-start | bytes 3145736 | tf_op jit(solution)/shard_map/ppermute | solution.py:67
  198.7 25.8 %collective-permute-start.23 = (bf16[128,4096]{1,0:T(8,128)(2,1)S(1)}, bf16[128,4096]{1,0:T(8,128)(2,1)S(1)}, u32[]{:S(2)}, u32[]{:S(2)}) collective-permute-start(bf16[128,4096]{1,0:T(8,128)(2,1)S(1)} %get-tuple-element.169), channel_id=1, source_target_pairs={{0,1},{1,0},{2,3},{3,2},{4,5},{5,4},{6,7},{7,6},{8,14},{9,15},{10,... | collective-permute-start | bytes 3145736 | tf_op jit(solution)/shard_map/ppermute | solution.py:67
  200.5 15.8 %collective-permute-start.24 = (bf16[64,4096]{1,0:T(8,128)(2,1)S(1)}, bf16[64,4096]{1,0:T(8,128)(2,1)S(1)}, u32[]{:S(2)}, u32[]{:S(2)}) collective-permute-start(bf16[64,4096]{1,0:T(8,128)(2,1)S(1)} %get-tuple-element.170), channel_id=1, source_target_pairs={{0,2},{1,3},{2,4},{3,5},{4,6},{5,7},{6,0},{7,1},{8,10},{9,11},{10,... | collective-permute-start | bytes 1572872 | tf_op jit(solution)/shard_map/ppermute | solution.py:67
  201.7 15.9 %collective-permute-start.25 = (bf16[64,4096]{1,0:T(8,128)(2,1)S(1)}, bf16[64,4096]{1,0:T(8,128)(2,1)S(1)}, u32[]{:S(2)}, u32[]{:S(2)}) collective-permute-start(bf16[64,4096]{1,0:T(8,128)(2,1)S(1)} %get-tuple-element.171), channel_id=1, source_target_pairs={{0,6},{1,7},{2,0},{3,1},{4,2},{5,3},{6,4},{7,5},{8,14},{9,15},{10,... | collective-permute-start | bytes 1572872 | tf_op jit(solution)/shard_map/ppermute | solution.py:67
  227.4 21.9 %collective-permute-start.26 = (bf16[128,4096]{1,0:T(8,128)(2,1)}, bf16[128,4096]{1,0:T(8,128)(2,1)}, u32[]{:S(2)}, u32[]{:S(2)}) collective-permute-start(bf16[128,4096]{1,0:T(8,128)(2,1)} %get-tuple-element.172), channel_id=1, source_target_pairs={{0,2},{1,3},{2,4},{3,5},{4,6},{5,7},{6,0},{7,1},{8,10},{9,11},{10,... | collective-permute-start | bytes 3145736 | tf_op jit(solution)/shard_map/ppermute | solution.py:67
  228.6 22.8 %collective-permute-start.27 = (bf16[128,4096]{1,0:T(8,128)(2,1)}, bf16[128,4096]{1,0:T(8,128)(2,1)}, u32[]{:S(2)}, u32[]{:S(2)}) collective-permute-start(bf16[128,4096]{1,0:T(8,128)(2,1)} %get-tuple-element.173), channel_id=1, source_target_pairs={{0,6},{1,7},{2,0},{3,1},{4,2},{5,3},{6,4},{7,5},{8,14},{9,15},{10,... | collective-permute-start | bytes 3145736 | tf_op jit(solution)/shard_map/ppermute | solution.py:67
  230.3 21.0 %collective-permute-start.28 = (bf16[128,4096]{1,0:T(8,128)(2,1)}, bf16[128,4096]{1,0:T(8,128)(2,1)}, u32[]{:S(2)}, u32[]{:S(2)}) collective-permute-start(bf16[128,4096]{1,0:T(8,128)(2,1)} %get-tuple-element.174), channel_id=1, source_target_pairs={{0,1},{1,0},{2,3},{3,2},{4,5},{5,4},{6,7},{7,6},{8,9},{9,8},{10,11... | collective-permute-start | bytes 3145736 | tf_op jit(solution)/shard_map/ppermute | solution.py:67
  258.2 9.5 %collective-permute-start.29 = (bf16[128,2048]{1,0:T(8,128)(2,1)S(1)}, bf16[128,2048]{1,0:T(8,128)(2,1)S(1)}, u32[]{:S(2)}, u32[]{:S(2)}) collective-permute-start(bf16[128,2048]{1,0:T(8,128)(2,1)S(1)} %get-tuple-element.183.refs_5_.refs_4_.refs_14_), channel_id=1, source_target_pairs={{0,2},{1,3},{2,4},{3,5},{4,6},{5,7},{6,0},{7,1},{8,10},{9,11},{10,... | collective-permute-start | bytes 1572872 | tf_op jit(solution)/shard_map/ppermute | solution.py:67
  259.9 11.5 %collective-permute-start.30 = (bf16[128,2048]{1,0:T(8,128)(2,1)S(1)}, bf16[128,2048]{1,0:T(8,128)(2,1)S(1)}, u32[]{:S(2)}, u32[]{:S(2)}) collective-permute-start(bf16[128,2048]{1,0:T(8,128)(2,1)S(1)} %get-tuple-element.183.refs_5_.refs_4_.refs_14_), channel_id=1, source_target_pairs={{0,6},{1,7},{2,0},{3,1},{4,2},{5,3},{6,4},{7,5},{8,14},{9,15},{10,... | collective-permute-start | bytes 1572872 | tf_op jit(solution)/shard_map/ppermute | solution.py:67
  260.6 10.9 %collective-permute-start.31 = (bf16[128,2048]{1,0:T(8,128)(2,1)S(1)}, bf16[128,2048]{1,0:T(8,128)(2,1)S(1)}, u32[]{:S(2)}, u32[]{:S(2)}) collective-permute-start(bf16[128,2048]{1,0:T(8,128)(2,1)S(1)} %get-tuple-element.183.refs_5_.refs_4_.refs_14_), channel_id=1, source_target_pairs={{0,1},{1,0},{2,3},{3,2},{4,5},{5,4},{6,7},{7,6},{8,9},{9,8},{10,11... | collective-permute-start | bytes 1572872 | tf_op jit(solution)/shard_map/ppermute | solution.py:67
  271.9 11.3 %collective-permute-start.43 = (bf16[128,2048]{1,0:T(8,128)(2,1)S(1)}, bf16[128,2048]{1,0:T(8,128)(2,1)S(1)}, u32[]{:S(2)}, u32[]{:S(2)}) collective-permute-start(bf16[128,2048]{1,0:T(8,128)(2,1)S(1)} %get-tuple-element.194), channel_id=1, source_target_pairs={{0,1},{1,0},{2,3},{3,2},{4,5},{5,4},{6,7},{7,6},{8,14},{9,15},{10,... | collective-permute-start | bytes 1572872 | tf_op jit(solution)/shard_map/ppermute | solution.py:67
  272.3 14.4 %collective-permute-start.44 = (bf16[128,2048]{1,0:T(8,128)(2,1)S(1)}, bf16[128,2048]{1,0:T(8,128)(2,1)S(1)}, u32[]{:S(2)}, u32[]{:S(2)}) collective-permute-start(bf16[128,2048]{1,0:T(8,128)(2,1)S(1)} %get-tuple-element.195), channel_id=1, source_target_pairs={{0,1},{1,0},{2,3},{3,2},{4,5},{5,4},{6,7},{7,6},{8,10},{9,11},{10,... | collective-permute-start | bytes 1572872 | tf_op jit(solution)/shard_map/ppermute | solution.py:67
  287.5 8.8 %collective-permute-start.46 = (bf16[64,2048]{1,0:T(8,128)(2,1)S(1)}, bf16[64,2048]{1,0:T(8,128)(2,1)S(1)}, u32[]{:S(2)}, u32[]{:S(2)}) collective-permute-start(bf16[64,2048]{1,0:T(8,128)(2,1)S(1)} %get-tuple-element.197), channel_id=1, source_target_pairs={{0,1},{1,0},{2,3},{3,2},{4,5},{5,4},{6,7},{7,6},{8,14},{9,15},{10,... | collective-permute-start | bytes 786440 | tf_op jit(solution)/shard_map/ppermute | solution.py:67
  307.6 11.0 %collective-permute-start.47 = (bf16[64,2048]{1,0:T(8,128)(2,1)S(1)}, bf16[64,2048]{1,0:T(8,128)(2,1)S(1)}, u32[]{:S(2)}, u32[]{:S(2)}) collective-permute-start(bf16[64,2048]{1,0:T(8,128)(2,1)S(1)} %get-tuple-element.200), channel_id=1, source_target_pairs={{0,1},{1,0},{2,3},{3,2},{4,5},{5,4},{6,7},{7,6},{8,10},{9,11},{10,... | collective-permute-start | bytes 786440 | tf_op jit(solution)/shard_map/ppermute | solution.py:67
  308.1 10.5 %collective-permute-start.48 = (bf16[64,2048]{1,0:T(8,128)(2,1)S(1)}, bf16[64,2048]{1,0:T(8,128)(2,1)S(1)}, u32[]{:S(2)}, u32[]{:S(2)}) collective-permute-start(bf16[64,2048]{1,0:T(8,128)(2,1)S(1)} %get-tuple-element.201), channel_id=1, source_target_pairs={{0,1},{1,0},{2,3},{3,2},{4,5},{5,4},{6,7},{7,6},{8,14},{9,15},{10,... | collective-permute-start | bytes 786440 | tf_op jit(solution)/shard_map/ppermute | solution.py:67
  329.0 94.6 %reduce-scatter.5.cloned.1.call-start = ((), (), s32[]{:S(2)}) async-start(), calls=%async_computation.6 | async-start | bytes 9437184 | tf_op jit(solution)/shard_map/reduce_scatter | solution.py:622
  331.5 14.0 %collective-permute-start.49 = (bf16[128,2048]{1,0:T(8,128)(2,1)S(1)}, bf16[128,2048]{1,0:T(8,128)(2,1)S(1)}, u32[]{:S(2)}, u32[]{:S(2)}) collective-permute-start(bf16[128,2048]{1,0:T(8,128)(2,1)S(1)} %get-tuple-element.210), channel_id=1, source_target_pairs={{0,1},{1,0},{2,3},{3,2},{4,5},{5,4},{6,7},{7,6},{8,10},{9,11},{10,... | collective-permute-start | bytes 1572872 | tf_op jit(solution)/shard_map/ppermute | solution.py:67
  331.9 20.9 %collective-permute-start.50 = (bf16[128,2048]{1,0:T(8,128)(2,1)S(1)}, bf16[128,2048]{1,0:T(8,128)(2,1)S(1)}, u32[]{:S(2)}, u32[]{:S(2)}) collective-permute-start(bf16[128,2048]{1,0:T(8,128)(2,1)S(1)} %get-tuple-element.211), channel_id=1, source_target_pairs={{0,1},{1,0},{2,3},{3,2},{4,5},{5,4},{6,7},{7,6},{8,14},{9,15},{10,... | collective-permute-start | bytes 1572872 | tf_op jit(solution)/shard_map/ppermute | solution.py:67
  333.6 8.7 %collective-permute-start.51 = (bf16[64,2048]{1,0:T(8,128)(2,1)S(1)}, bf16[64,2048]{1,0:T(8,128)(2,1)S(1)}, u32[]{:S(2)}, u32[]{:S(2)}) collective-permute-start(bf16[64,2048]{1,0:T(8,128)(2,1)S(1)} %get-tuple-element.212), channel_id=1, source_target_pairs={{0,2},{1,3},{2,4},{3,5},{4,6},{5,7},{6,0},{7,1},{8,10},{9,11},{10,... | collective-permute-start | bytes 786440 | tf_op jit(solution)/shard_map/ppermute | solution.py:67
  335.6 9.9 %collective-permute-start.52 = (bf16[64,2048]{1,0:T(8,128)(2,1)S(1)}, bf16[64,2048]{1,0:T(8,128)(2,1)S(1)}, u32[]{:S(2)}, u32[]{:S(2)}) collective-permute-start(bf16[64,2048]{1,0:T(8,128)(2,1)S(1)} %get-tuple-element.213), channel_id=1, source_target_pairs={{0,6},{1,7},{2,0},{3,1},{4,2},{5,3},{6,4},{7,5},{8,14},{9,15},{10,... | collective-permute-start | bytes 786440 | tf_op jit(solution)/shard_map/ppermute | solution.py:67
  354.9 14.9 %collective-permute-start.53 = (bf16[128,2048]{1,0:T(8,128)(2,1)S(1)}, bf16[128,2048]{1,0:T(8,128)(2,1)S(1)}, u32[]{:S(2)}, u32[]{:S(2)}) collective-permute-start(bf16[128,2048]{1,0:T(8,128)(2,1)S(1)} %get-tuple-element.214), channel_id=1, source_target_pairs={{0,2},{1,3},{2,4},{3,5},{4,6},{5,7},{6,0},{7,1},{8,10},{9,11},{10,... | collective-permute-start | bytes 1572872 | tf_op jit(solution)/shard_map/ppermute | solution.py:67
  357.1 16.5 %collective-permute-start.54 = (bf16[128,2048]{1,0:T(8,128)(2,1)S(1)}, bf16[128,2048]{1,0:T(8,128)(2,1)S(1)}, u32[]{:S(2)}, u32[]{:S(2)}) collective-permute-start(bf16[128,2048]{1,0:T(8,128)(2,1)S(1)} %get-tuple-element.215), channel_id=1, source_target_pairs={{0,6},{1,7},{2,0},{3,1},{4,2},{5,3},{6,4},{7,5},{8,14},{9,15},{10,... | collective-permute-start | bytes 1572872 | tf_op jit(solution)/shard_map/ppermute | solution.py:67
  357.1 16.5 %collective-permute-start.55 = (bf16[128,2048]{1,0:T(8,128)(2,1)S(1)}, bf16[128,2048]{1,0:T(8,128)(2,1)S(1)}, u32[]{:S(2)}, u32[]{:S(2)}) collective-permute-start(bf16[128,2048]{1,0:T(8,128)(2,1)S(1)} %get-tuple-element.216), channel_id=1, source_target_pairs={{0,1},{1,0},{2,3},{3,2},{4,5},{5,4},{6,7},{7,6},{8,9},{9,8},{10,11... | collective-permute-start | bytes 1572872 | tf_op jit(solution)/shard_map/ppermute | solution.py:67
  357.6 27.2 %collective-permute-start.33 = (bf16[128,2048]{1,0:T(8,128)(2,1)}, bf16[128,2048]{1,0:T(8,128)(2,1)S(1)}, u32[]{:S(2)}, u32[]{:S(2)}) collective-permute-start(bf16[128,2048]{1,0:T(8,128)(2,1)} %get-tuple-element.185.refs_1_), channel_id=1, source_target_pairs={{0,6},{1,7},{2,0},{3,1},{4,2},{5,3},{6,4},{7,5},{8,14},{9,15},{10,... | collective-permute-start | bytes 1572872 | tf_op jit(solution)/shard_map/ppermute | solution.py:67
  361.9 24.6 %collective-permute-start.34 = (bf16[128,2048]{1,0:T(8,128)(2,1)}, bf16[128,2048]{1,0:T(8,128)(2,1)S(1)}, u32[]{:S(2)}, u32[]{:S(2)}) collective-permute-start(bf16[128,2048]{1,0:T(8,128)(2,1)} %get-tuple-element.185.refs_1_), channel_id=1, source_target_pairs={{0,2},{1,3},{2,4},{3,5},{4,6},{5,7},{6,0},{7,1},{8,10},{9,11},{10,... | collective-permute-start | bytes 1572872 | tf_op jit(solution)/shard_map/ppermute | solution.py:67
  369.8 16.6 %collective-permute-start.35 = (bf16[128,2048]{1,0:T(8,128)(2,1)}, bf16[128,2048]{1,0:T(8,128)(2,1)S(1)}, u32[]{:S(2)}, u32[]{:S(2)}) collective-permute-start(bf16[128,2048]{1,0:T(8,128)(2,1)} %get-tuple-element.185.refs_1_), channel_id=1, source_target_pairs={{0,1},{1,0},{2,3},{3,2},{4,5},{5,4},{6,7},{7,6},{8,9},{9,8},{10,11... | collective-permute-start | bytes 1572872 | tf_op jit(solution)/shard_map/ppermute | solution.py:67
  374.6 14.9 %collective-permute-start.56 = (bf16[128,2048]{1,0:T(8,128)(2,1)S(1)}, bf16[128,2048]{1,0:T(8,128)(2,1)S(1)}, u32[]{:S(2)}, u32[]{:S(2)}) collective-permute-start(bf16[128,2048]{1,0:T(8,128)(2,1)S(1)} %shard_map.213.refs_1_), channel_id=1, source_target_pairs={{0,1},{1,0},{2,3},{3,2},{4,5},{5,4},{6,7},{7,6},{8,9},{9,8},{10,11... | collective-permute-start | bytes 1572872 | tf_op jit(solution)/shard_map/ppermute | solution.py:67
  374.7 21.2 %collective-permute-start.57 = (bf16[128,2048]{1,0:T(8,128)(2,1)S(1)}, bf16[128,2048]{1,0:T(8,128)(2,1)S(1)}, u32[]{:S(2)}, u32[]{:S(2)}) collective-permute-start(bf16[128,2048]{1,0:T(8,128)(2,1)S(1)} %shard_map.213.refs_1_), channel_id=1, source_target_pairs={{0,6},{1,7},{2,0},{3,1},{4,2},{5,3},{6,4},{7,5},{8,14},{9,15},{10,... | collective-permute-start | bytes 1572872 | tf_op jit(solution)/shard_map/ppermute | solution.py:67
  384.9 12.1 %collective-permute-start.58 = (bf16[128,2048]{1,0:T(8,128)(2,1)S(1)}, bf16[128,2048]{1,0:T(8,128)(2,1)S(1)}, u32[]{:S(2)}, u32[]{:S(2)}) collective-permute-start(bf16[128,2048]{1,0:T(8,128)(2,1)S(1)} %shard_map.213.refs_1_), channel_id=1, source_target_pairs={{0,2},{1,3},{2,4},{3,5},{4,6},{5,7},{6,0},{7,1},{8,10},{9,11},{10,... | collective-permute-start | bytes 1572872 | tf_op jit(solution)/shard_map/ppermute | solution.py:67
  387.7 17.3 %collective-permute-start.38 = (bf16[128,2048]{1,0:T(8,128)(2,1)}, bf16[128,2048]{1,0:T(8,128)(2,1)S(1)}, u32[]{:S(2)}, u32[]{:S(2)}) collective-permute-start(bf16[128,2048]{1,0:T(8,128)(2,1)} %get-tuple-element.188), channel_id=1, source_target_pairs={{0,1},{1,0},{2,3},{3,2},{4,5},{5,4},{6,7},{7,6},{8,14},{9,15},{10,... | collective-permute-start | bytes 1572872 | tf_op jit(solution)/shard_map/ppermute | solution.py:67
  387.8 12.9 %collective-permute-start.36 = (bf16[64,2048]{1,0:T(8,128)(2,1)S(1)}, bf16[64,2048]{1,0:T(8,128)(2,1)S(1)}, u32[]{:S(2)}, u32[]{:S(2)}) collective-permute-start(bf16[64,2048]{1,0:T(8,128)(2,1)S(1)} %get-tuple-element.186), channel_id=1, source_target_pairs={{0,2},{1,3},{2,4},{3,5},{4,6},{5,7},{6,0},{7,1},{8,10},{9,11},{10,... | collective-permute-start | bytes 786440 | tf_op jit(solution)/shard_map/ppermute | solution.py:67
  389.5 20.1 %collective-permute-start.39 = (bf16[128,2048]{1,0:T(8,128)(2,1)}, bf16[128,2048]{1,0:T(8,128)(2,1)}, u32[]{:S(2)}, u32[]{:S(2)}) collective-permute-start(bf16[128,2048]{1,0:T(8,128)(2,1)} %get-tuple-element.189), channel_id=1, source_target_pairs={{0,1},{1,0},{2,3},{3,2},{4,5},{5,4},{6,7},{7,6},{8,10},{9,11},{10,... | collective-permute-start | bytes 1572872 | tf_op jit(solution)/shard_map/ppermute | solution.py:67
  395.9 9.2 %collective-permute-start.37 = (bf16[64,2048]{1,0:T(8,128)(2,1)}, bf16[64,2048]{1,0:T(8,128)(2,1)}, u32[]{:S(2)}, u32[]{:S(2)}) collective-permute-start(bf16[64,2048]{1,0:T(8,128)(2,1)} %get-tuple-element.187), channel_id=1, source_target_pairs={{0,6},{1,7},{2,0},{3,1},{4,2},{5,3},{6,4},{7,5},{8,14},{9,15},{10,... | collective-permute-start | bytes 786440 | tf_op jit(solution)/shard_map/ppermute | solution.py:67
  399.0 18.3 %collective-permute-start.59 = (bf16[128,2048]{1,0:T(8,128)(2,1)}, bf16[128,2048]{1,0:T(8,128)(2,1)}, u32[]{:S(2)}, u32[]{:S(2)}) collective-permute-start(bf16[128,2048]{1,0:T(8,128)(2,1)} %get-tuple-element.218), channel_id=1, source_target_pairs={{0,1},{1,0},{2,3},{3,2},{4,5},{5,4},{6,7},{7,6},{8,14},{9,15},{10,... | collective-permute-start | bytes 1572872 | tf_op jit(solution)/shard_map/ppermute | solution.py:67
  400.7 16.7 %collective-permute-start.62 = (bf16[128,2048]{1,0:T(8,128)(2,1)}, bf16[128,2048]{1,0:T(8,128)(2,1)}, u32[]{:S(2)}, u32[]{:S(2)}) collective-permute-start(bf16[128,2048]{1,0:T(8,128)(2,1)} %get-tuple-element.221), channel_id=1, source_target_pairs={{0,1},{1,0},{2,3},{3,2},{4,5},{5,4},{6,7},{7,6},{8,10},{9,11},{10,... | collective-permute-start | bytes 1572872 | tf_op jit(solution)/shard_map/ppermute | solution.py:67
  405.1 10.2 %collective-permute-start.60 = (bf16[64,2048]{1,0:T(8,128)(2,1)}, bf16[64,2048]{1,0:T(8,128)(2,1)}, u32[]{:S(2)}, u32[]{:S(2)}) collective-permute-start(bf16[64,2048]{1,0:T(8,128)(2,1)} %copy-done.37), channel_id=1, source_target_pairs={{0,2},{1,3},{2,4},{3,5},{4,6},{5,7},{6,0},{7,1},{8,10},{9,11},{10,... | collective-permute-start | bytes 786440 | tf_op jit(solution)/shard_map/ppermute | solution.py:67
  405.9 10.6 %collective-permute-start.61 = (bf16[64,2048]{1,0:T(8,128)(2,1)}, bf16[64,2048]{1,0:T(8,128)(2,1)}, u32[]{:S(2)}, u32[]{:S(2)}) collective-permute-start(bf16[64,2048]{1,0:T(8,128)(2,1)} %copy-done.36), channel_id=1, source_target_pairs={{0,6},{1,7},{2,0},{3,1},{4,2},{5,3},{6,4},{7,5},{8,14},{9,15},{10,... | collective-permute-start | bytes 786440 | tf_op jit(solution)/shard_map/ppermute | solution.py:67
  409.6 15.9 %collective-permute-start.65 = (bf16[128,1152]{1,0:T(8,128)(2,1)}, bf16[128,1152]{1,0:T(8,128)(2,1)}, u32[]{:S(2)}, u32[]{:S(2)}) collective-permute-start(bf16[128,1152]{1,0:T(8,128)(2,1)} %constant_dynamic-slice_fusion.1), channel_id=1, source_target_pairs={{0,64},{64,0},{1,65},{65,1},{2,66},{66,2},{3,67},{67,3},{4,68},{68... | collective-permute-start | bytes 884744 | tf_op jit(solution)/shard_map/ppermute | solution.py:627
  415.3 20.1 %collective-permute-start.40 = (bf16[64,2048]{1,0:T(8,128)(2,1)}, bf16[64,2048]{1,0:T(8,128)(2,1)}, u32[]{:S(2)}, u32[]{:S(2)}) collective-permute-start(bf16[64,2048]{1,0:T(8,128)(2,1)} %get-tuple-element.190), channel_id=1, source_target_pairs={{0,1},{1,0},{2,3},{3,2},{4,5},{5,4},{6,7},{7,6},{8,10},{9,11},{10,... | collective-permute-start | bytes 786440 | tf_op jit(solution)/shard_map/ppermute | solution.py:67
  416.5 18.9 %collective-permute-start.41 = (bf16[64,2048]{1,0:T(8,128)(2,1)}, bf16[64,2048]{1,0:T(8,128)(2,1)}, u32[]{:S(2)}, u32[]{:S(2)}) collective-permute-start(bf16[64,2048]{1,0:T(8,128)(2,1)} %get-tuple-element.191), channel_id=1, source_target_pairs={{0,1},{1,0},{2,3},{3,2},{4,5},{5,4},{6,7},{7,6},{8,14},{9,15},{10,... | collective-permute-start | bytes 786440 | tf_op jit(solution)/shard_map/ppermute | solution.py:67
  419.5 23.5 %collective-permute-start.63 = (bf16[64,2048]{1,0:T(8,128)(2,1)}, bf16[64,2048]{1,0:T(8,128)(2,1)}, u32[]{:S(2)}, u32[]{:S(2)}) collective-permute-start(bf16[64,2048]{1,0:T(8,128)(2,1)} %get-tuple-element.222), channel_id=1, source_target_pairs={{0,1},{1,0},{2,3},{3,2},{4,5},{5,4},{6,7},{7,6},{8,10},{9,11},{10,... | collective-permute-start | bytes 786440 | tf_op jit(solution)/shard_map/ppermute | solution.py:67
  420.7 22.4 %collective-permute-start.64 = (bf16[64,2048]{1,0:T(8,128)(2,1)}, bf16[64,2048]{1,0:T(8,128)(2,1)}, u32[]{:S(2)}, u32[]{:S(2)}) collective-permute-start(bf16[64,2048]{1,0:T(8,128)(2,1)} %get-tuple-element.223), channel_id=1, source_target_pairs={{0,1},{1,0},{2,3},{3,2},{4,5},{5,4},{6,7},{7,6},{8,14},{9,15},{10,... | collective-permute-start | bytes 786440 | tf_op jit(solution)/shard_map/ppermute | solution.py:67
  425.5 23.7 %collective-permute-start.66 = (bf16[128,2048]{1,0:T(8,128)(2,1)}, bf16[128,2048]{1,0:T(8,128)(2,1)}, u32[]{:S(2)}, u32[]{:S(2)}) collective-permute-start(bf16[128,2048]{1,0:T(8,128)(2,1)} %constant_dynamic-slice_fusion), channel_id=1, source_target_pairs={{0,64},{64,0},{1,65},{65,1},{2,66},{66,2},{3,67},{67,3},{4,68},{68... | collective-permute-start | bytes 1572872 | tf_op jit(solution)/shard_map/ppermute | solution.py:627
  430.4 12.6 %all-to-all-start.1 = ((f32[8,4,128]{2,1,0:T(4,128)}), f32[8,4,128]{2,1,0:T(4,128)S(1)}, u32[]{:S(2)}, u32[]{:S(2)}) async-start(f32[8,4,128]{2,1,0:T(4,128)} %broadcast_in_dim.8), calls=%async_computation.2 | async-start | bytes 32768 | tf_op jit(solution)/shard_map/all_to_all | solution.py:287
  (64 other events, 661.9 us)
Sparse Core Ops, SparseCore 0:
  72.2 48.7 all-gather.1
  329.1 39.7 reduce-scatter.2
  371.9 51.6 reduce-scatter.4
